TPU v7x, 128 devices: a whole 4x4x4 slice. The times are simulated.
128 devices in a mesh: dp: 4 (over x), vocab: 32 (over y, z, core).
Axes of the slice: x: 4, y: 4, z: 4, core: 2. Of those that a mesh axis runs over, the one named last changes fastest.
Arguments:
- hidden: bfloat16 [2048, 4096], P('dp', 'vocab'), may hold values from -100 to 100
- head_weight: bfloat16 [4096, 75968], P(None, 'vocab'), may hold values from -1 to 1
- teacher_logits: bfloat16 [2048, 75968], P(('dp', 'vocab')), may hold values from -400 to 400
- row_weight: float32 [2048], P('dp'), may hold values from 9496 to 151936
Outputs:
- kl_rows: float32 [2048], P('dp')
- grad_hidden: bfloat16 [2048, 4096], P('dp', 'vocab')
- grad_head: bfloat16 [4096, 75968], P('dp', 'vocab')
All inputs are finite; a program needn't handle non-finite values.
Results may differ from a plain program's by a relative error of at most 0.017.
Values may be sent and summed in bfloat16 or wider, within the bound.
No kernel may reach another device: no remote copies, remote signals or barrier semaphores. Data moves between devices by JAX's collectives and lax.ppermute only.
A program may use at most 192 MiB of HBM per device.

v0:
```python
import jax
import jax.numpy as jnp
from jax import lax
from jax.sharding import PartitionSpec as P


def per_device(hidden, head_weight, teacher_logits, row_weight):
    full_hidden = lax.all_gather(hidden, "vocab", axis=1, tiled=True)
    teacher_tile = lax.all_to_all(teacher_logits, "vocab", split_axis=1, concat_axis=0, tiled=True)
    student = jnp.dot(full_hidden, head_weight, preferred_element_type=jnp.float32)
    teacher = teacher_tile.astype(jnp.float32)
    student_local = jnp.max(student, axis=1)
    teacher_local = jnp.max(teacher, axis=1)
    student_peak, teacher_peak = lax.pmax((student_local, teacher_local), "vocab")
    student_exp = jnp.exp(student - student_peak[:, None])
    teacher_exp = jnp.exp(teacher - teacher_peak[:, None])
    student_total, teacher_total, teacher_cross = lax.psum(
        (
            jnp.sum(student_exp, axis=1),
            jnp.sum(teacher_exp, axis=1),
            jnp.sum(teacher_exp * (teacher - student), axis=1),
        ),
        "vocab",
    )
    kl_rows = (
        teacher_cross / teacher_total
        - teacher_peak
        - jnp.log(teacher_total)
        + student_peak
        + jnp.log(student_total)
    )
    grad_logits = (
        row_weight[:, None]
        * (student_exp / student_total[:, None] - teacher_exp / teacher_total[:, None])
    ).astype(jnp.bfloat16)
    hidden_share = lax.psum_scatter(
        lax.dot_general(
            head_weight, grad_logits, (((1,), (1,)), ((), ())), preferred_element_type=jnp.float32
        ).astype(jnp.bfloat16),
        "vocab",
        scatter_dimension=0,
        tiled=True,
    ).astype(jnp.float32)
    grad_hidden = hidden_share.T.astype(jnp.bfloat16)
    grad_head = lax.psum_scatter(
        lax.dot_general(
            full_hidden, grad_logits, (((0,), (0,)), ((), ())), preferred_element_type=jnp.float32
        ).astype(jnp.bfloat16),
        "dp",
        scatter_dimension=0,
        tiled=True,
    )
    return (kl_rows, grad_hidden, grad_head)


def solution(mesh):
    in_specs = (P("dp", "vocab"), P(None, "vocab"), P(("dp", "vocab"), None), P("dp"))
    out_specs = (P("dp"), P("dp", "vocab"), P("dp", "vocab"))
    return jax.shard_map(
        per_device, mesh=mesh, in_specs=in_specs, out_specs=out_specs, check_vma=False
    )
```

profile of v0, /device:TPU:1, one launch (start us, length us, event | category | flops | bytes accessed | tf_op | source)
XLA Modules:
  0.0 512.5 jit_solution(5222578192296835662)
XLA Ops:
  7.2 0.0 all-gather.2.cloned.1.call-start
  7.2 0.7 all-gather.2.cloned.1.call-update
  7.9 0.0 reduce-scatter.7.cloned.1.call-start
  7.9 6.5 %all_to_all.12 = bf16[16,32,2374]{2,1,0:T(8,128)(2,1)S(1)} reshape(bf16[16,75968]{1,0:T(8,128)(2,1)} %param.6) | data formatting | bytes 4861952 | tf_op jit(solution)/shard_map/all_to_all | solution.py:9
  14.4 0.7 copy.11
  15.2 43.6 %all_to_all.16 = bf16[16,32,2374]{2,0,1:T(8,128)(2,1)S(1)} all-to-all(bf16[16,32,2374]{2,0,1:T(8,128)(2,1)S(1)} %copy.11), channel_id=1, replica_groups=mesh['dp'=4,'vocab'=32] {'vocab'}, dimensions={1} | all-to-all | bytes 4861952 | tf_op jit(solution)/shard_map/all_to_all | solution.py:9
  58.8 0.4 bitcast_reduce_fusion
  59.2 0.1 reshape.25
  59.3 2.6 bitcast_convert_fusion
  61.8 5.8 %copy.12 = f32[512,2374]{0,1:T(8,128)} copy(f32[512,2374]{1,0:T(8,128)} %bitcast.16) | data formatting | bytes 9723904 | tf_op jit(solution)/shard_map/convert_element_type | solution.py:11
  67.6 9.2 %all-gather.2.cloned.1.call-done = bf16[512,4096]{1,0:T(8,128)(2,1)} async-done(((bf16[512,128]{1,0:T(8,128)(2,1)}), bf16[512,4096]{1,0:T(8,128)(2,1)}) %all-gather.2.cloned.1.call-update) | async-done | bytes 4194320 | tf_op jit(solution)/shard_map/all_gather | solution.py:8
  76.8 15.9 %fusion.3 = (f32[512]{0:T(512)S(1)}, f32[512,2374]{0,1:T(8,128)}) fusion(bf16[512,4096]{1,0:T(8,128)(2,1)} %all-gather.2.cloned.1.call-done, bf16[4096,2374]{0,1:T(8,128)(2,1)} %param.5), kind=kOutput, calls=%fused_computation.13 | convolution fusion | flops 9958492160 | bytes 28506112 | tf_op jit(solution)/shard_map/dot_general | solution.py:10
  92.7 62.3 %all-reduce.1 = (f32[512]{0:T(512)S(1)}, f32[512]{0:T(512)S(1)}) all-reduce(f32[512]{0:T(512)S(1)} %reshape.25, f32[512]{0:T(512)S(1)} %get-tuple-element.10), channel_id=1, replica_groups=mesh['dp'=4,'vocab'=32] {'vocab'}, use_global_device_ids=true, to_apply=%region_1.0 | all-reduce | flops 1024 | bytes 8192 | tf_op jit(solution)/shard_map/pmax | solution.py:14
  155.0 0.1 sub.38
  155.0 0.9 exponential_reduce_fusion
  156.0 0.1 reduce_sum.31
  156.1 0.0 copy-start
  156.1 4.7 multiply_reduce_fusion
  160.8 66.4 %all-reduce = (f32[512]{0:T(512)S(1)}, f32[512]{0:T(512)S(1)}, f32[512]{0:T(512)S(1)}) all-reduce(f32[512]{0:T(512)S(1)} %get-tuple-element.4, f32[512]{0:T(512)S(1)} %reduce_sum.31, f32[512]{0:T(512)S(1)} %get-tuple-element.3), channel_id=1, replica_groups=mesh['dp'=4,'vocab'=32] {'vocab'}, use_global_device_ids=true, to_apply=%region_9.0 | all-reduce | flops 1536 | bytes 12288 | tf_op jit(solution)/shard_map/psum | solution.py:17
  227.2 0.0 copy-done
  227.2 21.4 %fusion.1 = bf16[4096,512]{0,1:T(8,128)(2,1)} fusion(bf16[4096,2374]{0,1:T(8,128)(2,1)} %param.5, f32[512,2374]{0,1:T(8,128)} %copy.12, f32[512,2374]{0,1:T(8,128)} %get-tuple-element.11, f32[512]{0:T(512)S(1)} %get-tuple-element.6, f32[512]{0:T(512)S(1)} %get-tuple-element.5, f32[512]{0:T(512)S(1)} %copy-done, f32[512]{0:T(512)S(1)} %get-tuple-element.9, ...), kind=kOutput, calls=%fused_computation.3 | convolution fusion | flops 9967883264 | bytes 33376256 | tf_op jit(solution)/shard_map/dot_general | solution.py:37
  248.5 6.5 %copy.14 = bf16[4096,512]{1,0:T(8,128)(2,1)} copy(bf16[4096,512]{0,1:T(8,128)(2,1)} %fusion.1) | data formatting | bytes 8388608
  255.0 0.0 reduce-scatter.7.cloned.1.call-update
  255.0 0.0 reduce-scatter.5.cloned.1.call-start
  255.1 20.0 %fusion = bf16[4096,2374]{0,1:T(8,128)(2,1)} fusion(bf16[512,4096]{1,0:T(8,128)(2,1)} %all-gather.2.cloned.1.call-done, f32[512,2374]{0,1:T(8,128)} %copy.12, f32[512,2374]{0,1:T(8,128)} %get-tuple-element.11, f32[512]{0:T(512)S(1)} %get-tuple-element.6, f32[512]{0:T(512)S(1)} %get-tuple-element.5, f32[512]{0:T(512)S(1)} %copy-done, ...), kind=kOutput, calls=%fused_computation.1 | convolution fusion | flops 9975510016 | bytes 33376256 | tf_op jit(solution)/shard_map/dot_general | solution.py:46
  275.1 0.0 reduce-scatter.5.cloned.1.call-update
  275.1 0.6 log_add_fusion
  275.7 56.2 %reduce-scatter.7.cloned.1.call-done = bf16[128,512]{1,0:T(8,128)(2,1)} async-done(((bf16[4096,512]{1,0:T(8,128)(2,1)}), bf16[128,512]{1,0:T(8,128)(2,1)}) %reduce-scatter.7.cloned.1.call-update) | async-done | bytes 131088
  331.9 1.7 copy.15
  333.6 172.4 %reduce-scatter.5.cloned.1.call-done = bf16[1024,2374]{0,1:T(8,128)(2,1)} async-done(((bf16[4096,2374]{0,1:T(8,128)(2,1)}), bf16[1024,2374]{0,1:T(8,128)(2,1)}) %reduce-scatter.5.cloned.1.call-update) | async-done | bytes 4861968 | tf_op jit(solution)/shard_map/reduce_scatter | solution.py:45
Async XLA Ops:
  7.2 69.6 %all-gather.2.cloned.1.call-start = ((), (), s32[]{:S(2)}) async-start(), calls=%async_computation.3 | async-start | bytes 4325376 | tf_op jit(solution)/shard_map/all_gather | solution.py:8
  7.9 324.0 %reduce-scatter.7.cloned.1.call-start = ((), (), s32[]{:S(2)}) async-start(), calls=%async_computation.5 | async-start | bytes 4325376
  156.1 71.1 %copy-start = (f32[512]{0:T(512)S(1)}, f32[512]{0:T(512)}, u32[]{:S(2)}) copy-start(f32[512]{0:T(512)} %param.7) | copy-start | bytes 6148
  255.0 251.0 %reduce-scatter.5.cloned.1.call-start = ((), (), s32[]{:S(2)}) async-start(), calls=%async_computation.4 | async-start | bytes 24330240 | tf_op jit(solution)/shard_map/reduce_scatter | solution.py:45
Sparse Core Ops, SparseCore 0:
  10.2 66.5 all-gather.1
  255.2 76.7 reduce-scatter.6
  335.2 170.8 reduce-scatter.4
where the time goes:
time: 513 us
  waiting for transfers between devices  239 us (47%)
  blocking collectives  172 us (34%)
  matrix products  57.3 us (11%)
  local copies, waits for them, and re-layouts  21.4 us (4%)
  between operations  13.8 us (3%)
  other arithmetic  9.21 us (2%)
    reduce_scatter x1, waiting for transfers between devices, per_device(): lax.psum_scatter(lax.dot_general(full_hidden, grad_logits, (((0,), (0,)),...  172 us
    psum x1, blocking collectives, per_device(): lax.psum((jnp.sum(student_exp, axis=1), jnp.sum(teacher_exp, axis=1), jnp...  66.4 us
    pmax x1, blocking collectives, per_device(): lax.pmax((student_local, teacher_local), 'vocab')  62.3 us
    unnamed x4, waiting for transfers between devices  56.9 us
    all_to_all x1, blocking collectives, per_device(): lax.all_to_all(teacher_logits, 'vocab', split_axis=1, concat_axis=0, tile...  43.6 us
    dot_general x1, matrix products, per_device(): lax.dot_general(head_weight, grad_logits, (((1,), (1,)), ((), ())), prefe...  21.4 us
    dot_general x1, matrix products, per_device(): lax.dot_general(full_hidden, grad_logits, (((0,), (0,)), ((), ())), prefe...  20 us
    dot_general x1, matrix products, per_device(): jnp.dot(full_hidden, head_weight, preferred_element_type=jnp.float32)  15.9 us
  transfers between devices with their start and end apart: 3, of which 3 were waited for; matrix products, arithmetic and copies ran while one was open for 6% of the time, Pallas kernels for 0%

commit v1 on v0

v1 whole, which is shorter than its diff:
```python
import functools

import jax
import jax.numpy as jnp
from jax import lax
from jax.experimental import pallas as pl
from jax.experimental.pallas import tpu as pltpu
from jax.sharding import Mesh
from jax.sharding import PartitionSpec as P

F32, BF16 = jnp.float32, jnp.bfloat16
V = ("y", "z", "c")
NV = 32
VL = 2374
VP = 2432
VB = 608
NB = VP // VB
KK = 10
TC = 256
NCH = 2
D = 4096
DX = 1024
LOW = -1e30
MIB = 1 << 20


def call(body, **kw):
    flops, nbytes = kw.pop("cost")
    limit = kw.pop("limit", 60)
    return pl.pallas_call(
        body,
        compiler_params=pltpu.CompilerParams(vmem_limit_bytes=limit * MIB),
        cost_estimate=pl.CostEstimate(flops=flops // 100, bytes_accessed=nbytes // 100, transcendentals=0),
        **kw,
    )


def whole(shape):
    return pl.BlockSpec(shape, lambda *_: (0,) * len(shape))


def prep_body(t_ref, *outs):
    for i in range(NV):
        lo = VL * i
        for k in range(KK):
            pair = []
            for n in (2 * k, 2 * k + 1):
                start = lo + n * 128
                if n * 128 >= VL:
                    pair.append(jnp.zeros((16, 128), F32))
                    continue
                if start + 128 <= NV * VL:
                    pair.append(t_ref[:, start : start + 128].astype(F32))
                else:
                    last = NV * VL - 128
                    tile = t_ref[:, last : last + 128].astype(F32)
                    pair.append(pltpu.roll(tile, 128 - (start - last), axis=1))
            for c in range(NCH):
                rows = slice(8 * c, 8 * c + 8)
                outs[c][i, k] = jnp.concatenate([pair[0][rows], pair[1][rows]], axis=0).astype(BF16)


def prep(teacher):
    shape = (NV, KK, 16, 128)
    return call(
        prep_body,
        out_shape=[jax.ShapeDtypeStruct(shape, BF16)] * NCH,
        grid=(1,),
        in_specs=[whole(teacher.shape)],
        out_specs=[whole(shape)] * NCH,
        cost=(0, 5 << 20),
    )(teacher)


def student_body(first, pos, w_ref, own_ref, sib_ref, *refs):
    s_ref, m_ref, h_ref = refs[-3:]
    step = pl.program_id(0)

    @pl.when(step == 0)
    def _():
        for a in range(4):
            for b in range(4):
                j = (((pos[1] + 4 - a) % 4) * 4 + (pos[2] + 4 - b) % 4) * 2
                for ref, c in ((own_ref, pos[3]), (sib_ref, 1 - pos[3])):
                    h_ref[:, pl.ds(pl.multiple_of((j + c) * 128, 128), 128)] = ref[a, b]
        m_ref[...] = refs[0][...] if first else jnp.full_like(m_ref, LOW)

    s = lax.dot_general(w_ref[...], h_ref[...], (((1,), (1,)), ((), ())), preferred_element_type=F32)
    rows = (first + step) * VB + lax.broadcasted_iota(jnp.int32, s.shape, 0)
    s = jnp.where(rows < VL, s, LOW)
    s_ref[...] = s
    m_ref[...] = jnp.maximum(m_ref[...], jnp.max(s.reshape(VB // 8, 8, TC), axis=0))


def student_chunk(pos, wt, own, sib, first=0, steps=NB, prior=()):
    specs = [
        pl.BlockSpec((VB, D), lambda i, p: (first + i, 0)),
        whole((4, 4, TC, 128)),
        whole((4, 4, TC, 128)),
    ]
    kw = {}
    if prior:
        specs += [whole((8, TC)), pl.BlockSpec(memory_space=pl.ANY)]
        kw["input_output_aliases"] = {5: 0}
    return call(
        functools.partial(student_body, first),
        out_shape=[jax.ShapeDtypeStruct((VP, TC), F32), jax.ShapeDtypeStruct((8, TC), F32)],
        grid_spec=pltpu.PrefetchScalarGridSpec(
            num_scalar_prefetch=1,
            grid=(steps,),
            in_specs=specs,
            out_specs=[pl.BlockSpec((VB, TC), lambda i, p: (first + i, 0)), whole((8, TC))],
            scratch_shapes=[pltpu.VMEM((TC, D), BF16)],
        ),
        cost=(2 * VP * TC * D, VP * D * 2 + VP * TC * 4 + 4 * MIB),
        **kw,
    )(pos, wt, own, sib, *prior[::-1])


def stats_body(s_ref, m_ref, t_ref, tt_ref, out_ref, x_ref):
    peak = jnp.full((8, TC), LOW, F32)
    for n in range(VP // 128):
        half = t_ref[:, n // 2].astype(F32)[:, 8 * (n % 2) : 8 * (n % 2) + 8, :]
        x = half.reshape(TC, 128).T
        if (n + 1) * 128 > VL:
            rows = n * 128 + lax.broadcasted_iota(jnp.int32, x.shape, 0)
            x = jnp.where(rows < VL, x, LOW)
        x_ref[n * 128 : (n + 1) * 128, :] = x
        tt_ref[n * 128 : (n + 1) * 128, :] = x.astype(BF16)
        peak = jnp.maximum(peak, jnp.max(x.reshape(16, 8, TC), axis=0))
    t_peak = jnp.max(peak, axis=0, keepdims=True)
    s_peak = jnp.max(m_ref[...], axis=0, keepdims=True)
    zero = jnp.zeros((8, TC), F32)

    def add(n, sums):
        s_sum, t_sum, cross = sums
        rows = pl.ds(n * 64, 64)
        s, t = s_ref[rows, :], x_ref[rows, :]
        es, et = jnp.exp(s - s_peak), jnp.exp(t - t_peak)
        fold = lambda v: jnp.sum(v.reshape(8, 8, TC), axis=0)
        return s_sum + fold(es), t_sum + fold(et), cross + fold(et * (t - s))

    sums = lax.fori_loop(0, VP // 64, add, (zero, zero, zero))
    sums = [jnp.sum(v, axis=0, keepdims=True) for v in sums]
    row = lax.broadcasted_iota(jnp.int32, (8, TC), 0)
    out = jnp.zeros((8, TC), F32)
    for n, v in enumerate([s_peak, t_peak] + sums):
        out = jnp.where(row == n, v, out)
    out_ref[...] = out


def stats_chunk(s, m, t):
    return call(
        stats_body,
        out_shape=[jax.ShapeDtypeStruct((VP, TC), BF16), jax.ShapeDtypeStruct((8, TC), F32)],
        grid=(1,),
        in_specs=[whole((VP, TC)), whole((8, TC)), whole((NV, KK, 16, 128))],
        out_specs=[whole((VP, TC)), whole((8, TC))],
        scratch_shapes=[pltpu.VMEM((VP, TC), F32)],
        cost=(VP * TC * 40, 6 * MIB),
    )(s, m, t)


def merged(refs):
    if len(refs) == 1:
        v = refs[0][...]
        s_peak, t_peak = jnp.max(v[:, 0:1, :], axis=0), jnp.max(v[:, 1:2, :], axis=0)
        se, te = jnp.exp(v[:, 0:1, :] - s_peak[None]), jnp.exp(v[:, 1:2, :] - t_peak[None])
        total = lambda scale, n: jnp.sum(scale * v[:, n : n + 1, :], axis=0)
        return s_peak, t_peak, total(se, 2), total(te, 3), total(te, 4)
    get = lambda n: [r[n : n + 1, :] for r in refs]
    s_peak, t_peak = functools.reduce(jnp.maximum, get(0)), functools.reduce(jnp.maximum, get(1))
    se = [jnp.exp(p - s_peak) for p in get(0)]
    te = [jnp.exp(p - t_peak) for p in get(1)]
    total = lambda scales, n: sum(a * b for a, b in zip(scales, get(n)))
    return s_peak, t_peak, total(se, 2), total(te, 3), total(te, 4)


def merge_body(*refs):
    refs[-1][...] = jnp.zeros((8, TC), F32)
    for n, v in enumerate(merged(refs[:-1])):
        refs[-1][n : n + 1, :] = v


def merge(parts):
    shape = (8, TC)
    return call(
        merge_body,
        out_shape=jax.ShapeDtypeStruct(shape, F32),
        grid=(1,),
        in_specs=[whole(shape)] * len(parts),
        out_specs=whole(shape),
        cost=(0, 8192),
    )(*parts)


def grad_body(*refs):
    w_ref, s_ref, t_ref, *g_refs, kl_ref, c_ref = refs[-7:]

    @pl.when(pl.program_id(0) == 0)
    def _():
        s_peak, t_peak, s_tot, t_tot, cross = merged(refs[:-7])
        kl_ref[...] = cross / t_tot - t_peak - jnp.log(t_tot) + s_peak + jnp.log(s_tot)
        c_ref[0:1, :] = s_peak
        c_ref[1:2, :] = t_peak
        c_ref[2:3, :] = w_ref[...] / s_tot
        c_ref[3:4, :] = w_ref[...] / t_tot

    es = jnp.exp(s_ref[...] - c_ref[0:1, :]) * c_ref[2:3, :]
    et = jnp.exp(t_ref[...].astype(F32) - c_ref[1:2, :]) * c_ref[3:4, :]
    g = (es - et).astype(BF16)
    for half in range(2):

        @pl.when(pl.program_id(0) // (NB // 2) == half)
        def _():
            g_refs[half][...] = g


def grad_chunk(shares, w, s, t):
    block = pl.BlockSpec((VB, TC), lambda i: (i, 0))
    return call(
        grad_body,
        out_shape=[jax.ShapeDtypeStruct((VP // 2, TC), BF16)] * 2 + [jax.ShapeDtypeStruct((1, TC), F32)],
        grid=(NB,),
        in_specs=[whole(x.shape) for x in shares] + [whole((1, TC)), block, block],
        out_specs=[
            pl.BlockSpec((VB, TC), lambda i: (jnp.minimum(i, NB // 2 - 1), 0)),
            pl.BlockSpec((VB, TC), lambda i: (jnp.maximum(i - NB // 2, 0), 0)),
            whole((1, TC)),
        ],
        scratch_shapes=[pltpu.VMEM((8, TC), F32)],
        cost=(VP * TC * 30, 6 * MIB),
    )(*shares, w, s, t)


def hidden_body(pos, g0_ref, g1_ref, w_ref, mine_ref, other_ref, gt_ref):
    @pl.when(pl.program_id(0) == 0)
    def _():
        half = VP // 2
        for lo in range(0, VP, 128):
            if lo + 128 <= half:
                x = g0_ref[lo : lo + 128, :]
            elif lo >= half:
                x = g1_ref[lo - half : lo - half + 128, :]
            else:
                x = jnp.concatenate([g0_ref[lo:half, :], g1_ref[0 : lo + 128 - half, :]], axis=0)
            gt_ref[:, lo : lo + 128] = x.astype(F32).T.astype(BF16)

    p = jnp.dot(gt_ref[:, :VL], w_ref[...], preferred_element_type=F32).astype(BF16)
    even = pos[3] == 0
    for z in range(4):
        first, second = p[:, 256 * z : 256 * z + 128], p[:, 256 * z + 128 : 256 * z + 256]
        mine_ref[0, z] = jnp.where(even, first, second)
        other_ref[0, z] = jnp.where(even, second, first)


def hidden_chunk(pos, g0, g1, wt):
    out = pl.BlockSpec((1, 4, TC, 128), lambda i, p: (i, 0, 0, 0))
    return call(
        hidden_body,
        out_shape=[jax.ShapeDtypeStruct((4, 4, TC, 128), BF16)] * 2,
        grid_spec=pltpu.PrefetchScalarGridSpec(
            num_scalar_prefetch=1,
            grid=(4,),
            in_specs=[whole((VP // 2, TC))] * 2 + [pl.BlockSpec((VL, 1024), lambda i, p: (0, i))],
            out_specs=[out, out],
            scratch_shapes=[pltpu.VMEM((TC, VP), BF16)],
        ),
        cost=(2 * VP * TC * D, VP * D * 2 + 4 * MIB),
    )(pos, g0, g1, wt)


def head_body(count, pos, *refs):
    g_refs, h_ref, out_ref, k_ref = refs[:4], refs[4], refs[-2], refs[-1]

    @pl.when(pl.program_id(0) == 0)
    def _():
        for s in range(4):
            group = (pos[0] + 4 - s) % 4
            for j in range(8):
                k_ref[s * TC : (s + 1) * TC, j * 128 : (j + 1) * 128] = h_ref[group * 8 + j]

    g = jnp.concatenate([r[...] for r in g_refs], axis=1)
    total = jnp.dot(g, k_ref[...], preferred_element_type=F32)
    if count > 0:
        total = total + refs[5][...].astype(F32)
    out_ref[...] = total.astype(BF16)


def head_chunk(pos, gs, h2, c, prior=None, first=0, steps=NB, other=None):
    specs = [pl.BlockSpec((VB, TC), lambda i, p: (i, 0))] * 4
    specs.append(pl.BlockSpec((NV, TC, 128), lambda i, p: (0, c, 0)))
    args = list(gs) + [h2]
    block = pl.BlockSpec((VB, DX), lambda i, p: (i + first, 0))
    kw = {}
    if prior is not None:
        specs.append(block)
        args.append(prior)
    if other is not None:
        specs.append(pl.BlockSpec(memory_space=pl.ANY))
        args.append(other)
        kw["input_output_aliases"] = {len(args): 0}
    return call(
        functools.partial(head_body, 0 if prior is None else 1),
        out_shape=jax.ShapeDtypeStruct((VP if prior is None else VL, DX), BF16),
        grid_spec=pltpu.PrefetchScalarGridSpec(
            num_scalar_prefetch=1,
            grid=(steps,),
            in_specs=specs,
            out_specs=block,
            scratch_shapes=[pltpu.VMEM((4 * TC, DX), BF16)],
        ),
        cost=(VP * 2048 * DX, 12 * MIB),
        **kw,
    )(pos, *args)


def shift(x, axis, n):
    return lax.ppermute(x, axis, [(i, (i + n) % 4) for i in range(4)])


def swap(x):
    return lax.ppermute(x, "c", [(0, 1), (1, 0)])


def spread(x, axis):
    return [x] + [shift(x, axis, n) for n in (1, 2, 3)]


def gather_hidden(by_z):
    by_y = jnp.stack(spread(by_z, "y"))
    return by_y, swap(by_y)


def chip_sum(mine, other):
    return (mine.astype(F32) + swap(other).astype(F32)).astype(BF16)


def reduce_hidden(both):
    got = lax.all_to_all(both.reshape(16, TC, 128), ("y", "z"), 0, 0, tiled=True)
    return jnp.sum(got.astype(F32), axis=0).astype(BF16)


def after(x, *others):
    return lax.optimization_barrier((x,) + others)[0]


def per_device(hidden, head_weight, teacher_logits, row_weight):
    pos = jnp.stack([lax.axis_index(a) for a in ("x", "y", "z", "c")]).astype(jnp.int32)
    wt = head_weight.T
    rows = hidden.reshape(NV, NCH, 8, 128)
    chunks = [rows[:, c].reshape(TC, 128) for c in range(NCH)]
    weights = row_weight.reshape(NV, NCH, 8)
    weights = [weights[:, c].reshape(1, TC) for c in range(NCH)]

    both = jnp.concatenate(chunks, axis=0)
    blocks = prep(teacher_logits)
    teacher0 = lax.all_to_all(blocks[0], V, 0, 0, tiled=True)
    by_z = after(jnp.stack(spread(both, "z")), blocks[0])
    own0, sib0 = gather_hidden(by_z[:, :TC])
    own1, sib1 = gather_hidden(after(by_z[:, TC:], own0))
    s0, m0 = student_chunk(pos, wt, own0, sib0)
    teacher1 = lax.all_to_all(after(blocks[1], teacher0), V, 0, 0, tiled=True)
    t0, x = stats_chunk(after(s0, own1), m0, teacher0)
    x = merge([x, swap(x)])
    xs = spread(x, "z")
    part = student_chunk(after(pos, x), wt, own1, sib1, 0, NB // 2)
    x = merge([after(xs[0], part[1])] + xs[1:])
    xs = spread(x, "y")
    s1, m1 = student_chunk(after(pos, x), wt, own1, sib1, NB // 2, NB // 2, part)

    across = lax.ppermute(both, ("x", "y"), [(x * 4 + y, y * 4 + x) for x in range(4) for y in range(4)])
    h2 = lax.all_gather(after(across, x), V)

    *g0, kl0 = grad_chunk(xs, after(weights[0], m1), s0, t0)
    upper0 = spread(g0[0], "x")
    lower0 = spread(after(g0[1], *upper0), "x")
    t1, x = stats_chunk(after(s1, kl0), m1, teacher1)
    x = lax.all_to_all(jnp.broadcast_to(x, (NV, 8, TC)), V, 0, 0, tiled=True)
    part0 = hidden_chunk(after(pos, t1, *upper0), *g0, wt)
    sum0 = chip_sum(part0[0], after(part0[1], x))
    share0 = reduce_hidden(sum0)
    *g1, kl1 = grad_chunk([x], after(weights[1], part0[0], *lower0), s1, t1)
    upper1 = spread(g1[0], "x")
    lower1 = spread(after(g1[1], *upper1), "x")
    part1 = hidden_chunk(pos, *g1, wt)
    share1 = reduce_hidden(chip_sum(part1[0], after(part1[1], share0, *upper1)))
    head = head_chunk(after(pos, part1[0], *upper1), upper0, h2, 0, None, 0, NB // 2)
    head = head_chunk(pos, lower0, h2, 0, None, NB // 2, NB // 2, head)
    done = head_chunk(pos, upper1, h2, 1, head, 0, NB // 2)
    head = head_chunk(pos, lower1, h2, 1, head, NB // 2, NB // 2, done)
    shares, kls = [share0, share1], [kl0, kl1]

    kl_rows = jnp.stack([k.reshape(NV, 8) for k in kls], axis=1).reshape(512)
    grad_hidden = jnp.stack([s.reshape(NV, 8, 128) for s in shares], axis=1).reshape(512, 128)
    return kl_rows, grad_hidden, head.T


def solution(mesh):
    fine = Mesh(mesh.devices.reshape(4, 4, 4, 2), ("x",) + V)
    in_specs = (P("x", V), P(None, V), P(("x",) + V, None), P("x"))
    out_specs = (P("x"), P("x", V), P("x", V))
    return jax.shard_map(per_device, mesh=fine, in_specs=in_specs, out_specs=out_specs, check_vma=False)
```

time: 513 us -> 315 us (0.61)
  blocking collectives: 172 us -> 0 us
  waiting for transfers between devices: 239 us -> 90.7 us
  Pallas kernels: 0 us -> 111 us
  starting transfers between devices: 0.12 us -> 65.9 us
  matrix products: 57.3 us -> 0 us
  local copies, waits for them, and re-layouts: 21.4 us -> 16 us
    reduce_scatter x1 -> x0, waiting for transfers between devices: 172 us -> none  [per_device(): lax.psum_scatter(lax.dot_general(full_hidden, grad_logits, (((0,), (0,)),...]
    pallas_call x0 -> x16, Pallas kernels: none -> 111 us  [the longest x4 29.8 us: head_chunk(): call(functools.partial(head_body, 0 if prior is None else 1), out_shape=j...]
    ppermute x0 -> x33, waiting for transfers between devices: none -> 85.9 us  [the longest x27 81.6 us: shift(): return lax.ppermute(x, axis, [(i, (i + n) % 4) for i in range(4)])]
    psum x1 -> x0, blocking collectives: 66.4 us -> none  [per_device(): lax.psum((jnp.sum(student_exp, axis=1), jnp.sum(teacher_exp, axis=1), jnp...]
    pmax x1 -> x0, blocking collectives: 62.3 us -> none  [per_device(): lax.pmax((student_local, teacher_local), 'vocab')]
    dot_general x3 -> x0, matrix products: 57.3 us -> none  [the longest x1 21.4 us: per_device(): lax.dot_general(head_weight, grad_logits, (((1,), (1,)), ((), ())), prefe...]
    unnamed x4 -> x1, waiting for transfers between devices: 56.9 us -> 0.02 us
    all_to_all x1 -> x0, blocking collectives: 43.6 us -> none  [per_device(): lax.all_to_all(teacher_logits, 'vocab', split_axis=1, concat_axis=0, tile...]
  transfers between devices with their start and end apart: 3 -> 39, of which waited for: 3 -> 19; matrix products, arithmetic and copies ran while one was open for 6% -> 7% of each run, Pallas kernels for 0% -> 33%
where the time goes in v1:
time: 315 us; the launch traced here: 311 us
  Pallas kernels  111 us (35%)
  waiting for transfers between devices  90.7 us (29%)
  starting transfers between devices  65.9 us (21%)
  local copies, waits for them, and re-layouts  16 us (5%)
  between operations  14.3 us (5%)
  other arithmetic  13.9 us (4%)
    ppermute x27, waiting for transfers between devices, shift(): return lax.ppermute(x, axis, [(i, (i + n) % 4) for i in range(4)])  81.6 us
    pallas_call x4, Pallas kernels, head_chunk(): call(functools.partial(head_body, 0 if prior is None else 1), out_shape=j...  29.8 us
    pallas_call x3, Pallas kernels, student_chunk(): call(functools.partial(student_body, first), out_shape=[jax.ShapeDtypeStr...  28.9 us
    ppermute x27, starting transfers between devices, shift(): return lax.ppermute(x, axis, [(i, (i + n) % 4) for i in range(4)])  26.5 us
    pallas_call x2, Pallas kernels, hidden_chunk(): call(hidden_body, out_shape=[jax.ShapeDtypeStruct((4, 4, TC, 128), BF16)]...  25.6 us
    all_to_all x1, starting transfers between devices, per_device(): teacher1 = lax.all_to_all(after(blocks[1], teacher0), V, 0, 0, tiled=True)  11.3 us
    all_to_all x2, starting transfers between devices, reduce_hidden(): lax.all_to_all(both.reshape(16, TC, 128), ('y', 'z'), 0, 0, tiled=True)  10.1 us
    pallas_call x2, Pallas kernels, grad_chunk(): call(grad_body, out_shape=[jax.ShapeDtypeStruct((VP // 2, TC), BF16)] * 2...  9.63 us
  transfers between devices with their start and end apart: 39, of which 19 were waited for; matrix products, arithmetic and copies ran while one was open for 7% of the time, Pallas kernels for 33%

profile of v1, /device:TPU:1, one launch (start us, length us, event | category | flops | bytes accessed | tf_op | source)
XLA Modules:
  0.0 311.4 jit_solution(16070813685843939395)
XLA Ops:
  8.1 4.7 %collective-permute-start.2 = (bf16[512,128]{1,0:T(8,128)(2,1)S(1)}, bf16[512,128]{1,0:T(8,128)(2,1)S(1)}, u32[]{:S(2)}, u32[]{:S(2)}) collective-permute-start(bf16[512,128]{1,0:T(8,128)(2,1)S(1)} %get-tuple-element.87), channel_id=1, source_target_pairs={{0,6},{2,0},{4,2},{6,4},{1,7},{3,1},{5,3},{7,5},{8,14},{10,8},{12,... | collective-permute-start | bytes 393224 | tf_op jit(solution)/shard_map/ppermute | solution.py:319
  13.4 4.6 %shard_map.67 = (bf16[32,10,16,128]{3,2,1,0:T(8,128)(2,1)}, bf16[32,10,16,128]{3,2,1,0:T(8,128)(2,1)}) custom-call(bf16[16,75968]{1,0:T(8,128)(2,1)} %t_ref.1), custom_call_target="tpu_custom_call" | custom-call | bytes 52428 | tf_op jit(solution)/shard_map/pallas_call | solution.py:65
  18.3 3.5 %collective-permute-done = bf16[512,128]{1,0:T(8,128)(2,1)S(1)} collective-permute-done((bf16[512,128]{1,0:T(8,128)(2,1)S(1)}, bf16[512,128]{1,0:T(8,128)(2,1)S(1)}, u32[]{:S(2)}, u32[]{:S(2)}) %collective-permute-start) | collective-permute-done | bytes 131104 | tf_op jit(solution)/shard_map/ppermute | solution.py:319
  22.0 3.0 collective-permute-start.4
  25.4 2.3 collective-permute-start.5
  27.7 2.9 collective-permute-done.4
  30.6 6.8 %collective-permute-done.3 = bf16[4,256,128]{2,1,0:T(8,128)(2,1)S(1)} collective-permute-done((bf16[4,256,128]{2,1,0:T(8,128)(2,1)S(1)}, bf16[4,256,128]{2,1,0:T(8,128)(2,1)S(1)}, u32[]{:S(2)}, u32[]{:S(2)}) %collective-permute-start.3) | collective-permute-done | bytes 262176 | tf_op jit(solution)/shard_map/ppermute | solution.py:319
  38.6 2.7 collective-permute-start.9
  41.9 5.7 %all-to-all-start = ((bf16[32,10,16,128]{3,2,1,0:T(8,128)(2,1)}), bf16[32,10,16,128]{3,2,1,0:T(8,128)(2,1)S(1)}, u32[]{:S(2)}, u32[]{:S(2)}) async-start(bf16[32,10,16,128]{3,2,1,0:T(8,128)(2,1)} %get-tuple-element.42), calls=%async_computation | async-start | bytes 2621440 | tf_op jit(solution)/shard_map/all_to_all | solution.py:358
  47.9 2.9 collective-permute-done.9
  50.8 6.1 %collective-permute-done.7 = bf16[4,256,128]{2,1,0:T(8,128)(2,1)S(1)} collective-permute-done((bf16[4,256,128]{2,1,0:T(8,128)(2,1)S(1)}, bf16[4,256,128]{2,1,0:T(8,128)(2,1)S(1)}, u32[]{:S(2)}, u32[]{:S(2)}) %collective-permute-start.7) | collective-permute-done | bytes 262176 | tf_op jit(solution)/shard_map/ppermute | solution.py:319
  57.9 1.3 collective-permute-start.32
  59.8 12.6 %shard_map.68 = (f32[2432,256]{1,0:T(8,128)}, f32[8,256]{1,0:T(8,128)}) custom-call(s32[4]{0:T(128)} %pad_add_fusion.pos, bf16[2374,4096]{1,0:T(8,128)(2,1)} %bitcast.35, bf16[4,4,256,128]{3,2,1,0:T(8,128)(2,1)} %pad_maximum_fusion.own_ref, bf16[4,4,256,128]{3,2,1,0:T(8,128)(2,1)} %collective-permute-done.6.sib_ref), custom_call_target="tpu_custom_call" | custom-call | flops 51002736 | bytes 266076 | tf_op jit(solution)/shard_map/pallas_call | solution.py:105
  73.4 4.7 %shard_map.69 = (bf16[2432,256]{1,0:T(8,128)(2,1)}, f32[8,256]{1,0:T(8,128)}) custom-call(f32[2432,256]{1,0:T(8,128)} %get-tuple-element.46.s_ref.refs_5_, f32[8,256]{1,0:T(8,128)} %get-tuple-element.47.m_ref, bf16[32,10,16,128]{3,2,1,0:T(8,128)(2,1)} %copy-done.1), custom_call_target="tpu_custom_call" | custom-call | flops 249036 | bytes 62914 | tf_op jit(solution)/shard_map/pallas_call | solution.py:153
  81.0 1.3 shard_map.70.refs_0_
  82.4 1.5 collective-permute-start.12
  84.8 8.1 %shard_map.71 = (f32[2432,256]{1,0:T(8,128)}, f32[8,256]{1,0:T(8,128)}) custom-call(s32[4]{0:T(128)} %pad_add_fusion.pos, bf16[2374,4096]{1,0:T(8,128)(2,1)} %bitcast.36, bf16[4,4,256,128]{3,2,1,0:T(8,128)(2,1)} %copy-done, bf16[4,4,256,128]{3,2,1,0:T(8,128)(2,1)} %copy-done.3), custom_call_target="tpu_custom_call" | custom-call | flops 51002736 | bytes 266076 | tf_op jit(solution)/shard_map/pallas_call | solution.py:105
  94.2 1.3 shard_map.72.refs_0_
  95.5 11.3 %all-to-all-start.1 = ((bf16[32,10,16,128]{3,2,1,0:T(8,128)(2,1)}), bf16[32,10,16,128]{3,2,1,0:T(8,128)(2,1)S(1)}, u32[]{:S(2)}, u32[]{:S(2)}) async-start(bf16[32,10,16,128]{3,2,1,0:T(8,128)(2,1)} %get-tuple-element.61), calls=%async_computation.1 | async-start | bytes 2621440 | tf_op jit(solution)/shard_map/all_to_all | solution.py:363
  106.9 2.9 collective-permute-start.17
  111.7 8.2 %shard_map.73 = (f32[2432,256]{1,0:T(8,128)}, f32[8,256]{1,0:T(8,128)}) custom-call(s32[4]{0:T(128)} %pad_add_fusion.pos, bf16[2374,4096]{1,0:T(8,128)(2,1)} %bitcast.37, bf16[4,4,256,128]{3,2,1,0:T(8,128)(2,1)} %copy-done, bf16[4,4,256,128]{3,2,1,0:T(8,128)(2,1)} %copy-done.3, f32[8,256]{1,0:T(8,128)} %get-tuple-element.50.refs_0_, ...), custom_call_target="tpu_custom_call", output_to_operand_aliasing={{0}: (5, {})} | custom-call | flops 51002736 | bytes 266076 | tf_op jit(solution)/shard_map/pallas_call | solution.py:105
  119.8 5.6 %collective-permute-done.17.refs_3_ = f32[8,256]{1,0:T(8,128)S(1)} collective-permute-done((f32[8,256]{1,0:T(8,128)S(1)}, f32[8,256]{1,0:T(8,128)S(1)}, u32[]{:S(2)}, u32[]{:S(2)}) %collective-permute-start.17) | collective-permute-done | bytes 8224 | tf_op jit(solution)/shard_map/ppermute | solution.py:319
  127.2 4.7 %shard_map.74 = (bf16[1216,256]{1,0:T(8,128)(2,1)}, bf16[1216,256]{1,0:T(8,128)(2,1)}, f32[1,256]{1,0:T(1,128)}) custom-call(f32[8,256]{1,0:T(8,128)} %shard_map.72.refs_0_, f32[8,256]{1,0:T(8,128)} %copy-done.18, f32[8,256]{1,0:T(8,128)} %copy-done.17, f32[8,256]{1,0:T(8,128)} %copy-done.16, f32[1,256]{1,0:T(1,128)} %reshape_squeeze.14.refs_4_, ...), custom_call_target="tpu_custom_call" | custom-call | flops 186777 | bytes 62914 | tf_op jit(solution)/shard_map/pallas_call | solution.py:221
  134.7 4.7 %shard_map.75 = (bf16[2432,256]{1,0:T(8,128)(2,1)}, f32[8,256]{1,0:T(8,128)}) custom-call(f32[2432,256]{1,0:T(8,128)} %get-tuple-element.59.s_ref.refs_2_, f32[8,256]{1,0:T(8,128)} %get-tuple-element.54.m_ref, bf16[32,10,16,128]{3,2,1,0:T(8,128)(2,1)} %copy-done.2), custom_call_target="tpu_custom_call" | custom-call | flops 249036 | bytes 62914 | tf_op jit(solution)/shard_map/pallas_call | solution.py:153
  139.4 1.4 broadcast_in_dim.3
  140.9 7.5 %all-to-all-start.2 = ((f32[32,8,256]{2,1,0:T(8,128)}), f32[32,8,256]{2,1,0:T(8,128)S(1)}, u32[]{:S(2)}, u32[]{:S(2)}) async-start(f32[32,8,256]{2,1,0:T(8,128)} %broadcast_in_dim.3), calls=%async_computation.2 | async-start | bytes 524288 | tf_op jit(solution)/shard_map/all_to_all | solution.py:379
  148.4 14.7 %collective-permute-done.18.refs_1_ = bf16[1216,256]{1,0:T(8,128)(2,1)} collective-permute-done((bf16[1216,256]{1,0:T(8,128)(2,1)}, bf16[1216,256]{1,0:T(8,128)(2,1)}, u32[]{:S(2)}, u32[]{:S(2)}) %collective-permute-start.18) | collective-permute-done | bytes 622624 | tf_op jit(solution)/shard_map/ppermute | solution.py:319
  163.1 13.4 %shard_map.76 = (bf16[4,4,256,128]{3,2,1,0:T(8,128)(2,1)}, bf16[4,4,256,128]{3,2,1,0:T(8,128)(2,1)}) custom-call(s32[4]{0:T(128)} %pad_add_fusion.pos, bf16[1216,256]{1,0:T(8,128)(2,1)} %get-tuple-element.64.g0_ref.refs_0_, bf16[1216,256]{1,0:T(8,128)(2,1)} %get-tuple-element.68.g1_ref.refs_0_, bf16[2374,4096]{1,0:T(8,128)(2,1)} %bitcast.38), custom_call_target="tpu_custom_call" | custom-call | flops 51002736 | bytes 241172 | tf_op jit(solution)/shard_map/pallas_call | solution.py:259
  179.6 2.5 add_convert_fusion.1
  182.2 5.1 %all-to-all-start.3 = ((bf16[16,256,128]{2,1,0:T(8,128)(2,1)}), bf16[16,256,128]{2,1,0:T(8,128)(2,1)S(1)}, u32[]{:S(2)}, u32[]{:S(2)}) async-start(bf16[16,256,128]{2,1,0:T(8,128)(2,1)} %bitcast.20), calls=%async_computation.3 | async-start | bytes 2097152 | tf_op jit(solution)/shard_map/all_to_all | solution.py:340
  187.9 4.8 %collective-permute-done.23.refs_3_ = bf16[1216,256]{1,0:T(8,128)(2,1)S(1)} collective-permute-done((bf16[1216,256]{1,0:T(8,128)(2,1)S(1)}, bf16[1216,256]{1,0:T(8,128)(2,1)S(1)}, u32[]{:S(2)}, u32[]{:S(2)}) %collective-permute-start.23) | collective-permute-done | bytes 622624 | tf_op jit(solution)/shard_map/ppermute | solution.py:319
  192.7 1.9 collective-permute-done.22.refs_2_
  194.6 14.1 %collective-permute-done.21.refs_1_ = bf16[1216,256]{1,0:T(8,128)(2,1)} collective-permute-done((bf16[1216,256]{1,0:T(8,128)(2,1)S(1)}, bf16[1216,256]{1,0:T(8,128)(2,1)}, u32[]{:S(2)}, u32[]{:S(2)}) %collective-permute-start.21) | collective-permute-done | bytes 622624 | tf_op jit(solution)/shard_map/ppermute | solution.py:319
  208.7 5.0 %shard_map.77 = (bf16[1216,256]{1,0:T(8,128)(2,1)}, bf16[1216,256]{1,0:T(8,128)(2,1)}, f32[1,256]{1,0:T(1,128)}) custom-call(f32[32,8,256]{2,1,0:T(8,128)} %copy-done.6, f32[1,256]{1,0:T(1,128)} %reshape_squeeze.15.refs_1_, f32[2432,256]{1,0:T(8,128)} %get-tuple-element.59.s_ref.refs_2_, bf16[2432,256]{1,0:T(8,128)(2,1)} %get-tuple-element.63.refs_3_), custom_call_target="tpu_custom_call" | custom-call | flops 186777 | bytes 62914 | tf_op jit(solution)/shard_map/pallas_call | solution.py:221
  215.2 12.2 %shard_map.78 = (bf16[4,4,256,128]{3,2,1,0:T(8,128)(2,1)}, bf16[4,4,256,128]{3,2,1,0:T(8,128)(2,1)}) custom-call(s32[4]{0:T(128)} %pad_add_fusion.pos, bf16[1216,256]{1,0:T(8,128)(2,1)} %get-tuple-element.73.g0_ref.refs_0_, bf16[1216,256]{1,0:T(8,128)(2,1)} %get-tuple-element.78.g1_ref.refs_0_, bf16[2374,4096]{1,0:T(8,128)(2,1)} %bitcast.39), custom_call_target="tpu_custom_call" | custom-call | flops 51002736 | bytes 241172 | tf_op jit(solution)/shard_map/pallas_call | solution.py:259
  230.1 14.8 %collective-permute-done.25.refs_1_ = bf16[1216,256]{1,0:T(8,128)(2,1)} collective-permute-done((bf16[1216,256]{1,0:T(8,128)(2,1)}, bf16[1216,256]{1,0:T(8,128)(2,1)}, u32[]{:S(2)}, u32[]{:S(2)}) %collective-permute-start.25) | collective-permute-done | bytes 622624 | tf_op jit(solution)/shard_map/ppermute | solution.py:319
  245.4 2.5 collective-permute-done.28
  247.9 2.5 add_convert_fusion
  250.4 5.0 %all-to-all-start.4 = ((bf16[16,256,128]{2,1,0:T(8,128)(2,1)}), bf16[16,256,128]{2,1,0:T(8,128)(2,1)S(1)}, u32[]{:S(2)}, u32[]{:S(2)}) async-start(bf16[16,256,128]{2,1,0:T(8,128)(2,1)} %bitcast.22), calls=%async_computation.4 | async-start | bytes 2097152 | tf_op jit(solution)/shard_map/all_to_all | solution.py:340
  259.6 1.9 reduce.16
  261.5 1.4 stack_reshape.13
  264.2 1.4 reshape.26
  265.7 4.8 %all-to-all-done.4 = bf16[16,256,128]{2,1,0:T(8,128)(2,1)S(1)} async-done(((bf16[16,256,128]{2,1,0:T(8,128)(2,1)}), bf16[16,256,128]{2,1,0:T(8,128)(2,1)S(1)}, u32[]{:S(2)}, u32[]{:S(2)}) %all-to-all-start.4) | async-done | bytes 1048608 | tf_op jit(solution)/shard_map/all_to_all | solution.py:340
  271.2 1.5 pad_maximum_fusion.4
  272.8 7.3 %shard_map.79.refs_5_ = bf16[2432,1024]{1,0:T(8,128)(2,1)} custom-call(s32[4]{0:T(128)} %pad_add_fusion.pos, bf16[1216,256]{1,0:T(8,128)(2,1)} %get-tuple-element.64.g0_ref.refs_0_, bf16[1216,256]{1,0:T(8,128)(2,1)} %collective-permute-done.18.refs_1_, bf16[1216,256]{1,0:T(8,128)(2,1)} %copy-done.8, bf16[1216,256]{1,0:T(8,128)(2,1)} %copy-done.7, ...), custom_call_target="tpu_custom_call" | custom-call | flops 51002736 | bytes 125829 | tf_op jit(solution)/shard_map/pallas_call | solution.py:303
  280.1 7.3 %shard_map.80.refs_5_ = bf16[2432,1024]{1,0:T(8,128)(2,1)} custom-call(s32[4]{0:T(128)} %pad_add_fusion.pos, bf16[1216,256]{1,0:T(8,128)(2,1)} %get-tuple-element.68.g1_ref.refs_0_, bf16[1216,256]{1,0:T(8,128)(2,1)} %collective-permute-done.21.refs_1_, bf16[1216,256]{1,0:T(8,128)(2,1)} %copy-done.10, ...), custom_call_target="tpu_custom_call", output_to_operand_aliasing={{}: (6, {})} | custom-call | flops 51002736 | bytes 125829 | tf_op jit(solution)/shard_map/pallas_call | solution.py:303
  287.4 7.6 %shard_map.81.refs_6_ = bf16[2374,1024]{1,0:T(8,128)(2,1)} custom-call(s32[4]{0:T(128)} %pad_add_fusion.pos, bf16[1216,256]{1,0:T(8,128)(2,1)} %get-tuple-element.73.g0_ref.refs_0_, bf16[1216,256]{1,0:T(8,128)(2,1)} %collective-permute-done.25.refs_1_, bf16[1216,256]{1,0:T(8,128)(2,1)} %collective-permute-done.26.refs_2_, bf16[1216,256]{1,0:T(8,128)(2,1)} %copy-done.11, ...), custom_call_target="tpu_custom_call" | custom-call | flops 51002736 | bytes 125829 | tf_op jit(solution)/shard_map/pallas_call | solution.py:303
  296.9 7.6 %shard_map.82 = bf16[2374,1024]{1,0:T(8,128)(2,1)} custom-call(s32[4]{0:T(128)} %pad_add_fusion.pos, bf16[1216,256]{1,0:T(8,128)(2,1)} %get-tuple-element.78.g1_ref.refs_0_, bf16[1216,256]{1,0:T(8,128)(2,1)} %copy-done.14, bf16[1216,256]{1,0:T(8,128)(2,1)} %copy-done.13, bf16[1216,256]{1,0:T(8,128)(2,1)} %copy-done.12, ...), custom_call_target="tpu_custom_call", output_to_operand_aliasing={{}: (7, {})} | custom-call | flops 51002736 | bytes 125829 | tf_op jit(solution)/shard_map/pallas_call | solution.py:303
  (122 shorter events, 35.6 us)
Async XLA Ops:
  8.1 10.2 %collective-permute-start.2 = (bf16[512,128]{1,0:T(8,128)(2,1)S(1)}, bf16[512,128]{1,0:T(8,128)(2,1)S(1)}, u32[]{:S(2)}, u32[]{:S(2)}) collective-permute-start(bf16[512,128]{1,0:T(8,128)(2,1)S(1)} %get-tuple-element.87), channel_id=1, source_target_pairs={{0,6},{2,0},{4,2},{6,4},{1,7},{3,1},{5,3},{7,5},{8,14},{10,8},{12,... | collective-permute-start | bytes 393224 | tf_op jit(solution)/shard_map/ppermute | solution.py:319
  12.7 5.6 %collective-permute-start.1 = (bf16[512,128]{1,0:T(8,128)(2,1)S(1)}, bf16[512,128]{1,0:T(8,128)(2,1)S(1)}, u32[]{:S(2)}, u32[]{:S(2)}) collective-permute-start(bf16[512,128]{1,0:T(8,128)(2,1)S(1)} %get-tuple-element.87), channel_id=1, source_target_pairs={{0,4},{2,6},{4,0},{6,2},{1,5},{3,7},{5,1},{7,3},{8,12},{10,14},{12... | collective-permute-start | bytes 393224 | tf_op jit(solution)/shard_map/ppermute | solution.py:319
  12.7 9.1 %collective-permute-start = (bf16[512,128]{1,0:T(8,128)(2,1)S(1)}, bf16[512,128]{1,0:T(8,128)(2,1)S(1)}, u32[]{:S(2)}, u32[]{:S(2)}) collective-permute-start(bf16[512,128]{1,0:T(8,128)(2,1)S(1)} %get-tuple-element.87), channel_id=1, source_target_pairs={{0,2},{2,4},{4,6},{6,0},{1,3},{3,5},{5,7},{7,1},{8,10},{10,12},{12... | collective-permute-start | bytes 393224 | tf_op jit(solution)/shard_map/ppermute | solution.py:319
  22.0 8.6 %collective-permute-start.4 = (bf16[4,256,128]{2,1,0:T(8,128)(2,1)S(1)}, bf16[4,256,128]{2,1,0:T(8,128)(2,1)S(1)}, u32[]{:S(2)}, u32[]{:S(2)}) collective-permute-start(bf16[4,256,128]{2,1,0:T(8,128)(2,1)S(1)} %get-tuple-element.85), channel_id=1, source_target_pairs={{0,16},{8,24},{16,0},{24,8},{1,17},{9,25},{17,1},{25,9},{2,18},{10... | collective-permute-start | bytes 786440 | tf_op jit(solution)/shard_map/ppermute | solution.py:319
  25.0 12.4 %collective-permute-start.3 = (bf16[4,256,128]{2,1,0:T(8,128)(2,1)S(1)}, bf16[4,256,128]{2,1,0:T(8,128)(2,1)S(1)}, u32[]{:S(2)}, u32[]{:S(2)}) collective-permute-start(bf16[4,256,128]{2,1,0:T(8,128)(2,1)S(1)} %get-tuple-element.85), channel_id=1, source_target_pairs={{0,8},{8,16},{16,24},{24,0},{1,9},{9,17},{17,25},{25,1},{2,10},{10... | collective-permute-start | bytes 786440 | tf_op jit(solution)/shard_map/ppermute | solution.py:319
  25.4 12.0 %collective-permute-start.5 = (bf16[4,256,128]{2,1,0:T(8,128)(2,1)S(1)}, bf16[4,256,128]{2,1,0:T(8,128)(2,1)S(1)}, u32[]{:S(2)}, u32[]{:S(2)}) collective-permute-start(bf16[4,256,128]{2,1,0:T(8,128)(2,1)S(1)} %get-tuple-element.85), channel_id=1, source_target_pairs={{0,24},{8,0},{16,8},{24,16},{1,25},{9,1},{17,9},{25,17},{2,26},{10... | collective-permute-start | bytes 786440 | tf_op jit(solution)/shard_map/ppermute | solution.py:319
  38.6 12.2 %collective-permute-start.9 = (bf16[4,256,128]{2,1,0:T(8,128)(2,1)S(1)}, bf16[4,256,128]{2,1,0:T(8,128)(2,1)S(1)}, u32[]{:S(2)}, u32[]{:S(2)}) collective-permute-start(bf16[4,256,128]{2,1,0:T(8,128)(2,1)S(1)} %get-tuple-element.45), channel_id=1, source_target_pairs={{0,24},{8,0},{16,8},{24,16},{1,25},{9,1},{17,9},{25,17},{2,26},{10... | collective-permute-start | bytes 786440 | tf_op jit(solution)/shard_map/ppermute | solution.py:319
  41.3 9.5 %collective-permute-start.8 = (bf16[4,256,128]{2,1,0:T(8,128)(2,1)S(1)}, bf16[4,256,128]{2,1,0:T(8,128)(2,1)S(1)}, u32[]{:S(2)}, u32[]{:S(2)}) collective-permute-start(bf16[4,256,128]{2,1,0:T(8,128)(2,1)S(1)} %get-tuple-element.45), channel_id=1, source_target_pairs={{0,16},{8,24},{16,0},{24,8},{1,17},{9,25},{17,1},{25,9},{2,18},{10... | collective-permute-start | bytes 786440 | tf_op jit(solution)/shard_map/ppermute | solution.py:319
  41.7 15.2 %collective-permute-start.7 = (bf16[4,256,128]{2,1,0:T(8,128)(2,1)S(1)}, bf16[4,256,128]{2,1,0:T(8,128)(2,1)S(1)}, u32[]{:S(2)}, u32[]{:S(2)}) collective-permute-start(bf16[4,256,128]{2,1,0:T(8,128)(2,1)S(1)} %get-tuple-element.45), channel_id=1, source_target_pairs={{0,8},{8,16},{16,24},{24,0},{1,9},{9,17},{17,25},{25,1},{2,10},{10... | collective-permute-start | bytes 786440 | tf_op jit(solution)/shard_map/ppermute | solution.py:319
  41.9 30.5 %all-to-all-start = ((bf16[32,10,16,128]{3,2,1,0:T(8,128)(2,1)}), bf16[32,10,16,128]{3,2,1,0:T(8,128)(2,1)S(1)}, u32[]{:S(2)}, u32[]{:S(2)}) async-start(bf16[32,10,16,128]{3,2,1,0:T(8,128)(2,1)} %get-tuple-element.42), calls=%async_computation | async-start | bytes 2621440 | tf_op jit(solution)/shard_map/all_to_all | solution.py:358
  47.6 225.2 %all-gather.3.cloned.1.call-start = ((), (), s32[]{:S(2)}) async-start(), calls=%async_computation.5 | async-start | bytes 4325376 | tf_op jit(solution)/shard_map/all_gather | solution.py:373
  47.6 12.2 %collective-permute-start.6 = (bf16[4,4,256,128]{3,2,1,0:T(8,128)(2,1)}, bf16[4,4,256,128]{3,2,1,0:T(8,128)(2,1)}, u32[]{:S(2)}, u32[]{:S(2)}) collective-permute-start(bf16[4,4,256,128]{3,2,1,0:T(8,128)(2,1)} %pad_maximum_fusion.own_ref), channel_id=1, source_target_pairs={{0,1},{1,0},{2,3},{3,2},{4,5},{5,4},{6,7},{7,6},{8,9},{9,8},{10,11... | collective-permute-start | bytes 3145736 | tf_op jit(solution)/shard_map/ppermute | solution.py:323
  57.0 15.3 %copy-start = (bf16[4,4,256,128]{3,2,1,0:T(8,128)(2,1)}, bf16[4,4,256,128]{3,2,1,0:T(8,128)(2,1)S(1)}, u32[]{:S(2)}) copy-start(bf16[4,4,256,128]{3,2,1,0:T(8,128)(2,1)S(1)} %pad_maximum_fusion.1.own_ref) | copy-start | bytes 3145732
  57.1 26.8 %collective-permute-start.11 = (bf16[4,4,256,128]{3,2,1,0:T(8,128)(2,1)S(1)}, bf16[4,4,256,128]{3,2,1,0:T(8,128)(2,1)S(1)}, u32[]{:S(2)}, u32[]{:S(2)}) collective-permute-start(bf16[4,4,256,128]{3,2,1,0:T(8,128)(2,1)S(1)} %pad_maximum_fusion.1.own_ref), channel_id=1, source_target_pairs={{0,1},{1,0},{2,3},{3,2},{4,5},{5,4},{6,7},{7,6},{8,9},{9,8},{10,11... | collective-permute-start | bytes 3145736 | tf_op jit(solution)/shard_map/ppermute | solution.py:323
  57.9 37.6 %collective-permute-start.32 = (bf16[512,128]{1,0:T(8,128)(2,1)S(1)}, bf16[512,128]{1,0:T(8,128)(2,1)}, u32[]{:S(2)}, u32[]{:S(2)}) collective-permute-start(bf16[512,128]{1,0:T(8,128)(2,1)S(1)} %get-tuple-element.87), channel_id=1, source_target_pairs={{0,0},{8,32},{16,64},{24,96},{32,8},{40,40},{48,72},{56,104},{64,1... | collective-permute-start | bytes 393224 | tf_op jit(solution)/shard_map/ppermute | solution.py:372
  78.1 2.3 collective-permute-start.10
  82.4 10.6 %collective-permute-start.14 = (f32[8,256]{1,0:T(8,128)}, f32[8,256]{1,0:T(8,128)S(1)}, u32[]{:S(2)}, u32[]{:S(2)}) collective-permute-start(f32[8,256]{1,0:T(8,128)} %shard_map.70.refs_0_), channel_id=1, source_target_pairs={{0,6},{2,0},{4,2},{6,4},{1,7},{3,1},{5,3},{7,5},{8,14},{10,8},{12,... | collective-permute-start | bytes 24584 | tf_op jit(solution)/shard_map/ppermute | solution.py:319
  82.4 10.6 %collective-permute-start.13 = (f32[8,256]{1,0:T(8,128)}, f32[8,256]{1,0:T(8,128)S(1)}, u32[]{:S(2)}, u32[]{:S(2)}) collective-permute-start(f32[8,256]{1,0:T(8,128)} %shard_map.70.refs_0_), channel_id=1, source_target_pairs={{0,4},{2,6},{4,0},{6,2},{1,5},{3,7},{5,1},{7,3},{8,12},{10,14},{12... | collective-permute-start | bytes 24584 | tf_op jit(solution)/shard_map/ppermute | solution.py:319
  82.4 10.6 %collective-permute-start.12 = (f32[8,256]{1,0:T(8,128)}, f32[8,256]{1,0:T(8,128)S(1)}, u32[]{:S(2)}, u32[]{:S(2)}) collective-permute-start(f32[8,256]{1,0:T(8,128)} %shard_map.70.refs_0_), channel_id=1, source_target_pairs={{0,2},{2,4},{4,6},{6,0},{1,3},{3,5},{5,7},{7,1},{8,10},{10,12},{12... | collective-permute-start | bytes 24584 | tf_op jit(solution)/shard_map/ppermute | solution.py:319
  92.9 13.9 %copy-start.23 = (f32[512]{0:T(512)S(1)}, f32[512]{0:T(512)}, u32[]{:S(2)}) copy-start(f32[512]{0:T(512)} %param.7) | copy-start | bytes 6148
  95.5 11.4 %copy-start.15 = (f32[8,256]{1,0:T(8,128)S(1)}, f32[8,256]{1,0:T(8,128)}, u32[]{:S(2)}) copy-start(f32[8,256]{1,0:T(8,128)} %shard_map.72.refs_0_) | copy-start | bytes 24580
  95.5 38.1 %all-to-all-start.1 = ((bf16[32,10,16,128]{3,2,1,0:T(8,128)(2,1)}), bf16[32,10,16,128]{3,2,1,0:T(8,128)(2,1)S(1)}, u32[]{:S(2)}, u32[]{:S(2)}) async-start(bf16[32,10,16,128]{3,2,1,0:T(8,128)(2,1)} %get-tuple-element.61), calls=%async_computation.1 | async-start | bytes 2621440 | tf_op jit(solution)/shard_map/all_to_all | solution.py:363
  106.9 18.5 %collective-permute-start.17 = (f32[8,256]{1,0:T(8,128)S(1)}, f32[8,256]{1,0:T(8,128)S(1)}, u32[]{:S(2)}, u32[]{:S(2)}) collective-permute-start(f32[8,256]{1,0:T(8,128)S(1)} %copy-done.15), channel_id=1, source_target_pairs={{0,24},{8,0},{16,8},{24,16},{1,25},{9,1},{17,9},{25,17},{2,26},{10... | collective-permute-start | bytes 24584 | tf_op jit(solution)/shard_map/ppermute | solution.py:319
  109.8 16.8 %collective-permute-start.16 = (f32[8,256]{1,0:T(8,128)S(1)}, f32[8,256]{1,0:T(8,128)S(1)}, u32[]{:S(2)}, u32[]{:S(2)}) collective-permute-start(f32[8,256]{1,0:T(8,128)S(1)} %copy-done.15), channel_id=1, source_target_pairs={{0,16},{8,24},{16,0},{24,8},{1,17},{9,25},{17,1},{25,9},{2,18},{10... | collective-permute-start | bytes 24584 | tf_op jit(solution)/shard_map/ppermute | solution.py:319
  110.4 16.3 %collective-permute-start.15 = (f32[8,256]{1,0:T(8,128)S(1)}, f32[8,256]{1,0:T(8,128)S(1)}, u32[]{:S(2)}, u32[]{:S(2)}) collective-permute-start(f32[8,256]{1,0:T(8,128)S(1)} %copy-done.15), channel_id=1, source_target_pairs={{0,8},{8,16},{16,24},{24,0},{1,9},{9,17},{17,25},{25,1},{2,10},{10... | collective-permute-start | bytes 24584 | tf_op jit(solution)/shard_map/ppermute | solution.py:319
  131.9 16.5 %collective-permute-start.20 = (bf16[1216,256]{1,0:T(8,128)(2,1)}, bf16[1216,256]{1,0:T(8,128)(2,1)S(1)}, u32[]{:S(2)}, u32[]{:S(2)}) collective-permute-start(bf16[1216,256]{1,0:T(8,128)(2,1)} %get-tuple-element.64.g0_ref.refs_0_), channel_id=1, source_target_pairs={{0,96},{32,0},{64,32},{96,64},{1,97},{33,1},{65,33},{97,65},{2,98}... | collective-permute-start | bytes 1867784 | tf_op jit(solution)/shard_map/ppermute | solution.py:319
  132.0 16.4 %collective-permute-start.19 = (bf16[1216,256]{1,0:T(8,128)(2,1)}, bf16[1216,256]{1,0:T(8,128)(2,1)S(1)}, u32[]{:S(2)}, u32[]{:S(2)}) collective-permute-start(bf16[1216,256]{1,0:T(8,128)(2,1)} %get-tuple-element.64.g0_ref.refs_0_), channel_id=1, source_target_pairs={{0,64},{32,96},{64,0},{96,32},{1,65},{33,97},{65,1},{97,33},{2,66}... | collective-permute-start | bytes 1867784 | tf_op jit(solution)/shard_map/ppermute | solution.py:319
  133.0 30.2 %collective-permute-start.18 = (bf16[1216,256]{1,0:T(8,128)(2,1)}, bf16[1216,256]{1,0:T(8,128)(2,1)}, u32[]{:S(2)}, u32[]{:S(2)}) collective-permute-start(bf16[1216,256]{1,0:T(8,128)(2,1)} %get-tuple-element.64.g0_ref.refs_0_), channel_id=1, source_target_pairs={{0,32},{32,64},{64,96},{96,0},{1,33},{33,65},{65,97},{97,1},{2,34}... | collective-permute-start | bytes 1867784 | tf_op jit(solution)/shard_map/ppermute | solution.py:319
  140.9 35.7 %all-to-all-start.2 = ((f32[32,8,256]{2,1,0:T(8,128)}), f32[32,8,256]{2,1,0:T(8,128)S(1)}, u32[]{:S(2)}, u32[]{:S(2)}) async-start(f32[32,8,256]{2,1,0:T(8,128)} %broadcast_in_dim.3), calls=%async_computation.2 | async-start | bytes 524288 | tf_op jit(solution)/shard_map/all_to_all | solution.py:379
  148.4 28.1 %copy-start.7 = (bf16[1216,256]{1,0:T(8,128)(2,1)}, bf16[1216,256]{1,0:T(8,128)(2,1)S(1)}, u32[]{:S(2)}) copy-start(bf16[1216,256]{1,0:T(8,128)(2,1)S(1)} %collective-permute-done.20.refs_3_) | copy-start | bytes 1867780
  148.4 28.1 %copy-start.8 = (bf16[1216,256]{1,0:T(8,128)(2,1)}, bf16[1216,256]{1,0:T(8,128)(2,1)S(1)}, u32[]{:S(2)}) copy-start(bf16[1216,256]{1,0:T(8,128)(2,1)S(1)} %collective-permute-done.19.refs_2_) | copy-start | bytes 1867780
  163.1 14.0 %copy-start.4 = (bf16[1216,256]{1,0:T(8,128)(2,1)S(1)}, bf16[1216,256]{1,0:T(8,128)(2,1)}, u32[]{:S(2)}) copy-start(bf16[1216,256]{1,0:T(8,128)(2,1)} %get-tuple-element.68.g1_ref.refs_0_) | copy-start | bytes 1867780
  176.6 3.1 collective-permute-start.24
  177.1 15.6 %collective-permute-start.23 = (bf16[1216,256]{1,0:T(8,128)(2,1)S(1)}, bf16[1216,256]{1,0:T(8,128)(2,1)S(1)}, u32[]{:S(2)}, u32[]{:S(2)}) collective-permute-start(bf16[1216,256]{1,0:T(8,128)(2,1)S(1)} %copy-done.4), channel_id=1, source_target_pairs={{0,96},{32,0},{64,32},{96,64},{1,97},{33,1},{65,33},{97,65},{2,98}... | collective-permute-start | bytes 1867784 | tf_op jit(solution)/shard_map/ppermute | solution.py:319
  177.8 16.8 %collective-permute-start.22 = (bf16[1216,256]{1,0:T(8,128)(2,1)S(1)}, bf16[1216,256]{1,0:T(8,128)(2,1)S(1)}, u32[]{:S(2)}, u32[]{:S(2)}) collective-permute-start(bf16[1216,256]{1,0:T(8,128)(2,1)S(1)} %copy-done.4), channel_id=1, source_target_pairs={{0,64},{32,96},{64,0},{96,32},{1,65},{33,97},{65,1},{97,33},{2,66}... | collective-permute-start | bytes 1867784 | tf_op jit(solution)/shard_map/ppermute | solution.py:319
  178.4 30.3 %collective-permute-start.21 = (bf16[1216,256]{1,0:T(8,128)(2,1)S(1)}, bf16[1216,256]{1,0:T(8,128)(2,1)}, u32[]{:S(2)}, u32[]{:S(2)}) collective-permute-start(bf16[1216,256]{1,0:T(8,128)(2,1)S(1)} %copy-done.4), channel_id=1, source_target_pairs={{0,32},{32,64},{64,96},{96,0},{1,33},{33,65},{65,97},{97,1},{2,34}... | collective-permute-start | bytes 1867784 | tf_op jit(solution)/shard_map/ppermute | solution.py:319
  182.2 45.2 %all-to-all-start.3 = ((bf16[16,256,128]{2,1,0:T(8,128)(2,1)}), bf16[16,256,128]{2,1,0:T(8,128)(2,1)S(1)}, u32[]{:S(2)}, u32[]{:S(2)}) async-start(bf16[16,256,128]{2,1,0:T(8,128)(2,1)} %bitcast.20), calls=%async_computation.3 | async-start | bytes 2097152 | tf_op jit(solution)/shard_map/all_to_all | solution.py:340
  192.7 34.6 %copy-start.9 = (bf16[1216,256]{1,0:T(8,128)(2,1)}, bf16[1216,256]{1,0:T(8,128)(2,1)S(1)}, u32[]{:S(2)}) copy-start(bf16[1216,256]{1,0:T(8,128)(2,1)S(1)} %collective-permute-done.23.refs_3_) | copy-start | bytes 1867780
  194.6 32.7 %copy-start.10 = (bf16[1216,256]{1,0:T(8,128)(2,1)}, bf16[1216,256]{1,0:T(8,128)(2,1)S(1)}, u32[]{:S(2)}) copy-start(bf16[1216,256]{1,0:T(8,128)(2,1)S(1)} %collective-permute-done.22.refs_2_) | copy-start | bytes 1867780
  213.7 15.4 %collective-permute-start.27 = (bf16[1216,256]{1,0:T(8,128)(2,1)}, bf16[1216,256]{1,0:T(8,128)(2,1)S(1)}, u32[]{:S(2)}, u32[]{:S(2)}) collective-permute-start(bf16[1216,256]{1,0:T(8,128)(2,1)} %get-tuple-element.73.g0_ref.refs_0_), channel_id=1, source_target_pairs={{0,96},{32,0},{64,32},{96,64},{1,97},{33,1},{65,33},{97,65},{2,98}... | collective-permute-start | bytes 1867784 | tf_op jit(solution)/shard_map/ppermute | solution.py:319
  213.7 16.4 %collective-permute-start.26 = (bf16[1216,256]{1,0:T(8,128)(2,1)}, bf16[1216,256]{1,0:T(8,128)(2,1)}, u32[]{:S(2)}, u32[]{:S(2)}) collective-permute-start(bf16[1216,256]{1,0:T(8,128)(2,1)} %get-tuple-element.73.g0_ref.refs_0_), channel_id=1, source_target_pairs={{0,64},{32,96},{64,0},{96,32},{1,65},{33,97},{65,1},{97,33},{2,66}... | collective-permute-start | bytes 1867784 | tf_op jit(solution)/shard_map/ppermute | solution.py:319
  214.4 30.5 %collective-permute-start.25 = (bf16[1216,256]{1,0:T(8,128)(2,1)}, bf16[1216,256]{1,0:T(8,128)(2,1)}, u32[]{:S(2)}, u32[]{:S(2)}) collective-permute-start(bf16[1216,256]{1,0:T(8,128)(2,1)} %get-tuple-element.73.g0_ref.refs_0_), channel_id=1, source_target_pairs={{0,32},{32,64},{64,96},{96,0},{1,33},{33,65},{65,97},{97,1},{2,34}... | collective-permute-start | bytes 1867784 | tf_op jit(solution)/shard_map/ppermute | solution.py:319
  229.1 18.8 %copy-start.11 = (bf16[1216,256]{1,0:T(8,128)(2,1)}, bf16[1216,256]{1,0:T(8,128)(2,1)S(1)}, u32[]{:S(2)}) copy-start(bf16[1216,256]{1,0:T(8,128)(2,1)S(1)} %collective-permute-done.27.refs_3_) | copy-start | bytes 1867780
  244.9 3.0 collective-permute-start.28
  250.4 20.0 %all-to-all-start.4 = ((bf16[16,256,128]{2,1,0:T(8,128)(2,1)}), bf16[16,256,128]{2,1,0:T(8,128)(2,1)S(1)}, u32[]{:S(2)}, u32[]{:S(2)}) async-start(bf16[16,256,128]{2,1,0:T(8,128)(2,1)} %bitcast.22), calls=%async_computation.4 | async-start | bytes 2097152 | tf_op jit(solution)/shard_map/all_to_all | solution.py:340
  255.5 39.5 %collective-permute-start.31 = (bf16[1216,256]{1,0:T(8,128)(2,1)S(1)}, bf16[1216,256]{1,0:T(8,128)(2,1)S(1)}, u32[]{:S(2)}, u32[]{:S(2)}) collective-permute-start(bf16[1216,256]{1,0:T(8,128)(2,1)S(1)} %copy-done.5), channel_id=1, source_target_pairs={{0,96},{32,0},{64,32},{96,64},{1,97},{33,1},{65,33},{97,65},{2,98}... | collective-permute-start | bytes 1867784 | tf_op jit(solution)/shard_map/ppermute | solution.py:319
  256.3 38.8 %collective-permute-start.30 = (bf16[1216,256]{1,0:T(8,128)(2,1)S(1)}, bf16[1216,256]{1,0:T(8,128)(2,1)S(1)}, u32[]{:S(2)}, u32[]{:S(2)}) collective-permute-start(bf16[1216,256]{1,0:T(8,128)(2,1)S(1)} %copy-done.5), channel_id=1, source_target_pairs={{0,64},{32,96},{64,0},{96,32},{1,65},{33,97},{65,1},{97,33},{2,66}... | collective-permute-start | bytes 1867784 | tf_op jit(solution)/shard_map/ppermute | solution.py:319
  256.6 38.5 %collective-permute-start.29 = (bf16[1216,256]{1,0:T(8,128)(2,1)S(1)}, bf16[1216,256]{1,0:T(8,128)(2,1)S(1)}, u32[]{:S(2)}, u32[]{:S(2)}) collective-permute-start(bf16[1216,256]{1,0:T(8,128)(2,1)S(1)} %copy-done.5), channel_id=1, source_target_pairs={{0,32},{32,64},{64,96},{96,0},{1,33},{33,65},{65,97},{97,1},{2,34}... | collective-permute-start | bytes 1867784 | tf_op jit(solution)/shard_map/ppermute | solution.py:319
  (16 other events, 33.5 us)
Sparse Core Ops, SparseCore 0:
  95.6 55.8 all-gather.2

commit v2 on v0

v2 whole, which is shorter than its diff:
```python
import functools

import jax
import jax.numpy as jnp
from jax import lax
from jax.experimental import pallas as pl
from jax.experimental.pallas import tpu as pltpu
from jax.sharding import Mesh
from jax.sharding import PartitionSpec as P

F32, BF16 = jnp.float32, jnp.bfloat16
V = ("y", "z", "c")
NV = 32
VL = 2374
KT = 19
SB = 512
NS = 5
GB = 608
VP = 2432
CUTS = ((0, 2), (2, 1), (3, 1))
T = 512
D = 4096
DX = 1024
LOW = -1e30
MIB = 1 << 20


def call(body, limit=60, **kw):
    return pl.pallas_call(
        body,
        compiler_params=pltpu.CompilerParams(vmem_limit_bytes=limit * MIB),
        cost_estimate=pl.CostEstimate(flops=1 << 20, bytes_accessed=1 << 16, transcendentals=0),
        **kw,
    )


def whole(shape):
    return pl.BlockSpec(shape, lambda *_: (0,) * len(shape))


def prep_body(t_ref, out_ref):
    end = NV * VL
    for i in range(NV):
        for k in range(KT):
            start = VL * i + 128 * k
            if start + 128 <= end:
                out_ref[i, k] = t_ref[:, start : start + 128]
            else:
                tile = t_ref[:, end - 128 : end].astype(F32)
                out_ref[i, k] = pltpu.roll(tile, end - start, axis=1).astype(BF16)


def prep(teacher):
    shape = (NV, KT, 16, 128)
    return call(
        prep_body,
        out_shape=jax.ShapeDtypeStruct(shape, BF16),
        grid=(1,),
        in_specs=[whole(teacher.shape)],
        out_specs=whole(shape),
    )(teacher)


def fold(x, op):
    return op(x.reshape(-1, 8, T), axis=0)


def student_body(pos, w_ref, own_ref, sib_ref, s_ref, m_ref, l_ref, h_ref):
    step = pl.program_id(0)

    @pl.when(step == 0)
    def _():
        for a in range(4):
            for b in range(4):
                for ref, c in ((own_ref, pos[3]), (sib_ref, 1 - pos[3])):
                    y = (pos[1] + 4 - jnp.where(c == 0, a, b)) % 4
                    z = (pos[2] + 4 - jnp.where(c == 0, b, a)) % 4
                    at = pl.multiple_of(((y * 4 + z) * 2 + c) * 128, 128)
                    h_ref[:, pl.ds(at, 128)] = ref[a, b]
        m_ref[...] = jnp.full_like(m_ref, LOW)
        l_ref[...] = jnp.zeros_like(l_ref)

    s = lax.dot_general(w_ref[...], h_ref[...], (((1,), (1,)), ((), ())), preferred_element_type=F32)
    rows = step * SB + lax.broadcasted_iota(jnp.int32, s.shape, 0)
    s = jnp.where(rows < VL, s, LOW)
    s_ref[...] = s
    old = m_ref[...]
    peak = jnp.maximum(old, fold(s, jnp.max))
    m_ref[...] = peak
    es = jnp.exp(s.reshape(-1, 8, T) - peak[None])
    l_ref[...] = l_ref[...] * jnp.exp(old - peak) + jnp.sum(es, axis=0)


def student(pos, wt, own, sib):
    part = jax.ShapeDtypeStruct((8, T), F32)
    return call(
        student_body,
        out_shape=[jax.ShapeDtypeStruct((NS * SB, T), F32), part, part],
        grid_spec=pltpu.PrefetchScalarGridSpec(
            num_scalar_prefetch=1,
            grid=(NS,),
            in_specs=[
                pl.BlockSpec((SB, D), lambda i, p: (i, 0)),
                whole((4, 4, T, 128)),
                whole((4, 4, T, 128)),
            ],
            out_specs=[pl.BlockSpec((SB, T), lambda i, p: (i, 0)), whole((8, T)), whole((8, T))],
            scratch_shapes=[pltpu.VMEM((T, D), BF16)],
        ),
    )(pos, wt, own, sib)


def stats_body(m_ref, l_ref, s_ref, t_ref, tt_ref, out_ref, p_ref, sum_ref, cross_ref):
    step = pl.program_id(0)

    @pl.when(step == 0)
    def _():
        p_ref[...] = jnp.full_like(p_ref, LOW)
        sum_ref[...] = jnp.zeros_like(sum_ref)
        cross_ref[...] = jnp.zeros_like(cross_ref)

    for n in range(SB // 128):

        @pl.when(step * (SB // 128) + n < KT)
        def _():
            t = t_ref[:, n].reshape(T, 128).astype(F32).T
            rows = step * SB + n * 128 + lax.broadcasted_iota(jnp.int32, t.shape, 0)
            t = jnp.where(rows < VL, t, LOW)
            tt_ref[n * 128 : (n + 1) * 128, :] = t.astype(BF16)
            old = p_ref[...]
            peak = jnp.maximum(old, fold(t, jnp.max))
            p_ref[...] = peak
            scale = jnp.exp(old - peak)
            t = t.reshape(-1, 8, T)
            et = jnp.exp(t - peak[None])
            s = s_ref[n * 128 : (n + 1) * 128, :].reshape(-1, 8, T)
            sum_ref[...] = sum_ref[...] * scale + jnp.sum(et, axis=0)
            cross_ref[...] = cross_ref[...] * scale + jnp.sum(et * (t - s), axis=0)

    @pl.when(step == NS - 1)
    def _():
        s_peak = jnp.max(m_ref[...], axis=0, keepdims=True)
        t_peak = jnp.max(p_ref[...], axis=0, keepdims=True)
        se, te = jnp.exp(m_ref[...] - s_peak), jnp.exp(p_ref[...] - t_peak)
        total = lambda scale, ref: jnp.sum(scale * ref[...], axis=0, keepdims=True)
        values = [s_peak, t_peak, total(se, l_ref), total(te, sum_ref), total(te, cross_ref)]
        row = lax.broadcasted_iota(jnp.int32, (8, T), 0)
        out = jnp.zeros((8, T), F32)
        for n, v in enumerate(values):
            out = jnp.where(row == n, v, out)
        for i in range(NV):
            out_ref[i] = out


def stats(m, l, s, t):
    block = pl.BlockSpec((SB, T), lambda i: (i, 0))
    return call(
        stats_body,
        out_shape=[jax.ShapeDtypeStruct((NS * SB, T), BF16), jax.ShapeDtypeStruct((NV, 8, T), F32)],
        grid=(NS,),
        in_specs=[
            whole((8, T)),
            whole((8, T)),
            block,
            pl.BlockSpec((NV, SB // 128, 16, 128), lambda i: (0, i, 0, 0)),
        ],
        out_specs=[block, whole((NV, 8, T))],
        scratch_shapes=[pltpu.VMEM((8, T), F32)] * 3,
    )(m, l, s, t)


def grad_body(all_ref, w_ref, s_ref, t_ref, *refs):
    kl_ref, c_ref = refs[-2:]
    step = pl.program_id(0)

    @pl.when(step == 0)
    def _():
        v = all_ref[...]
        s_peak, t_peak = jnp.max(v[:, 0:1, :], axis=0), jnp.max(v[:, 1:2, :], axis=0)
        se, te = jnp.exp(v[:, 0:1, :] - s_peak[None]), jnp.exp(v[:, 1:2, :] - t_peak[None])
        total = lambda scale, n: jnp.sum(scale * v[:, n : n + 1, :], axis=0)
        s_tot, t_tot, cross = total(se, 2), total(te, 3), total(te, 4)
        kl_ref[...] = cross / t_tot - t_peak - jnp.log(t_tot) + s_peak + jnp.log(s_tot)
        c_ref[0:1, :] = s_peak
        c_ref[1:2, :] = t_peak
        c_ref[2:3, :] = w_ref[...] / s_tot
        c_ref[3:4, :] = w_ref[...] / t_tot

    es = jnp.exp(s_ref[...] - c_ref[0:1, :]) * c_ref[2:3, :]
    et = jnp.exp(t_ref[...].astype(F32) - c_ref[1:2, :]) * c_ref[3:4, :]
    g = (es - et).astype(BF16)

    for (first, steps), g_ref in zip(CUTS, refs):

        @pl.when((step >= first) & (step < first + steps))
        def _():
            g_ref[...] = g


def piece(first, steps):
    return pl.BlockSpec((GB, T), lambda i: (jnp.clip(i - first, 0, steps - 1), 0))


def grad(gathered, w, s, t):
    block = pl.BlockSpec((GB, T), lambda i: (i, 0))
    return call(
        grad_body,
        out_shape=[jax.ShapeDtypeStruct((n * GB, T), BF16) for _, n in CUTS] + [jax.ShapeDtypeStruct((1, T), F32)],
        grid=(VP // GB,),
        in_specs=[whole((NV, 8, T)), whole((1, T)), block, block],
        out_specs=[piece(*cut) for cut in CUTS] + [whole((1, T))],
        scratch_shapes=[pltpu.VMEM((8, T), F32)],
    )(gathered, w, s, t)


def hidden_body(pos, *refs):
    g_refs, (w_ref, mine_ref, other_ref, gt_ref) = refs[: len(CUTS)], refs[len(CUTS) :]

    @pl.when(pl.program_id(0) == 0)
    def _():
        for lo in range(0, VP, 128):
            rows = []
            for (first, steps), ref in zip(CUTS, g_refs):
                start, end = max(lo - first * GB, 0), min(lo + 128 - first * GB, steps * GB)
                if start < end:
                    rows.append(ref[start:end, :])
            x = jnp.concatenate(rows, axis=0)
            gt_ref[:, lo : lo + 128] = x.astype(F32).T.astype(BF16)

    p = jnp.dot(gt_ref[:, :VL], w_ref[...], preferred_element_type=F32).astype(BF16)
    even = pos[3] == 0
    for z in range(4):
        first, second = p[:, 256 * z : 256 * z + 128], p[:, 256 * z + 128 : 256 * z + 256]
        mine_ref[0, z] = jnp.where(even, first, second)
        other_ref[0, z] = jnp.where(even, second, first)


def hidden_part(pos, gs, wt):
    out = pl.BlockSpec((1, 4, T, 128), lambda i, p: (i, 0, 0, 0))
    return call(
        hidden_body,
        out_shape=[jax.ShapeDtypeStruct((4, 4, T, 128), BF16)] * 2,
        grid_spec=pltpu.PrefetchScalarGridSpec(
            num_scalar_prefetch=1,
            grid=(4,),
            in_specs=[whole(g.shape) for g in gs] + [pl.BlockSpec((VL, 1024), lambda i, p: (0, i))],
            out_specs=[out, out],
            scratch_shapes=[pltpu.VMEM((T, VP), BF16)],
        ),
    )(pos, *gs, wt)


def head_body(pos, *refs):
    g_refs, (far0, far1, h_ref), out_ref, k_ref = refs[:3], refs[3:6], refs[-2], refs[-1]

    @pl.when(pl.program_id(0) == 0)
    def _():
        for n, away in enumerate((0, 3, 1, 2)):
            group = (pos[0] + away) % 4
            for j in range(8):
                k_ref[n * T : (n + 1) * T, j * 128 : (j + 1) * 128] = h_ref[group * 8 + j]

    if far0.shape[0] < GB:
        far = jnp.concatenate([far0[...], far1[...]], axis=0)
    else:
        far = jnp.where(pl.program_id(0) == 0, far0[...], far1[...])
    g = jnp.concatenate([r[...] for r in g_refs] + [far], axis=1)
    out_ref[...] = jnp.dot(g, k_ref[...], preferred_element_type=F32).astype(BF16)


def head_piece(pos, gs, h2, first, steps, other):
    specs = [pl.BlockSpec((GB, T), lambda i, p: (i, 0))] * 3 + [whole(g.shape) for g in gs[3:]]
    specs.append(whole((NV, T, 128)))
    args = list(gs) + [h2]
    kw = {}
    if other is not None:
        specs.append(pl.BlockSpec(memory_space=pl.ANY))
        args.append(other)
        kw["input_output_aliases"] = {len(args): 0}
    return call(
        head_body,
        out_shape=jax.ShapeDtypeStruct((VL, DX), BF16),
        grid_spec=pltpu.PrefetchScalarGridSpec(
            num_scalar_prefetch=1,
            grid=(steps,),
            in_specs=specs,
            out_specs=pl.BlockSpec((GB, DX), lambda i, p: (i + first, 0)),
            scratch_shapes=[pltpu.VMEM((4 * T, DX), BF16)],
        ),
        **kw,
    )(pos, *args)


def shift(x, n):
    return lax.ppermute(x, "x", [(i, (i + n) % 4) for i in range(4)])


def swap(x):
    return lax.ppermute(x, "c", [(0, 1), (1, 0)])


def spread(x, first):
    got = [x]
    for n in (1, 2, 3):
        pairs = []
        for y in range(4):
            for z in range(4):
                for c in range(2):
                    to = (y, (z + n) % 4) if c == first else ((y + n) % 4, z)
                    pairs.append(((y * 4 + z) * 2 + c, (to[0] * 4 + to[1]) * 2 + c))
        got.append(lax.ppermute(x, V, pairs))
    return jnp.stack(got)


def after(x, *others):
    return lax.optimization_barrier((x,) + others)[0]


def per_device(hidden, head_weight, teacher_logits, row_weight):
    pos = jnp.stack([lax.axis_index(a) for a in ("x", "y", "z", "c")]).astype(jnp.int32)
    wt = head_weight.T
    blocks = prep(teacher_logits)
    teacher = lax.all_to_all(blocks, V, 0, 0, tiled=True)
    one = spread(hidden, 0)
    own = spread(after(one, blocks), 1)
    sib = swap(own)
    s, m, l = student(pos, wt, own, sib)
    t, share = stats(m, l, s, teacher)
    gathered = lax.all_to_all(share, V, 0, 0, tiled=True)

    across = lax.ppermute(hidden, ("x", "y"), [(x * 4 + y, y * 4 + x) for x in range(4) for y in range(4)])
    h2 = lax.all_gather(after(across, share), V)

    *gs, kl = grad(gathered, row_weight.reshape(1, T), s, t)
    pieces = []
    for g in gs:
        if pieces:
            g = after(g, pieces[-1][1], pieces[-1][2])
        left, right = shift(g, 1), shift(g, 3)
        half = g.shape[0] // 2
        pieces.append([g, left, right, shift(left[:half], 1), shift(right[half:], 3)])
    mine, other = hidden_part(pos, gs, wt)
    both = (mine.astype(F32) + swap(after(other, *pieces[0][1:3])).astype(F32)).astype(BF16)
    both = after(both, *pieces[1][1:3])
    got = lax.all_to_all(both.reshape(16, T, 128), ("y", "z"), 0, 0, tiled=True)
    grad_hidden = jnp.sum(got.astype(F32), axis=0).astype(BF16)

    head = None
    for cut, parts in zip(CUTS, pieces):
        head = head_piece(pos, parts, h2, *cut, head)
    return kl.reshape(T), grad_hidden, head.T


def solution(mesh):
    fine = Mesh(mesh.devices.reshape(4, 4, 4, 2), ("x",) + V)
    in_specs = (P("x", V), P(None, V), P(("x",) + V, None), P("x"))
    out_specs = (P("x"), P("x", V), P("x", V))
    return jax.shard_map(per_device, mesh=fine, in_specs=in_specs, out_specs=out_specs, check_vma=False)
```

time: 513 us -> 236 us (0.46)
  waiting for transfers between devices: 239 us -> 60.9 us
  blocking collectives: 172 us -> 18.9 us
  Pallas kernels: 0 us -> 84.3 us
  matrix products: 57.3 us -> 0 us
  starting transfers between devices: 0.12 us -> 36.9 us
  local copies, waits for them, and re-layouts: 21.4 us -> 9 us
    reduce_scatter x1 -> x0, waiting for transfers between devices: 172 us -> none  [per_device(): lax.psum_scatter(lax.dot_general(full_hidden, grad_logits, (((0,), (0,)),...]
    pallas_call x0 -> x8, Pallas kernels: none -> 84.3 us  [the longest x3 27.2 us: head_piece(): call(head_body, out_shape=jax.ShapeDtypeStruct((VL, DX), BF16), grid_spec...]
    psum x1 -> x0, blocking collectives: 66.4 us -> none  [per_device(): lax.psum((jnp.sum(student_exp, axis=1), jnp.sum(teacher_exp, axis=1), jnp...]
    pmax x1 -> x0, blocking collectives: 62.3 us -> none  [per_device(): lax.pmax((student_local, teacher_local), 'vocab')]
    ppermute x0 -> x21, waiting for transfers between devices: none -> 60.9 us  [the longest x12 36.9 us: shift(): return lax.ppermute(x, 'x', [(i, (i + n) % 4) for i in range(4)])]
    dot_general x3 -> x0, matrix products: 57.3 us -> none  [the longest x1 21.4 us: per_device(): lax.dot_general(head_weight, grad_logits, (((1,), (1,)), ((), ())), prefe...]
    unnamed x4 -> x1, waiting for transfers between devices: 56.9 us -> 0.02 us
    ppermute x0 -> x21, starting transfers between devices: none -> 26.1 us  [the longest x12 13.3 us: shift(): return lax.ppermute(x, 'x', [(i, (i + n) % 4) for i in range(4)])]
  transfers between devices with their start and end apart: 3 -> 24, of which waited for: 3 -> 10; matrix products, arithmetic and copies ran while one was open for 6% -> 6% of each run, Pallas kernels for 0% -> 33%
where the time goes in v2:
time: 236 us; the launch traced here: 233 us
  Pallas kernels  84.3 us (36%)
  waiting for transfers between devices  60.9 us (26%)
  starting transfers between devices  36.9 us (16%)
  blocking collectives  18.9 us (8%)
  between operations  14.1 us (6%)
  local copies, waits for them, and re-layouts  9 us (4%)
  other arithmetic  8.83 us (4%)
    ppermute x12, waiting for transfers between devices, shift(): return lax.ppermute(x, 'x', [(i, (i + n) % 4) for i in range(4)])  36.9 us
    pallas_call x3, Pallas kernels, head_piece(): call(head_body, out_shape=jax.ShapeDtypeStruct((VL, DX), BF16), grid_spec...  27.2 us
    ppermute x6, waiting for transfers between devices, spread(): got.append(lax.ppermute(x, V, pairs))  20.8 us
    pallas_call x1, Pallas kernels, student(): call(student_body, out_shape=[jax.ShapeDtypeStruct((NS * SB, T), F32), pa...  19.3 us
    all_to_all x1, blocking collectives, per_device(): gathered = lax.all_to_all(share, V, 0, 0, tiled=True)  18.9 us
    pallas_call x1, Pallas kernels, hidden_part(): call(hidden_body, out_shape=[jax.ShapeDtypeStruct((4, 4, T, 128), BF16)]...  18.4 us
    ppermute x12, starting transfers between devices, shift(): return lax.ppermute(x, 'x', [(i, (i + n) % 4) for i in range(4)])  13.3 us
    ppermute x6, starting transfers between devices, spread(): got.append(lax.ppermute(x, V, pairs))  8.9 us
  transfers between devices with their start and end apart: 24, of which 10 were waited for; matrix products, arithmetic and copies ran while one was open for 6% of the time, Pallas kernels for 33%

profile of v2, /device:TPU:1, one launch (start us, length us, event | category | flops | bytes accessed | tf_op | source)
XLA Modules:
  0.0 232.9 jit_solution(6601439949023058733)
XLA Ops:
  7.2 3.6 %collective-permute-start.2 = (bf16[512,128]{1,0:T(8,128)(2,1)}, bf16[512,128]{1,0:T(8,128)(2,1)S(1)}, u32[]{:S(2)}, u32[]{:S(2)}) collective-permute-start(bf16[512,128]{1,0:T(8,128)(2,1)} %param.4), channel_id=1, source_target_pairs={{0,6},{1,25},{2,0},{3,27},{4,2},{5,29},{6,4},{7,31},{8,14},{9,1},{... | collective-permute-start | bytes 393224 | tf_op jit(solution)/shard_map/ppermute | solution.py:311
  11.1 0.7 collective-permute-start
  11.8 4.4 %shard_map.67 = bf16[32,19,16,128]{3,2,1,0:T(8,128)(2,1)} custom-call(bf16[16,75968]{1,0:T(8,128)(2,1)} %t_ref.1), custom_call_target="tpu_custom_call" | custom-call | flops 1048576 | bytes 65536 | tf_op jit(solution)/shard_map/pallas_call | solution.py:55
  16.4 1.6 collective-permute-done
  18.0 1.0 pad_maximum_fusion.1
  19.0 3.5 %collective-permute-start.5 = (bf16[4,512,128]{2,1,0:T(8,128)(2,1)S(1)}, bf16[4,512,128]{2,1,0:T(8,128)(2,1)S(1)}, u32[]{:S(2)}, u32[]{:S(2)}) collective-permute-start(bf16[4,512,128]{2,1,0:T(8,128)(2,1)S(1)} %pad_maximum_fusion.1), channel_id=1, source_target_pairs={{0,24},{1,7},{2,26},{3,1},{4,28},{5,3},{6,30},{7,5},{8,0},{9,15},{... | collective-permute-start | bytes 1572872 | tf_op jit(solution)/shard_map/ppermute | solution.py:311
  22.5 0.7 collective-permute-start.3
  23.2 7.0 %all-to-all-start = ((bf16[32,19,16,128]{3,2,1,0:T(8,128)(2,1)}), bf16[32,19,16,128]{3,2,1,0:T(8,128)(2,1)S(1)}, u32[]{:S(2)}, u32[]{:S(2)}) async-start(bf16[32,19,16,128]{3,2,1,0:T(8,128)(2,1)} %shard_map.67), calls=%async_computation | async-start | bytes 4980736 | tf_op jit(solution)/shard_map/all_to_all | solution.py:323
  30.3 16.6 %collective-permute-done.5 = bf16[4,512,128]{2,1,0:T(8,128)(2,1)S(1)} collective-permute-done((bf16[4,512,128]{2,1,0:T(8,128)(2,1)S(1)}, bf16[4,512,128]{2,1,0:T(8,128)(2,1)S(1)}, u32[]{:S(2)}, u32[]{:S(2)}) %collective-permute-start.5) | collective-permute-done | bytes 524320 | tf_op jit(solution)/shard_map/ppermute | solution.py:311
  46.9 2.5 %collective-permute-done.3 = bf16[4,512,128]{2,1,0:T(8,128)(2,1)} collective-permute-done((bf16[4,512,128]{2,1,0:T(8,128)(2,1)S(1)}, bf16[4,512,128]{2,1,0:T(8,128)(2,1)}, u32[]{:S(2)}, u32[]{:S(2)}) %collective-permute-start.3) | collective-permute-done | bytes 524320 | tf_op jit(solution)/shard_map/ppermute | solution.py:311
  49.4 2.8 %pad_maximum_fusion.own_ref = bf16[4,4,512,128]{3,2,1,0:T(8,128)(2,1)} fusion(bf16[1,4,512,128]{3,2,1,0:T(8,128)(2,1)S(1)} %bitcast.25, bf16[1,4,512,128]{3,2,1,0:T(8,128)(2,1)} %bitcast.11, bf16[1,4,512,128]{3,2,1,0:T(8,128)(2,1)} %bitcast.10, bf16[1,4,512,128]{3,2,1,0:T(8,128)(2,1)S(1)} %bitcast.24), kind=kLoop, calls=%fused_computation.1 | loop fusion | flops 3145728 | bytes 4194304 | tf_op jit(solution)/shard_map/stack | solution.py:312
  52.2 1.9 collective-permute-start.6
  54.1 1.6 collective-permute-start.16
  55.7 0.6 pad_add_fusion.pos
  56.3 2.0 collective-permute-done.6.sib_ref
  58.3 19.3 %shard_map.68 = (f32[2560,512]{1,0:T(8,128)}, f32[8,512]{1,0:T(8,128)}, f32[8,512]{1,0:T(8,128)}) custom-call(s32[4]{0:T(128)} %pad_add_fusion.pos, bf16[2374,4096]{1,0:T(8,128)(2,1)} %bitcast.18, bf16[4,4,512,128]{3,2,1,0:T(8,128)(2,1)} %pad_maximum_fusion.own_ref, bf16[4,4,512,128]{3,2,1,0:T(8,128)(2,1)} %collective-permute-done.6.sib_ref), custom_call_target="tpu_custom_call" | custom-call | flops 1048576 | bytes 65536 | tf_op jit(solution)/shard_map/pallas_call | solution.py:96
  77.6 1.5 copy-done
  79.0 7.4 %shard_map.69 = (bf16[2560,512]{1,0:T(8,128)(2,1)}, f32[32,8,512]{2,1,0:T(8,128)}) custom-call(f32[8,512]{1,0:T(8,128)} %get-tuple-element.21.m_ref, f32[8,512]{1,0:T(8,128)} %get-tuple-element.22.l_ref, f32[2560,512]{1,0:T(8,128)} %get-tuple-element.23.s_ref, bf16[32,19,16,128]{3,2,1,0:T(8,128)(2,1)} %copy-done), custom_call_target="tpu_custom_call" | custom-call | flops 1048576 | bytes 65536 | tf_op jit(solution)/shard_map/pallas_call | solution.py:157
  86.5 0.7 copy-done.11
  87.2 18.9 %all_to_all.15.all_ref = f32[32,8,512]{2,1,0:T(8,128)} all-to-all(f32[32,8,512]{2,1,0:T(8,128)} %get-tuple-element.24), channel_id=1, replica_groups=mesh['x'=4,'y'=4,'z'=4,'c'=2] {'y','z','c'}, dimensions={0} | all-to-all | bytes 1048576 | tf_op jit(solution)/shard_map/all_to_all | solution.py:329
  106.0 7.5 %shard_map.70 = (bf16[1216,512]{1,0:T(8,128)(2,1)}, bf16[608,512]{1,0:T(8,128)(2,1)}, bf16[608,512]{1,0:T(8,128)(2,1)}, f32[1,512]{1,0:T(1,128)}) custom-call(f32[32,8,512]{2,1,0:T(8,128)} %all_to_all.15.all_ref, f32[1,512]{1,0:T(1,128)} %bitcast.29, f32[2560,512]{1,0:T(8,128)} %get-tuple-element.23.s_ref, bf16[2560,512]{1,0:T(8,128)(2,1)} %get-tuple-element.25.t_ref), custom_call_target="tpu_custom_call" | custom-call | flops 1048576 | bytes 65536 | tf_op jit(solution)/shard_map/pallas_call | solution.py:206
  113.6 2.7 %collective-permute-start.8 = (bf16[1216,512]{1,0:T(8,128)(2,1)}, bf16[1216,512]{1,0:T(8,128)(2,1)}, u32[]{:S(2)}, u32[]{:S(2)}) collective-permute-start(bf16[1216,512]{1,0:T(8,128)(2,1)} %get-tuple-element.27.refs_0_), channel_id=1, source_target_pairs={{0,96},{32,0},{64,32},{96,64},{1,97},{33,1},{65,33},{97,65},{2,98}... | collective-permute-start | bytes 3735560 | tf_op jit(solution)/shard_map/ppermute | solution.py:295
  116.3 18.4 %shard_map.71 = (bf16[4,4,512,128]{3,2,1,0:T(8,128)(2,1)}, bf16[4,4,512,128]{3,2,1,0:T(8,128)(2,1)}) custom-call(s32[4]{0:T(128)} %pad_add_fusion.pos, bf16[1216,512]{1,0:T(8,128)(2,1)} %get-tuple-element.27.refs_0_, bf16[608,512]{1,0:T(8,128)(2,1)} %get-tuple-element.33.refs_1_.refs_0_, bf16[608,512]{1,0:T(8,128)(2,1)} %get-tuple-element.35.refs_2_.refs_0_, ...), custom_call_target="tpu_custom_call" | custom-call | flops 1048576 | bytes 65536 | tf_op jit(solution)/shard_map/pallas_call | solution.py:240
  134.7 9.7 %collective-permute-done.7.refs_1_ = bf16[1216,512]{1,0:T(8,128)(2,1)S(1)} collective-permute-done((bf16[1216,512]{1,0:T(8,128)(2,1)}, bf16[1216,512]{1,0:T(8,128)(2,1)S(1)}, u32[]{:S(2)}, u32[]{:S(2)}) %collective-permute-start.7) | collective-permute-done | bytes 1245216 | tf_op jit(solution)/shard_map/ppermute | solution.py:295
  144.8 2.8 %collective-permute-start.11 = (bf16[608,512]{1,0:T(8,128)(2,1)S(1)}, bf16[608,512]{1,0:T(8,128)(2,1)S(1)}, u32[]{:S(2)}, u32[]{:S(2)}) collective-permute-start(bf16[608,512]{1,0:T(8,128)(2,1)S(1)} %copy-done.2), channel_id=1, source_target_pairs={{0,96},{32,0},{64,32},{96,64},{1,97},{33,1},{65,33},{97,65},{2,98}... | collective-permute-start | bytes 1867784 | tf_op jit(solution)/shard_map/ppermute | solution.py:295
  147.6 1.2 collective-permute-done.9
  148.8 3.5 %add_convert_fusion = bf16[4,4,512,128]{3,2,1,0:T(8,128)(2,1)} fusion(bf16[4,4,512,128]{3,2,1,0:T(8,128)(2,1)S(1)} %collective-permute-done.9, bf16[4,4,512,128]{3,2,1,0:T(8,128)(2,1)} %get-tuple-element.30), kind=kLoop, calls=%fused_computation | loop fusion | flops 4194304 | bytes 6291456 | tf_op jit(solution)/shard_map/convert_element_type | solution.py:343
  152.2 9.6 %collective-permute-done.10.refs_1_ = bf16[608,512]{1,0:T(8,128)(2,1)S(1)} collective-permute-done((bf16[608,512]{1,0:T(8,128)(2,1)S(1)}, bf16[608,512]{1,0:T(8,128)(2,1)S(1)}, u32[]{:S(2)}, u32[]{:S(2)}) %collective-permute-start.10) | collective-permute-done | bytes 622624 | tf_op jit(solution)/shard_map/ppermute | solution.py:295
  161.8 0.9 copy-done.3
  162.8 3.7 %all-to-all-start.2 = ((bf16[16,512,128]{2,1,0:T(8,128)(2,1)}), bf16[16,512,128]{2,1,0:T(8,128)(2,1)S(1)}, u32[]{:S(2)}, u32[]{:S(2)}) async-start(bf16[16,512,128]{2,1,0:T(8,128)(2,1)} %bitcast.15), calls=%async_computation.2 | async-start | bytes 4194304 | tf_op jit(solution)/shard_map/all_to_all | solution.py:345
  166.6 0.7 collective-permute-start.12
  167.3 2.0 collective-permute-start.13
  169.5 1.9 slice.29
  171.4 2.7 %collective-permute-start.20 = (bf16[608,512]{1,0:T(8,128)(2,1)}, bf16[608,512]{1,0:T(8,128)(2,1)S(1)}, u32[]{:S(2)}, u32[]{:S(2)}) collective-permute-start(bf16[608,512]{1,0:T(8,128)(2,1)} %slice.29), channel_id=1, source_target_pairs={{0,96},{32,0},{64,32},{96,64},{1,97},{33,1},{65,33},{97,65},{2,98}... | collective-permute-start | bytes 1867784 | tf_op jit(solution)/shard_map/ppermute | solution.py:295
  174.1 0.8 slice.26
  174.8 0.8 slice.27
  175.6 7.3 %collective-permute-done.12.refs_1_ = bf16[608,512]{1,0:T(8,128)(2,1)S(1)} collective-permute-done((bf16[608,512]{1,0:T(8,128)(2,1)}, bf16[608,512]{1,0:T(8,128)(2,1)S(1)}, u32[]{:S(2)}, u32[]{:S(2)}) %collective-permute-start.12) | collective-permute-done | bytes 622624 | tf_op jit(solution)/shard_map/ppermute | solution.py:295
  182.9 0.6 collective-permute-start.18
  183.4 0.8 slice.24
  184.2 0.9 collective-permute-start.14
  185.1 0.7 slice.25
  185.8 10.4 %collective-permute-done.19.refs_3_ = bf16[608,512]{1,0:T(8,128)(2,1)S(1)} collective-permute-done((bf16[608,512]{1,0:T(8,128)(2,1)S(1)}, bf16[608,512]{1,0:T(8,128)(2,1)S(1)}, u32[]{:S(2)}, u32[]{:S(2)}) %collective-permute-start.19) | collective-permute-done | bytes 622624 | tf_op jit(solution)/shard_map/ppermute | solution.py:295
  196.2 0.9 collective-permute-start.15
  197.1 1.0 reduce_sum.12
  198.0 0.8 copy-done.10
  198.9 11.8 %shard_map.72.refs_6_ = bf16[2374,1024]{1,0:T(8,128)(2,1)} custom-call(s32[4]{0:T(128)} %pad_add_fusion.pos, bf16[1216,512]{1,0:T(8,128)(2,1)} %get-tuple-element.27.refs_0_, bf16[1216,512]{1,0:T(8,128)(2,1)} %copy-done.1, bf16[1216,512]{1,0:T(8,128)(2,1)} %collective-permute-done.8.refs_2_, bf16[608,512]{1,0:T(8,128)(2,1)} %copy-done.9, ...), custom_call_target="tpu_custom_call" | custom-call | flops 1048576 | bytes 65536 | tf_op jit(solution)/shard_map/pallas_call | solution.py:280
  210.6 7.7 %shard_map.73.refs_6_ = bf16[2374,1024]{1,0:T(8,128)(2,1)} custom-call(s32[4]{0:T(128)} %pad_add_fusion.pos, bf16[608,512]{1,0:T(8,128)(2,1)} %get-tuple-element.33.refs_1_.refs_0_, bf16[608,512]{1,0:T(8,128)(2,1)} %copy-done.3, bf16[608,512]{1,0:T(8,128)(2,1)} %copy-done.5, ...), custom_call_target="tpu_custom_call", output_to_operand_aliasing={{}: (7, {})} | custom-call | flops 1048576 | bytes 65536 | tf_op jit(solution)/shard_map/pallas_call | solution.py:280
  218.4 7.7 %shard_map.74 = bf16[2374,1024]{1,0:T(8,128)(2,1)} custom-call(s32[4]{0:T(128)} %pad_add_fusion.pos, bf16[608,512]{1,0:T(8,128)(2,1)} %get-tuple-element.35.refs_2_.refs_0_, bf16[608,512]{1,0:T(8,128)(2,1)} %copy-done.7, bf16[608,512]{1,0:T(8,128)(2,1)} %copy-done.8, ...), custom_call_target="tpu_custom_call", output_to_operand_aliasing={{}: (7, {})} | custom-call | flops 1048576 | bytes 65536 | tf_op jit(solution)/shard_map/pallas_call | solution.py:280
  (45 shorter events, 1.4 us)
Async XLA Ops:
  7.2 9.1 %collective-permute-start.2 = (bf16[512,128]{1,0:T(8,128)(2,1)}, bf16[512,128]{1,0:T(8,128)(2,1)S(1)}, u32[]{:S(2)}, u32[]{:S(2)}) collective-permute-start(bf16[512,128]{1,0:T(8,128)(2,1)} %param.4), channel_id=1, source_target_pairs={{0,6},{1,25},{2,0},{3,27},{4,2},{5,29},{6,4},{7,31},{8,14},{9,1},{... | collective-permute-start | bytes 393224 | tf_op jit(solution)/shard_map/ppermute | solution.py:311
  10.8 5.6 %collective-permute-start.1 = (bf16[512,128]{1,0:T(8,128)(2,1)}, bf16[512,128]{1,0:T(8,128)(2,1)S(1)}, u32[]{:S(2)}, u32[]{:S(2)}) collective-permute-start(bf16[512,128]{1,0:T(8,128)(2,1)} %param.4), channel_id=1, source_target_pairs={{0,4},{1,17},{2,6},{3,19},{4,0},{5,21},{6,2},{7,23},{8,12},{9,25},... | collective-permute-start | bytes 393224 | tf_op jit(solution)/shard_map/ppermute | solution.py:311
  11.1 6.9 %collective-permute-start = (bf16[512,128]{1,0:T(8,128)(2,1)}, bf16[512,128]{1,0:T(8,128)(2,1)S(1)}, u32[]{:S(2)}, u32[]{:S(2)}) collective-permute-start(bf16[512,128]{1,0:T(8,128)(2,1)} %param.4), channel_id=1, source_target_pairs={{0,2},{1,9},{2,4},{3,11},{4,6},{5,13},{6,0},{7,15},{8,10},{9,17},{... | collective-permute-start | bytes 393224 | tf_op jit(solution)/shard_map/ppermute | solution.py:311
  19.0 27.9 %collective-permute-start.5 = (bf16[4,512,128]{2,1,0:T(8,128)(2,1)S(1)}, bf16[4,512,128]{2,1,0:T(8,128)(2,1)S(1)}, u32[]{:S(2)}, u32[]{:S(2)}) collective-permute-start(bf16[4,512,128]{2,1,0:T(8,128)(2,1)S(1)} %pad_maximum_fusion.1), channel_id=1, source_target_pairs={{0,24},{1,7},{2,26},{3,1},{4,28},{5,3},{6,30},{7,5},{8,0},{9,15},{... | collective-permute-start | bytes 1572872 | tf_op jit(solution)/shard_map/ppermute | solution.py:311
  22.5 24.4 %collective-permute-start.4 = (bf16[4,512,128]{2,1,0:T(8,128)(2,1)S(1)}, bf16[4,512,128]{2,1,0:T(8,128)(2,1)}, u32[]{:S(2)}, u32[]{:S(2)}) collective-permute-start(bf16[4,512,128]{2,1,0:T(8,128)(2,1)S(1)} %pad_maximum_fusion.1), channel_id=1, source_target_pairs={{0,16},{1,5},{2,18},{3,7},{4,20},{5,1},{6,22},{7,3},{8,24},{9,13},... | collective-permute-start | bytes 1572872 | tf_op jit(solution)/shard_map/ppermute | solution.py:311
  22.5 26.9 %collective-permute-start.3 = (bf16[4,512,128]{2,1,0:T(8,128)(2,1)S(1)}, bf16[4,512,128]{2,1,0:T(8,128)(2,1)}, u32[]{:S(2)}, u32[]{:S(2)}) collective-permute-start(bf16[4,512,128]{2,1,0:T(8,128)(2,1)S(1)} %pad_maximum_fusion.1), channel_id=1, source_target_pairs={{0,8},{1,3},{2,10},{3,5},{4,12},{5,7},{6,14},{7,1},{8,16},{9,11},{... | collective-permute-start | bytes 1572872 | tf_op jit(solution)/shard_map/ppermute | solution.py:311
  23.2 54.3 %all-to-all-start = ((bf16[32,19,16,128]{3,2,1,0:T(8,128)(2,1)}), bf16[32,19,16,128]{3,2,1,0:T(8,128)(2,1)S(1)}, u32[]{:S(2)}, u32[]{:S(2)}) async-start(bf16[32,19,16,128]{3,2,1,0:T(8,128)(2,1)} %shard_map.67), calls=%async_computation | async-start | bytes 4980736 | tf_op jit(solution)/shard_map/all_to_all | solution.py:323
  30.3 167.7 %all-gather.3.cloned.1.call-start = ((), (), s32[]{:S(2)}) async-start(), calls=%async_computation.3 | async-start | bytes 4325376 | tf_op jit(solution)/shard_map/all_gather | solution.py:332
  52.2 6.0 %collective-permute-start.6 = (bf16[4,4,512,128]{3,2,1,0:T(8,128)(2,1)}, bf16[4,4,512,128]{3,2,1,0:T(8,128)(2,1)}, u32[]{:S(2)}, u32[]{:S(2)}) collective-permute-start(bf16[4,4,512,128]{3,2,1,0:T(8,128)(2,1)} %pad_maximum_fusion.own_ref), channel_id=1, source_target_pairs={{0,1},{1,0},{2,3},{3,2},{4,5},{5,4},{6,7},{7,6},{8,9},{9,8},{10,11... | collective-permute-start | bytes 6291464 | tf_op jit(solution)/shard_map/ppermute | solution.py:299
  54.1 32.3 %collective-permute-start.16 = (bf16[512,128]{1,0:T(8,128)(2,1)}, bf16[512,128]{1,0:T(8,128)(2,1)S(1)}, u32[]{:S(2)}, u32[]{:S(2)}) collective-permute-start(bf16[512,128]{1,0:T(8,128)(2,1)} %param.4), channel_id=1, source_target_pairs={{0,0},{8,32},{16,64},{24,96},{32,8},{40,40},{48,72},{56,104},{64,1... | collective-permute-start | bytes 393224 | tf_op jit(solution)/shard_map/ppermute | solution.py:331
  77.6 1.5 copy-start
  86.5 0.7 copy-start.11
  113.6 30.8 %collective-permute-start.7 = (bf16[1216,512]{1,0:T(8,128)(2,1)}, bf16[1216,512]{1,0:T(8,128)(2,1)S(1)}, u32[]{:S(2)}, u32[]{:S(2)}) collective-permute-start(bf16[1216,512]{1,0:T(8,128)(2,1)} %get-tuple-element.27.refs_0_), channel_id=1, source_target_pairs={{0,32},{32,64},{64,96},{96,0},{1,33},{33,65},{65,97},{97,1},{2,34}... | collective-permute-start | bytes 3735560 | tf_op jit(solution)/shard_map/ppermute | solution.py:295
  113.6 30.8 %collective-permute-start.8 = (bf16[1216,512]{1,0:T(8,128)(2,1)}, bf16[1216,512]{1,0:T(8,128)(2,1)}, u32[]{:S(2)}, u32[]{:S(2)}) collective-permute-start(bf16[1216,512]{1,0:T(8,128)(2,1)} %get-tuple-element.27.refs_0_), channel_id=1, source_target_pairs={{0,96},{32,0},{64,32},{96,64},{1,97},{33,1},{65,33},{97,65},{2,98}... | collective-permute-start | bytes 3735560 | tf_op jit(solution)/shard_map/ppermute | solution.py:295
  116.3 28.5 %copy-start.2 = (bf16[608,512]{1,0:T(8,128)(2,1)S(1)}, bf16[608,512]{1,0:T(8,128)(2,1)}, u32[]{:S(2)}) copy-start(bf16[608,512]{1,0:T(8,128)(2,1)} %get-tuple-element.33.refs_1_.refs_0_) | copy-start | bytes 1867780
  144.4 25.0 %copy-start.1 = (bf16[1216,512]{1,0:T(8,128)(2,1)}, bf16[1216,512]{1,0:T(8,128)(2,1)S(1)}, u32[]{:S(2)}) copy-start(bf16[1216,512]{1,0:T(8,128)(2,1)S(1)} %collective-permute-done.7.refs_1_) | copy-start | bytes 3735556
  144.4 4.4 %collective-permute-start.9 = (bf16[4,4,512,128]{3,2,1,0:T(8,128)(2,1)}, bf16[4,4,512,128]{3,2,1,0:T(8,128)(2,1)S(1)}, u32[]{:S(2)}, u32[]{:S(2)}) collective-permute-start(bf16[4,4,512,128]{3,2,1,0:T(8,128)(2,1)} %get-tuple-element.32), channel_id=1, source_target_pairs={{0,1},{1,0},{2,3},{3,2},{4,5},{5,4},{6,7},{7,6},{8,9},{9,8},{10,11... | collective-permute-start | bytes 6291464 | tf_op jit(solution)/shard_map/ppermute | solution.py:299
  144.8 17.0 %collective-permute-start.10 = (bf16[608,512]{1,0:T(8,128)(2,1)S(1)}, bf16[608,512]{1,0:T(8,128)(2,1)S(1)}, u32[]{:S(2)}, u32[]{:S(2)}) collective-permute-start(bf16[608,512]{1,0:T(8,128)(2,1)S(1)} %copy-done.2), channel_id=1, source_target_pairs={{0,32},{32,64},{64,96},{96,0},{1,33},{33,65},{65,97},{97,1},{2,34}... | collective-permute-start | bytes 1867784 | tf_op jit(solution)/shard_map/ppermute | solution.py:295
  144.8 17.0 %collective-permute-start.11 = (bf16[608,512]{1,0:T(8,128)(2,1)S(1)}, bf16[608,512]{1,0:T(8,128)(2,1)S(1)}, u32[]{:S(2)}, u32[]{:S(2)}) collective-permute-start(bf16[608,512]{1,0:T(8,128)(2,1)S(1)} %copy-done.2), channel_id=1, source_target_pairs={{0,96},{32,0},{64,32},{96,64},{1,97},{33,1},{65,33},{97,65},{2,98}... | collective-permute-start | bytes 1867784 | tf_op jit(solution)/shard_map/ppermute | solution.py:295
  161.8 0.9 copy-start.3
  161.8 1.0 copy-start.5
  162.8 34.2 %all-to-all-start.2 = ((bf16[16,512,128]{2,1,0:T(8,128)(2,1)}), bf16[16,512,128]{2,1,0:T(8,128)(2,1)S(1)}, u32[]{:S(2)}, u32[]{:S(2)}) async-start(bf16[16,512,128]{2,1,0:T(8,128)(2,1)} %bitcast.15), calls=%async_computation.2 | async-start | bytes 4194304 | tf_op jit(solution)/shard_map/all_to_all | solution.py:345
  166.6 7.5 %copy-start.4 = (bf16[608,512]{1,0:T(8,128)(2,1)S(1)}, bf16[608,512]{1,0:T(8,128)(2,1)}, u32[]{:S(2)}) copy-start(bf16[608,512]{1,0:T(8,128)(2,1)} %copy-done.3) | copy-start | bytes 1867780
  166.6 8.3 %copy-start.6 = (bf16[608,512]{1,0:T(8,128)(2,1)S(1)}, bf16[608,512]{1,0:T(8,128)(2,1)}, u32[]{:S(2)}) copy-start(bf16[608,512]{1,0:T(8,128)(2,1)} %copy-done.5) | copy-start | bytes 1867780
  166.6 16.3 %collective-permute-start.12 = (bf16[608,512]{1,0:T(8,128)(2,1)}, bf16[608,512]{1,0:T(8,128)(2,1)S(1)}, u32[]{:S(2)}, u32[]{:S(2)}) collective-permute-start(bf16[608,512]{1,0:T(8,128)(2,1)} %get-tuple-element.35.refs_2_.refs_0_), channel_id=1, source_target_pairs={{0,32},{32,64},{64,96},{96,0},{1,33},{33,65},{65,97},{97,1},{2,34}... | collective-permute-start | bytes 1867784 | tf_op jit(solution)/shard_map/ppermute | solution.py:295
  167.3 16.9 %collective-permute-start.13 = (bf16[608,512]{1,0:T(8,128)(2,1)}, bf16[608,512]{1,0:T(8,128)(2,1)S(1)}, u32[]{:S(2)}, u32[]{:S(2)}) collective-permute-start(bf16[608,512]{1,0:T(8,128)(2,1)} %get-tuple-element.35.refs_2_.refs_0_), channel_id=1, source_target_pairs={{0,96},{32,0},{64,32},{96,64},{1,97},{33,1},{65,33},{97,65},{2,98}... | collective-permute-start | bytes 1867784 | tf_op jit(solution)/shard_map/ppermute | solution.py:295
  169.4 26.8 %collective-permute-start.19 = (bf16[608,512]{1,0:T(8,128)(2,1)S(1)}, bf16[608,512]{1,0:T(8,128)(2,1)S(1)}, u32[]{:S(2)}, u32[]{:S(2)}) collective-permute-start(bf16[608,512]{1,0:T(8,128)(2,1)S(1)} %slice.28), channel_id=1, source_target_pairs={{0,32},{32,64},{64,96},{96,0},{1,33},{33,65},{65,97},{97,1},{2,34}... | collective-permute-start | bytes 1867784 | tf_op jit(solution)/shard_map/ppermute | solution.py:295
  171.4 26.6 %collective-permute-start.20 = (bf16[608,512]{1,0:T(8,128)(2,1)}, bf16[608,512]{1,0:T(8,128)(2,1)S(1)}, u32[]{:S(2)}, u32[]{:S(2)}) collective-permute-start(bf16[608,512]{1,0:T(8,128)(2,1)} %slice.29), channel_id=1, source_target_pairs={{0,96},{32,0},{64,32},{96,64},{1,97},{33,1},{65,33},{97,65},{2,98}... | collective-permute-start | bytes 1867784 | tf_op jit(solution)/shard_map/ppermute | solution.py:295
  174.8 35.8 %collective-permute-start.17 = (bf16[304,512]{1,0:T(8,128)(2,1)}, bf16[304,512]{1,0:T(8,128)(2,1)}, u32[]{:S(2)}, u32[]{:S(2)}) collective-permute-start(bf16[304,512]{1,0:T(8,128)(2,1)} %slice.26), channel_id=1, source_target_pairs={{0,32},{32,64},{64,96},{96,0},{1,33},{33,65},{65,97},{97,1},{2,34}... | collective-permute-start | bytes 933896 | tf_op jit(solution)/shard_map/ppermute | solution.py:295
  182.9 13.3 %copy-start.7 = (bf16[608,512]{1,0:T(8,128)(2,1)}, bf16[608,512]{1,0:T(8,128)(2,1)S(1)}, u32[]{:S(2)}) copy-start(bf16[608,512]{1,0:T(8,128)(2,1)S(1)} %collective-permute-done.12.refs_1_) | copy-start | bytes 1867780
  182.9 27.8 %collective-permute-start.18 = (bf16[304,512]{1,0:T(8,128)(2,1)}, bf16[304,512]{1,0:T(8,128)(2,1)}, u32[]{:S(2)}, u32[]{:S(2)}) collective-permute-start(bf16[304,512]{1,0:T(8,128)(2,1)} %slice.27), channel_id=1, source_target_pairs={{0,96},{32,0},{64,32},{96,64},{1,97},{33,1},{65,33},{97,65},{2,98}... | collective-permute-start | bytes 933896 | tf_op jit(solution)/shard_map/ppermute | solution.py:295
  184.2 12.0 %copy-start.8 = (bf16[608,512]{1,0:T(8,128)(2,1)}, bf16[608,512]{1,0:T(8,128)(2,1)S(1)}, u32[]{:S(2)}) copy-start(bf16[608,512]{1,0:T(8,128)(2,1)S(1)} %collective-permute-done.13.refs_2_) | copy-start | bytes 1867780
  184.2 34.2 %collective-permute-start.14 = (bf16[304,512]{1,0:T(8,128)(2,1)}, bf16[304,512]{1,0:T(8,128)(2,1)}, u32[]{:S(2)}, u32[]{:S(2)}) collective-permute-start(bf16[304,512]{1,0:T(8,128)(2,1)} %slice.24), channel_id=1, source_target_pairs={{0,32},{32,64},{64,96},{96,0},{1,33},{33,65},{65,97},{97,1},{2,34}... | collective-permute-start | bytes 933896 | tf_op jit(solution)/shard_map/ppermute | solution.py:295
  196.2 1.8 copy-start.9
  196.2 22.2 %collective-permute-start.15 = (bf16[304,512]{1,0:T(8,128)(2,1)}, bf16[304,512]{1,0:T(8,128)(2,1)}, u32[]{:S(2)}, u32[]{:S(2)}) collective-permute-start(bf16[304,512]{1,0:T(8,128)(2,1)} %slice.25), channel_id=1, source_target_pairs={{0,96},{32,0},{64,32},{96,64},{1,97},{33,1},{65,33},{97,65},{2,98}... | collective-permute-start | bytes 933896 | tf_op jit(solution)/shard_map/ppermute | solution.py:295
  198.0 0.8 copy-start.10
Sparse Core Ops, SparseCore 0:
  87.3 45.3 all-gather.2

commit v3 on v2

--- a/solution.py
+++ b/solution.py
@@ -25,10 +25,10 @@
 MIB = 1 << 20
 
 
-def call(body, limit=60, **kw):
+def call(body, **kw):
     return pl.pallas_call(
         body,
-        compiler_params=pltpu.CompilerParams(vmem_limit_bytes=limit * MIB),
+        compiler_params=pltpu.CompilerParams(vmem_limit_bytes=60 * MIB),
         cost_estimate=pl.CostEstimate(flops=1 << 20, bytes_accessed=1 << 16, transcendentals=0),
         **kw,
     )
@@ -65,18 +65,19 @@
     return op(x.reshape(-1, 8, T), axis=0)
 
 
-def student_body(pos, w_ref, own_ref, sib_ref, s_ref, m_ref, l_ref, h_ref):
+def student_body(pos, w_ref, *refs):
+    own_refs, sib_refs, (s_ref, m_ref, l_ref, h_ref) = refs[:4], refs[4:8], refs[8:]
     step = pl.program_id(0)
 
     @pl.when(step == 0)
     def _():
         for a in range(4):
             for b in range(4):
-                for ref, c in ((own_ref, pos[3]), (sib_ref, 1 - pos[3])):
+                for ref, c in ((own_refs[a], pos[3]), (sib_refs[a], 1 - pos[3])):
                     y = (pos[1] + 4 - jnp.where(c == 0, a, b)) % 4
                     z = (pos[2] + 4 - jnp.where(c == 0, b, a)) % 4
                     at = pl.multiple_of(((y * 4 + z) * 2 + c) * 128, 128)
-                    h_ref[:, pl.ds(at, 128)] = ref[a, b]
+                    h_ref[:, pl.ds(at, 128)] = ref[b]
         m_ref[...] = jnp.full_like(m_ref, LOW)
         l_ref[...] = jnp.zeros_like(l_ref)
 
@@ -99,15 +100,11 @@
         grid_spec=pltpu.PrefetchScalarGridSpec(
             num_scalar_prefetch=1,
             grid=(NS,),
-            in_specs=[
-                pl.BlockSpec((SB, D), lambda i, p: (i, 0)),
-                whole((4, 4, T, 128)),
-                whole((4, 4, T, 128)),
-            ],
+            in_specs=[pl.BlockSpec((SB, D), lambda i, p: (i, 0))] + [whole((4, T, 128))] * 8,
             out_specs=[pl.BlockSpec((SB, T), lambda i, p: (i, 0)), whole((8, T)), whole((8, T))],
             scratch_shapes=[pltpu.VMEM((T, D), BF16)],
         ),
-    )(pos, wt, own, sib)
+    )(pos, wt, *own, *sib)
 
 
 def stats_body(m_ref, l_ref, s_ref, t_ref, tt_ref, out_ref, p_ref, sum_ref, cross_ref):
@@ -169,7 +166,7 @@
     )(m, l, s, t)
 
 
-def grad_body(all_ref, w_ref, s_ref, t_ref, *refs):
+def grad_body(cuts, all_ref, w_ref, s_ref, t_ref, *refs):
     kl_ref, c_ref = refs[-2:]
     step = pl.program_id(0)
 
@@ -189,26 +186,27 @@
     es = jnp.exp(s_ref[...] - c_ref[0:1, :]) * c_ref[2:3, :]
     et = jnp.exp(t_ref[...].astype(F32) - c_ref[1:2, :]) * c_ref[3:4, :]
     g = (es - et).astype(BF16)
-
-    for (first, steps), g_ref in zip(CUTS, refs):
-
-        @pl.when((step >= first) & (step < first + steps))
+    at = step + cuts[0][0]
+    for (first, steps), g_ref in zip(cuts, refs):
+
+        @pl.when((at >= first) & (at < first + steps))
         def _():
             g_ref[...] = g
 
 
-def piece(first, steps):
-    return pl.BlockSpec((GB, T), lambda i: (jnp.clip(i - first, 0, steps - 1), 0))
-
-
-def grad(gathered, w, s, t):
-    block = pl.BlockSpec((GB, T), lambda i: (i, 0))
-    return call(
-        grad_body,
-        out_shape=[jax.ShapeDtypeStruct((n * GB, T), BF16) for _, n in CUTS] + [jax.ShapeDtypeStruct((1, T), F32)],
-        grid=(VP // GB,),
+def piece(start, first, steps):
+    return pl.BlockSpec((GB, T), lambda i: (jnp.clip(i + start - first, 0, steps - 1), 0))
+
+
+def grad(gathered, w, s, t, cuts):
+    start = cuts[0][0]
+    block = pl.BlockSpec((GB, T), lambda i: (i + start, 0))
+    return call(
+        functools.partial(grad_body, cuts),
+        out_shape=[jax.ShapeDtypeStruct((n * GB, T), BF16) for _, n in cuts] + [jax.ShapeDtypeStruct((1, T), F32)],
+        grid=(sum(n for _, n in cuts),),
         in_specs=[whole((NV, 8, T)), whole((1, T)), block, block],
-        out_specs=[piece(*cut) for cut in CUTS] + [whole((1, T))],
+        out_specs=[piece(start, *cut) for cut in cuts] + [whole((1, T))],
         scratch_shapes=[pltpu.VMEM((8, T), F32)],
     )(gathered, w, s, t)
 
@@ -250,45 +248,65 @@
     )(pos, *gs, wt)
 
 
-def head_body(pos, *refs):
-    g_refs, (far0, far1, h_ref), out_ref, k_ref = refs[:3], refs[3:6], refs[-2], refs[-1]
-
-    @pl.when(pl.program_id(0) == 0)
-    def _():
-        for n, away in enumerate((0, 3, 1, 2)):
-            group = (pos[0] + away) % 4
-            for j in range(8):
-                k_ref[n * T : (n + 1) * T, j * 128 : (j + 1) * 128] = h_ref[group * 8 + j]
-
-    if far0.shape[0] < GB:
-        far = jnp.concatenate([far0[...], far1[...]], axis=0)
-    else:
-        far = jnp.where(pl.program_id(0) == 0, far0[...], far1[...])
-    g = jnp.concatenate([r[...] for r in g_refs] + [far], axis=1)
-    out_ref[...] = jnp.dot(g, k_ref[...], preferred_element_type=F32).astype(BF16)
-
-
-def head_piece(pos, gs, h2, first, steps, other):
-    specs = [pl.BlockSpec((GB, T), lambda i, p: (i, 0))] * 3 + [whole(g.shape) for g in gs[3:]]
-    specs.append(whole((NV, T, 128)))
-    args = list(gs) + [h2]
+def tokens_body(pos, h_ref, k_ref):
+    for j in range(8):
+        k_ref[:, j * 128 : (j + 1) * 128] = h_ref[j]
+
+
+def tokens(pos, h2):
+    group = lambda i, p: (p[0] + jnp.where(i == 0, 0, jnp.where(i == 1, 3, i - 1))) % 4
+    return call(
+        tokens_body,
+        out_shape=jax.ShapeDtypeStruct((4 * T, DX), BF16),
+        grid_spec=pltpu.PrefetchScalarGridSpec(
+            num_scalar_prefetch=1,
+            grid=(4,),
+            in_specs=[pl.BlockSpec((8, T, 128), lambda i, p: (group(i, p), 0, 0))],
+            out_specs=pl.BlockSpec((T, DX), lambda i, p: (i, 0)),
+        ),
+    )(pos, h2)
+
+
+def head_body(near, far, prior, *refs):
+    refs = list(refs)
+    parts = [refs.pop(0)[...] for _ in range(3)] if near else []
+    if far:
+        far0, far1 = refs.pop(0), refs.pop(0)
+        if far0.shape[0] < GB:
+            parts.append(jnp.concatenate([far0[...], far1[...]], axis=0))
+        else:
+            parts.append(jnp.where(pl.program_id(0) == 0, far0[...], far1[...]))
+    total = jnp.dot(jnp.concatenate(parts, axis=1), refs.pop(0)[...], preferred_element_type=F32)
+    if prior:
+        total = total + refs.pop(0)[...]
+    refs[-1][...] = total.astype(refs[-1].dtype)
+
+
+def head_piece(near, far, k, first, steps, prior=None, other=None):
+    specs = [pl.BlockSpec((GB, T), lambda i: (i, 0))] * len(near) + [whole(g.shape) for g in far]
+    rows = T * (len(near) + len(far) // 2)
+    specs.append(pl.BlockSpec((rows, DX), lambda i: (0 if near else 3, 0)))
+    args = [*near, *far, k]
     kw = {}
+    if prior is not None:
+        specs.append(pl.BlockSpec((GB, DX), lambda i: (i, 0)))
+        args.append(prior)
     if other is not None:
         specs.append(pl.BlockSpec(memory_space=pl.ANY))
         args.append(other)
-        kw["input_output_aliases"] = {len(args): 0}
-    return call(
-        head_body,
-        out_shape=jax.ShapeDtypeStruct((VL, DX), BF16),
-        grid_spec=pltpu.PrefetchScalarGridSpec(
-            num_scalar_prefetch=1,
-            grid=(steps,),
-            in_specs=specs,
-            out_specs=pl.BlockSpec((GB, DX), lambda i, p: (i + first, 0)),
-            scratch_shapes=[pltpu.VMEM((4 * T, DX), BF16)],
-        ),
+        kw["input_output_aliases"] = {len(args) - 1: 0}
+    if far:
+        out = jax.ShapeDtypeStruct((VL, DX), BF16)
+    else:
+        out, first = jax.ShapeDtypeStruct((steps * GB, DX), F32), 0
+    return call(
+        functools.partial(head_body, bool(near), bool(far), prior is not None),
+        out_shape=out,
+        grid=(steps,),
+        in_specs=specs,
+        out_specs=pl.BlockSpec((GB, DX), lambda i: (i + first, 0)),
         **kw,
-    )(pos, *args)
+    )(*args)
 
 
 def shift(x, n):
@@ -309,7 +327,7 @@
                     to = (y, (z + n) % 4) if c == first else ((y + n) % 4, z)
                     pairs.append(((y * 4 + z) * 2 + c, (to[0] * 4 + to[1]) * 2 + c))
         got.append(lax.ppermute(x, V, pairs))
-    return jnp.stack(got)
+    return got
 
 
 def after(x, *others):
@@ -320,34 +338,38 @@
     pos = jnp.stack([lax.axis_index(a) for a in ("x", "y", "z", "c")]).astype(jnp.int32)
     wt = head_weight.T
     blocks = prep(teacher_logits)
+    one = jnp.stack(spread(hidden, 0))
+    own = spread(after(one, blocks), 1)
     teacher = lax.all_to_all(blocks, V, 0, 0, tiled=True)
-    one = spread(hidden, 0)
-    own = spread(after(one, blocks), 1)
-    sib = swap(own)
-    s, m, l = student(pos, wt, own, sib)
+    s, m, l = student(pos, wt, own, [swap(x) for x in own])
     t, share = stats(m, l, s, teacher)
     gathered = lax.all_to_all(share, V, 0, 0, tiled=True)
 
+    w = row_weight.reshape(1, T)
+    gu, kl = grad(gathered, w, s, t, CUTS[:1])
+    gm, gl, _ = grad(gathered, after(w, gu), s, t, CUTS[1:])
     across = lax.ppermute(hidden, ("x", "y"), [(x * 4 + y, y * 4 + x) for x in range(4) for y in range(4)])
-    h2 = lax.all_gather(after(across, share), V)
-
-    *gs, kl = grad(gathered, row_weight.reshape(1, T), s, t)
-    pieces = []
-    for g in gs:
-        if pieces:
-            g = after(g, pieces[-1][1], pieces[-1][2])
+    h2 = lax.all_gather(after(across, kl), V)
+
+    def ring(g):
         left, right = shift(g, 1), shift(g, 3)
         half = g.shape[0] // 2
-        pieces.append([g, left, right, shift(left[:half], 1), shift(right[half:], 3)])
-    mine, other = hidden_part(pos, gs, wt)
-    both = (mine.astype(F32) + swap(after(other, *pieces[0][1:3])).astype(F32)).astype(BF16)
-    both = after(both, *pieces[1][1:3])
+        return [g, left, right], [shift(left[:half], 1), shift(right[half:], 3)]
+
+    near_u, far_u = ring(gu)
+    near_m, far_m = ring(gm)
+    near_l, far_l = ring(after(gl, *near_m))
+    mine, other = hidden_part(pos, (gu, gm, gl), wt)
+    both = (mine.astype(F32) + swap(after(other, *near_u)).astype(F32)).astype(BF16)
+    both = after(both, *near_m)
     got = lax.all_to_all(both.reshape(16, T, 128), ("y", "z"), 0, 0, tiled=True)
     grad_hidden = jnp.sum(got.astype(F32), axis=0).astype(BF16)
 
-    head = None
-    for cut, parts in zip(CUTS, pieces):
-        head = head_piece(pos, parts, h2, *cut, head)
+    k = tokens(pos, h2)
+    head = head_piece(near_u, far_u, k, *CUTS[0])
+    head = head_piece(near_m, far_m, k, *CUTS[1], other=head)
+    part = head_piece(near_l, [], k, *CUTS[2])
+    head = head_piece([], far_l, k, *CUTS[2], prior=part, other=head)
     return kl.reshape(T), grad_hidden, head.T
 
 

time: 236 us -> 259 us (1.097)
  waiting for transfers between devices: 60.9 us -> 86.8 us
  blocking collectives: 18.9 us -> 0 us
  starting transfers between devices: 36.9 us -> 48.3 us
  Pallas kernels: 84.3 us -> 91.6 us
  other arithmetic: 8.83 us -> 5.21 us
    all_to_all x1 -> x0, blocking collectives: 18.9 us -> none  [per_device(): gathered = lax.all_to_all(share, V, 0, 0, tiled=True)]
    ppermute x6, waiting for transfers between devices: 20.8 us -> 37.8 us  [spread(): got.append(lax.ppermute(x, V, pairs))]
    all_to_all x0 -> x1, waiting for transfers between devices: none -> 10.9 us  [per_device(): gathered = lax.all_to_all(share, V, 0, 0, tiled=True)]
    pallas_call x4 -> x7, Pallas kernels: 34.7 us -> 41.9 us  [the longest x4 26.7 us: head_piece(): call(functools.partial(head_body, bool(near), bool(far), prior is not Non...]
    all_to_all x0 -> x1, starting transfers between devices: none -> 5.18 us  [per_device(): gathered = lax.all_to_all(share, V, 0, 0, tiled=True)]
    another operation x2 -> x1, other arithmetic: 3.8 us -> 0.07 us  [per_device(): one = jnp.stack(spread(hidden, 0))]
    all_to_all x1, starting transfers between devices: 7.04 us -> 9.74 us  [per_device(): teacher = lax.all_to_all(blocks, V, 0, 0, tiled=True)]
  transfers between devices with their start and end apart: 24 -> 28, of which waited for: 10 -> 15; matrix products, arithmetic and copies ran while one was open for 6% -> 4% of each run, Pallas kernels for 33% -> 30%
where the time goes in v3:
time: 259 us; the launch traced here: 255 us
  Pallas kernels  91.6 us (35%)
  waiting for transfers between devices  86.8 us (34%)
  starting transfers between devices  48.3 us (19%)
  between operations  14.2 us (5%)
  local copies, waits for them, and re-layouts  8.55 us (3%)
  other arithmetic  5.21 us (2%)
    ppermute x6, waiting for transfers between devices, spread(): got.append(lax.ppermute(x, V, pairs))  37.8 us
    ppermute x12, waiting for transfers between devices, shift(): return lax.ppermute(x, 'x', [(i, (i + n) % 4) for i in range(4)])  34.6 us
    pallas_call x4, Pallas kernels, head_piece(): call(functools.partial(head_body, bool(near), bool(far), prior is not Non...  26.7 us
    pallas_call x1, Pallas kernels, student(): call(student_body, out_shape=[jax.ShapeDtypeStruct((NS * SB, T), F32), pa...  19.3 us
    pallas_call x1, Pallas kernels, hidden_part(): call(hidden_body, out_shape=[jax.ShapeDtypeStruct((4, 4, T, 128), BF16)]...  18.5 us
    ppermute x12, starting transfers between devices, shift(): return lax.ppermute(x, 'x', [(i, (i + n) % 4) for i in range(4)])  15.6 us
    all_to_all x1, waiting for transfers between devices, per_device(): gathered = lax.all_to_all(share, V, 0, 0, tiled=True)  10.9 us
    all_to_all x1, starting transfers between devices, per_device(): teacher = lax.all_to_all(blocks, V, 0, 0, tiled=True)  9.74 us
  transfers between devices with their start and end apart: 28, of which 15 were waited for; matrix products, arithmetic and copies ran while one was open for 4% of the time, Pallas kernels for 30%

profile of v3, /device:TPU:1, one launch (start us, length us, event | category | flops | bytes accessed | tf_op | source)
XLA Modules:
  0.0 254.7 jit_solution(14418117016756948611)
XLA Ops:
  7.2 4.5 %shard_map.67 = bf16[32,19,16,128]{3,2,1,0:T(8,128)(2,1)} custom-call(bf16[16,75968]{1,0:T(8,128)(2,1)} %t_ref.1), custom_call_target="tpu_custom_call" | custom-call | flops 1048576 | bytes 65536 | tf_op jit(solution)/shard_map/pallas_call | solution.py:55
  11.6 9.7 %all-to-all-start = ((bf16[32,19,16,128]{3,2,1,0:T(8,128)(2,1)}), bf16[32,19,16,128]{3,2,1,0:T(8,128)(2,1)S(1)}, u32[]{:S(2)}, u32[]{:S(2)}) async-start(bf16[32,19,16,128]{3,2,1,0:T(8,128)(2,1)} %shard_map.67), calls=%async_computation | async-start | bytes 4980736 | tf_op jit(solution)/shard_map/all_to_all | solution.py:343
  21.4 2.7 %collective-permute-start.2 = (bf16[512,128]{1,0:T(8,128)(2,1)S(1)}, bf16[512,128]{1,0:T(8,128)(2,1)S(1)}, u32[]{:S(2)}, u32[]{:S(2)}) collective-permute-start(bf16[512,128]{1,0:T(8,128)(2,1)S(1)} %copy-done.15), channel_id=1, source_target_pairs={{0,6},{1,25},{2,0},{3,27},{4,2},{5,29},{6,4},{7,31},{8,14},{9,1},{... | collective-permute-start | bytes 393224 | tf_op jit(solution)/shard_map/ppermute | solution.py:329
  25.2 27.7 %collective-permute-done.2 = bf16[512,128]{1,0:T(8,128)(2,1)S(1)} collective-permute-done((bf16[512,128]{1,0:T(8,128)(2,1)S(1)}, bf16[512,128]{1,0:T(8,128)(2,1)S(1)}, u32[]{:S(2)}, u32[]{:S(2)}) %collective-permute-start.2) | collective-permute-done | bytes 131104 | tf_op jit(solution)/shard_map/ppermute | solution.py:329
  52.9 1.1 collective-permute-done.1
  54.7 1.2 collective-permute-start.3
  55.9 2.4 collective-permute-start.4
  58.3 1.2 collective-permute-start.5
  59.6 1.4 collective-permute-start.6
  61.0 3.3 %collective-permute-done.3.refs_1_ = bf16[4,512,128]{2,1,0:T(8,128)(2,1)S(1)} collective-permute-done((bf16[4,512,128]{2,1,0:T(8,128)(2,1)S(1)}, bf16[4,512,128]{2,1,0:T(8,128)(2,1)S(1)}, u32[]{:S(2)}, u32[]{:S(2)}) %collective-permute-start.3) | collective-permute-done | bytes 524320 | tf_op jit(solution)/shard_map/ppermute | solution.py:329
  64.3 1.5 collective-permute-start.7
  65.8 5.1 %collective-permute-done.4.refs_2_ = bf16[4,512,128]{2,1,0:T(8,128)(2,1)} collective-permute-done((bf16[4,512,128]{2,1,0:T(8,128)(2,1)S(1)}, bf16[4,512,128]{2,1,0:T(8,128)(2,1)}, u32[]{:S(2)}, u32[]{:S(2)}) %collective-permute-start.4) | collective-permute-done | bytes 524320 | tf_op jit(solution)/shard_map/ppermute | solution.py:329
  70.9 1.6 collective-permute-start.8
  73.1 1.2 collective-permute-done.8.refs_6_
  74.3 0.7 collective-permute-done.9.refs_7_
  75.1 19.3 %shard_map.68 = (f32[2560,512]{1,0:T(8,128)}, f32[8,512]{1,0:T(8,128)}, f32[8,512]{1,0:T(8,128)}) custom-call(s32[4]{0:T(128)} %pad_add_fusion.pos, bf16[2374,4096]{1,0:T(8,128)(2,1)} %bitcast.14, bf16[4,512,128]{2,1,0:T(8,128)(2,1)} %copy-done.5, bf16[4,512,128]{2,1,0:T(8,128)(2,1)} %copy-done.13, bf16[4,512,128]{2,1,0:T(8,128)(2,1)} %collective-permute-done.4.refs_2_, ...), custom_call_target="tpu_custom_call" | custom-call | flops 1048576 | bytes 65536 | tf_op jit(solution)/shard_map/pallas_call | solution.py:97
  94.4 1.4 copy-done
  95.8 7.5 %shard_map.69 = (bf16[2560,512]{1,0:T(8,128)(2,1)}, f32[32,8,512]{2,1,0:T(8,128)}) custom-call(f32[8,512]{1,0:T(8,128)} %get-tuple-element.21.m_ref, f32[8,512]{1,0:T(8,128)} %get-tuple-element.22.l_ref, f32[2560,512]{1,0:T(8,128)} %get-tuple-element.23.s_ref, bf16[32,19,16,128]{3,2,1,0:T(8,128)(2,1)} %copy-done), custom_call_target="tpu_custom_call" | custom-call | flops 1048576 | bytes 65536 | tf_op jit(solution)/shard_map/pallas_call | solution.py:154
  103.3 5.2 %all-to-all-start.1 = ((f32[32,8,512]{2,1,0:T(8,128)}), f32[32,8,512]{2,1,0:T(8,128)S(1)}, u32[]{:S(2)}, u32[]{:S(2)}) async-start(f32[32,8,512]{2,1,0:T(8,128)} %get-tuple-element.24), calls=%async_computation.1 | async-start | bytes 1048576 | tf_op jit(solution)/shard_map/all_to_all | solution.py:346
  109.2 10.9 %all-to-all-done.1.all_ref = f32[32,8,512]{2,1,0:T(8,128)S(1)} async-done(((f32[32,8,512]{2,1,0:T(8,128)}), f32[32,8,512]{2,1,0:T(8,128)S(1)}, u32[]{:S(2)}, u32[]{:S(2)}) %all-to-all-start.1) | async-done | bytes 524320 | tf_op jit(solution)/shard_map/all_to_all | solution.py:346
  120.1 0.8 copy-done.1
  120.9 4.5 %shard_map.70 = (bf16[1216,512]{1,0:T(8,128)(2,1)}, f32[1,512]{1,0:T(1,128)}) custom-call(f32[32,8,512]{2,1,0:T(8,128)} %copy-done.1, f32[1,512]{1,0:T(1,128)} %bitcast.22, f32[2560,512]{1,0:T(8,128)} %get-tuple-element.23.s_ref, bf16[2560,512]{1,0:T(8,128)(2,1)} %get-tuple-element.25.t_ref), custom_call_target="tpu_custom_call" | custom-call | flops 1048576 | bytes 65536 | tf_op jit(solution)/shard_map/pallas_call | solution.py:204
  126.1 5.6 %collective-permute-start.10 = (bf16[1216,512]{1,0:T(8,128)(2,1)}, bf16[1216,512]{1,0:T(8,128)(2,1)S(1)}, u32[]{:S(2)}, u32[]{:S(2)}) collective-permute-start(bf16[1216,512]{1,0:T(8,128)(2,1)} %get-tuple-element.27.refs_0_), channel_id=1, source_target_pairs={{0,32},{32,64},{64,96},{96,0},{1,33},{33,65},{65,97},{97,1},{2,34}... | collective-permute-start | bytes 3735560 | tf_op jit(solution)/shard_map/ppermute | solution.py:313
  131.6 4.8 %shard_map.71 = (bf16[608,512]{1,0:T(8,128)(2,1)}, bf16[608,512]{1,0:T(8,128)(2,1)}, f32[1,512]{1,0:T(1,128)}) custom-call(f32[32,8,512]{2,1,0:T(8,128)} %copy-done.1, f32[1,512]{1,0:T(1,128)} %bitcast.23, f32[2560,512]{1,0:T(8,128)} %get-tuple-element.23.s_ref, bf16[2560,512]{1,0:T(8,128)(2,1)} %get-tuple-element.25.t_ref), custom_call_target="tpu_custom_call" | custom-call | flops 1048576 | bytes 65536 | tf_op jit(solution)/shard_map/pallas_call | solution.py:204
  136.5 18.5 %shard_map.72 = (bf16[4,4,512,128]{3,2,1,0:T(8,128)(2,1)}, bf16[4,4,512,128]{3,2,1,0:T(8,128)(2,1)}) custom-call(s32[4]{0:T(128)} %pad_add_fusion.pos, bf16[1216,512]{1,0:T(8,128)(2,1)} %get-tuple-element.27.refs_0_, bf16[608,512]{1,0:T(8,128)(2,1)} %get-tuple-element.29.refs_1_.refs_0_, bf16[608,512]{1,0:T(8,128)(2,1)} %get-tuple-element.35.refs_2_.refs_0_, ...), custom_call_target="tpu_custom_call" | custom-call | flops 1048576 | bytes 65536 | tf_op jit(solution)/shard_map/pallas_call | solution.py:238
  155.0 3.8 %collective-permute-done.10.refs_1_ = bf16[1216,512]{1,0:T(8,128)(2,1)S(1)} collective-permute-done((bf16[1216,512]{1,0:T(8,128)(2,1)}, bf16[1216,512]{1,0:T(8,128)(2,1)S(1)}, u32[]{:S(2)}, u32[]{:S(2)}) %collective-permute-start.10) | collective-permute-done | bytes 1245216 | tf_op jit(solution)/shard_map/ppermute | solution.py:313
  158.8 3.6 %collective-permute-done.11.refs_2_ = bf16[1216,512]{1,0:T(8,128)(2,1)S(1)} collective-permute-done((bf16[1216,512]{1,0:T(8,128)(2,1)}, bf16[1216,512]{1,0:T(8,128)(2,1)S(1)}, u32[]{:S(2)}, u32[]{:S(2)}) %collective-permute-start.11) | collective-permute-done | bytes 1245216 | tf_op jit(solution)/shard_map/ppermute | solution.py:313
  162.6 1.6 collective-permute-start.13
  164.2 1.1 collective-permute-start.14
  165.3 1.5 collective-permute-done.12
  166.8 3.5 %add_convert_fusion = bf16[4,4,512,128]{3,2,1,0:T(8,128)(2,1)} fusion(bf16[4,4,512,128]{3,2,1,0:T(8,128)(2,1)S(1)} %collective-permute-done.12, bf16[4,4,512,128]{3,2,1,0:T(8,128)(2,1)} %get-tuple-element.31), kind=kLoop, calls=%fused_computation | loop fusion | flops 4194304 | bytes 6291456 | tf_op jit(solution)/shard_map/convert_element_type | solution.py:363
  170.3 8.9 %collective-permute-done.13.refs_1_ = bf16[608,512]{1,0:T(8,128)(2,1)S(1)} collective-permute-done((bf16[608,512]{1,0:T(8,128)(2,1)S(1)}, bf16[608,512]{1,0:T(8,128)(2,1)S(1)}, u32[]{:S(2)}, u32[]{:S(2)}) %collective-permute-start.13) | collective-permute-done | bytes 622624 | tf_op jit(solution)/shard_map/ppermute | solution.py:313
  180.0 0.8 copy-done.8
  180.8 3.7 %all-to-all-start.2 = ((bf16[16,512,128]{2,1,0:T(8,128)(2,1)}), bf16[16,512,128]{2,1,0:T(8,128)(2,1)S(1)}, u32[]{:S(2)}, u32[]{:S(2)}) async-start(bf16[16,512,128]{2,1,0:T(8,128)(2,1)} %bitcast.11), calls=%async_computation.2 | async-start | bytes 4194304 | tf_op jit(solution)/shard_map/all_to_all | solution.py:365
  185.3 2.1 collective-permute-start.17
  187.5 1.1 slice.29
  188.6 2.7 %collective-permute-start.23 = (bf16[608,512]{1,0:T(8,128)(2,1)S(1)}, bf16[608,512]{1,0:T(8,128)(2,1)}, u32[]{:S(2)}, u32[]{:S(2)}) collective-permute-start(bf16[608,512]{1,0:T(8,128)(2,1)S(1)} %slice.29), channel_id=1, source_target_pairs={{0,96},{32,0},{64,32},{96,64},{1,97},{33,1},{65,33},{97,65},{2,98}... | collective-permute-start | bytes 1867784 | tf_op jit(solution)/shard_map/ppermute | solution.py:313
  191.3 0.8 slice.26
  192.9 7.6 %collective-permute-done.15.refs_1_ = bf16[608,512]{1,0:T(8,128)(2,1)S(1)} collective-permute-done((bf16[608,512]{1,0:T(8,128)(2,1)}, bf16[608,512]{1,0:T(8,128)(2,1)S(1)}, u32[]{:S(2)}, u32[]{:S(2)}) %collective-permute-start.15) | collective-permute-done | bytes 622624 | tf_op jit(solution)/shard_map/ppermute | solution.py:313
  200.5 0.8 slice.24
  201.3 1.4 collective-permute-start.16
  203.5 10.4 %collective-permute-done.22.refs_3_ = bf16[608,512]{1,0:T(8,128)(2,1)S(1)} collective-permute-done((bf16[608,512]{1,0:T(8,128)(2,1)S(1)}, bf16[608,512]{1,0:T(8,128)(2,1)S(1)}, u32[]{:S(2)}, u32[]{:S(2)}) %collective-permute-start.22) | collective-permute-done | bytes 622624 | tf_op jit(solution)/shard_map/ppermute | solution.py:313
  214.2 1.0 reduce_sum.12
  215.2 5.8 %shard_map.73.refs_3_.refs_5_.refs_2_ = bf16[2048,1024]{1,0:T(8,128)(2,1)} custom-call(s32[4]{0:T(128)} %pad_add_fusion.pos, bf16[32,512,128]{2,1,0:T(8,128)(2,1)} %bitcast.17), custom_call_target="tpu_custom_call" | custom-call | flops 1048576 | bytes 65536 | tf_op jit(solution)/shard_map/pallas_call | solution.py:258
  221.1 6.1 %shard_map.74.refs_3_ = f32[608,1024]{1,0:T(8,128)} custom-call(bf16[608,512]{1,0:T(8,128)(2,1)} %get-tuple-element.35.refs_2_.refs_0_, bf16[608,512]{1,0:T(8,128)(2,1)} %copy-done.10, bf16[608,512]{1,0:T(8,128)(2,1)} %copy-done.11, bf16[2048,1024]{1,0:T(8,128)(2,1)} %shard_map.73.refs_3_.refs_5_.refs_2_), custom_call_target="tpu_custom_call" | custom-call | flops 1048576 | bytes 65536 | tf_op jit(solution)/shard_map/pallas_call | solution.py:302
  227.1 9.9 %shard_map.75.refs_6_ = bf16[2374,1024]{1,0:T(8,128)(2,1)} custom-call(bf16[1216,512]{1,0:T(8,128)(2,1)} %get-tuple-element.27.refs_0_, bf16[1216,512]{1,0:T(8,128)(2,1)} %copy-done.2, bf16[1216,512]{1,0:T(8,128)(2,1)} %copy-done.3, bf16[608,512]{1,0:T(8,128)(2,1)} %copy-done.12, bf16[608,512]{1,0:T(8,128)(2,1)} %collective-permute-done.23.refs_4_, ...), custom_call_target="tpu_custom_call" | custom-call | flops 1048576 | bytes 65536 | tf_op jit(solution)/shard_map/pallas_call | solution.py:302
  237.0 6.7 %shard_map.76.refs_4_ = bf16[2374,1024]{1,0:T(8,128)(2,1)} custom-call(bf16[608,512]{1,0:T(8,128)(2,1)} %get-tuple-element.29.refs_1_.refs_0_, bf16[608,512]{1,0:T(8,128)(2,1)} %copy-done.6, bf16[608,512]{1,0:T(8,128)(2,1)} %copy-done.8, bf16[304,512]{1,0:T(8,128)(2,1)} %collective-permute-done.20.refs_3_, ...), custom_call_target="tpu_custom_call", output_to_operand_aliasing={{}: (6, {})} | custom-call | flops 1048576 | bytes 65536 | tf_op jit(solution)/shard_map/pallas_call | solution.py:302
  243.8 4.0 %shard_map.77 = bf16[2374,1024]{1,0:T(8,128)(2,1)} custom-call(bf16[304,512]{1,0:T(8,128)(2,1)} %collective-permute-done.16.refs_0_, bf16[304,512]{1,0:T(8,128)(2,1)} %collective-permute-done.18.refs_1_, bf16[2048,1024]{1,0:T(8,128)(2,1)} %shard_map.73.refs_3_.refs_5_.refs_2_, f32[608,1024]{1,0:T(8,128)} %shard_map.74.refs_3_, ...), custom_call_target="tpu_custom_call", output_to_operand_aliasing={{}: (4, {})} | custom-call | flops 1048576 | bytes 65536 | tf_op jit(solution)/shard_map/pallas_call | solution.py:302
  (64 shorter events, 7.6 us)
Async XLA Ops:
  11.6 9.7 %copy-start.15 = (bf16[512,128]{1,0:T(8,128)(2,1)S(1)}, bf16[512,128]{1,0:T(8,128)(2,1)}, u32[]{:S(2)}) copy-start(bf16[512,128]{1,0:T(8,128)(2,1)} %param.4) | copy-start | bytes 393220
  11.6 82.8 %all-to-all-start = ((bf16[32,19,16,128]{3,2,1,0:T(8,128)(2,1)}), bf16[32,19,16,128]{3,2,1,0:T(8,128)(2,1)S(1)}, u32[]{:S(2)}, u32[]{:S(2)}) async-start(bf16[32,19,16,128]{3,2,1,0:T(8,128)(2,1)} %shard_map.67), calls=%async_computation | async-start | bytes 4980736 | tf_op jit(solution)/shard_map/all_to_all | solution.py:343
  21.4 31.5 %collective-permute-start.2 = (bf16[512,128]{1,0:T(8,128)(2,1)S(1)}, bf16[512,128]{1,0:T(8,128)(2,1)S(1)}, u32[]{:S(2)}, u32[]{:S(2)}) collective-permute-start(bf16[512,128]{1,0:T(8,128)(2,1)S(1)} %copy-done.15), channel_id=1, source_target_pairs={{0,6},{1,25},{2,0},{3,27},{4,2},{5,29},{6,4},{7,31},{8,14},{9,1},{... | collective-permute-start | bytes 393224 | tf_op jit(solution)/shard_map/ppermute | solution.py:329
  24.1 29.9 %collective-permute-start.1 = (bf16[512,128]{1,0:T(8,128)(2,1)S(1)}, bf16[512,128]{1,0:T(8,128)(2,1)S(1)}, u32[]{:S(2)}, u32[]{:S(2)}) collective-permute-start(bf16[512,128]{1,0:T(8,128)(2,1)S(1)} %copy-done.15), channel_id=1, source_target_pairs={{0,4},{1,17},{2,6},{3,19},{4,0},{5,21},{6,2},{7,23},{8,12},{9,25},... | collective-permute-start | bytes 393224 | tf_op jit(solution)/shard_map/ppermute | solution.py:329
  24.6 30.0 %collective-permute-start = (bf16[512,128]{1,0:T(8,128)(2,1)S(1)}, bf16[512,128]{1,0:T(8,128)(2,1)S(1)}, u32[]{:S(2)}, u32[]{:S(2)}) collective-permute-start(bf16[512,128]{1,0:T(8,128)(2,1)S(1)} %copy-done.15), channel_id=1, source_target_pairs={{0,2},{1,9},{2,4},{3,11},{4,6},{5,13},{6,0},{7,15},{8,10},{9,17},{... | collective-permute-start | bytes 393224 | tf_op jit(solution)/shard_map/ppermute | solution.py:329
  54.7 20.4 %copy-start.5 = (bf16[4,512,128]{2,1,0:T(8,128)(2,1)}, bf16[4,512,128]{2,1,0:T(8,128)(2,1)S(1)}, u32[]{:S(2)}) copy-start(bf16[4,512,128]{2,1,0:T(8,128)(2,1)S(1)} %pad_maximum_fusion.refs_0_) | copy-start | bytes 1572868
  54.7 9.6 %collective-permute-start.3 = (bf16[4,512,128]{2,1,0:T(8,128)(2,1)S(1)}, bf16[4,512,128]{2,1,0:T(8,128)(2,1)S(1)}, u32[]{:S(2)}, u32[]{:S(2)}) collective-permute-start(bf16[4,512,128]{2,1,0:T(8,128)(2,1)S(1)} %pad_maximum_fusion.refs_0_), channel_id=1, source_target_pairs={{0,8},{1,3},{2,10},{3,5},{4,12},{5,7},{6,14},{7,1},{8,16},{9,11},{... | collective-permute-start | bytes 1572872 | tf_op jit(solution)/shard_map/ppermute | solution.py:329
  55.9 15.0 %collective-permute-start.4 = (bf16[4,512,128]{2,1,0:T(8,128)(2,1)S(1)}, bf16[4,512,128]{2,1,0:T(8,128)(2,1)}, u32[]{:S(2)}, u32[]{:S(2)}) collective-permute-start(bf16[4,512,128]{2,1,0:T(8,128)(2,1)S(1)} %pad_maximum_fusion.refs_0_), channel_id=1, source_target_pairs={{0,16},{1,5},{2,18},{3,7},{4,20},{5,1},{6,22},{7,3},{8,24},{9,13},... | collective-permute-start | bytes 1572872 | tf_op jit(solution)/shard_map/ppermute | solution.py:329
  58.3 14.1 %collective-permute-start.5 = (bf16[4,512,128]{2,1,0:T(8,128)(2,1)S(1)}, bf16[4,512,128]{2,1,0:T(8,128)(2,1)}, u32[]{:S(2)}, u32[]{:S(2)}) collective-permute-start(bf16[4,512,128]{2,1,0:T(8,128)(2,1)S(1)} %pad_maximum_fusion.refs_0_), channel_id=1, source_target_pairs={{0,24},{1,7},{2,26},{3,1},{4,28},{5,3},{6,30},{7,5},{8,0},{9,15},{... | collective-permute-start | bytes 1572872 | tf_op jit(solution)/shard_map/ppermute | solution.py:329
  59.6 13.5 %collective-permute-start.6 = (bf16[4,512,128]{2,1,0:T(8,128)(2,1)S(1)}, bf16[4,512,128]{2,1,0:T(8,128)(2,1)}, u32[]{:S(2)}, u32[]{:S(2)}) collective-permute-start(bf16[4,512,128]{2,1,0:T(8,128)(2,1)S(1)} %pad_maximum_fusion.refs_0_), channel_id=1, source_target_pairs={{0,1},{1,0},{2,3},{3,2},{4,5},{5,4},{6,7},{7,6},{8,9},{9,8},{10,11... | collective-permute-start | bytes 1572872 | tf_op jit(solution)/shard_map/ppermute | solution.py:317
  64.3 10.8 %copy-start.13 = (bf16[4,512,128]{2,1,0:T(8,128)(2,1)}, bf16[4,512,128]{2,1,0:T(8,128)(2,1)S(1)}, u32[]{:S(2)}) copy-start(bf16[4,512,128]{2,1,0:T(8,128)(2,1)S(1)} %collective-permute-done.3.refs_1_) | copy-start | bytes 1572868
  64.3 8.8 %collective-permute-start.7 = (bf16[4,512,128]{2,1,0:T(8,128)(2,1)S(1)}, bf16[4,512,128]{2,1,0:T(8,128)(2,1)}, u32[]{:S(2)}, u32[]{:S(2)}) collective-permute-start(bf16[4,512,128]{2,1,0:T(8,128)(2,1)S(1)} %collective-permute-done.3.refs_1_), channel_id=1, source_target_pairs={{0,1},{1,0},{2,3},{3,2},{4,5},{5,4},{6,7},{7,6},{8,9},{9,8},{10,11... | collective-permute-start | bytes 1572872 | tf_op jit(solution)/shard_map/ppermute | solution.py:317
  70.9 3.4 %collective-permute-start.8 = (bf16[4,512,128]{2,1,0:T(8,128)(2,1)}, bf16[4,512,128]{2,1,0:T(8,128)(2,1)}, u32[]{:S(2)}, u32[]{:S(2)}) collective-permute-start(bf16[4,512,128]{2,1,0:T(8,128)(2,1)} %collective-permute-done.4.refs_2_), channel_id=1, source_target_pairs={{0,1},{1,0},{2,3},{3,2},{4,5},{5,4},{6,7},{7,6},{8,9},{9,8},{10,11... | collective-permute-start | bytes 1572872 | tf_op jit(solution)/shard_map/ppermute | solution.py:317
  72.4 2.6 %collective-permute-start.9 = (bf16[4,512,128]{2,1,0:T(8,128)(2,1)}, bf16[4,512,128]{2,1,0:T(8,128)(2,1)}, u32[]{:S(2)}, u32[]{:S(2)}) collective-permute-start(bf16[4,512,128]{2,1,0:T(8,128)(2,1)} %collective-permute-done.5.refs_3_), channel_id=1, source_target_pairs={{0,1},{1,0},{2,3},{3,2},{4,5},{5,4},{6,7},{7,6},{8,9},{9,8},{10,11... | collective-permute-start | bytes 1572872 | tf_op jit(solution)/shard_map/ppermute | solution.py:317
  94.4 1.4 copy-start
  95.8 12.7 %copy-start.16 = (bf16[512,128]{1,0:T(8,128)(2,1)S(1)}, bf16[512,128]{1,0:T(8,128)(2,1)}, u32[]{:S(2)}) copy-start(bf16[512,128]{1,0:T(8,128)(2,1)} %param.4) | copy-start | bytes 393220
  103.3 16.8 %all-to-all-start.1 = ((f32[32,8,512]{2,1,0:T(8,128)}), f32[32,8,512]{2,1,0:T(8,128)S(1)}, u32[]{:S(2)}, u32[]{:S(2)}) async-start(f32[32,8,512]{2,1,0:T(8,128)} %get-tuple-element.24), calls=%async_computation.1 | async-start | bytes 1048576 | tf_op jit(solution)/shard_map/all_to_all | solution.py:346
  108.5 106.7 %all-gather.3.cloned.1.call-start = ((), (), s32[]{:S(2)}) async-start(), calls=%async_computation.3 | async-start | bytes 4325376 | tf_op jit(solution)/shard_map/all_gather | solution.py:352
  108.5 16.8 %collective-permute-start.19 = (bf16[512,128]{1,0:T(8,128)(2,1)S(1)}, bf16[512,128]{1,0:T(8,128)(2,1)S(1)}, u32[]{:S(2)}, u32[]{:S(2)}) collective-permute-start(bf16[512,128]{1,0:T(8,128)(2,1)S(1)} %copy-done.16), channel_id=1, source_target_pairs={{0,0},{8,32},{16,64},{24,96},{32,8},{40,40},{48,72},{56,104},{64,1... | collective-permute-start | bytes 393224 | tf_op jit(solution)/shard_map/ppermute | solution.py:351
  120.1 0.8 copy-start.1
  125.4 0.7 copy-start.14
  126.1 32.7 %collective-permute-start.10 = (bf16[1216,512]{1,0:T(8,128)(2,1)}, bf16[1216,512]{1,0:T(8,128)(2,1)S(1)}, u32[]{:S(2)}, u32[]{:S(2)}) collective-permute-start(bf16[1216,512]{1,0:T(8,128)(2,1)} %get-tuple-element.27.refs_0_), channel_id=1, source_target_pairs={{0,32},{32,64},{64,96},{96,0},{1,33},{33,65},{65,97},{97,1},{2,34}... | collective-permute-start | bytes 3735560 | tf_op jit(solution)/shard_map/ppermute | solution.py:313
  131.6 30.8 %collective-permute-start.11 = (bf16[1216,512]{1,0:T(8,128)(2,1)}, bf16[1216,512]{1,0:T(8,128)(2,1)S(1)}, u32[]{:S(2)}, u32[]{:S(2)}) collective-permute-start(bf16[1216,512]{1,0:T(8,128)(2,1)} %get-tuple-element.27.refs_0_), channel_id=1, source_target_pairs={{0,96},{32,0},{64,32},{96,64},{1,97},{33,1},{65,33},{97,65},{2,98}... | collective-permute-start | bytes 3735560 | tf_op jit(solution)/shard_map/ppermute | solution.py:313
  136.5 26.2 %copy-start.4 = (bf16[608,512]{1,0:T(8,128)(2,1)S(1)}, bf16[608,512]{1,0:T(8,128)(2,1)}, u32[]{:S(2)}) copy-start(bf16[608,512]{1,0:T(8,128)(2,1)} %get-tuple-element.29.refs_1_.refs_0_) | copy-start | bytes 1867780
  158.8 28.6 %copy-start.2 = (bf16[1216,512]{1,0:T(8,128)(2,1)}, bf16[1216,512]{1,0:T(8,128)(2,1)S(1)}, u32[]{:S(2)}) copy-start(bf16[1216,512]{1,0:T(8,128)(2,1)S(1)} %collective-permute-done.10.refs_1_) | copy-start | bytes 3735556
  162.4 7.9 %copy-start.3 = (bf16[1216,512]{1,0:T(8,128)(2,1)}, bf16[1216,512]{1,0:T(8,128)(2,1)S(1)}, u32[]{:S(2)}) copy-start(bf16[1216,512]{1,0:T(8,128)(2,1)S(1)} %collective-permute-done.11.refs_2_) | copy-start | bytes 3735556
  162.4 4.4 %collective-permute-start.12 = (bf16[4,4,512,128]{3,2,1,0:T(8,128)(2,1)}, bf16[4,4,512,128]{3,2,1,0:T(8,128)(2,1)S(1)}, u32[]{:S(2)}, u32[]{:S(2)}) collective-permute-start(bf16[4,4,512,128]{3,2,1,0:T(8,128)(2,1)} %get-tuple-element.33), channel_id=1, source_target_pairs={{0,1},{1,0},{2,3},{3,2},{4,5},{5,4},{6,7},{7,6},{8,9},{9,8},{10,11... | collective-permute-start | bytes 6291464 | tf_op jit(solution)/shard_map/ppermute | solution.py:317
  162.6 16.5 %collective-permute-start.13 = (bf16[608,512]{1,0:T(8,128)(2,1)S(1)}, bf16[608,512]{1,0:T(8,128)(2,1)S(1)}, u32[]{:S(2)}, u32[]{:S(2)}) collective-permute-start(bf16[608,512]{1,0:T(8,128)(2,1)S(1)} %copy-done.4), channel_id=1, source_target_pairs={{0,32},{32,64},{64,96},{96,0},{1,33},{33,65},{65,97},{97,1},{2,34}... | collective-permute-start | bytes 1867784 | tf_op jit(solution)/shard_map/ppermute | solution.py:313
  164.2 15.3 %collective-permute-start.14 = (bf16[608,512]{1,0:T(8,128)(2,1)S(1)}, bf16[608,512]{1,0:T(8,128)(2,1)S(1)}, u32[]{:S(2)}, u32[]{:S(2)}) collective-permute-start(bf16[608,512]{1,0:T(8,128)(2,1)S(1)} %copy-done.4), channel_id=1, source_target_pairs={{0,96},{32,0},{64,32},{96,64},{1,97},{33,1},{65,33},{97,65},{2,98}... | collective-permute-start | bytes 1867784 | tf_op jit(solution)/shard_map/ppermute | solution.py:313
  179.2 0.8 copy-start.6
  180.0 0.8 copy-start.8
  180.8 33.4 %all-to-all-start.2 = ((bf16[16,512,128]{2,1,0:T(8,128)(2,1)}), bf16[16,512,128]{2,1,0:T(8,128)(2,1)S(1)}, u32[]{:S(2)}, u32[]{:S(2)}) async-start(bf16[16,512,128]{2,1,0:T(8,128)(2,1)} %bitcast.11), calls=%async_computation.2 | async-start | bytes 4194304 | tf_op jit(solution)/shard_map/all_to_all | solution.py:365
  184.6 6.8 %copy-start.7 = (bf16[608,512]{1,0:T(8,128)(2,1)S(1)}, bf16[608,512]{1,0:T(8,128)(2,1)}, u32[]{:S(2)}) copy-start(bf16[608,512]{1,0:T(8,128)(2,1)} %copy-done.6) | copy-start | bytes 1867780
  184.6 7.5 %copy-start.9 = (bf16[608,512]{1,0:T(8,128)(2,1)S(1)}, bf16[608,512]{1,0:T(8,128)(2,1)}, u32[]{:S(2)}) copy-start(bf16[608,512]{1,0:T(8,128)(2,1)} %copy-done.8) | copy-start | bytes 1867780
  184.6 15.9 %collective-permute-start.15 = (bf16[608,512]{1,0:T(8,128)(2,1)}, bf16[608,512]{1,0:T(8,128)(2,1)S(1)}, u32[]{:S(2)}, u32[]{:S(2)}) collective-permute-start(bf16[608,512]{1,0:T(8,128)(2,1)} %get-tuple-element.35.refs_2_.refs_0_), channel_id=1, source_target_pairs={{0,32},{32,64},{64,96},{96,0},{1,33},{33,65},{65,97},{97,1},{2,34}... | collective-permute-start | bytes 1867784 | tf_op jit(solution)/shard_map/ppermute | solution.py:313
  185.3 16.0 %collective-permute-start.17 = (bf16[608,512]{1,0:T(8,128)(2,1)}, bf16[608,512]{1,0:T(8,128)(2,1)S(1)}, u32[]{:S(2)}, u32[]{:S(2)}) collective-permute-start(bf16[608,512]{1,0:T(8,128)(2,1)} %get-tuple-element.35.refs_2_.refs_0_), channel_id=1, source_target_pairs={{0,96},{32,0},{64,32},{96,64},{1,97},{33,1},{65,33},{97,65},{2,98}... | collective-permute-start | bytes 1867784 | tf_op jit(solution)/shard_map/ppermute | solution.py:313
  187.4 26.5 %collective-permute-start.22 = (bf16[608,512]{1,0:T(8,128)(2,1)S(1)}, bf16[608,512]{1,0:T(8,128)(2,1)S(1)}, u32[]{:S(2)}, u32[]{:S(2)}) collective-permute-start(bf16[608,512]{1,0:T(8,128)(2,1)S(1)} %slice.28), channel_id=1, source_target_pairs={{0,32},{32,64},{64,96},{96,0},{1,33},{33,65},{65,97},{97,1},{2,34}... | collective-permute-start | bytes 1867784 | tf_op jit(solution)/shard_map/ppermute | solution.py:313
  188.6 38.5 %collective-permute-start.23 = (bf16[608,512]{1,0:T(8,128)(2,1)S(1)}, bf16[608,512]{1,0:T(8,128)(2,1)}, u32[]{:S(2)}, u32[]{:S(2)}) collective-permute-start(bf16[608,512]{1,0:T(8,128)(2,1)S(1)} %slice.29), channel_id=1, source_target_pairs={{0,96},{32,0},{64,32},{96,64},{1,97},{33,1},{65,33},{97,65},{2,98}... | collective-permute-start | bytes 1867784 | tf_op jit(solution)/shard_map/ppermute | solution.py:313
  192.1 44.9 %collective-permute-start.20 = (bf16[304,512]{1,0:T(8,128)(2,1)}, bf16[304,512]{1,0:T(8,128)(2,1)}, u32[]{:S(2)}, u32[]{:S(2)}) collective-permute-start(bf16[304,512]{1,0:T(8,128)(2,1)} %slice.26), channel_id=1, source_target_pairs={{0,32},{32,64},{64,96},{96,0},{1,33},{33,65},{65,97},{97,1},{2,34}... | collective-permute-start | bytes 933896 | tf_op jit(solution)/shard_map/ppermute | solution.py:313
  200.5 13.3 %copy-start.10 = (bf16[608,512]{1,0:T(8,128)(2,1)}, bf16[608,512]{1,0:T(8,128)(2,1)S(1)}, u32[]{:S(2)}) copy-start(bf16[608,512]{1,0:T(8,128)(2,1)S(1)} %collective-permute-done.15.refs_1_) | copy-start | bytes 1867780
  200.5 36.5 %collective-permute-start.21 = (bf16[304,512]{1,0:T(8,128)(2,1)}, bf16[304,512]{1,0:T(8,128)(2,1)}, u32[]{:S(2)}, u32[]{:S(2)}) collective-permute-start(bf16[304,512]{1,0:T(8,128)(2,1)} %slice.27), channel_id=1, source_target_pairs={{0,96},{32,0},{64,32},{96,64},{1,97},{33,1},{65,33},{97,65},{2,98}... | collective-permute-start | bytes 933896 | tf_op jit(solution)/shard_map/ppermute | solution.py:313
  201.3 12.5 %copy-start.11 = (bf16[608,512]{1,0:T(8,128)(2,1)}, bf16[608,512]{1,0:T(8,128)(2,1)S(1)}, u32[]{:S(2)}) copy-start(bf16[608,512]{1,0:T(8,128)(2,1)S(1)} %collective-permute-done.17.refs_2_) | copy-start | bytes 1867780
  201.3 42.5 %collective-permute-start.16 = (bf16[304,512]{1,0:T(8,128)(2,1)}, bf16[304,512]{1,0:T(8,128)(2,1)}, u32[]{:S(2)}, u32[]{:S(2)}) collective-permute-start(bf16[304,512]{1,0:T(8,128)(2,1)} %slice.24), channel_id=1, source_target_pairs={{0,32},{32,64},{64,96},{96,0},{1,33},{33,65},{65,97},{97,1},{2,34}... | collective-permute-start | bytes 933896 | tf_op jit(solution)/shard_map/ppermute | solution.py:313
  213.8 7.2 %copy-start.12 = (bf16[608,512]{1,0:T(8,128)(2,1)}, bf16[608,512]{1,0:T(8,128)(2,1)S(1)}, u32[]{:S(2)}) copy-start(bf16[608,512]{1,0:T(8,128)(2,1)S(1)} %collective-permute-done.22.refs_3_) | copy-start | bytes 1867780
  213.9 29.9 %collective-permute-start.18 = (bf16[304,512]{1,0:T(8,128)(2,1)}, bf16[304,512]{1,0:T(8,128)(2,1)}, u32[]{:S(2)}, u32[]{:S(2)}) collective-permute-start(bf16[304,512]{1,0:T(8,128)(2,1)} %slice.25), channel_id=1, source_target_pairs={{0,96},{32,0},{64,32},{96,64},{1,97},{33,1},{65,33},{97,65},{2,98}... | collective-permute-start | bytes 933896 | tf_op jit(solution)/shard_map/ppermute | solution.py:313
Sparse Core Ops, SparseCore 0:
  126.2 49.2 all-gather.2

commit v4 on v3

--- a/solution.py
+++ b/solution.py
@@ -340,7 +340,7 @@
     blocks = prep(teacher_logits)
     one = jnp.stack(spread(hidden, 0))
     own = spread(after(one, blocks), 1)
-    teacher = lax.all_to_all(blocks, V, 0, 0, tiled=True)
+    teacher = lax.all_to_all(after(blocks, *own[1:]), V, 0, 0, tiled=True)
     s, m, l = student(pos, wt, own, [swap(x) for x in own])
     t, share = stats(m, l, s, teacher)
     gathered = lax.all_to_all(share, V, 0, 0, tiled=True)
@@ -351,24 +351,28 @@
     across = lax.ppermute(hidden, ("x", "y"), [(x * 4 + y, y * 4 + x) for x in range(4) for y in range(4)])
     h2 = lax.all_gather(after(across, kl), V)
 
-    def ring(g):
-        left, right = shift(g, 1), shift(g, 3)
-        half = g.shape[0] // 2
-        return [g, left, right], [shift(left[:half], 1), shift(right[half:], 3)]
-
-    near_u, far_u = ring(gu)
-    near_m, far_m = ring(gm)
-    near_l, far_l = ring(after(gl, *near_m))
+    def near(g):
+        return [g, shift(g, 1), shift(g, 3)]
+
+    def far(parts, *first):
+        half = parts[0].shape[0] // 2
+        left, right = after(parts[1], *first), after(parts[2], *first)
+        return [shift(left[:half], 1), shift(right[half:], 3)]
+
+    near_u, near_m = near(gu), near(gm)
+    far_u, far_m = far(near_u), far(near_m)
+    near_l = near(after(gl, *far_u))
     mine, other = hidden_part(pos, (gu, gm, gl), wt)
-    both = (mine.astype(F32) + swap(after(other, *near_u)).astype(F32)).astype(BF16)
-    both = after(both, *near_m)
+    both = (mine.astype(F32) + swap(after(other, *near_u[1:], *near_m[1:])).astype(F32)).astype(BF16)
+    both = after(both, *far_u)
     got = lax.all_to_all(both.reshape(16, T, 128), ("y", "z"), 0, 0, tiled=True)
-    grad_hidden = jnp.sum(got.astype(F32), axis=0).astype(BF16)
 
     k = tokens(pos, h2)
     head = head_piece(near_u, far_u, k, *CUTS[0])
     head = head_piece(near_m, far_m, k, *CUTS[1], other=head)
+    far_l = far(near_l, head)
     part = head_piece(near_l, [], k, *CUTS[2])
+    grad_hidden = jnp.sum(after(got, part).astype(F32), axis=0).astype(BF16)
     head = head_piece([], far_l, k, *CUTS[2], prior=part, other=head)
     return kl.reshape(T), grad_hidden, head.T
 

time: 259 us -> 235 us (0.907)
  waiting for transfers between devices: 86.8 us -> 67 us
    ppermute x6, waiting for transfers between devices: 37.8 us -> 13.5 us  [spread(): got.append(lax.ppermute(x, V, pairs))]
    all_to_all x1, waiting for transfers between devices: 0.01 us -> 8.66 us  [per_device(): teacher = lax.all_to_all(after(blocks, *own[1:]), V, 0, 0, tiled=True)]
    ppermute x12, waiting for transfers between devices: 34.6 us -> 29.8 us  [shift(): return lax.ppermute(x, 'x', [(i, (i + n) % 4) for i in range(4)])]
    ppermute x12, starting transfers between devices: 15.6 us -> 20.1 us  [shift(): return lax.ppermute(x, 'x', [(i, (i + n) % 4) for i in range(4)])]
    all_to_all x1, starting transfers between devices: 9.74 us -> 6.6 us  [per_device(): teacher = lax.all_to_all(after(blocks, *own[1:]), V, 0, 0, tiled=True)]
    ppermute x5, starting transfers between devices: 4.7 us -> 1.57 us  [swap(): return lax.ppermute(x, 'c', [(0, 1), (1, 0)])]
    unnamed x34 -> x40, local copies, waits for them, and re-layouts: 4.33 us -> 7.3 us
  transfers between devices with their start and end apart: 28 -> 28, of which waited for: 15 -> 15; matrix products, arithmetic and copies ran while one was open for 4% -> 3% of each run, Pallas kernels for 30% -> 34%
where the time goes in v4:
time: 235 us; the launch traced here: 233 us
  Pallas kernels  90 us (38%)
  waiting for transfers between devices  67 us (29%)
  starting transfers between devices  47.3 us (20%)
  between operations  14.2 us (6%)
  local copies, waits for them, and re-layouts  11.1 us (5%)
  other arithmetic  3.5 us (1%)
    ppermute x12, waiting for transfers between devices, shift(): return lax.ppermute(x, 'x', [(i, (i + n) % 4) for i in range(4)])  29.8 us
    pallas_call x4, Pallas kernels, head_piece(): call(functools.partial(head_body, bool(near), bool(far), prior is not Non...  26.7 us
    ppermute x12, starting transfers between devices, shift(): return lax.ppermute(x, 'x', [(i, (i + n) % 4) for i in range(4)])  20.1 us
    pallas_call x1, Pallas kernels, student(): call(student_body, out_shape=[jax.ShapeDtypeStruct((NS * SB, T), F32), pa...  19.3 us
    pallas_call x1, Pallas kernels, hidden_part(): call(hidden_body, out_shape=[jax.ShapeDtypeStruct((4, 4, T, 128), BF16)]...  17 us
    ppermute x6, waiting for transfers between devices, spread(): got.append(lax.ppermute(x, V, pairs))  13.5 us
    all_to_all x1, waiting for transfers between devices, per_device(): gathered = lax.all_to_all(share, V, 0, 0, tiled=True)  11 us
    ppermute x6, starting transfers between devices, spread(): got.append(lax.ppermute(x, V, pairs))  10.1 us
  transfers between devices with their start and end apart: 28, of which 15 were waited for; matrix products, arithmetic and copies ran while one was open for 3% of the time, Pallas kernels for 34%

profile of v4, /device:TPU:1, one launch (start us, length us, event | category | flops | bytes accessed | tf_op | source)
XLA Modules:
  0.0 233.1 jit_solution(1347534245370281421)
XLA Ops:
  7.2 3.6 %collective-permute-start.2 = (bf16[512,128]{1,0:T(8,128)(2,1)}, bf16[512,128]{1,0:T(8,128)(2,1)S(1)}, u32[]{:S(2)}, u32[]{:S(2)}) collective-permute-start(bf16[512,128]{1,0:T(8,128)(2,1)} %param.4), channel_id=1, source_target_pairs={{0,6},{1,25},{2,0},{3,27},{4,2},{5,29},{6,4},{7,31},{8,14},{9,1},{... | collective-permute-start | bytes 393224 | tf_op jit(solution)/shard_map/ppermute | solution.py:329
  11.9 4.4 %shard_map.67 = bf16[32,19,16,128]{3,2,1,0:T(8,128)(2,1)} custom-call(bf16[16,75968]{1,0:T(8,128)(2,1)} %t_ref.1), custom_call_target="tpu_custom_call" | custom-call | flops 1048576 | bytes 65536 | tf_op jit(solution)/shard_map/pallas_call | solution.py:55
  16.4 1.6 collective-permute-done
  18.1 1.4 collective-permute-start.3
  19.5 3.3 %collective-permute-start.4 = (bf16[4,512,128]{2,1,0:T(8,128)(2,1)S(1)}, bf16[4,512,128]{2,1,0:T(8,128)(2,1)S(1)}, u32[]{:S(2)}, u32[]{:S(2)}) collective-permute-start(bf16[4,512,128]{2,1,0:T(8,128)(2,1)S(1)} %pad_maximum_fusion.refs_0_), channel_id=1, source_target_pairs={{0,16},{1,5},{2,18},{3,7},{4,20},{5,1},{6,22},{7,3},{8,24},{9,13},... | collective-permute-start | bytes 1572872 | tf_op jit(solution)/shard_map/ppermute | solution.py:329
  22.8 0.7 collective-permute-start.5
  23.6 5.0 %collective-permute-done.3.refs_1_ = bf16[4,512,128]{2,1,0:T(8,128)(2,1)S(1)} collective-permute-done((bf16[4,512,128]{2,1,0:T(8,128)(2,1)S(1)}, bf16[4,512,128]{2,1,0:T(8,128)(2,1)S(1)}, u32[]{:S(2)}, u32[]{:S(2)}) %collective-permute-start.3) | collective-permute-done | bytes 524320 | tf_op jit(solution)/shard_map/ppermute | solution.py:329
  28.5 6.8 %collective-permute-done.4.refs_2_ = bf16[4,512,128]{2,1,0:T(8,128)(2,1)S(1)} collective-permute-done((bf16[4,512,128]{2,1,0:T(8,128)(2,1)S(1)}, bf16[4,512,128]{2,1,0:T(8,128)(2,1)S(1)}, u32[]{:S(2)}, u32[]{:S(2)}) %collective-permute-start.4) | collective-permute-done | bytes 524320 | tf_op jit(solution)/shard_map/ppermute | solution.py:329
  35.3 0.8 copy-done.13
  36.1 6.6 %all-to-all-start = ((bf16[32,19,16,128]{3,2,1,0:T(8,128)(2,1)}), bf16[32,19,16,128]{3,2,1,0:T(8,128)(2,1)S(1)}, u32[]{:S(2)}, u32[]{:S(2)}) async-start(bf16[32,19,16,128]{3,2,1,0:T(8,128)(2,1)} %shard_map.67), calls=%async_computation | async-start | bytes 4980736 | tf_op jit(solution)/shard_map/all_to_all | solution.py:343
  44.9 1.5 collective-permute-done.7.refs_5_
  46.6 0.8 collective-permute-done.9.refs_7_
  47.3 19.3 %shard_map.68 = (f32[2560,512]{1,0:T(8,128)}, f32[8,512]{1,0:T(8,128)}, f32[8,512]{1,0:T(8,128)}) custom-call(s32[4]{0:T(128)} %pad_add_fusion.pos, bf16[2374,4096]{1,0:T(8,128)(2,1)} %bitcast.14, bf16[4,512,128]{2,1,0:T(8,128)(2,1)} %copy-done.6, bf16[4,512,128]{2,1,0:T(8,128)(2,1)} %copy-done.12, bf16[4,512,128]{2,1,0:T(8,128)(2,1)} %copy-done.13, ...), custom_call_target="tpu_custom_call" | custom-call | flops 1048576 | bytes 65536 | tf_op jit(solution)/shard_map/pallas_call | solution.py:97
  66.6 8.7 %all-to-all-done.t_ref = bf16[32,19,16,128]{3,2,1,0:T(8,128)(2,1)S(1)} async-done(((bf16[32,19,16,128]{3,2,1,0:T(8,128)(2,1)}), bf16[32,19,16,128]{3,2,1,0:T(8,128)(2,1)S(1)}, u32[]{:S(2)}, u32[]{:S(2)}) %all-to-all-start) | async-done | bytes 2490400 | tf_op jit(solution)/shard_map/all_to_all | solution.py:343
  75.3 1.5 copy-done
  76.7 7.5 %shard_map.69 = (bf16[2560,512]{1,0:T(8,128)(2,1)}, f32[32,8,512]{2,1,0:T(8,128)}) custom-call(f32[8,512]{1,0:T(8,128)} %get-tuple-element.25.m_ref, f32[8,512]{1,0:T(8,128)} %get-tuple-element.26.l_ref, f32[2560,512]{1,0:T(8,128)} %get-tuple-element.27.s_ref, bf16[32,19,16,128]{3,2,1,0:T(8,128)(2,1)} %copy-done), custom_call_target="tpu_custom_call" | custom-call | flops 1048576 | bytes 65536 | tf_op jit(solution)/shard_map/pallas_call | solution.py:154
  84.2 4.5 %all-to-all-start.1 = ((f32[32,8,512]{2,1,0:T(8,128)}), f32[32,8,512]{2,1,0:T(8,128)S(1)}, u32[]{:S(2)}, u32[]{:S(2)}) async-start(f32[32,8,512]{2,1,0:T(8,128)} %get-tuple-element.29), calls=%async_computation.1 | async-start | bytes 1048576 | tf_op jit(solution)/shard_map/all_to_all | solution.py:346
  89.4 11.0 %all-to-all-done.1.all_ref = f32[32,8,512]{2,1,0:T(8,128)S(1)} async-done(((f32[32,8,512]{2,1,0:T(8,128)}), f32[32,8,512]{2,1,0:T(8,128)S(1)}, u32[]{:S(2)}, u32[]{:S(2)}) %all-to-all-start.1) | async-done | bytes 524320 | tf_op jit(solution)/shard_map/all_to_all | solution.py:346
  100.4 0.8 copy-done.1
  101.2 4.5 %shard_map.70 = (bf16[1216,512]{1,0:T(8,128)(2,1)}, f32[1,512]{1,0:T(1,128)}) custom-call(f32[32,8,512]{2,1,0:T(8,128)} %copy-done.1, f32[1,512]{1,0:T(1,128)} %bitcast.22, f32[2560,512]{1,0:T(8,128)} %get-tuple-element.27.s_ref, bf16[2560,512]{1,0:T(8,128)(2,1)} %get-tuple-element.30.t_ref), custom_call_target="tpu_custom_call" | custom-call | flops 1048576 | bytes 65536 | tf_op jit(solution)/shard_map/pallas_call | solution.py:204
  106.4 5.5 %collective-permute-start.10 = (bf16[1216,512]{1,0:T(8,128)(2,1)}, bf16[1216,512]{1,0:T(8,128)(2,1)S(1)}, u32[]{:S(2)}, u32[]{:S(2)}) collective-permute-start(bf16[1216,512]{1,0:T(8,128)(2,1)} %get-tuple-element.32.refs_0_), channel_id=1, source_target_pairs={{0,32},{32,64},{64,96},{96,0},{1,33},{33,65},{65,97},{97,1},{2,34}... | collective-permute-start | bytes 3735560 | tf_op jit(solution)/shard_map/ppermute | solution.py:313
  111.9 4.8 %shard_map.71 = (bf16[608,512]{1,0:T(8,128)(2,1)}, bf16[608,512]{1,0:T(8,128)(2,1)}, f32[1,512]{1,0:T(1,128)}) custom-call(f32[32,8,512]{2,1,0:T(8,128)} %copy-done.1, f32[1,512]{1,0:T(1,128)} %bitcast.23, f32[2560,512]{1,0:T(8,128)} %get-tuple-element.27.s_ref, bf16[2560,512]{1,0:T(8,128)(2,1)} %get-tuple-element.30.t_ref), custom_call_target="tpu_custom_call" | custom-call | flops 1048576 | bytes 65536 | tf_op jit(solution)/shard_map/pallas_call | solution.py:204
  116.7 2.6 %collective-permute-start.12 = (bf16[608,512]{1,0:T(8,128)(2,1)}, bf16[608,512]{1,0:T(8,128)(2,1)S(1)}, u32[]{:S(2)}, u32[]{:S(2)}) collective-permute-start(bf16[608,512]{1,0:T(8,128)(2,1)} %get-tuple-element.34.refs_1_.refs_0_), channel_id=1, source_target_pairs={{0,32},{32,64},{64,96},{96,0},{1,33},{33,65},{65,97},{97,1},{2,34}... | collective-permute-start | bytes 1867784 | tf_op jit(solution)/shard_map/ppermute | solution.py:313
  119.3 0.9 collective-permute-start.13
  120.3 17.0 %shard_map.72 = (bf16[4,4,512,128]{3,2,1,0:T(8,128)(2,1)}, bf16[4,4,512,128]{3,2,1,0:T(8,128)(2,1)}) custom-call(s32[4]{0:T(128)} %pad_add_fusion.pos, bf16[1216,512]{1,0:T(8,128)(2,1)} %get-tuple-element.32.refs_0_, bf16[608,512]{1,0:T(8,128)(2,1)} %get-tuple-element.34.refs_1_.refs_0_, bf16[608,512]{1,0:T(8,128)(2,1)} %get-tuple-element.40.refs_2_.refs_0_, ...), custom_call_target="tpu_custom_call" | custom-call | flops 1048576 | bytes 65536 | tf_op jit(solution)/shard_map/pallas_call | solution.py:238
  137.3 15.1 %collective-permute-done.12.refs_1_ = bf16[608,512]{1,0:T(8,128)(2,1)S(1)} collective-permute-done((bf16[608,512]{1,0:T(8,128)(2,1)}, bf16[608,512]{1,0:T(8,128)(2,1)S(1)}, u32[]{:S(2)}, u32[]{:S(2)}) %collective-permute-start.12) | collective-permute-done | bytes 622624 | tf_op jit(solution)/shard_map/ppermute | solution.py:313
  152.4 3.5 %collective-permute-done.13.refs_2_ = bf16[608,512]{1,0:T(8,128)(2,1)S(1)} collective-permute-done((bf16[608,512]{1,0:T(8,128)(2,1)}, bf16[608,512]{1,0:T(8,128)(2,1)S(1)}, u32[]{:S(2)}, u32[]{:S(2)}) %collective-permute-start.13) | collective-permute-done | bytes 622624 | tf_op jit(solution)/shard_map/ppermute | solution.py:313
  156.4 1.6 collective-permute-start.15
  158.1 1.2 collective-permute-start.16
  159.3 1.1 collective-permute-done.14
  160.4 1.9 add_convert_fusion
  162.3 11.0 %collective-permute-done.15.refs_3_ = bf16[608,512]{1,0:T(8,128)(2,1)S(1)} collective-permute-done((bf16[608,512]{1,0:T(8,128)(2,1)S(1)}, bf16[608,512]{1,0:T(8,128)(2,1)S(1)}, u32[]{:S(2)}, u32[]{:S(2)}) %collective-permute-start.15) | collective-permute-done | bytes 622624 | tf_op jit(solution)/shard_map/ppermute | solution.py:313
  174.0 0.8 copy-done.11
  174.9 3.7 %all-to-all-start.2 = ((bf16[16,512,128]{2,1,0:T(8,128)(2,1)}), bf16[16,512,128]{2,1,0:T(8,128)(2,1)S(1)}, u32[]{:S(2)}, u32[]{:S(2)}) async-start(bf16[16,512,128]{2,1,0:T(8,128)(2,1)} %bitcast.11), calls=%async_computation.2 | async-start | bytes 4194304 | tf_op jit(solution)/shard_map/all_to_all | solution.py:368
  179.2 2.2 collective-permute-start.18
  181.3 0.7 slice.26
  182.1 1.0 slice.27
  183.1 2.7 %collective-permute-start.21 = (bf16[304,512]{1,0:T(8,128)(2,1)S(1)}, bf16[304,512]{1,0:T(8,128)(2,1)}, u32[]{:S(2)}, u32[]{:S(2)}) collective-permute-start(bf16[304,512]{1,0:T(8,128)(2,1)S(1)} %slice.27), channel_id=1, source_target_pairs={{0,96},{32,0},{64,32},{96,64},{1,97},{33,1},{65,33},{97,65},{2,98}... | collective-permute-start | bytes 933896 | tf_op jit(solution)/shard_map/ppermute | solution.py:313
  185.8 5.8 %shard_map.73.refs_3_.refs_5_.refs_2_ = bf16[2048,1024]{1,0:T(8,128)(2,1)} custom-call(s32[4]{0:T(128)} %pad_add_fusion.pos, bf16[32,512,128]{2,1,0:T(8,128)(2,1)} %bitcast.17), custom_call_target="tpu_custom_call" | custom-call | flops 1048576 | bytes 65536 | tf_op jit(solution)/shard_map/pallas_call | solution.py:258
  191.7 9.9 %shard_map.75.refs_6_ = bf16[2374,1024]{1,0:T(8,128)(2,1)} custom-call(bf16[1216,512]{1,0:T(8,128)(2,1)} %get-tuple-element.32.refs_0_, bf16[1216,512]{1,0:T(8,128)(2,1)} %copy-done.2, bf16[1216,512]{1,0:T(8,128)(2,1)} %copy-done.3, bf16[608,512]{1,0:T(8,128)(2,1)} %copy-done.10, bf16[608,512]{1,0:T(8,128)(2,1)} %copy-done.11, ...), custom_call_target="tpu_custom_call" | custom-call | flops 1048576 | bytes 65536 | tf_op jit(solution)/shard_map/pallas_call | solution.py:302
  202.3 6.7 %shard_map.76.refs_4_ = bf16[2374,1024]{1,0:T(8,128)(2,1)} custom-call(bf16[608,512]{1,0:T(8,128)(2,1)} %get-tuple-element.34.refs_1_.refs_0_, bf16[608,512]{1,0:T(8,128)(2,1)} %copy-done.7, bf16[608,512]{1,0:T(8,128)(2,1)} %copy-done.9, bf16[304,512]{1,0:T(8,128)(2,1)} %copy-done.15, ...), custom_call_target="tpu_custom_call", output_to_operand_aliasing={{}: (6, {})} | custom-call | flops 1048576 | bytes 65536 | tf_op jit(solution)/shard_map/pallas_call | solution.py:302
  209.0 1.0 slice.22
  210.1 1.0 slice.23
  211.1 2.7 %collective-permute-start.23 = (bf16[304,512]{1,0:T(8,128)(2,1)S(1)}, bf16[304,512]{1,0:T(8,128)(2,1)S(1)}, u32[]{:S(2)}, u32[]{:S(2)}) collective-permute-start(bf16[304,512]{1,0:T(8,128)(2,1)S(1)} %slice.23), channel_id=1, source_target_pairs={{0,96},{32,0},{64,32},{96,64},{1,97},{33,1},{65,33},{97,65},{2,98}... | collective-permute-start | bytes 933896 | tf_op jit(solution)/shard_map/ppermute | solution.py:313
  213.8 6.0 %shard_map.74.refs_3_ = f32[608,1024]{1,0:T(8,128)} custom-call(bf16[608,512]{1,0:T(8,128)(2,1)} %get-tuple-element.40.refs_2_.refs_0_, bf16[608,512]{1,0:T(8,128)(2,1)} %collective-permute-done.17.refs_1_, bf16[608,512]{1,0:T(8,128)(2,1)} %collective-permute-done.18.refs_2_, bf16[2048,1024]{1,0:T(8,128)(2,1)} %shard_map.73.refs_3_.refs_5_.refs_2_), custom_call_target="tpu_custom_call" | custom-call | flops 1048576 | bytes 65536 | tf_op jit(solution)/shard_map/pallas_call | solution.py:302
  219.8 1.0 reduce_sum.12
  221.5 0.7 copy-done.16
  222.3 4.0 %shard_map.77 = bf16[2374,1024]{1,0:T(8,128)(2,1)} custom-call(bf16[304,512]{1,0:T(8,128)(2,1)} %copy-done.14, bf16[304,512]{1,0:T(8,128)(2,1)} %copy-done.16, bf16[2048,1024]{1,0:T(8,128)(2,1)} %shard_map.73.refs_3_.refs_5_.refs_2_, f32[608,1024]{1,0:T(8,128)} %shard_map.74.refs_3_, ...), custom_call_target="tpu_custom_call", output_to_operand_aliasing={{}: (4, {})} | custom-call | flops 1048576 | bytes 65536 | tf_op jit(solution)/shard_map/pallas_call | solution.py:302
  (70 shorter events, 8.5 us)
Async XLA Ops:
  7.2 10.9 %copy-start.18 = (bf16[512,128]{1,0:T(8,128)(2,1)S(1)}, bf16[512,128]{1,0:T(8,128)(2,1)}, u32[]{:S(2)}) copy-start(bf16[512,128]{1,0:T(8,128)(2,1)} %param.4) | copy-start | bytes 393220
  7.2 9.1 %collective-permute-start.2 = (bf16[512,128]{1,0:T(8,128)(2,1)}, bf16[512,128]{1,0:T(8,128)(2,1)S(1)}, u32[]{:S(2)}, u32[]{:S(2)}) collective-permute-start(bf16[512,128]{1,0:T(8,128)(2,1)} %param.4), channel_id=1, source_target_pairs={{0,6},{1,25},{2,0},{3,27},{4,2},{5,29},{6,4},{7,31},{8,14},{9,1},{... | collective-permute-start | bytes 393224 | tf_op jit(solution)/shard_map/ppermute | solution.py:329
  10.8 5.6 %collective-permute-start.1 = (bf16[512,128]{1,0:T(8,128)(2,1)}, bf16[512,128]{1,0:T(8,128)(2,1)S(1)}, u32[]{:S(2)}, u32[]{:S(2)}) collective-permute-start(bf16[512,128]{1,0:T(8,128)(2,1)} %param.4), channel_id=1, source_target_pairs={{0,4},{1,17},{2,6},{3,19},{4,0},{5,21},{6,2},{7,23},{8,12},{9,25},... | collective-permute-start | bytes 393224 | tf_op jit(solution)/shard_map/ppermute | solution.py:329
  11.2 6.9 %collective-permute-start = (bf16[512,128]{1,0:T(8,128)(2,1)}, bf16[512,128]{1,0:T(8,128)(2,1)S(1)}, u32[]{:S(2)}, u32[]{:S(2)}) collective-permute-start(bf16[512,128]{1,0:T(8,128)(2,1)} %param.4), channel_id=1, source_target_pairs={{0,2},{1,9},{2,4},{3,11},{4,6},{5,13},{6,0},{7,15},{8,10},{9,17},{... | collective-permute-start | bytes 393224 | tf_op jit(solution)/shard_map/ppermute | solution.py:329
  18.1 24.6 %copy-start.6 = (bf16[4,512,128]{2,1,0:T(8,128)(2,1)}, bf16[4,512,128]{2,1,0:T(8,128)(2,1)S(1)}, u32[]{:S(2)}) copy-start(bf16[4,512,128]{2,1,0:T(8,128)(2,1)S(1)} %pad_maximum_fusion.refs_0_) | copy-start | bytes 1572868
  18.1 10.4 %collective-permute-start.3 = (bf16[4,512,128]{2,1,0:T(8,128)(2,1)S(1)}, bf16[4,512,128]{2,1,0:T(8,128)(2,1)S(1)}, u32[]{:S(2)}, u32[]{:S(2)}) collective-permute-start(bf16[4,512,128]{2,1,0:T(8,128)(2,1)S(1)} %pad_maximum_fusion.refs_0_), channel_id=1, source_target_pairs={{0,8},{1,3},{2,10},{3,5},{4,12},{5,7},{6,14},{7,1},{8,16},{9,11},{... | collective-permute-start | bytes 1572872 | tf_op jit(solution)/shard_map/ppermute | solution.py:329
  19.5 15.8 %collective-permute-start.4 = (bf16[4,512,128]{2,1,0:T(8,128)(2,1)S(1)}, bf16[4,512,128]{2,1,0:T(8,128)(2,1)S(1)}, u32[]{:S(2)}, u32[]{:S(2)}) collective-permute-start(bf16[4,512,128]{2,1,0:T(8,128)(2,1)S(1)} %pad_maximum_fusion.refs_0_), channel_id=1, source_target_pairs={{0,16},{1,5},{2,18},{3,7},{4,20},{5,1},{6,22},{7,3},{8,24},{9,13},... | collective-permute-start | bytes 1572872 | tf_op jit(solution)/shard_map/ppermute | solution.py:329
  22.8 13.3 %collective-permute-start.5 = (bf16[4,512,128]{2,1,0:T(8,128)(2,1)S(1)}, bf16[4,512,128]{2,1,0:T(8,128)(2,1)}, u32[]{:S(2)}, u32[]{:S(2)}) collective-permute-start(bf16[4,512,128]{2,1,0:T(8,128)(2,1)S(1)} %pad_maximum_fusion.refs_0_), channel_id=1, source_target_pairs={{0,24},{1,7},{2,26},{3,1},{4,28},{5,3},{6,30},{7,5},{8,0},{9,15},{... | collective-permute-start | bytes 1572872 | tf_op jit(solution)/shard_map/ppermute | solution.py:329
  28.5 14.5 %copy-start.12 = (bf16[4,512,128]{2,1,0:T(8,128)(2,1)}, bf16[4,512,128]{2,1,0:T(8,128)(2,1)S(1)}, u32[]{:S(2)}) copy-start(bf16[4,512,128]{2,1,0:T(8,128)(2,1)S(1)} %collective-permute-done.3.refs_1_) | copy-start | bytes 1572868
  35.3 0.8 copy-start.13
  36.1 39.1 %all-to-all-start = ((bf16[32,19,16,128]{3,2,1,0:T(8,128)(2,1)}), bf16[32,19,16,128]{3,2,1,0:T(8,128)(2,1)S(1)}, u32[]{:S(2)}, u32[]{:S(2)}) async-start(bf16[32,19,16,128]{3,2,1,0:T(8,128)(2,1)} %shard_map.67), calls=%async_computation | async-start | bytes 4980736 | tf_op jit(solution)/shard_map/all_to_all | solution.py:343
  42.7 2.1 collective-permute-start.6
  43.1 3.3 %collective-permute-start.7 = (bf16[4,512,128]{2,1,0:T(8,128)(2,1)S(1)}, bf16[4,512,128]{2,1,0:T(8,128)(2,1)}, u32[]{:S(2)}, u32[]{:S(2)}) collective-permute-start(bf16[4,512,128]{2,1,0:T(8,128)(2,1)S(1)} %collective-permute-done.3.refs_1_), channel_id=1, source_target_pairs={{0,1},{1,0},{2,3},{3,2},{4,5},{5,4},{6,7},{7,6},{8,9},{9,8},{10,11... | collective-permute-start | bytes 1572872 | tf_op jit(solution)/shard_map/ppermute | solution.py:317
  43.3 3.2 %collective-permute-start.8 = (bf16[4,512,128]{2,1,0:T(8,128)(2,1)}, bf16[4,512,128]{2,1,0:T(8,128)(2,1)}, u32[]{:S(2)}, u32[]{:S(2)}) collective-permute-start(bf16[4,512,128]{2,1,0:T(8,128)(2,1)} %copy-done.13), channel_id=1, source_target_pairs={{0,1},{1,0},{2,3},{3,2},{4,5},{5,4},{6,7},{7,6},{8,9},{9,8},{10,11... | collective-permute-start | bytes 1572872 | tf_op jit(solution)/shard_map/ppermute | solution.py:317
  43.6 3.8 %collective-permute-start.9 = (bf16[4,512,128]{2,1,0:T(8,128)(2,1)}, bf16[4,512,128]{2,1,0:T(8,128)(2,1)}, u32[]{:S(2)}, u32[]{:S(2)}) collective-permute-start(bf16[4,512,128]{2,1,0:T(8,128)(2,1)} %collective-permute-done.5.refs_3_), channel_id=1, source_target_pairs={{0,1},{1,0},{2,3},{3,2},{4,5},{5,4},{6,7},{7,6},{8,9},{9,8},{10,11... | collective-permute-start | bytes 1572872 | tf_op jit(solution)/shard_map/ppermute | solution.py:317
  75.3 1.5 copy-start
  76.7 12.0 %copy-start.19 = (bf16[512,128]{1,0:T(8,128)(2,1)S(1)}, bf16[512,128]{1,0:T(8,128)(2,1)}, u32[]{:S(2)}) copy-start(bf16[512,128]{1,0:T(8,128)(2,1)} %param.4) | copy-start | bytes 393220
  84.2 16.2 %all-to-all-start.1 = ((f32[32,8,512]{2,1,0:T(8,128)}), f32[32,8,512]{2,1,0:T(8,128)S(1)}, u32[]{:S(2)}, u32[]{:S(2)}) async-start(f32[32,8,512]{2,1,0:T(8,128)} %get-tuple-element.29), calls=%async_computation.1 | async-start | bytes 1048576 | tf_op jit(solution)/shard_map/all_to_all | solution.py:346
  88.7 97.2 %all-gather.3.cloned.1.call-start = ((), (), s32[]{:S(2)}) async-start(), calls=%async_computation.3 | async-start | bytes 4325376 | tf_op jit(solution)/shard_map/all_gather | solution.py:352
  88.7 17.0 %collective-permute-start.19 = (bf16[512,128]{1,0:T(8,128)(2,1)S(1)}, bf16[512,128]{1,0:T(8,128)(2,1)S(1)}, u32[]{:S(2)}, u32[]{:S(2)}) collective-permute-start(bf16[512,128]{1,0:T(8,128)(2,1)S(1)} %copy-done.19), channel_id=1, source_target_pairs={{0,0},{8,32},{16,64},{24,96},{32,8},{40,40},{48,72},{56,104},{64,1... | collective-permute-start | bytes 393224 | tf_op jit(solution)/shard_map/ppermute | solution.py:351
  100.4 0.8 copy-start.1
  105.7 0.7 copy-start.17
  106.4 49.5 %collective-permute-start.10 = (bf16[1216,512]{1,0:T(8,128)(2,1)}, bf16[1216,512]{1,0:T(8,128)(2,1)S(1)}, u32[]{:S(2)}, u32[]{:S(2)}) collective-permute-start(bf16[1216,512]{1,0:T(8,128)(2,1)} %get-tuple-element.32.refs_0_), channel_id=1, source_target_pairs={{0,32},{32,64},{64,96},{96,0},{1,33},{33,65},{65,97},{97,1},{2,34}... | collective-permute-start | bytes 3735560 | tf_op jit(solution)/shard_map/ppermute | solution.py:313
  111.9 44.0 %collective-permute-start.11 = (bf16[1216,512]{1,0:T(8,128)(2,1)}, bf16[1216,512]{1,0:T(8,128)(2,1)S(1)}, u32[]{:S(2)}, u32[]{:S(2)}) collective-permute-start(bf16[1216,512]{1,0:T(8,128)(2,1)} %get-tuple-element.32.refs_0_), channel_id=1, source_target_pairs={{0,96},{32,0},{64,32},{96,64},{1,97},{33,1},{65,33},{97,65},{2,98}... | collective-permute-start | bytes 3735560 | tf_op jit(solution)/shard_map/ppermute | solution.py:313
  116.7 35.6 %collective-permute-start.12 = (bf16[608,512]{1,0:T(8,128)(2,1)}, bf16[608,512]{1,0:T(8,128)(2,1)S(1)}, u32[]{:S(2)}, u32[]{:S(2)}) collective-permute-start(bf16[608,512]{1,0:T(8,128)(2,1)} %get-tuple-element.34.refs_1_.refs_0_), channel_id=1, source_target_pairs={{0,32},{32,64},{64,96},{96,0},{1,33},{33,65},{65,97},{97,1},{2,34}... | collective-permute-start | bytes 1867784 | tf_op jit(solution)/shard_map/ppermute | solution.py:313
  119.3 36.6 %collective-permute-start.13 = (bf16[608,512]{1,0:T(8,128)(2,1)}, bf16[608,512]{1,0:T(8,128)(2,1)S(1)}, u32[]{:S(2)}, u32[]{:S(2)}) collective-permute-start(bf16[608,512]{1,0:T(8,128)(2,1)} %get-tuple-element.34.refs_1_.refs_0_), channel_id=1, source_target_pairs={{0,96},{32,0},{64,32},{96,64},{1,97},{33,1},{65,33},{97,65},{2,98}... | collective-permute-start | bytes 1867784 | tf_op jit(solution)/shard_map/ppermute | solution.py:313
  137.3 23.1 %copy-start.5 = (bf16[4,4,512,128]{3,2,1,0:T(8,128)(2,1)S(1)}, bf16[4,4,512,128]{3,2,1,0:T(8,128)(2,1)}, u32[]{:S(2)}) copy-start(bf16[4,4,512,128]{3,2,1,0:T(8,128)(2,1)} %get-tuple-element.36) | copy-start | bytes 6291460
  152.4 9.9 %copy-start.7 = (bf16[608,512]{1,0:T(8,128)(2,1)}, bf16[608,512]{1,0:T(8,128)(2,1)S(1)}, u32[]{:S(2)}) copy-start(bf16[608,512]{1,0:T(8,128)(2,1)S(1)} %collective-permute-done.12.refs_1_) | copy-start | bytes 1867780
  155.9 6.4 %copy-start.9 = (bf16[608,512]{1,0:T(8,128)(2,1)}, bf16[608,512]{1,0:T(8,128)(2,1)S(1)}, u32[]{:S(2)}) copy-start(bf16[608,512]{1,0:T(8,128)(2,1)S(1)} %collective-permute-done.13.refs_2_) | copy-start | bytes 1867780
  155.9 6.4 %copy-start.2 = (bf16[1216,512]{1,0:T(8,128)(2,1)}, bf16[1216,512]{1,0:T(8,128)(2,1)S(1)}, u32[]{:S(2)}) copy-start(bf16[1216,512]{1,0:T(8,128)(2,1)S(1)} %collective-permute-done.10.refs_1_) | copy-start | bytes 3735556
  155.9 6.4 %copy-start.3 = (bf16[1216,512]{1,0:T(8,128)(2,1)}, bf16[1216,512]{1,0:T(8,128)(2,1)S(1)}, u32[]{:S(2)}) copy-start(bf16[1216,512]{1,0:T(8,128)(2,1)S(1)} %collective-permute-done.11.refs_2_) | copy-start | bytes 3735556
  155.9 4.5 %collective-permute-start.14 = (bf16[4,4,512,128]{3,2,1,0:T(8,128)(2,1)}, bf16[4,4,512,128]{3,2,1,0:T(8,128)(2,1)S(1)}, u32[]{:S(2)}, u32[]{:S(2)}) collective-permute-start(bf16[4,4,512,128]{3,2,1,0:T(8,128)(2,1)} %get-tuple-element.38), channel_id=1, source_target_pairs={{0,1},{1,0},{2,3},{3,2},{4,5},{5,4},{6,7},{7,6},{8,9},{9,8},{10,11... | collective-permute-start | bytes 6291464 | tf_op jit(solution)/shard_map/ppermute | solution.py:317
  156.4 16.8 %collective-permute-start.15 = (bf16[608,512]{1,0:T(8,128)(2,1)S(1)}, bf16[608,512]{1,0:T(8,128)(2,1)S(1)}, u32[]{:S(2)}, u32[]{:S(2)}) collective-permute-start(bf16[608,512]{1,0:T(8,128)(2,1)S(1)} %slice.24), channel_id=1, source_target_pairs={{0,32},{32,64},{64,96},{96,0},{1,33},{33,65},{65,97},{97,1},{2,34}... | collective-permute-start | bytes 1867784 | tf_op jit(solution)/shard_map/ppermute | solution.py:313
  158.1 15.4 %collective-permute-start.16 = (bf16[608,512]{1,0:T(8,128)(2,1)S(1)}, bf16[608,512]{1,0:T(8,128)(2,1)S(1)}, u32[]{:S(2)}, u32[]{:S(2)}) collective-permute-start(bf16[608,512]{1,0:T(8,128)(2,1)S(1)} %slice.25), channel_id=1, source_target_pairs={{0,96},{32,0},{64,32},{96,64},{1,97},{33,1},{65,33},{97,65},{2,98}... | collective-permute-start | bytes 1867784 | tf_op jit(solution)/shard_map/ppermute | solution.py:313
  173.2 0.8 copy-start.10
  173.2 5.4 %copy-start.4 = (bf16[608,512]{1,0:T(8,128)(2,1)S(1)}, bf16[608,512]{1,0:T(8,128)(2,1)}, u32[]{:S(2)}) copy-start(bf16[608,512]{1,0:T(8,128)(2,1)} %get-tuple-element.40.refs_2_.refs_0_) | copy-start | bytes 1867780
  173.2 8.1 %copy-start.8 = (bf16[608,512]{1,0:T(8,128)(2,1)S(1)}, bf16[608,512]{1,0:T(8,128)(2,1)}, u32[]{:S(2)}) copy-start(bf16[608,512]{1,0:T(8,128)(2,1)} %copy-done.7) | copy-start | bytes 1867780
  174.0 0.8 copy-start.11
  174.9 45.0 %all-to-all-start.2 = ((bf16[16,512,128]{2,1,0:T(8,128)(2,1)}), bf16[16,512,128]{2,1,0:T(8,128)(2,1)S(1)}, u32[]{:S(2)}, u32[]{:S(2)}) async-start(bf16[16,512,128]{2,1,0:T(8,128)(2,1)} %bitcast.11), calls=%async_computation.2 | async-start | bytes 4194304 | tf_op jit(solution)/shard_map/all_to_all | solution.py:368
  178.6 30.4 %collective-permute-start.17 = (bf16[608,512]{1,0:T(8,128)(2,1)S(1)}, bf16[608,512]{1,0:T(8,128)(2,1)}, u32[]{:S(2)}, u32[]{:S(2)}) collective-permute-start(bf16[608,512]{1,0:T(8,128)(2,1)S(1)} %copy-done.4), channel_id=1, source_target_pairs={{0,32},{32,64},{64,96},{96,0},{1,33},{33,65},{65,97},{97,1},{2,34}... | collective-permute-start | bytes 1867784 | tf_op jit(solution)/shard_map/ppermute | solution.py:313
  179.2 30.9 %collective-permute-start.18 = (bf16[608,512]{1,0:T(8,128)(2,1)S(1)}, bf16[608,512]{1,0:T(8,128)(2,1)}, u32[]{:S(2)}, u32[]{:S(2)}) collective-permute-start(bf16[608,512]{1,0:T(8,128)(2,1)S(1)} %copy-done.4), channel_id=1, source_target_pairs={{0,96},{32,0},{64,32},{96,64},{1,97},{33,1},{65,33},{97,65},{2,98}... | collective-permute-start | bytes 1867784 | tf_op jit(solution)/shard_map/ppermute | solution.py:313
  182.1 19.5 %collective-permute-start.20 = (bf16[304,512]{1,0:T(8,128)(2,1)}, bf16[304,512]{1,0:T(8,128)(2,1)S(1)}, u32[]{:S(2)}, u32[]{:S(2)}) collective-permute-start(bf16[304,512]{1,0:T(8,128)(2,1)} %slice.26), channel_id=1, source_target_pairs={{0,32},{32,64},{64,96},{96,0},{1,33},{33,65},{65,97},{97,1},{2,34}... | collective-permute-start | bytes 933896 | tf_op jit(solution)/shard_map/ppermute | solution.py:313
  183.1 18.5 %collective-permute-start.21 = (bf16[304,512]{1,0:T(8,128)(2,1)S(1)}, bf16[304,512]{1,0:T(8,128)(2,1)}, u32[]{:S(2)}, u32[]{:S(2)}) collective-permute-start(bf16[304,512]{1,0:T(8,128)(2,1)S(1)} %slice.27), channel_id=1, source_target_pairs={{0,96},{32,0},{64,32},{96,64},{1,97},{33,1},{65,33},{97,65},{2,98}... | collective-permute-start | bytes 933896 | tf_op jit(solution)/shard_map/ppermute | solution.py:313
  201.6 0.7 copy-start.15
  210.0 10.8 %collective-permute-start.22 = (bf16[304,512]{1,0:T(8,128)(2,1)S(1)}, bf16[304,512]{1,0:T(8,128)(2,1)S(1)}, u32[]{:S(2)}, u32[]{:S(2)}) collective-permute-start(bf16[304,512]{1,0:T(8,128)(2,1)S(1)} %slice.22), channel_id=1, source_target_pairs={{0,32},{32,64},{64,96},{96,0},{1,33},{33,65},{65,97},{97,1},{2,34}... | collective-permute-start | bytes 933896 | tf_op jit(solution)/shard_map/ppermute | solution.py:313
  211.1 9.7 %collective-permute-start.23 = (bf16[304,512]{1,0:T(8,128)(2,1)S(1)}, bf16[304,512]{1,0:T(8,128)(2,1)S(1)}, u32[]{:S(2)}, u32[]{:S(2)}) collective-permute-start(bf16[304,512]{1,0:T(8,128)(2,1)S(1)} %slice.23), channel_id=1, source_target_pairs={{0,96},{32,0},{64,32},{96,64},{1,97},{33,1},{65,33},{97,65},{2,98}... | collective-permute-start | bytes 933896 | tf_op jit(solution)/shard_map/ppermute | solution.py:313
  220.8 0.7 copy-start.14
  221.5 0.7 copy-start.16
Sparse Core Ops, SparseCore 0:
  106.5 49.2 all-gather.2

commit v5 on v4

--- a/solution.py
+++ b/solution.py
@@ -96,13 +96,12 @@
     part = jax.ShapeDtypeStruct((8, T), F32)
     return call(
         student_body,
-        out_shape=[jax.ShapeDtypeStruct((NS * SB, T), F32), part, part],
+        out_shape=[jax.ShapeDtypeStruct((NS * SB, T), F32), part, part, jax.ShapeDtypeStruct((T, D), BF16)],
         grid_spec=pltpu.PrefetchScalarGridSpec(
             num_scalar_prefetch=1,
             grid=(NS,),
             in_specs=[pl.BlockSpec((SB, D), lambda i, p: (i, 0))] + [whole((4, T, 128))] * 8,
-            out_specs=[pl.BlockSpec((SB, T), lambda i, p: (i, 0)), whole((8, T)), whole((8, T))],
-            scratch_shapes=[pltpu.VMEM((T, D), BF16)],
+            out_specs=[pl.BlockSpec((SB, T), lambda i, p: (i, 0)), whole((8, T)), whole((8, T)), whole((T, D))],
         ),
     )(pos, wt, *own, *sib)
 
@@ -120,7 +119,7 @@
 
         @pl.when(step * (SB // 128) + n < KT)
         def _():
-            t = t_ref[:, n].reshape(T, 128).astype(F32).T
+            t = t_ref[:, n].reshape(T, 128).T.astype(F32)
             rows = step * SB + n * 128 + lax.broadcasted_iota(jnp.int32, t.shape, 0)
             t = jnp.where(rows < VL, t, LOW)
             tt_ref[n * 128 : (n + 1) * 128, :] = t.astype(BF16)
@@ -248,23 +247,47 @@
     )(pos, *gs, wt)
 
 
-def tokens_body(pos, h_ref, k_ref):
-    for j in range(8):
-        k_ref[:, j * 128 : (j + 1) * 128] = h_ref[j]
-
-
-def tokens(pos, h2):
-    group = lambda i, p: (p[0] + jnp.where(i == 0, 0, jnp.where(i == 1, 3, i - 1))) % 4
+def pick_body(pos, h_ref, *out_refs):
+    for n, out_ref in enumerate(out_refs, 1):
+        for z in range(4):
+            at = pl.multiple_of((pos[0] + n) % 4 * DX + (2 * z + pos[3]) * 128, 128)
+            out_ref[z] = h_ref[:, pl.ds(at, 128)]
+
+
+def pick(pos, h):
+    return call(
+        pick_body,
+        out_shape=[jax.ShapeDtypeStruct((4, T, 128), BF16)] * 3,
+        grid_spec=pltpu.PrefetchScalarGridSpec(
+            num_scalar_prefetch=1,
+            grid=(1,),
+            in_specs=[whole((T, D))],
+            out_specs=[whole((4, T, 128))] * 3,
+        ),
+    )(pos, h)
+
+
+def tokens_body(pos, h_ref, *refs):
+    k_ref = refs[-1]
+    k_ref[0:T, :] = h_ref[...]
+    for n in range(3):
+        rows = slice((n + 1) * T, (n + 2) * T)
+        for ref, c in ((refs[2 * n], pos[3]), (refs[2 * n + 1], 1 - pos[3])):
+            for z in range(4):
+                k_ref[rows, pl.ds(pl.multiple_of((2 * z + c) * 128, 128), 128)] = ref[z]
+
+
+def tokens(pos, h, parts):
     return call(
         tokens_body,
         out_shape=jax.ShapeDtypeStruct((4 * T, DX), BF16),
         grid_spec=pltpu.PrefetchScalarGridSpec(
             num_scalar_prefetch=1,
-            grid=(4,),
-            in_specs=[pl.BlockSpec((8, T, 128), lambda i, p: (group(i, p), 0, 0))],
-            out_specs=pl.BlockSpec((T, DX), lambda i, p: (i, 0)),
+            grid=(1,),
+            in_specs=[pl.BlockSpec((T, DX), lambda i, p: (0, p[0]))] + [whole((4, T, 128))] * 6,
+            out_specs=whole((4 * T, DX)),
         ),
-    )(pos, h2)
+    )(pos, h, *parts)
 
 
 def head_body(near, far, prior, *refs):
@@ -313,6 +336,10 @@
     return lax.ppermute(x, "x", [(i, (i + n) % 4) for i in range(4)])
 
 
+def hop(x):
+    return lax.ppermute(x, ("x", "c"), [(2 * i + c, (i + 1 + 2 * c) % 4 * 2 + c) for i in range(4) for c in range(2)])
+
+
 def swap(x):
     return lax.ppermute(x, "c", [(0, 1), (1, 0)])
 
@@ -341,15 +368,16 @@
     one = jnp.stack(spread(hidden, 0))
     own = spread(after(one, blocks), 1)
     teacher = lax.all_to_all(after(blocks, *own[1:]), V, 0, 0, tiled=True)
-    s, m, l = student(pos, wt, own, [swap(x) for x in own])
+    s, m, l, h = student(pos, wt, own, [swap(x) for x in own])
     t, share = stats(m, l, s, teacher)
     gathered = lax.all_to_all(share, V, 0, 0, tiled=True)
 
+    to_right, to_far, to_left = pick(pos, h)
+    others = [shift(to_right, 1), shift(to_left, 3), hop(after(hop(to_far), share))]
+
     w = row_weight.reshape(1, T)
-    gu, kl = grad(gathered, w, s, t, CUTS[:1])
+    gu, kl = grad(gathered, after(w, *others), s, t, CUTS[:1])
     gm, gl, _ = grad(gathered, after(w, gu), s, t, CUTS[1:])
-    across = lax.ppermute(hidden, ("x", "y"), [(x * 4 + y, y * 4 + x) for x in range(4) for y in range(4)])
-    h2 = lax.all_gather(after(across, kl), V)
 
     def near(g):
         return [g, shift(g, 1), shift(g, 3)]
@@ -363,17 +391,18 @@
     far_u, far_m = far(near_u), far(near_m)
     near_l = near(after(gl, *far_u))
     mine, other = hidden_part(pos, (gu, gm, gl), wt)
-    both = (mine.astype(F32) + swap(after(other, *near_u[1:], *near_m[1:])).astype(F32)).astype(BF16)
-    both = after(both, *far_u)
+    k = tokens(after(pos, mine), h, [x for other in others for x in (other, swap(other))])
+    part_u = head_piece(near_u, [], k, *CUTS[0])
+    both = (mine.astype(F32) + swap(after(other, *near_u[1:])).astype(F32)).astype(BF16)
+    both = after(both, part_u, *near_m[1:])
     got = lax.all_to_all(both.reshape(16, T, 128), ("y", "z"), 0, 0, tiled=True)
 
-    k = tokens(pos, h2)
-    head = head_piece(near_u, far_u, k, *CUTS[0])
+    head = head_piece([], far_u, k, *CUTS[0], prior=part_u)
     head = head_piece(near_m, far_m, k, *CUTS[1], other=head)
     far_l = far(near_l, head)
-    part = head_piece(near_l, [], k, *CUTS[2])
-    grad_hidden = jnp.sum(after(got, part).astype(F32), axis=0).astype(BF16)
-    head = head_piece([], far_l, k, *CUTS[2], prior=part, other=head)
+    part_l = head_piece(near_l, [], k, *CUTS[2])
+    grad_hidden = jnp.sum(after(got, part_l).astype(F32), axis=0).astype(BF16)
+    head = head_piece([], far_l, k, *CUTS[2], prior=after(part_l, grad_hidden), other=head)
     return kl.reshape(T), grad_hidden, head.T
 
 

time: 235 us -> 234 us (level)
  between operations: 14.2 us -> 0.82 us
  Pallas kernels: 90 us -> 101 us
  starting transfers between devices: 47.3 us -> 54.7 us
  waiting for transfers between devices: 67 us -> 60.3 us
    all_to_all x1, waiting for transfers between devices: 8.66 us -> 0.01 us  [per_device(): teacher = lax.all_to_all(after(blocks, *own[1:]), V, 0, 0, tiled=True)]
    pallas_call x0 -> x1, Pallas kernels: none -> 4.44 us  [pick(): call(pick_body, out_shape=[jax.ShapeDtypeStruct((4, T, 128), BF16)] * 3,...]
    all_to_all x1, starting transfers between devices: 4.48 us -> 8.29 us  [per_device(): gathered = lax.all_to_all(share, V, 0, 0, tiled=True)]
    pallas_call x4 -> x5, Pallas kernels: 26.7 us -> 30.2 us  [head_piece(): call(functools.partial(head_body, bool(near), bool(far), prior is not Non...]
    ppermute x1 -> x2, starting transfers between devices: 0.67 us -> 3.69 us  [hop(): lax.ppermute(x, ('x', 'c'), [(2 * i + c, (i + 1 + 2 * c) % 4 * 2 + c) for...]
    ppermute x5 -> x8, waiting for transfers between devices: 3.95 us -> 6.73 us  [swap(): return lax.ppermute(x, 'c', [(0, 1), (1, 0)])]
    unnamed x40 -> x34, local copies, waits for them, and re-layouts: 7.3 us -> 4.84 us
    ppermute x12 -> x14, waiting for transfers between devices: 29.8 us -> 28.5 us  [shift(): return lax.ppermute(x, 'x', [(i, (i + n) % 4) for i in range(4)])]
  transfers between devices with their start and end apart: 28 -> 33, of which waited for: 15 -> 14; matrix products, arithmetic and copies ran while one was open for 3% -> 4% of each run, Pallas kernels for 34% -> 40%
where the time goes in v5:
time: 234 us; the launch traced here: 232 us
  Pallas kernels  101 us (43%)
  waiting for transfers between devices  60.3 us (26%)
  starting transfers between devices  54.7 us (23%)
  local copies, waits for them, and re-layouts  9.41 us (4%)
  other arithmetic  5.77 us (2%)
    pallas_call x5, Pallas kernels, head_piece(): call(functools.partial(head_body, bool(near), bool(far), prior is not Non...  30.2 us
    ppermute x14, waiting for transfers between devices, shift(): return lax.ppermute(x, 'x', [(i, (i + n) % 4) for i in range(4)])  28.5 us
    pallas_call x1, Pallas kernels, student(): call(student_body, out_shape=[jax.ShapeDtypeStruct((NS * SB, T), F32), pa...  20.7 us
    ppermute x14, starting transfers between devices, shift(): return lax.ppermute(x, 'x', [(i, (i + n) % 4) for i in range(4)])  19.7 us
    pallas_call x1, Pallas kernels, hidden_part(): call(hidden_body, out_shape=[jax.ShapeDtypeStruct((4, 4, T, 128), BF16)]...  18.4 us
    ppermute x6, waiting for transfers between devices, spread(): got.append(lax.ppermute(x, V, pairs))  13.5 us
    ppermute x6, starting transfers between devices, spread(): got.append(lax.ppermute(x, V, pairs))  10.1 us
    all_to_all x1, waiting for transfers between devices, per_device(): gathered = lax.all_to_all(share, V, 0, 0, tiled=True)  9.46 us
  transfers between devices with their start and end apart: 33, of which 14 were waited for; matrix products, arithmetic and copies ran while one was open for 4% of the time, Pallas kernels for 40%

profile of v5, /device:TPU:1, one launch (start us, length us, event | category | flops | bytes accessed | tf_op | source)
XLA Modules:
  0.0 231.6 jit_solution(10563481047322290250)
XLA Ops:
  0.6 3.6 %collective-permute-start.2 = (bf16[512,128]{1,0:T(8,128)(2,1)}, bf16[512,128]{1,0:T(8,128)(2,1)S(1)}, u32[]{:S(2)}, u32[]{:S(2)}) collective-permute-start(bf16[512,128]{1,0:T(8,128)(2,1)} %param.4), channel_id=1, source_target_pairs={{0,6},{1,25},{2,0},{3,27},{4,2},{5,29},{6,4},{7,31},{8,14},{9,1},{... | collective-permute-start | bytes 393224 | tf_op jit(solution)/shard_map/ppermute | solution.py:356
  5.3 4.5 %shard_map.67 = bf16[32,19,16,128]{3,2,1,0:T(8,128)(2,1)} custom-call(bf16[16,75968]{1,0:T(8,128)(2,1)} %t_ref.1), custom_call_target="tpu_custom_call" | custom-call | flops 1048576 | bytes 65536 | tf_op jit(solution)/shard_map/pallas_call | solution.py:55
  9.9 1.6 collective-permute-done
  11.6 1.4 collective-permute-start.3
  13.0 3.3 %collective-permute-start.4 = (bf16[4,512,128]{2,1,0:T(8,128)(2,1)S(1)}, bf16[4,512,128]{2,1,0:T(8,128)(2,1)S(1)}, u32[]{:S(2)}, u32[]{:S(2)}) collective-permute-start(bf16[4,512,128]{2,1,0:T(8,128)(2,1)S(1)} %pad_maximum_fusion.refs_0_), channel_id=1, source_target_pairs={{0,16},{1,5},{2,18},{3,7},{4,20},{5,1},{6,22},{7,3},{8,24},{9,13},... | collective-permute-start | bytes 1572872 | tf_op jit(solution)/shard_map/ppermute | solution.py:356
  17.0 5.0 %collective-permute-done.3.refs_1_ = bf16[4,512,128]{2,1,0:T(8,128)(2,1)S(1)} collective-permute-done((bf16[4,512,128]{2,1,0:T(8,128)(2,1)S(1)}, bf16[4,512,128]{2,1,0:T(8,128)(2,1)S(1)}, u32[]{:S(2)}, u32[]{:S(2)}) %collective-permute-start.3) | collective-permute-done | bytes 524320 | tf_op jit(solution)/shard_map/ppermute | solution.py:356
  22.0 6.8 %collective-permute-done.4.refs_2_ = bf16[4,512,128]{2,1,0:T(8,128)(2,1)S(1)} collective-permute-done((bf16[4,512,128]{2,1,0:T(8,128)(2,1)S(1)}, bf16[4,512,128]{2,1,0:T(8,128)(2,1)S(1)}, u32[]{:S(2)}, u32[]{:S(2)}) %collective-permute-start.4) | collective-permute-done | bytes 524320 | tf_op jit(solution)/shard_map/ppermute | solution.py:356
  29.6 6.6 %all-to-all-start = ((bf16[32,19,16,128]{3,2,1,0:T(8,128)(2,1)}), bf16[32,19,16,128]{3,2,1,0:T(8,128)(2,1)S(1)}, u32[]{:S(2)}, u32[]{:S(2)}) async-start(bf16[32,19,16,128]{3,2,1,0:T(8,128)(2,1)} %shard_map.67), calls=%async_computation | async-start | bytes 4980736 | tf_op jit(solution)/shard_map/all_to_all | solution.py:370
  38.3 1.5 collective-permute-done.7.refs_5_
  40.8 20.7 %shard_map.68 = (f32[2560,512]{1,0:T(8,128)}, f32[8,512]{1,0:T(8,128)}, f32[8,512]{1,0:T(8,128)}, bf16[512,4096]{1,0:T(8,128)(2,1)}) custom-call(s32[4]{0:T(128)} %pad_add_fusion.pos, bf16[2374,4096]{1,0:T(8,128)(2,1)} %bitcast.13, bf16[4,512,128]{2,1,0:T(8,128)(2,1)} %copy-done.6, bf16[4,512,128]{2,1,0:T(8,128)(2,1)} %copy-done.13, ...), custom_call_target="tpu_custom_call" | custom-call | flops 1048576 | bytes 65536 | tf_op jit(solution)/shard_map/pallas_call | solution.py:97
  61.5 4.4 %shard_map.70 = (bf16[4,512,128]{2,1,0:T(8,128)(2,1)}, bf16[4,512,128]{2,1,0:T(8,128)(2,1)}, bf16[4,512,128]{2,1,0:T(8,128)(2,1)}) custom-call(s32[4]{0:T(128)} %pad_add_fusion.pos, bf16[512,4096]{1,0:T(8,128)(2,1)} %get-tuple-element.37.h_ref), custom_call_target="tpu_custom_call" | custom-call | flops 1048576 | bytes 65536 | tf_op jit(solution)/shard_map/pallas_call | solution.py:258
  65.9 2.5 %collective-permute-start.12 = (bf16[4,512,128]{2,1,0:T(8,128)(2,1)}, bf16[4,512,128]{2,1,0:T(8,128)(2,1)S(1)}, u32[]{:S(2)}, u32[]{:S(2)}) collective-permute-start(bf16[4,512,128]{2,1,0:T(8,128)(2,1)} %get-tuple-element.40), channel_id=1, source_target_pairs={{0,32},{1,97},{32,64},{33,1},{64,96},{65,33},{96,0},{97,65},{2,34}... | collective-permute-start | bytes 1572872 | tf_op jit(solution)/shard_map/ppermute | solution.py:340
  68.4 2.7 %collective-permute-start.11 = (bf16[4,512,128]{2,1,0:T(8,128)(2,1)}, bf16[4,512,128]{2,1,0:T(8,128)(2,1)}, u32[]{:S(2)}, u32[]{:S(2)}) collective-permute-start(bf16[4,512,128]{2,1,0:T(8,128)(2,1)} %get-tuple-element.39), channel_id=1, source_target_pairs={{0,96},{32,0},{64,32},{96,64},{1,97},{33,1},{65,33},{97,65},{2,98}... | collective-permute-start | bytes 1572872 | tf_op jit(solution)/shard_map/ppermute | solution.py:336
  71.1 1.5 copy-done
  72.6 7.3 %shard_map.69 = (bf16[2560,512]{1,0:T(8,128)(2,1)}, f32[32,8,512]{2,1,0:T(8,128)}) custom-call(f32[8,512]{1,0:T(8,128)} %get-tuple-element.32.m_ref, f32[8,512]{1,0:T(8,128)} %get-tuple-element.33.l_ref, f32[2560,512]{1,0:T(8,128)} %get-tuple-element.34.s_ref, bf16[32,19,16,128]{3,2,1,0:T(8,128)(2,1)} %copy-done), custom_call_target="tpu_custom_call" | custom-call | flops 1048576 | bytes 65536 | tf_op jit(solution)/shard_map/pallas_call | solution.py:153
  79.9 1.2 collective-permute-start.13
  81.2 8.3 %all-to-all-start.1 = ((f32[32,8,512]{2,1,0:T(8,128)}), f32[32,8,512]{2,1,0:T(8,128)S(1)}, u32[]{:S(2)}, u32[]{:S(2)}) async-start(f32[32,8,512]{2,1,0:T(8,128)} %get-tuple-element.36), calls=%async_computation.1 | async-start | bytes 1048576 | tf_op jit(solution)/shard_map/all_to_all | solution.py:373
  89.5 2.1 collective-permute-done.13.refs_4_
  91.6 9.5 %all-to-all-done.1.all_ref = f32[32,8,512]{2,1,0:T(8,128)S(1)} async-done(((f32[32,8,512]{2,1,0:T(8,128)}), f32[32,8,512]{2,1,0:T(8,128)S(1)}, u32[]{:S(2)}, u32[]{:S(2)}) %all-to-all-start.1) | async-done | bytes 524320 | tf_op jit(solution)/shard_map/all_to_all | solution.py:373
  101.9 4.5 %shard_map.71 = (bf16[1216,512]{1,0:T(8,128)(2,1)}, f32[1,512]{1,0:T(1,128)}) custom-call(f32[32,8,512]{2,1,0:T(8,128)} %copy-done.1, f32[1,512]{1,0:T(1,128)} %bitcast.20, f32[2560,512]{1,0:T(8,128)} %get-tuple-element.34.s_ref, bf16[2560,512]{1,0:T(8,128)(2,1)} %get-tuple-element.43.t_ref), custom_call_target="tpu_custom_call" | custom-call | flops 1048576 | bytes 65536 | tf_op jit(solution)/shard_map/pallas_call | solution.py:203
  106.3 1.1 collective-permute-start.14
  107.4 1.6 collective-permute-start.15
  109.0 4.8 %shard_map.72 = (bf16[608,512]{1,0:T(8,128)(2,1)}, bf16[608,512]{1,0:T(8,128)(2,1)}, f32[1,512]{1,0:T(1,128)}) custom-call(f32[32,8,512]{2,1,0:T(8,128)} %copy-done.1, f32[1,512]{1,0:T(1,128)} %bitcast.21, f32[2560,512]{1,0:T(8,128)} %get-tuple-element.34.s_ref, bf16[2560,512]{1,0:T(8,128)(2,1)} %get-tuple-element.43.t_ref), custom_call_target="tpu_custom_call" | custom-call | flops 1048576 | bytes 65536 | tf_op jit(solution)/shard_map/pallas_call | solution.py:203
  113.8 18.4 %shard_map.73 = (bf16[4,4,512,128]{3,2,1,0:T(8,128)(2,1)}, bf16[4,4,512,128]{3,2,1,0:T(8,128)(2,1)}) custom-call(s32[4]{0:T(128)} %pad_add_fusion.pos, bf16[1216,512]{1,0:T(8,128)(2,1)} %get-tuple-element.45.refs_0_, bf16[608,512]{1,0:T(8,128)(2,1)} %get-tuple-element.47.refs_1_.refs_0_, bf16[608,512]{1,0:T(8,128)(2,1)} %get-tuple-element.54.refs_2_.refs_0_, ...), custom_call_target="tpu_custom_call" | custom-call | flops 1048576 | bytes 65536 | tf_op jit(solution)/shard_map/pallas_call | solution.py:237
  132.2 4.7 %collective-permute-done.14.refs_1_ = bf16[1216,512]{1,0:T(8,128)(2,1)S(1)} collective-permute-done((bf16[1216,512]{1,0:T(8,128)(2,1)}, bf16[1216,512]{1,0:T(8,128)(2,1)S(1)}, u32[]{:S(2)}, u32[]{:S(2)}) %collective-permute-start.14) | collective-permute-done | bytes 1245216 | tf_op jit(solution)/shard_map/ppermute | solution.py:336
  138.2 0.9 collective-permute-start.20
  139.1 3.9 %collective-permute-done.17.refs_1_ = bf16[4,512,128]{2,1,0:T(8,128)(2,1)S(1)} collective-permute-done((bf16[4,512,128]{2,1,0:T(8,128)(2,1)}, bf16[4,512,128]{2,1,0:T(8,128)(2,1)S(1)}, u32[]{:S(2)}, u32[]{:S(2)}) %collective-permute-start.17) | collective-permute-done | bytes 524320 | tf_op jit(solution)/shard_map/ppermute | solution.py:344
  143.0 2.6 %collective-permute-start.21 = (bf16[608,512]{1,0:T(8,128)(2,1)S(1)}, bf16[608,512]{1,0:T(8,128)(2,1)}, u32[]{:S(2)}, u32[]{:S(2)}) collective-permute-start(bf16[608,512]{1,0:T(8,128)(2,1)S(1)} %copy-done.5), channel_id=1, source_target_pairs={{0,96},{32,0},{64,32},{96,64},{1,97},{33,1},{65,33},{97,65},{2,98}... | collective-permute-start | bytes 1867784 | tf_op jit(solution)/shard_map/ppermute | solution.py:336
  145.6 5.8 %shard_map.74.refs_3_.refs_2_.refs_5_ = bf16[2048,1024]{1,0:T(8,128)(2,1)} custom-call(s32[4]{0:T(128)} %pad_add_fusion.pos, bf16[512,4096]{1,0:T(8,128)(2,1)} %get-tuple-element.37.h_ref, bf16[4,512,128]{2,1,0:T(8,128)(2,1)} %collective-permute-done.10.refs_0_, bf16[4,512,128]{2,1,0:T(8,128)(2,1)} %copy-done.15, ...), custom_call_target="tpu_custom_call" | custom-call | flops 1048576 | bytes 65536 | tf_op jit(solution)/shard_map/pallas_call | solution.py:281
  151.4 8.4 %shard_map.75.refs_3_ = f32[1216,1024]{1,0:T(8,128)} custom-call(bf16[1216,512]{1,0:T(8,128)(2,1)} %get-tuple-element.45.refs_0_, bf16[1216,512]{1,0:T(8,128)(2,1)} %copy-done.4, bf16[1216,512]{1,0:T(8,128)(2,1)} %copy-done.2, bf16[2048,1024]{1,0:T(8,128)(2,1)} %shard_map.74.refs_3_.refs_2_.refs_5_), custom_call_target="tpu_custom_call" | custom-call | flops 1048576 | bytes 65536 | tf_op jit(solution)/shard_map/pallas_call | solution.py:325
  159.8 4.1 %add_convert_fusion = bf16[4,4,512,128]{3,2,1,0:T(8,128)(2,1)} fusion(bf16[4,4,512,128]{3,2,1,0:T(8,128)(2,1)} %collective-permute-done.16, bf16[4,4,512,128]{3,2,1,0:T(8,128)(2,1)} %get-tuple-element.49), kind=kLoop, calls=%fused_computation | loop fusion | flops 4194304 | bytes 6291456 | tf_op jit(solution)/shard_map/convert_element_type | solution.py:396
  163.9 0.8 copy-done.7
  164.7 3.8 %all-to-all-start.2 = ((bf16[16,512,128]{2,1,0:T(8,128)(2,1)}), bf16[16,512,128]{2,1,0:T(8,128)(2,1)S(1)}, u32[]{:S(2)}, u32[]{:S(2)}) async-start(bf16[16,512,128]{2,1,0:T(8,128)(2,1)} %bitcast.11), calls=%async_computation.2 | async-start | bytes 4194304 | tf_op jit(solution)/shard_map/all_to_all | solution.py:398
  168.6 1.2 slice.24
  169.9 2.7 %collective-permute-start.23 = (bf16[608,512]{1,0:T(8,128)(2,1)S(1)}, bf16[608,512]{1,0:T(8,128)(2,1)S(1)}, u32[]{:S(2)}, u32[]{:S(2)}) collective-permute-start(bf16[608,512]{1,0:T(8,128)(2,1)S(1)} %slice.25), channel_id=1, source_target_pairs={{0,96},{32,0},{64,32},{96,64},{1,97},{33,1},{65,33},{97,65},{2,98}... | collective-permute-start | bytes 1867784 | tf_op jit(solution)/shard_map/ppermute | solution.py:336
  172.6 13.6 %collective-permute-done.22.refs_0_ = bf16[608,512]{1,0:T(8,128)(2,1)S(1)} collective-permute-done((bf16[608,512]{1,0:T(8,128)(2,1)S(1)}, bf16[608,512]{1,0:T(8,128)(2,1)S(1)}, u32[]{:S(2)}, u32[]{:S(2)}) %collective-permute-start.22) | collective-permute-done | bytes 622624 | tf_op jit(solution)/shard_map/ppermute | solution.py:336
  186.2 0.9 copy-done.12
  187.1 2.7 %collective-permute-start.25 = (bf16[608,512]{1,0:T(8,128)(2,1)}, bf16[608,512]{1,0:T(8,128)(2,1)S(1)}, u32[]{:S(2)}, u32[]{:S(2)}) collective-permute-start(bf16[608,512]{1,0:T(8,128)(2,1)} %get-tuple-element.54.refs_2_.refs_0_), channel_id=1, source_target_pairs={{0,96},{32,0},{64,32},{96,64},{1,97},{33,1},{65,33},{97,65},{2,98}... | collective-permute-start | bytes 1867784 | tf_op jit(solution)/shard_map/ppermute | solution.py:336
  189.9 1.7 slice.27
  191.6 2.7 %collective-permute-start.27 = (bf16[304,512]{1,0:T(8,128)(2,1)}, bf16[304,512]{1,0:T(8,128)(2,1)}, u32[]{:S(2)}, u32[]{:S(2)}) collective-permute-start(bf16[304,512]{1,0:T(8,128)(2,1)} %slice.27), channel_id=1, source_target_pairs={{0,96},{32,0},{64,32},{96,64},{1,97},{33,1},{65,33},{97,65},{2,98}... | collective-permute-start | bytes 933896 | tf_op jit(solution)/shard_map/ppermute | solution.py:336
  194.3 5.1 %shard_map.77.refs_6_ = bf16[2374,1024]{1,0:T(8,128)(2,1)} custom-call(bf16[608,512]{1,0:T(8,128)(2,1)} %copy-done.11, bf16[608,512]{1,0:T(8,128)(2,1)} %copy-done.12, bf16[2048,1024]{1,0:T(8,128)(2,1)} %shard_map.74.refs_3_.refs_2_.refs_5_, f32[1216,1024]{1,0:T(8,128)} %shard_map.75.refs_3_), custom_call_target="tpu_custom_call" | custom-call | flops 1048576 | bytes 65536 | tf_op jit(solution)/shard_map/pallas_call | solution.py:325
  199.3 10.2 %collective-permute-done.26.refs_3_ = bf16[304,512]{1,0:T(8,128)(2,1)} collective-permute-done((bf16[304,512]{1,0:T(8,128)(2,1)S(1)}, bf16[304,512]{1,0:T(8,128)(2,1)}, u32[]{:S(2)}, u32[]{:S(2)}) %collective-permute-start.26) | collective-permute-done | bytes 311328 | tf_op jit(solution)/shard_map/ppermute | solution.py:336
  209.6 6.7 %shard_map.78.refs_4_ = bf16[2374,1024]{1,0:T(8,128)(2,1)} custom-call(bf16[608,512]{1,0:T(8,128)(2,1)} %get-tuple-element.47.refs_1_.refs_0_, bf16[608,512]{1,0:T(8,128)(2,1)} %copy-done.7, bf16[608,512]{1,0:T(8,128)(2,1)} %collective-permute-done.21.refs_2_, bf16[304,512]{1,0:T(8,128)(2,1)} %collective-permute-done.26.refs_3_, ...), custom_call_target="tpu_custom_call", output_to_operand_aliasing={{}: (6, {})} | custom-call | flops 1048576 | bytes 65536 | tf_op jit(solution)/shard_map/pallas_call | solution.py:325
  216.3 0.8 slice.22
  218.2 2.3 %collective-permute-start.29 = (bf16[304,512]{1,0:T(8,128)(2,1)}, bf16[304,512]{1,0:T(8,128)(2,1)}, u32[]{:S(2)}, u32[]{:S(2)}) collective-permute-start(bf16[304,512]{1,0:T(8,128)(2,1)} %slice.23), channel_id=1, source_target_pairs={{0,96},{32,0},{64,32},{96,64},{1,97},{33,1},{65,33},{97,65},{2,98}... | collective-permute-start | bytes 933896 | tf_op jit(solution)/shard_map/ppermute | solution.py:336
  220.6 6.0 %shard_map.76.refs_3_ = f32[608,1024]{1,0:T(8,128)} custom-call(bf16[608,512]{1,0:T(8,128)(2,1)} %get-tuple-element.54.refs_2_.refs_0_, bf16[608,512]{1,0:T(8,128)(2,1)} %copy-done.9, bf16[608,512]{1,0:T(8,128)(2,1)} %copy-done.10, bf16[2048,1024]{1,0:T(8,128)(2,1)} %shard_map.74.refs_3_.refs_2_.refs_5_), custom_call_target="tpu_custom_call" | custom-call | flops 1048576 | bytes 65536 | tf_op jit(solution)/shard_map/pallas_call | solution.py:325
  226.6 1.0 reduce_sum.12
  227.6 4.0 %shard_map.79 = bf16[2374,1024]{1,0:T(8,128)(2,1)} custom-call(bf16[304,512]{1,0:T(8,128)(2,1)} %collective-permute-done.28.refs_0_, bf16[304,512]{1,0:T(8,128)(2,1)} %collective-permute-done.29.refs_1_, bf16[2048,1024]{1,0:T(8,128)(2,1)} %shard_map.74.refs_3_.refs_2_.refs_5_, f32[608,1024]{1,0:T(8,128)} %shard_map.76.refs_3_, ...), custom_call_target="tpu_custom_call", output_to_operand_aliasing={{}: (4, {})} | custom-call | flops 1048576 | bytes 65536 | tf_op jit(solution)/shard_map/pallas_call | solution.py:325
  (75 shorter events, 9.4 us)
Async XLA Ops:
  0.6 10.9 %copy-start.16 = (bf16[512,128]{1,0:T(8,128)(2,1)S(1)}, bf16[512,128]{1,0:T(8,128)(2,1)}, u32[]{:S(2)}) copy-start(bf16[512,128]{1,0:T(8,128)(2,1)} %param.4) | copy-start | bytes 393220
  0.6 9.2 %collective-permute-start.2 = (bf16[512,128]{1,0:T(8,128)(2,1)}, bf16[512,128]{1,0:T(8,128)(2,1)S(1)}, u32[]{:S(2)}, u32[]{:S(2)}) collective-permute-start(bf16[512,128]{1,0:T(8,128)(2,1)} %param.4), channel_id=1, source_target_pairs={{0,6},{1,25},{2,0},{3,27},{4,2},{5,29},{6,4},{7,31},{8,14},{9,1},{... | collective-permute-start | bytes 393224 | tf_op jit(solution)/shard_map/ppermute | solution.py:356
  4.3 5.6 %collective-permute-start.1 = (bf16[512,128]{1,0:T(8,128)(2,1)}, bf16[512,128]{1,0:T(8,128)(2,1)S(1)}, u32[]{:S(2)}, u32[]{:S(2)}) collective-permute-start(bf16[512,128]{1,0:T(8,128)(2,1)} %param.4), channel_id=1, source_target_pairs={{0,4},{1,17},{2,6},{3,19},{4,0},{5,21},{6,2},{7,23},{8,12},{9,25},... | collective-permute-start | bytes 393224 | tf_op jit(solution)/shard_map/ppermute | solution.py:356
  4.6 6.9 %collective-permute-start = (bf16[512,128]{1,0:T(8,128)(2,1)}, bf16[512,128]{1,0:T(8,128)(2,1)S(1)}, u32[]{:S(2)}, u32[]{:S(2)}) collective-permute-start(bf16[512,128]{1,0:T(8,128)(2,1)} %param.4), channel_id=1, source_target_pairs={{0,2},{1,9},{2,4},{3,11},{4,6},{5,13},{6,0},{7,15},{8,10},{9,17},{... | collective-permute-start | bytes 393224 | tf_op jit(solution)/shard_map/ppermute | solution.py:356
  11.6 24.6 %copy-start.6 = (bf16[4,512,128]{2,1,0:T(8,128)(2,1)}, bf16[4,512,128]{2,1,0:T(8,128)(2,1)S(1)}, u32[]{:S(2)}) copy-start(bf16[4,512,128]{2,1,0:T(8,128)(2,1)S(1)} %pad_maximum_fusion.refs_0_) | copy-start | bytes 1572868
  11.6 10.4 %collective-permute-start.3 = (bf16[4,512,128]{2,1,0:T(8,128)(2,1)S(1)}, bf16[4,512,128]{2,1,0:T(8,128)(2,1)S(1)}, u32[]{:S(2)}, u32[]{:S(2)}) collective-permute-start(bf16[4,512,128]{2,1,0:T(8,128)(2,1)S(1)} %pad_maximum_fusion.refs_0_), channel_id=1, source_target_pairs={{0,8},{1,3},{2,10},{3,5},{4,12},{5,7},{6,14},{7,1},{8,16},{9,11},{... | collective-permute-start | bytes 1572872 | tf_op jit(solution)/shard_map/ppermute | solution.py:356
  13.0 15.8 %collective-permute-start.4 = (bf16[4,512,128]{2,1,0:T(8,128)(2,1)S(1)}, bf16[4,512,128]{2,1,0:T(8,128)(2,1)S(1)}, u32[]{:S(2)}, u32[]{:S(2)}) collective-permute-start(bf16[4,512,128]{2,1,0:T(8,128)(2,1)S(1)} %pad_maximum_fusion.refs_0_), channel_id=1, source_target_pairs={{0,16},{1,5},{2,18},{3,7},{4,20},{5,1},{6,22},{7,3},{8,24},{9,13},... | collective-permute-start | bytes 1572872 | tf_op jit(solution)/shard_map/ppermute | solution.py:356
  16.3 13.3 %collective-permute-start.5 = (bf16[4,512,128]{2,1,0:T(8,128)(2,1)S(1)}, bf16[4,512,128]{2,1,0:T(8,128)(2,1)}, u32[]{:S(2)}, u32[]{:S(2)}) collective-permute-start(bf16[4,512,128]{2,1,0:T(8,128)(2,1)S(1)} %pad_maximum_fusion.refs_0_), channel_id=1, source_target_pairs={{0,24},{1,7},{2,26},{3,1},{4,28},{5,3},{6,30},{7,5},{8,0},{9,15},{... | collective-permute-start | bytes 1572872 | tf_op jit(solution)/shard_map/ppermute | solution.py:356
  22.0 14.5 %copy-start.13 = (bf16[4,512,128]{2,1,0:T(8,128)(2,1)}, bf16[4,512,128]{2,1,0:T(8,128)(2,1)S(1)}, u32[]{:S(2)}) copy-start(bf16[4,512,128]{2,1,0:T(8,128)(2,1)S(1)} %collective-permute-done.3.refs_1_) | copy-start | bytes 1572868
  29.6 41.5 %all-to-all-start = ((bf16[32,19,16,128]{3,2,1,0:T(8,128)(2,1)}), bf16[32,19,16,128]{3,2,1,0:T(8,128)(2,1)S(1)}, u32[]{:S(2)}, u32[]{:S(2)}) async-start(bf16[32,19,16,128]{3,2,1,0:T(8,128)(2,1)} %shard_map.67), calls=%async_computation | async-start | bytes 4980736 | tf_op jit(solution)/shard_map/all_to_all | solution.py:370
  36.2 2.1 collective-permute-start.6
  36.5 3.3 %collective-permute-start.7 = (bf16[4,512,128]{2,1,0:T(8,128)(2,1)S(1)}, bf16[4,512,128]{2,1,0:T(8,128)(2,1)}, u32[]{:S(2)}, u32[]{:S(2)}) collective-permute-start(bf16[4,512,128]{2,1,0:T(8,128)(2,1)S(1)} %collective-permute-done.3.refs_1_), channel_id=1, source_target_pairs={{0,1},{1,0},{2,3},{3,2},{4,5},{5,4},{6,7},{7,6},{8,9},{9,8},{10,11... | collective-permute-start | bytes 1572872 | tf_op jit(solution)/shard_map/ppermute | solution.py:344
  36.8 3.2 %collective-permute-start.8 = (bf16[4,512,128]{2,1,0:T(8,128)(2,1)}, bf16[4,512,128]{2,1,0:T(8,128)(2,1)}, u32[]{:S(2)}, u32[]{:S(2)}) collective-permute-start(bf16[4,512,128]{2,1,0:T(8,128)(2,1)} %copy-done.14), channel_id=1, source_target_pairs={{0,1},{1,0},{2,3},{3,2},{4,5},{5,4},{6,7},{7,6},{8,9},{9,8},{10,11... | collective-permute-start | bytes 1572872 | tf_op jit(solution)/shard_map/ppermute | solution.py:344
  37.0 3.8 %collective-permute-start.9 = (bf16[4,512,128]{2,1,0:T(8,128)(2,1)}, bf16[4,512,128]{2,1,0:T(8,128)(2,1)}, u32[]{:S(2)}, u32[]{:S(2)}) collective-permute-start(bf16[4,512,128]{2,1,0:T(8,128)(2,1)} %collective-permute-done.5.refs_3_), channel_id=1, source_target_pairs={{0,1},{1,0},{2,3},{3,2},{4,5},{5,4},{6,7},{7,6},{8,9},{9,8},{10,11... | collective-permute-start | bytes 1572872 | tf_op jit(solution)/shard_map/ppermute | solution.py:344
  65.9 14.0 %collective-permute-start.12 = (bf16[4,512,128]{2,1,0:T(8,128)(2,1)}, bf16[4,512,128]{2,1,0:T(8,128)(2,1)S(1)}, u32[]{:S(2)}, u32[]{:S(2)}) collective-permute-start(bf16[4,512,128]{2,1,0:T(8,128)(2,1)} %get-tuple-element.40), channel_id=1, source_target_pairs={{0,32},{1,97},{32,64},{33,1},{64,96},{65,33},{96,0},{97,65},{2,34}... | collective-permute-start | bytes 1572872 | tf_op jit(solution)/shard_map/ppermute | solution.py:340
  68.4 21.0 %collective-permute-start.10 = (bf16[4,512,128]{2,1,0:T(8,128)(2,1)}, bf16[4,512,128]{2,1,0:T(8,128)(2,1)}, u32[]{:S(2)}, u32[]{:S(2)}) collective-permute-start(bf16[4,512,128]{2,1,0:T(8,128)(2,1)} %get-tuple-element.38), channel_id=1, source_target_pairs={{0,32},{32,64},{64,96},{96,0},{1,33},{33,65},{65,97},{97,1},{2,34}... | collective-permute-start | bytes 1572872 | tf_op jit(solution)/shard_map/ppermute | solution.py:336
  68.4 21.0 %collective-permute-start.11 = (bf16[4,512,128]{2,1,0:T(8,128)(2,1)}, bf16[4,512,128]{2,1,0:T(8,128)(2,1)}, u32[]{:S(2)}, u32[]{:S(2)}) collective-permute-start(bf16[4,512,128]{2,1,0:T(8,128)(2,1)} %get-tuple-element.39), channel_id=1, source_target_pairs={{0,96},{32,0},{64,32},{96,64},{1,97},{33,1},{65,33},{97,65},{2,98}... | collective-permute-start | bytes 1572872 | tf_op jit(solution)/shard_map/ppermute | solution.py:336
  71.1 1.5 copy-start
  79.9 11.7 %collective-permute-start.13 = (bf16[4,512,128]{2,1,0:T(8,128)(2,1)S(1)}, bf16[4,512,128]{2,1,0:T(8,128)(2,1)}, u32[]{:S(2)}, u32[]{:S(2)}) collective-permute-start(bf16[4,512,128]{2,1,0:T(8,128)(2,1)S(1)} %collective-permute-done.12), channel_id=1, source_target_pairs={{0,32},{1,97},{32,64},{33,1},{64,96},{65,33},{96,0},{97,65},{2,34}... | collective-permute-start | bytes 1572872 | tf_op jit(solution)/shard_map/ppermute | solution.py:340
  81.2 19.9 %all-to-all-start.1 = ((f32[32,8,512]{2,1,0:T(8,128)}), f32[32,8,512]{2,1,0:T(8,128)S(1)}, u32[]{:S(2)}, u32[]{:S(2)}) async-start(f32[32,8,512]{2,1,0:T(8,128)} %get-tuple-element.36), calls=%async_computation.1 | async-start | bytes 1048576 | tf_op jit(solution)/shard_map/all_to_all | solution.py:373
  106.3 30.6 %collective-permute-start.14 = (bf16[1216,512]{1,0:T(8,128)(2,1)}, bf16[1216,512]{1,0:T(8,128)(2,1)S(1)}, u32[]{:S(2)}, u32[]{:S(2)}) collective-permute-start(bf16[1216,512]{1,0:T(8,128)(2,1)} %get-tuple-element.45.refs_0_), channel_id=1, source_target_pairs={{0,32},{32,64},{64,96},{96,0},{1,33},{33,65},{65,97},{97,1},{2,34}... | collective-permute-start | bytes 3735560 | tf_op jit(solution)/shard_map/ppermute | solution.py:336
  107.4 29.5 %collective-permute-start.15 = (bf16[1216,512]{1,0:T(8,128)(2,1)}, bf16[1216,512]{1,0:T(8,128)(2,1)S(1)}, u32[]{:S(2)}, u32[]{:S(2)}) collective-permute-start(bf16[1216,512]{1,0:T(8,128)(2,1)} %get-tuple-element.45.refs_0_), channel_id=1, source_target_pairs={{0,96},{32,0},{64,32},{96,64},{1,97},{33,1},{65,33},{97,65},{2,98}... | collective-permute-start | bytes 3735560 | tf_op jit(solution)/shard_map/ppermute | solution.py:336
  113.8 24.4 %copy-start.5 = (bf16[608,512]{1,0:T(8,128)(2,1)S(1)}, bf16[608,512]{1,0:T(8,128)(2,1)}, u32[]{:S(2)}) copy-start(bf16[608,512]{1,0:T(8,128)(2,1)} %get-tuple-element.47.refs_1_.refs_0_) | copy-start | bytes 1867780
  136.9 14.5 %copy-start.4 = (bf16[1216,512]{1,0:T(8,128)(2,1)}, bf16[1216,512]{1,0:T(8,128)(2,1)S(1)}, u32[]{:S(2)}) copy-start(bf16[1216,512]{1,0:T(8,128)(2,1)S(1)} %collective-permute-done.14.refs_1_) | copy-start | bytes 3735556
  136.9 14.5 %copy-start.2 = (bf16[1216,512]{1,0:T(8,128)(2,1)}, bf16[1216,512]{1,0:T(8,128)(2,1)S(1)}, u32[]{:S(2)}) copy-start(bf16[1216,512]{1,0:T(8,128)(2,1)S(1)} %collective-permute-done.15.refs_2_) | copy-start | bytes 3735556
  136.9 22.9 %collective-permute-start.16 = (bf16[4,4,512,128]{3,2,1,0:T(8,128)(2,1)}, bf16[4,4,512,128]{3,2,1,0:T(8,128)(2,1)}, u32[]{:S(2)}, u32[]{:S(2)}) collective-permute-start(bf16[4,4,512,128]{3,2,1,0:T(8,128)(2,1)} %get-tuple-element.51), channel_id=1, source_target_pairs={{0,1},{1,0},{2,3},{3,2},{4,5},{5,4},{6,7},{7,6},{8,9},{9,8},{10,11... | collective-permute-start | bytes 6291464 | tf_op jit(solution)/shard_map/ppermute | solution.py:344
  137.6 5.4 %collective-permute-start.17 = (bf16[4,512,128]{2,1,0:T(8,128)(2,1)}, bf16[4,512,128]{2,1,0:T(8,128)(2,1)S(1)}, u32[]{:S(2)}, u32[]{:S(2)}) collective-permute-start(bf16[4,512,128]{2,1,0:T(8,128)(2,1)} %collective-permute-done.10.refs_0_), channel_id=1, source_target_pairs={{0,1},{1,0},{2,3},{3,2},{4,5},{5,4},{6,7},{7,6},{8,9},{9,8},{10,11... | collective-permute-start | bytes 1572872 | tf_op jit(solution)/shard_map/ppermute | solution.py:344
  137.7 7.9 %collective-permute-start.18 = (bf16[4,512,128]{2,1,0:T(8,128)(2,1)}, bf16[4,512,128]{2,1,0:T(8,128)(2,1)}, u32[]{:S(2)}, u32[]{:S(2)}) collective-permute-start(bf16[4,512,128]{2,1,0:T(8,128)(2,1)} %collective-permute-done.11.refs_2_), channel_id=1, source_target_pairs={{0,1},{1,0},{2,3},{3,2},{4,5},{5,4},{6,7},{7,6},{8,9},{9,8},{10,11... | collective-permute-start | bytes 1572872 | tf_op jit(solution)/shard_map/ppermute | solution.py:344
  138.1 7.5 %collective-permute-start.19 = (bf16[4,512,128]{2,1,0:T(8,128)(2,1)}, bf16[4,512,128]{2,1,0:T(8,128)(2,1)}, u32[]{:S(2)}, u32[]{:S(2)}) collective-permute-start(bf16[4,512,128]{2,1,0:T(8,128)(2,1)} %collective-permute-done.13.refs_4_), channel_id=1, source_target_pairs={{0,1},{1,0},{2,3},{3,2},{4,5},{5,4},{6,7},{7,6},{8,9},{9,8},{10,11... | collective-permute-start | bytes 1572872 | tf_op jit(solution)/shard_map/ppermute | solution.py:344
  138.2 25.7 %collective-permute-start.20 = (bf16[608,512]{1,0:T(8,128)(2,1)S(1)}, bf16[608,512]{1,0:T(8,128)(2,1)S(1)}, u32[]{:S(2)}, u32[]{:S(2)}) collective-permute-start(bf16[608,512]{1,0:T(8,128)(2,1)S(1)} %copy-done.5), channel_id=1, source_target_pairs={{0,32},{32,64},{64,96},{96,0},{1,33},{33,65},{65,97},{97,1},{2,34}... | collective-permute-start | bytes 1867784 | tf_op jit(solution)/shard_map/ppermute | solution.py:336
  143.0 2.6 %copy-start.15 = (bf16[4,512,128]{2,1,0:T(8,128)(2,1)}, bf16[4,512,128]{2,1,0:T(8,128)(2,1)S(1)}, u32[]{:S(2)}) copy-start(bf16[4,512,128]{2,1,0:T(8,128)(2,1)S(1)} %collective-permute-done.17.refs_1_) | copy-start | bytes 1572868
  143.0 20.9 %collective-permute-start.21 = (bf16[608,512]{1,0:T(8,128)(2,1)S(1)}, bf16[608,512]{1,0:T(8,128)(2,1)}, u32[]{:S(2)}, u32[]{:S(2)}) collective-permute-start(bf16[608,512]{1,0:T(8,128)(2,1)S(1)} %copy-done.5), channel_id=1, source_target_pairs={{0,96},{32,0},{64,32},{96,64},{1,97},{33,1},{65,33},{97,65},{2,98}... | collective-permute-start | bytes 1867784 | tf_op jit(solution)/shard_map/ppermute | solution.py:336
  163.9 0.8 copy-start.7
  164.7 5.1 %copy-start.3 = (bf16[1216,512]{1,0:T(8,128)(2,1)S(1)}, bf16[1216,512]{1,0:T(8,128)(2,1)}, u32[]{:S(2)}) copy-start(bf16[1216,512]{1,0:T(8,128)(2,1)} %copy-done.2) | copy-start | bytes 3735556
  164.7 61.9 %all-to-all-start.2 = ((bf16[16,512,128]{2,1,0:T(8,128)(2,1)}), bf16[16,512,128]{2,1,0:T(8,128)(2,1)S(1)}, u32[]{:S(2)}, u32[]{:S(2)}) async-start(bf16[16,512,128]{2,1,0:T(8,128)(2,1)} %bitcast.11), calls=%async_computation.2 | async-start | bytes 4194304 | tf_op jit(solution)/shard_map/all_to_all | solution.py:398
  168.6 21.2 %copy-start.8 = (bf16[608,512]{1,0:T(8,128)(2,1)S(1)}, bf16[608,512]{1,0:T(8,128)(2,1)}, u32[]{:S(2)}) copy-start(bf16[608,512]{1,0:T(8,128)(2,1)} %copy-done.7) | copy-start | bytes 1867780
  169.8 16.5 %collective-permute-start.22 = (bf16[608,512]{1,0:T(8,128)(2,1)S(1)}, bf16[608,512]{1,0:T(8,128)(2,1)S(1)}, u32[]{:S(2)}, u32[]{:S(2)}) collective-permute-start(bf16[608,512]{1,0:T(8,128)(2,1)S(1)} %slice.24), channel_id=1, source_target_pairs={{0,32},{32,64},{64,96},{96,0},{1,33},{33,65},{65,97},{97,1},{2,34}... | collective-permute-start | bytes 1867784 | tf_op jit(solution)/shard_map/ppermute | solution.py:336
  169.9 16.3 %collective-permute-start.23 = (bf16[608,512]{1,0:T(8,128)(2,1)S(1)}, bf16[608,512]{1,0:T(8,128)(2,1)S(1)}, u32[]{:S(2)}, u32[]{:S(2)}) collective-permute-start(bf16[608,512]{1,0:T(8,128)(2,1)S(1)} %slice.25), channel_id=1, source_target_pairs={{0,96},{32,0},{64,32},{96,64},{1,97},{33,1},{65,33},{97,65},{2,98}... | collective-permute-start | bytes 1867784 | tf_op jit(solution)/shard_map/ppermute | solution.py:336
  186.2 3.6 %copy-start.11 = (bf16[608,512]{1,0:T(8,128)(2,1)}, bf16[608,512]{1,0:T(8,128)(2,1)S(1)}, u32[]{:S(2)}) copy-start(bf16[608,512]{1,0:T(8,128)(2,1)S(1)} %collective-permute-done.22.refs_0_) | copy-start | bytes 1867780
  186.2 0.9 copy-start.12
  187.1 29.2 %collective-permute-start.24 = (bf16[608,512]{1,0:T(8,128)(2,1)}, bf16[608,512]{1,0:T(8,128)(2,1)S(1)}, u32[]{:S(2)}, u32[]{:S(2)}) collective-permute-start(bf16[608,512]{1,0:T(8,128)(2,1)} %get-tuple-element.54.refs_2_.refs_0_), channel_id=1, source_target_pairs={{0,32},{32,64},{64,96},{96,0},{1,33},{33,65},{65,97},{97,1},{2,34}... | collective-permute-start | bytes 1867784 | tf_op jit(solution)/shard_map/ppermute | solution.py:336
  187.1 30.3 %collective-permute-start.25 = (bf16[608,512]{1,0:T(8,128)(2,1)}, bf16[608,512]{1,0:T(8,128)(2,1)S(1)}, u32[]{:S(2)}, u32[]{:S(2)}) collective-permute-start(bf16[608,512]{1,0:T(8,128)(2,1)} %get-tuple-element.54.refs_2_.refs_0_), channel_id=1, source_target_pairs={{0,96},{32,0},{64,32},{96,64},{1,97},{33,1},{65,33},{97,65},{2,98}... | collective-permute-start | bytes 1867784 | tf_op jit(solution)/shard_map/ppermute | solution.py:336
  189.8 19.7 %collective-permute-start.26 = (bf16[304,512]{1,0:T(8,128)(2,1)S(1)}, bf16[304,512]{1,0:T(8,128)(2,1)}, u32[]{:S(2)}, u32[]{:S(2)}) collective-permute-start(bf16[304,512]{1,0:T(8,128)(2,1)S(1)} %slice.26), channel_id=1, source_target_pairs={{0,32},{32,64},{64,96},{96,0},{1,33},{33,65},{65,97},{97,1},{2,34}... | collective-permute-start | bytes 933896 | tf_op jit(solution)/shard_map/ppermute | solution.py:336
  191.6 17.9 %collective-permute-start.27 = (bf16[304,512]{1,0:T(8,128)(2,1)}, bf16[304,512]{1,0:T(8,128)(2,1)}, u32[]{:S(2)}, u32[]{:S(2)}) collective-permute-start(bf16[304,512]{1,0:T(8,128)(2,1)} %slice.27), channel_id=1, source_target_pairs={{0,96},{32,0},{64,32},{96,64},{1,97},{33,1},{65,33},{97,65},{2,98}... | collective-permute-start | bytes 933896 | tf_op jit(solution)/shard_map/ppermute | solution.py:336
  216.3 4.3 %copy-start.9 = (bf16[608,512]{1,0:T(8,128)(2,1)}, bf16[608,512]{1,0:T(8,128)(2,1)S(1)}, u32[]{:S(2)}) copy-start(bf16[608,512]{1,0:T(8,128)(2,1)S(1)} %collective-permute-done.24.refs_1_) | copy-start | bytes 1867780
  217.1 10.5 %collective-permute-start.28 = (bf16[304,512]{1,0:T(8,128)(2,1)}, bf16[304,512]{1,0:T(8,128)(2,1)}, u32[]{:S(2)}, u32[]{:S(2)}) collective-permute-start(bf16[304,512]{1,0:T(8,128)(2,1)} %slice.22), channel_id=1, source_target_pairs={{0,32},{32,64},{64,96},{96,0},{1,33},{33,65},{65,97},{97,1},{2,34}... | collective-permute-start | bytes 933896 | tf_op jit(solution)/shard_map/ppermute | solution.py:336
  217.4 3.1 %copy-start.10 = (bf16[608,512]{1,0:T(8,128)(2,1)}, bf16[608,512]{1,0:T(8,128)(2,1)S(1)}, u32[]{:S(2)}) copy-start(bf16[608,512]{1,0:T(8,128)(2,1)S(1)} %collective-permute-done.25.refs_2_) | copy-start | bytes 1867780
  218.2 9.3 %collective-permute-start.29 = (bf16[304,512]{1,0:T(8,128)(2,1)}, bf16[304,512]{1,0:T(8,128)(2,1)}, u32[]{:S(2)}, u32[]{:S(2)}) collective-permute-start(bf16[304,512]{1,0:T(8,128)(2,1)} %slice.23), channel_id=1, source_target_pairs={{0,96},{32,0},{64,32},{96,64},{1,97},{33,1},{65,33},{97,65},{2,98}... | collective-permute-start | bytes 933896 | tf_op jit(solution)/shard_map/ppermute | solution.py:336
  (2 other events, 1.6 us)

commit v6 on v5

--- a/solution.py
+++ b/solution.py
@@ -66,7 +66,8 @@
 
 
 def student_body(pos, w_ref, *refs):
-    own_refs, sib_refs, (s_ref, m_ref, l_ref, h_ref) = refs[:4], refs[4:8], refs[8:]
+    own_refs, sib_refs, (s_ref, m_ref, l_ref) = refs[:4], refs[4:8], refs[8:11]
+    mine_ref, *next_refs, h_ref = refs[11:]
     step = pl.program_id(0)
 
     @pl.when(step == 0)
@@ -78,6 +79,11 @@
                     z = (pos[2] + 4 - jnp.where(c == 0, b, a)) % 4
                     at = pl.multiple_of(((y * 4 + z) * 2 + c) * 128, 128)
                     h_ref[:, pl.ds(at, 128)] = ref[b]
+        mine_ref[...] = h_ref[:, pl.ds(pl.multiple_of(pos[0] * DX, 128), DX)]
+        for n, out_ref in enumerate(next_refs, 1):
+            for z in range(4):
+                at = pl.multiple_of((pos[0] + n) % 4 * DX + (2 * z + pos[3]) * 128, 128)
+                out_ref[z] = h_ref[:, pl.ds(at, 128)]
         m_ref[...] = jnp.full_like(m_ref, LOW)
         l_ref[...] = jnp.zeros_like(l_ref)
 
@@ -96,12 +102,25 @@
     part = jax.ShapeDtypeStruct((8, T), F32)
     return call(
         student_body,
-        out_shape=[jax.ShapeDtypeStruct((NS * SB, T), F32), part, part, jax.ShapeDtypeStruct((T, D), BF16)],
+        out_shape=[
+            jax.ShapeDtypeStruct((NS * SB, T), F32),
+            part,
+            part,
+            jax.ShapeDtypeStruct((T, DX), BF16),
+            *[jax.ShapeDtypeStruct((4, T, 128), BF16)] * 3,
+        ],
         grid_spec=pltpu.PrefetchScalarGridSpec(
             num_scalar_prefetch=1,
             grid=(NS,),
             in_specs=[pl.BlockSpec((SB, D), lambda i, p: (i, 0))] + [whole((4, T, 128))] * 8,
-            out_specs=[pl.BlockSpec((SB, T), lambda i, p: (i, 0)), whole((8, T)), whole((8, T)), whole((T, D))],
+            out_specs=[
+                pl.BlockSpec((SB, T), lambda i, p: (i, 0)),
+                whole((8, T)),
+                whole((8, T)),
+                whole((T, DX)),
+                *[whole((4, T, 128))] * 3,
+            ],
+            scratch_shapes=[pltpu.VMEM((T, D), BF16)],
         ),
     )(pos, wt, *own, *sib)
 
@@ -247,26 +266,6 @@
     )(pos, *gs, wt)
 
 
-def pick_body(pos, h_ref, *out_refs):
-    for n, out_ref in enumerate(out_refs, 1):
-        for z in range(4):
-            at = pl.multiple_of((pos[0] + n) % 4 * DX + (2 * z + pos[3]) * 128, 128)
-            out_ref[z] = h_ref[:, pl.ds(at, 128)]
-
-
-def pick(pos, h):
-    return call(
-        pick_body,
-        out_shape=[jax.ShapeDtypeStruct((4, T, 128), BF16)] * 3,
-        grid_spec=pltpu.PrefetchScalarGridSpec(
-            num_scalar_prefetch=1,
-            grid=(1,),
-            in_specs=[whole((T, D))],
-            out_specs=[whole((4, T, 128))] * 3,
-        ),
-    )(pos, h)
-
-
 def tokens_body(pos, h_ref, *refs):
     k_ref = refs[-1]
     k_ref[0:T, :] = h_ref[...]
@@ -284,7 +283,7 @@
         grid_spec=pltpu.PrefetchScalarGridSpec(
             num_scalar_prefetch=1,
             grid=(1,),
-            in_specs=[pl.BlockSpec((T, DX), lambda i, p: (0, p[0]))] + [whole((4, T, 128))] * 6,
+            in_specs=[whole((T, DX))] + [whole((4, T, 128))] * 6,
             out_specs=whole((4 * T, DX)),
         ),
     )(pos, h, *parts)
@@ -332,6 +331,36 @@
     )(*args)
 
 
+def head_all_body(pos, *refs):
+    g = jnp.concatenate([r[0] for r in refs[:4]], axis=1)
+    refs[-1][...] = jnp.dot(g, refs[4][...], preferred_element_type=F32).astype(BF16)
+
+
+def head_all(pos, g, k, first, steps, other=None):
+    specs = [
+        pl.BlockSpec((1, GB, T), functools.partial(lambda away, i, p: ((p[0] + away) % 4, i, 0), away))
+        for away in (0, 3, 1, 2)
+    ]
+    specs.append(whole((4 * T, DX)))
+    args = [g] * 4 + [k]
+    kw = {}
+    if other is not None:
+        specs.append(pl.BlockSpec(memory_space=pl.ANY))
+        args.append(other)
+        kw["input_output_aliases"] = {len(args): 0}
+    return call(
+        head_all_body,
+        out_shape=jax.ShapeDtypeStruct((VL, DX), BF16),
+        grid_spec=pltpu.PrefetchScalarGridSpec(
+            num_scalar_prefetch=1,
+            grid=(steps,),
+            in_specs=specs,
+            out_specs=pl.BlockSpec((GB, DX), lambda i, p: (i + first, 0)),
+        ),
+        **kw,
+    )(pos, *args)
+
+
 def shift(x, n):
     return lax.ppermute(x, "x", [(i, (i + n) % 4) for i in range(4)])
 
@@ -368,11 +397,10 @@
     one = jnp.stack(spread(hidden, 0))
     own = spread(after(one, blocks), 1)
     teacher = lax.all_to_all(after(blocks, *own[1:]), V, 0, 0, tiled=True)
-    s, m, l, h = student(pos, wt, own, [swap(x) for x in own])
+    s, m, l, h, to_right, to_far, to_left = student(pos, wt, own, [swap(x) for x in own])
     t, share = stats(m, l, s, teacher)
     gathered = lax.all_to_all(share, V, 0, 0, tiled=True)
 
-    to_right, to_far, to_left = pick(pos, h)
     others = [shift(to_right, 1), shift(to_left, 3), hop(after(hop(to_far), share))]
 
     w = row_weight.reshape(1, T)
@@ -387,22 +415,18 @@
         left, right = after(parts[1], *first), after(parts[2], *first)
         return [shift(left[:half], 1), shift(right[half:], 3)]
 
-    near_u, near_m = near(gu), near(gm)
-    far_u, far_m = far(near_u), far(near_m)
-    near_l = near(after(gl, *far_u))
+    all_u, all_m = lax.all_gather(gu, "x"), lax.all_gather(gm, "x")
+    near_l = near(gl)
+    far_l = far(near_l)
     mine, other = hidden_part(pos, (gu, gm, gl), wt)
     k = tokens(after(pos, mine), h, [x for other in others for x in (other, swap(other))])
-    part_u = head_piece(near_u, [], k, *CUTS[0])
-    both = (mine.astype(F32) + swap(after(other, *near_u[1:])).astype(F32)).astype(BF16)
-    both = after(both, part_u, *near_m[1:])
+    both = (mine.astype(F32) + swap(after(other, *near_l[1:])).astype(F32)).astype(BF16)
     got = lax.all_to_all(both.reshape(16, T, 128), ("y", "z"), 0, 0, tiled=True)
 
-    head = head_piece([], far_u, k, *CUTS[0], prior=part_u)
-    head = head_piece(near_m, far_m, k, *CUTS[1], other=head)
-    far_l = far(near_l, head)
-    part_l = head_piece(near_l, [], k, *CUTS[2])
-    grad_hidden = jnp.sum(after(got, part_l).astype(F32), axis=0).astype(BF16)
-    head = head_piece([], far_l, k, *CUTS[2], prior=after(part_l, grad_hidden), other=head)
+    head = head_all(pos, all_u, k, *CUTS[0])
+    head = head_piece(near_l, far_l, k, *CUTS[2], other=head)
+    grad_hidden = jnp.sum(after(got, head).astype(F32), axis=0).astype(BF16)
+    head = head_all(pos, all_m, k, *CUTS[1], other=head)
     return kl.reshape(T), grad_hidden, head.T
 
 

time: 234 us -> 226 us (0.966)
  between operations: 0.82 us -> 14.2 us
  Pallas kernels: 101 us -> 89.2 us
  starting transfers between devices: 54.7 us -> 43.3 us
  waiting for transfers between devices: 60.3 us -> 67.5 us
  local copies, waits for them, and re-layouts: 9.41 us -> 6.2 us
    all_gather x0 -> x2, waiting for transfers between devices: none -> 25.1 us  [per_device(): all_u, all_m = (lax.all_gather(gu, 'x'), lax.all_gather(gm, 'x'))]
    pallas_call x5 -> x1, Pallas kernels: 30.2 us -> 6.69 us  [head_piece(): call(functools.partial(head_body, bool(near), bool(far), prior is not Non...]
    ppermute x14 -> x6, waiting for transfers between devices: 28.5 us -> 8.46 us  [shift(): return lax.ppermute(x, 'x', [(i, (i + n) % 4) for i in range(4)])]
    pallas_call x1 -> x2, Pallas kernels: 4.44 us -> 17.7 us  [head_all(): call(head_all_body, out_shape=jax.ShapeDtypeStruct((VL, DX), BF16), grid_...]
    ppermute x14 -> x6, starting transfers between devices: 19.7 us -> 9.07 us  [shift(): return lax.ppermute(x, 'x', [(i, (i + n) % 4) for i in range(4)])]
    slice x6 -> x2, local copies, waits for them, and re-layouts: 4.56 us -> 0.77 us  [far(): return [shift(left[:half], 1), shift(right[half:], 3)]]
    all_to_all x1, starting transfers between devices: 8.29 us -> 4.77 us  [per_device(): gathered = lax.all_to_all(share, V, 0, 0, tiled=True)]
    unnamed x34 -> x28, local copies, waits for them, and re-layouts: 4.84 us -> 5.42 us
  transfers between devices with their start and end apart: 33 -> 27, of which waited for: 14 -> 16; matrix products, arithmetic and copies ran while one was open for 4% -> 2% of each run, Pallas kernels for 40% -> 34%
where the time goes in v6:
time: 226 us
  Pallas kernels  89.2 us (39%)
  waiting for transfers between devices  67.5 us (30%)
  starting transfers between devices  43.3 us (19%)
  between operations  14.2 us (6%)
  local copies, waits for them, and re-layouts  6.2 us (3%)
  other arithmetic  5.21 us (2%)
    all_gather x2, waiting for transfers between devices, per_device(): all_u, all_m = (lax.all_gather(gu, 'x'), lax.all_gather(gm, 'x'))  25.1 us
    pallas_call x1, Pallas kernels, student(): call(student_body, out_shape=[jax.ShapeDtypeStruct((NS * SB, T), F32), pa...  20.4 us
    pallas_call x2, Pallas kernels, head_all(): call(head_all_body, out_shape=jax.ShapeDtypeStruct((VL, DX), BF16), grid_...  17.7 us
    pallas_call x1, Pallas kernels, hidden_part(): call(hidden_body, out_shape=[jax.ShapeDtypeStruct((4, 4, T, 128), BF16)]...  17.5 us
    ppermute x6, waiting for transfers between devices, spread(): got.append(lax.ppermute(x, V, pairs))  13.5 us
    ppermute x6, starting transfers between devices, spread(): got.append(lax.ppermute(x, V, pairs))  10.1 us
    all_to_all x1, waiting for transfers between devices, per_device(): gathered = lax.all_to_all(share, V, 0, 0, tiled=True)  9.46 us
    pallas_call x2, Pallas kernels, grad(): call(functools.partial(grad_body, cuts), out_shape=[jax.ShapeDtypeStruct(...  9.32 us
  transfers between devices with their start and end apart: 27, of which 16 were waited for; matrix products, arithmetic and copies ran while one was open for 2% of the time, Pallas kernels for 34%

profile of v6, /device:TPU:1, one launch (start us, length us, event | category | flops | bytes accessed | tf_op | source)
XLA Modules:
  0.0 225.5 jit_solution(9360102395823018816)
XLA Ops:
  7.2 3.6 %collective-permute-start.2 = (bf16[512,128]{1,0:T(8,128)(2,1)}, bf16[512,128]{1,0:T(8,128)(2,1)S(1)}, u32[]{:S(2)}, u32[]{:S(2)}) collective-permute-start(bf16[512,128]{1,0:T(8,128)(2,1)} %param.4), channel_id=1, source_target_pairs={{0,6},{1,25},{2,0},{3,27},{4,2},{5,29},{6,4},{7,31},{8,14},{9,1},{... | collective-permute-start | bytes 393224 | tf_op jit(solution)/shard_map/ppermute | solution.py:385
  11.2 0.7 collective-permute-start
  11.8 4.4 %shard_map.67 = bf16[32,19,16,128]{3,2,1,0:T(8,128)(2,1)} custom-call(bf16[16,75968]{1,0:T(8,128)(2,1)} %t_ref.1), custom_call_target="tpu_custom_call" | custom-call | flops 1048576 | bytes 65536 | tf_op jit(solution)/shard_map/pallas_call | solution.py:55
  16.4 1.6 collective-permute-done
  18.1 1.4 collective-permute-start.3
  19.5 3.3 %collective-permute-start.4 = (bf16[4,512,128]{2,1,0:T(8,128)(2,1)S(1)}, bf16[4,512,128]{2,1,0:T(8,128)(2,1)S(1)}, u32[]{:S(2)}, u32[]{:S(2)}) collective-permute-start(bf16[4,512,128]{2,1,0:T(8,128)(2,1)S(1)} %pad_maximum_fusion.refs_0_), channel_id=1, source_target_pairs={{0,16},{1,5},{2,18},{3,7},{4,20},{5,1},{6,22},{7,3},{8,24},{9,13},... | collective-permute-start | bytes 1572872 | tf_op jit(solution)/shard_map/ppermute | solution.py:385
  22.8 0.7 collective-permute-start.5
  23.6 5.0 %collective-permute-done.3.refs_1_ = bf16[4,512,128]{2,1,0:T(8,128)(2,1)S(1)} collective-permute-done((bf16[4,512,128]{2,1,0:T(8,128)(2,1)S(1)}, bf16[4,512,128]{2,1,0:T(8,128)(2,1)S(1)}, u32[]{:S(2)}, u32[]{:S(2)}) %collective-permute-start.3) | collective-permute-done | bytes 524320 | tf_op jit(solution)/shard_map/ppermute | solution.py:385
  28.5 6.8 %collective-permute-done.4.refs_2_ = bf16[4,512,128]{2,1,0:T(8,128)(2,1)S(1)} collective-permute-done((bf16[4,512,128]{2,1,0:T(8,128)(2,1)S(1)}, bf16[4,512,128]{2,1,0:T(8,128)(2,1)S(1)}, u32[]{:S(2)}, u32[]{:S(2)}) %collective-permute-start.4) | collective-permute-done | bytes 524320 | tf_op jit(solution)/shard_map/ppermute | solution.py:385
  35.3 0.8 copy-done.9
  36.2 6.6 %all-to-all-start = ((bf16[32,19,16,128]{3,2,1,0:T(8,128)(2,1)}), bf16[32,19,16,128]{3,2,1,0:T(8,128)(2,1)S(1)}, u32[]{:S(2)}, u32[]{:S(2)}) async-start(bf16[32,19,16,128]{3,2,1,0:T(8,128)(2,1)} %shard_map.67), calls=%async_computation | async-start | bytes 4980736 | tf_op jit(solution)/shard_map/all_to_all | solution.py:399
  43.8 0.7 pad_add_fusion.pos
  44.9 1.5 collective-permute-done.7.refs_5_
  46.6 0.8 collective-permute-done.9.refs_7_
  47.3 20.4 %shard_map.68 = (f32[2560,512]{1,0:T(8,128)}, f32[8,512]{1,0:T(8,128)}, f32[8,512]{1,0:T(8,128)}, bf16[512,1024]{1,0:T(8,128)(2,1)}, bf16[4,512,128]{2,1,0:T(8,1...) custom-call(s32[4]{0:T(128)} %pad_add_fusion.pos, bf16[2374,4096]{1,0:T(8,128)(2,1)} %bitcast.19, ...), custom_call_target="tpu_custom_call" | custom-call | flops 1048576 | bytes 65536 | tf_op jit(solution)/shard_map/pallas_call | solution.py:103
  67.8 2.5 %collective-permute-start.12 = (bf16[4,512,128]{2,1,0:T(8,128)(2,1)}, bf16[4,512,128]{2,1,0:T(8,128)(2,1)}, u32[]{:S(2)}, u32[]{:S(2)}) collective-permute-start(bf16[4,512,128]{2,1,0:T(8,128)(2,1)} %get-tuple-element.34), channel_id=1, source_target_pairs={{0,32},{1,97},{32,64},{33,1},{64,96},{65,33},{96,0},{97,65},{2,34}... | collective-permute-start | bytes 1572872 | tf_op jit(solution)/shard_map/ppermute | solution.py:369
  70.3 2.7 %collective-permute-start.11 = (bf16[4,512,128]{2,1,0:T(8,128)(2,1)}, bf16[4,512,128]{2,1,0:T(8,128)(2,1)S(1)}, u32[]{:S(2)}, u32[]{:S(2)}) collective-permute-start(bf16[4,512,128]{2,1,0:T(8,128)(2,1)} %get-tuple-element.33), channel_id=1, source_target_pairs={{0,96},{32,0},{64,32},{96,64},{1,97},{33,1},{65,33},{97,65},{2,98}... | collective-permute-start | bytes 1572872 | tf_op jit(solution)/shard_map/ppermute | solution.py:365
  73.0 2.3 %all-to-all-done.t_ref = bf16[32,19,16,128]{3,2,1,0:T(8,128)(2,1)S(1)} async-done(((bf16[32,19,16,128]{3,2,1,0:T(8,128)(2,1)}), bf16[32,19,16,128]{3,2,1,0:T(8,128)(2,1)S(1)}, u32[]{:S(2)}, u32[]{:S(2)}) %all-to-all-start) | async-done | bytes 2490400 | tf_op jit(solution)/shard_map/all_to_all | solution.py:399
  75.3 1.5 copy-done
  76.8 7.3 %shard_map.69 = (bf16[2560,512]{1,0:T(8,128)(2,1)}, f32[32,8,512]{2,1,0:T(8,128)}) custom-call(f32[8,512]{1,0:T(8,128)} %get-tuple-element.27.m_ref, f32[8,512]{1,0:T(8,128)} %get-tuple-element.28.l_ref, f32[2560,512]{1,0:T(8,128)} %get-tuple-element.29.s_ref, bf16[32,19,16,128]{3,2,1,0:T(8,128)(2,1)} %copy-done), custom_call_target="tpu_custom_call" | custom-call | flops 1048576 | bytes 65536 | tf_op jit(solution)/shard_map/pallas_call | solution.py:172
  84.1 2.5 %collective-permute-start.13 = (bf16[4,512,128]{2,1,0:T(8,128)(2,1)}, bf16[4,512,128]{2,1,0:T(8,128)(2,1)S(1)}, u32[]{:S(2)}, u32[]{:S(2)}) collective-permute-start(bf16[4,512,128]{2,1,0:T(8,128)(2,1)} %collective-permute-done.12), channel_id=1, source_target_pairs={{0,32},{1,97},{32,64},{33,1},{64,96},{65,33},{96,0},{97,65},{2,34}... | collective-permute-start | bytes 1572872 | tf_op jit(solution)/shard_map/ppermute | solution.py:369
  86.7 4.8 %all-to-all-start.1 = ((f32[32,8,512]{2,1,0:T(8,128)}), f32[32,8,512]{2,1,0:T(8,128)S(1)}, u32[]{:S(2)}, u32[]{:S(2)}) async-start(f32[32,8,512]{2,1,0:T(8,128)} %get-tuple-element.31), calls=%async_computation.1 | async-start | bytes 1048576 | tf_op jit(solution)/shard_map/all_to_all | solution.py:402
  91.7 1.9 collective-permute-done.13.refs_4_
  93.6 9.5 %all-to-all-done.1.all_ref = f32[32,8,512]{2,1,0:T(8,128)S(1)} async-done(((f32[32,8,512]{2,1,0:T(8,128)}), f32[32,8,512]{2,1,0:T(8,128)S(1)}, u32[]{:S(2)}, u32[]{:S(2)}) %all-to-all-start.1) | async-done | bytes 524320 | tf_op jit(solution)/shard_map/all_to_all | solution.py:402
  103.1 0.8 copy-done.1
  103.9 4.5 %shard_map.70 = (bf16[1216,512]{1,0:T(8,128)(2,1)}, f32[1,512]{1,0:T(1,128)}) custom-call(f32[32,8,512]{2,1,0:T(8,128)} %copy-done.1, f32[1,512]{1,0:T(1,128)} %bitcast.30, f32[2560,512]{1,0:T(8,128)} %get-tuple-element.29.s_ref, bf16[2560,512]{1,0:T(8,128)(2,1)} %get-tuple-element.37.t_ref), custom_call_target="tpu_custom_call" | custom-call | flops 1048576 | bytes 65536 | tf_op jit(solution)/shard_map/pallas_call | solution.py:222
  108.4 4.8 %shard_map.71 = (bf16[608,512]{1,0:T(8,128)(2,1)}, bf16[608,512]{1,0:T(8,128)(2,1)}, f32[1,512]{1,0:T(1,128)}) custom-call(f32[32,8,512]{2,1,0:T(8,128)} %copy-done.1, f32[1,512]{1,0:T(1,128)} %bitcast.31, f32[2560,512]{1,0:T(8,128)} %get-tuple-element.29.s_ref, bf16[2560,512]{1,0:T(8,128)(2,1)} %get-tuple-element.37.t_ref), custom_call_target="tpu_custom_call" | custom-call | flops 1048576 | bytes 65536 | tf_op jit(solution)/shard_map/pallas_call | solution.py:222
  113.3 1.1 collective-permute-start.14
  114.4 1.7 collective-permute-start.15
  116.1 17.5 %shard_map.72 = (bf16[4,4,512,128]{3,2,1,0:T(8,128)(2,1)}, bf16[4,4,512,128]{3,2,1,0:T(8,128)(2,1)}) custom-call(s32[4]{0:T(128)} %pad_add_fusion.pos, bf16[1216,512]{1,0:T(8,128)(2,1)} %get-tuple-element.39.refs_0_, bf16[608,512]{1,0:T(8,128)(2,1)} %get-tuple-element.41.refs_1_, bf16[608,512]{1,0:T(8,128)(2,1)} %get-tuple-element.42.refs_2_.refs_0_, ...), custom_call_target="tpu_custom_call" | custom-call | flops 1048576 | bytes 65536 | tf_op jit(solution)/shard_map/pallas_call | solution.py:256
  133.6 7.5 %collective-permute-done.14.refs_1_ = bf16[608,512]{1,0:T(8,128)(2,1)S(1)} collective-permute-done((bf16[608,512]{1,0:T(8,128)(2,1)}, bf16[608,512]{1,0:T(8,128)(2,1)S(1)}, u32[]{:S(2)}, u32[]{:S(2)}) %collective-permute-start.14) | collective-permute-done | bytes 622624 | tf_op jit(solution)/shard_map/ppermute | solution.py:365
  141.1 0.9 collective-permute-done.15.refs_2_
  142.0 1.7 collective-permute-start.16
  143.7 4.0 %collective-permute-done.16 = bf16[4,4,512,128]{3,2,1,0:T(8,128)(2,1)S(1)} collective-permute-done((bf16[4,4,512,128]{3,2,1,0:T(8,128)(2,1)}, bf16[4,4,512,128]{3,2,1,0:T(8,128)(2,1)S(1)}, u32[]{:S(2)}, u32[]{:S(2)}) %collective-permute-start.16) | collective-permute-done | bytes 2097184 | tf_op jit(solution)/shard_map/ppermute | solution.py:373
  147.7 3.5 %add_convert_fusion = bf16[4,4,512,128]{3,2,1,0:T(8,128)(2,1)} fusion(bf16[4,4,512,128]{3,2,1,0:T(8,128)(2,1)S(1)} %collective-permute-done.16, bf16[4,4,512,128]{3,2,1,0:T(8,128)(2,1)} %get-tuple-element.43), kind=kLoop, calls=%fused_computation | loop fusion | flops 4194304 | bytes 6291456 | tf_op jit(solution)/shard_map/convert_element_type | solution.py:423
  151.2 3.7 %all-to-all-start.2 = ((bf16[16,512,128]{2,1,0:T(8,128)(2,1)}), bf16[16,512,128]{2,1,0:T(8,128)(2,1)S(1)}, u32[]{:S(2)}, u32[]{:S(2)}) async-start(bf16[16,512,128]{2,1,0:T(8,128)(2,1)} %bitcast.11), calls=%async_computation.2 | async-start | bytes 4194304 | tf_op jit(solution)/shard_map/all_to_all | solution.py:424
  155.9 0.8 slice.8
  156.7 3.6 %collective-permute-start.18 = (bf16[304,512]{1,0:T(8,128)(2,1)S(1)}, bf16[304,512]{1,0:T(8,128)(2,1)S(1)}, u32[]{:S(2)}, u32[]{:S(2)}) collective-permute-start(bf16[304,512]{1,0:T(8,128)(2,1)S(1)} %slice.9), channel_id=1, source_target_pairs={{0,96},{32,0},{64,32},{96,64},{1,97},{33,1},{65,33},{97,65},{2,98}... | collective-permute-start | bytes 933896 | tf_op jit(solution)/shard_map/ppermute | solution.py:365
  160.3 0.8 copy-done.10
  161.1 5.7 %shard_map.73.refs_4_.refs_5_ = bf16[2048,1024]{1,0:T(8,128)(2,1)} custom-call(s32[4]{0:T(128)} %pad_add_fusion.pos, bf16[512,1024]{1,0:T(8,128)(2,1)} %get-tuple-element.47.h_ref, bf16[4,512,128]{2,1,0:T(8,128)(2,1)} %copy-done.5, bf16[4,512,128]{2,1,0:T(8,128)(2,1)} %copy-done.10, bf16[4,512,128]{2,1,0:T(8,128)(2,1)} %copy-done.6, ...), custom_call_target="tpu_custom_call" | custom-call | flops 1048576 | bytes 65536 | tf_op jit(solution)/shard_map/pallas_call | solution.py:280
  166.8 11.1 %all-gather.5.cloned.1.call-done = bf16[4864,512]{1,0:T(8,128)(2,1)} async-done(((bf16[1216,512]{1,0:T(8,128)(2,1)}), bf16[4864,512]{1,0:T(8,128)(2,1)}) %all-gather.5.cloned.1.call-update) | async-done | bytes 4980752 | tf_op jit(solution)/shard_map/all_gather | solution.py:418
  177.9 10.4 %shard_map.74.refs_6_ = bf16[2374,1024]{1,0:T(8,128)(2,1)} custom-call(s32[4]{0:T(128)} %pad_add_fusion.pos, bf16[4,1216,512]{2,1,0:T(8,128)(2,1)} %bitcast.15, bf16[4,1216,512]{2,1,0:T(8,128)(2,1)} %bitcast.16, bf16[4,1216,512]{2,1,0:T(8,128)(2,1)} %bitcast.17, bf16[4,1216,512]{2,1,0:T(8,128)(2,1)} %bitcast.18, bf16[2048,1024]{1,0:T(8,128)(2,1)} %shard_map.73.refs_4_.refs_5_), custom_call_target="tpu_custom_call" | custom-call | flops 1048576 | bytes 65536 | tf_op jit(solution)/shard_map/pallas_call | solution.py:351
  188.4 0.7 copy-done.11
  189.1 0.7 copy-done.12
  189.8 6.7 %shard_map.75.refs_5_ = bf16[2374,1024]{1,0:T(8,128)(2,1)} custom-call(bf16[608,512]{1,0:T(8,128)(2,1)} %get-tuple-element.42.refs_2_.refs_0_, bf16[608,512]{1,0:T(8,128)(2,1)} %copy-done.3, bf16[608,512]{1,0:T(8,128)(2,1)} %copy-done.4, bf16[304,512]{1,0:T(8,128)(2,1)} %copy-done.11, bf16[304,512]{1,0:T(8,128)(2,1)} %copy-done.12, ...), custom_call_target="tpu_custom_call", output_to_operand_aliasing={{}: (6, {})} | custom-call | flops 1048576 | bytes 65536 | tf_op jit(solution)/shard_map/pallas_call | solution.py:324
  196.5 14.0 %all-gather.7.cloned.1.call-done = bf16[2432,512]{1,0:T(8,128)(2,1)} async-done(((bf16[608,512]{1,0:T(8,128)(2,1)}), bf16[2432,512]{1,0:T(8,128)(2,1)}) %all-gather.7.cloned.1.call-update) | async-done | bytes 2490384 | tf_op jit(solution)/shard_map/all_gather | solution.py:418
  210.4 7.3 %shard_map.76 = bf16[2374,1024]{1,0:T(8,128)(2,1)} custom-call(s32[4]{0:T(128)} %pad_add_fusion.pos, bf16[4,608,512]{2,1,0:T(8,128)(2,1)} %bitcast.22, bf16[4,608,512]{2,1,0:T(8,128)(2,1)} %bitcast.23, bf16[4,608,512]{2,1,0:T(8,128)(2,1)} %bitcast.24, bf16[4,608,512]{2,1,0:T(8,128)(2,1)} %bitcast.25, ...), custom_call_target="tpu_custom_call", output_to_operand_aliasing={{}: (6, {})} | custom-call | flops 1048576 | bytes 65536 | tf_op jit(solution)/shard_map/pallas_call | solution.py:351
  217.7 1.0 reduce_sum.12
  (52 shorter events, 3.6 us)
Async XLA Ops:
  7.2 10.9 %copy-start.13 = (bf16[512,128]{1,0:T(8,128)(2,1)S(1)}, bf16[512,128]{1,0:T(8,128)(2,1)}, u32[]{:S(2)}) copy-start(bf16[512,128]{1,0:T(8,128)(2,1)} %param.4) | copy-start | bytes 393220
  7.2 9.1 %collective-permute-start.2 = (bf16[512,128]{1,0:T(8,128)(2,1)}, bf16[512,128]{1,0:T(8,128)(2,1)S(1)}, u32[]{:S(2)}, u32[]{:S(2)}) collective-permute-start(bf16[512,128]{1,0:T(8,128)(2,1)} %param.4), channel_id=1, source_target_pairs={{0,6},{1,25},{2,0},{3,27},{4,2},{5,29},{6,4},{7,31},{8,14},{9,1},{... | collective-permute-start | bytes 393224 | tf_op jit(solution)/shard_map/ppermute | solution.py:385
  10.8 5.6 %collective-permute-start.1 = (bf16[512,128]{1,0:T(8,128)(2,1)}, bf16[512,128]{1,0:T(8,128)(2,1)S(1)}, u32[]{:S(2)}, u32[]{:S(2)}) collective-permute-start(bf16[512,128]{1,0:T(8,128)(2,1)} %param.4), channel_id=1, source_target_pairs={{0,4},{1,17},{2,6},{3,19},{4,0},{5,21},{6,2},{7,23},{8,12},{9,25},... | collective-permute-start | bytes 393224 | tf_op jit(solution)/shard_map/ppermute | solution.py:385
  11.2 6.9 %collective-permute-start = (bf16[512,128]{1,0:T(8,128)(2,1)}, bf16[512,128]{1,0:T(8,128)(2,1)S(1)}, u32[]{:S(2)}, u32[]{:S(2)}) collective-permute-start(bf16[512,128]{1,0:T(8,128)(2,1)} %param.4), channel_id=1, source_target_pairs={{0,2},{1,9},{2,4},{3,11},{4,6},{5,13},{6,0},{7,15},{8,10},{9,17},{... | collective-permute-start | bytes 393224 | tf_op jit(solution)/shard_map/ppermute | solution.py:385
  18.1 24.6 %copy-start.2 = (bf16[4,512,128]{2,1,0:T(8,128)(2,1)}, bf16[4,512,128]{2,1,0:T(8,128)(2,1)S(1)}, u32[]{:S(2)}) copy-start(bf16[4,512,128]{2,1,0:T(8,128)(2,1)S(1)} %pad_maximum_fusion.refs_0_) | copy-start | bytes 1572868
  18.1 10.4 %collective-permute-start.3 = (bf16[4,512,128]{2,1,0:T(8,128)(2,1)S(1)}, bf16[4,512,128]{2,1,0:T(8,128)(2,1)S(1)}, u32[]{:S(2)}, u32[]{:S(2)}) collective-permute-start(bf16[4,512,128]{2,1,0:T(8,128)(2,1)S(1)} %pad_maximum_fusion.refs_0_), channel_id=1, source_target_pairs={{0,8},{1,3},{2,10},{3,5},{4,12},{5,7},{6,14},{7,1},{8,16},{9,11},{... | collective-permute-start | bytes 1572872 | tf_op jit(solution)/shard_map/ppermute | solution.py:385
  19.5 15.8 %collective-permute-start.4 = (bf16[4,512,128]{2,1,0:T(8,128)(2,1)S(1)}, bf16[4,512,128]{2,1,0:T(8,128)(2,1)S(1)}, u32[]{:S(2)}, u32[]{:S(2)}) collective-permute-start(bf16[4,512,128]{2,1,0:T(8,128)(2,1)S(1)} %pad_maximum_fusion.refs_0_), channel_id=1, source_target_pairs={{0,16},{1,5},{2,18},{3,7},{4,20},{5,1},{6,22},{7,3},{8,24},{9,13},... | collective-permute-start | bytes 1572872 | tf_op jit(solution)/shard_map/ppermute | solution.py:385
  22.8 13.3 %collective-permute-start.5 = (bf16[4,512,128]{2,1,0:T(8,128)(2,1)S(1)}, bf16[4,512,128]{2,1,0:T(8,128)(2,1)}, u32[]{:S(2)}, u32[]{:S(2)}) collective-permute-start(bf16[4,512,128]{2,1,0:T(8,128)(2,1)S(1)} %pad_maximum_fusion.refs_0_), channel_id=1, source_target_pairs={{0,24},{1,7},{2,26},{3,1},{4,28},{5,3},{6,30},{7,5},{8,0},{9,15},{... | collective-permute-start | bytes 1572872 | tf_op jit(solution)/shard_map/ppermute | solution.py:385
  28.5 14.5 %copy-start.8 = (bf16[4,512,128]{2,1,0:T(8,128)(2,1)}, bf16[4,512,128]{2,1,0:T(8,128)(2,1)S(1)}, u32[]{:S(2)}) copy-start(bf16[4,512,128]{2,1,0:T(8,128)(2,1)S(1)} %collective-permute-done.3.refs_1_) | copy-start | bytes 1572868
  35.3 0.9 copy-start.9
  36.2 39.1 %all-to-all-start = ((bf16[32,19,16,128]{3,2,1,0:T(8,128)(2,1)}), bf16[32,19,16,128]{3,2,1,0:T(8,128)(2,1)S(1)}, u32[]{:S(2)}, u32[]{:S(2)}) async-start(bf16[32,19,16,128]{3,2,1,0:T(8,128)(2,1)} %shard_map.67), calls=%async_computation | async-start | bytes 4980736 | tf_op jit(solution)/shard_map/all_to_all | solution.py:399
  42.7 2.1 collective-permute-start.6
  43.1 3.3 %collective-permute-start.7 = (bf16[4,512,128]{2,1,0:T(8,128)(2,1)S(1)}, bf16[4,512,128]{2,1,0:T(8,128)(2,1)}, u32[]{:S(2)}, u32[]{:S(2)}) collective-permute-start(bf16[4,512,128]{2,1,0:T(8,128)(2,1)S(1)} %collective-permute-done.3.refs_1_), channel_id=1, source_target_pairs={{0,1},{1,0},{2,3},{3,2},{4,5},{5,4},{6,7},{7,6},{8,9},{9,8},{10,11... | collective-permute-start | bytes 1572872 | tf_op jit(solution)/shard_map/ppermute | solution.py:373
  43.3 3.2 %collective-permute-start.8 = (bf16[4,512,128]{2,1,0:T(8,128)(2,1)}, bf16[4,512,128]{2,1,0:T(8,128)(2,1)}, u32[]{:S(2)}, u32[]{:S(2)}) collective-permute-start(bf16[4,512,128]{2,1,0:T(8,128)(2,1)} %copy-done.9), channel_id=1, source_target_pairs={{0,1},{1,0},{2,3},{3,2},{4,5},{5,4},{6,7},{7,6},{8,9},{9,8},{10,11... | collective-permute-start | bytes 1572872 | tf_op jit(solution)/shard_map/ppermute | solution.py:373
  43.6 3.8 %collective-permute-start.9 = (bf16[4,512,128]{2,1,0:T(8,128)(2,1)}, bf16[4,512,128]{2,1,0:T(8,128)(2,1)}, u32[]{:S(2)}, u32[]{:S(2)}) collective-permute-start(bf16[4,512,128]{2,1,0:T(8,128)(2,1)} %collective-permute-done.5.refs_3_), channel_id=1, source_target_pairs={{0,1},{1,0},{2,3},{3,2},{4,5},{5,4},{6,7},{7,6},{8,9},{9,8},{10,11... | collective-permute-start | bytes 1572872 | tf_op jit(solution)/shard_map/ppermute | solution.py:373
  67.8 16.4 %collective-permute-start.12 = (bf16[4,512,128]{2,1,0:T(8,128)(2,1)}, bf16[4,512,128]{2,1,0:T(8,128)(2,1)}, u32[]{:S(2)}, u32[]{:S(2)}) collective-permute-start(bf16[4,512,128]{2,1,0:T(8,128)(2,1)} %get-tuple-element.34), channel_id=1, source_target_pairs={{0,32},{1,97},{32,64},{33,1},{64,96},{65,33},{96,0},{97,65},{2,34}... | collective-permute-start | bytes 1572872 | tf_op jit(solution)/shard_map/ppermute | solution.py:369
  70.3 21.4 %collective-permute-start.10 = (bf16[4,512,128]{2,1,0:T(8,128)(2,1)}, bf16[4,512,128]{2,1,0:T(8,128)(2,1)S(1)}, u32[]{:S(2)}, u32[]{:S(2)}) collective-permute-start(bf16[4,512,128]{2,1,0:T(8,128)(2,1)} %get-tuple-element.32), channel_id=1, source_target_pairs={{0,32},{32,64},{64,96},{96,0},{1,33},{33,65},{65,97},{97,1},{2,34}... | collective-permute-start | bytes 1572872 | tf_op jit(solution)/shard_map/ppermute | solution.py:365
  70.3 21.4 %collective-permute-start.11 = (bf16[4,512,128]{2,1,0:T(8,128)(2,1)}, bf16[4,512,128]{2,1,0:T(8,128)(2,1)S(1)}, u32[]{:S(2)}, u32[]{:S(2)}) collective-permute-start(bf16[4,512,128]{2,1,0:T(8,128)(2,1)} %get-tuple-element.33), channel_id=1, source_target_pairs={{0,96},{32,0},{64,32},{96,64},{1,97},{33,1},{65,33},{97,65},{2,98}... | collective-permute-start | bytes 1572872 | tf_op jit(solution)/shard_map/ppermute | solution.py:365
  75.3 1.5 copy-start
  84.1 9.5 %collective-permute-start.13 = (bf16[4,512,128]{2,1,0:T(8,128)(2,1)}, bf16[4,512,128]{2,1,0:T(8,128)(2,1)S(1)}, u32[]{:S(2)}, u32[]{:S(2)}) collective-permute-start(bf16[4,512,128]{2,1,0:T(8,128)(2,1)} %collective-permute-done.12), channel_id=1, source_target_pairs={{0,32},{1,97},{32,64},{33,1},{64,96},{65,33},{96,0},{97,65},{2,34}... | collective-permute-start | bytes 1572872 | tf_op jit(solution)/shard_map/ppermute | solution.py:369
  86.7 16.4 %all-to-all-start.1 = ((f32[32,8,512]{2,1,0:T(8,128)}), f32[32,8,512]{2,1,0:T(8,128)S(1)}, u32[]{:S(2)}, u32[]{:S(2)}) async-start(f32[32,8,512]{2,1,0:T(8,128)} %get-tuple-element.31), calls=%async_computation.1 | async-start | bytes 1048576 | tf_op jit(solution)/shard_map/all_to_all | solution.py:402
  91.4 86.5 %all-gather.5.cloned.1.call-start = ((), (), s32[]{:S(2)}) async-start(), calls=%async_computation.3 | async-start | bytes 6225920 | tf_op jit(solution)/shard_map/all_gather | solution.py:418
  91.7 21.6 %copy-start.5 = (bf16[4,512,128]{2,1,0:T(8,128)(2,1)}, bf16[4,512,128]{2,1,0:T(8,128)(2,1)S(1)}, u32[]{:S(2)}) copy-start(bf16[4,512,128]{2,1,0:T(8,128)(2,1)S(1)} %collective-permute-done.10.refs_0_) | copy-start | bytes 1572868
  91.7 21.6 %copy-start.6 = (bf16[4,512,128]{2,1,0:T(8,128)(2,1)}, bf16[4,512,128]{2,1,0:T(8,128)(2,1)S(1)}, u32[]{:S(2)}) copy-start(bf16[4,512,128]{2,1,0:T(8,128)(2,1)S(1)} %collective-permute-done.11.refs_2_) | copy-start | bytes 1572868
  93.6 19.7 %copy-start.7 = (bf16[4,512,128]{2,1,0:T(8,128)(2,1)}, bf16[4,512,128]{2,1,0:T(8,128)(2,1)S(1)}, u32[]{:S(2)}) copy-start(bf16[4,512,128]{2,1,0:T(8,128)(2,1)S(1)} %collective-permute-done.13.refs_4_) | copy-start | bytes 1572868
  103.1 0.8 copy-start.1
  108.4 102.1 %all-gather.7.cloned.1.call-start = ((), (), s32[]{:S(2)}) async-start(), calls=%async_computation.4 | async-start | bytes 3112960 | tf_op jit(solution)/shard_map/all_gather | solution.py:418
  113.3 27.8 %collective-permute-start.14 = (bf16[608,512]{1,0:T(8,128)(2,1)}, bf16[608,512]{1,0:T(8,128)(2,1)S(1)}, u32[]{:S(2)}, u32[]{:S(2)}) collective-permute-start(bf16[608,512]{1,0:T(8,128)(2,1)} %get-tuple-element.42.refs_2_.refs_0_), channel_id=1, source_target_pairs={{0,32},{32,64},{64,96},{96,0},{1,33},{33,65},{65,97},{97,1},{2,34}... | collective-permute-start | bytes 1867784 | tf_op jit(solution)/shard_map/ppermute | solution.py:365
  114.4 27.6 %collective-permute-start.15 = (bf16[608,512]{1,0:T(8,128)(2,1)}, bf16[608,512]{1,0:T(8,128)(2,1)S(1)}, u32[]{:S(2)}, u32[]{:S(2)}) collective-permute-start(bf16[608,512]{1,0:T(8,128)(2,1)} %get-tuple-element.42.refs_2_.refs_0_), channel_id=1, source_target_pairs={{0,96},{32,0},{64,32},{96,64},{1,97},{33,1},{65,33},{97,65},{2,98}... | collective-permute-start | bytes 1867784 | tf_op jit(solution)/shard_map/ppermute | solution.py:365
  141.1 14.8 %copy-start.3 = (bf16[608,512]{1,0:T(8,128)(2,1)}, bf16[608,512]{1,0:T(8,128)(2,1)S(1)}, u32[]{:S(2)}) copy-start(bf16[608,512]{1,0:T(8,128)(2,1)S(1)} %collective-permute-done.14.refs_1_) | copy-start | bytes 1867780
  142.0 14.6 %copy-start.4 = (bf16[608,512]{1,0:T(8,128)(2,1)}, bf16[608,512]{1,0:T(8,128)(2,1)S(1)}, u32[]{:S(2)}) copy-start(bf16[608,512]{1,0:T(8,128)(2,1)S(1)} %collective-permute-done.15.refs_2_) | copy-start | bytes 1867780
  142.0 5.7 %collective-permute-start.16 = (bf16[4,4,512,128]{3,2,1,0:T(8,128)(2,1)}, bf16[4,4,512,128]{3,2,1,0:T(8,128)(2,1)S(1)}, u32[]{:S(2)}, u32[]{:S(2)}) collective-permute-start(bf16[4,4,512,128]{3,2,1,0:T(8,128)(2,1)} %get-tuple-element.45), channel_id=1, source_target_pairs={{0,1},{1,0},{2,3},{3,2},{4,5},{5,4},{6,7},{7,6},{8,9},{9,8},{10,11... | collective-permute-start | bytes 6291464 | tf_op jit(solution)/shard_map/ppermute | solution.py:373
  151.2 45.3 %all-to-all-start.2 = ((bf16[16,512,128]{2,1,0:T(8,128)(2,1)}), bf16[16,512,128]{2,1,0:T(8,128)(2,1)S(1)}, u32[]{:S(2)}, u32[]{:S(2)}) async-start(bf16[16,512,128]{2,1,0:T(8,128)(2,1)} %bitcast.11), calls=%async_computation.2 | async-start | bytes 4194304 | tf_op jit(solution)/shard_map/all_to_all | solution.py:424
  154.9 5.4 %collective-permute-start.19 = (bf16[4,512,128]{2,1,0:T(8,128)(2,1)}, bf16[4,512,128]{2,1,0:T(8,128)(2,1)S(1)}, u32[]{:S(2)}, u32[]{:S(2)}) collective-permute-start(bf16[4,512,128]{2,1,0:T(8,128)(2,1)} %copy-done.5), channel_id=1, source_target_pairs={{0,1},{1,0},{2,3},{3,2},{4,5},{5,4},{6,7},{7,6},{8,9},{9,8},{10,11... | collective-permute-start | bytes 1572872 | tf_op jit(solution)/shard_map/ppermute | solution.py:373
  155.4 4.9 %collective-permute-start.20 = (bf16[4,512,128]{2,1,0:T(8,128)(2,1)}, bf16[4,512,128]{2,1,0:T(8,128)(2,1)}, u32[]{:S(2)}, u32[]{:S(2)}) collective-permute-start(bf16[4,512,128]{2,1,0:T(8,128)(2,1)} %copy-done.6), channel_id=1, source_target_pairs={{0,1},{1,0},{2,3},{3,2},{4,5},{5,4},{6,7},{7,6},{8,9},{9,8},{10,11... | collective-permute-start | bytes 1572872 | tf_op jit(solution)/shard_map/ppermute | solution.py:373
  155.5 4.8 %collective-permute-start.21 = (bf16[4,512,128]{2,1,0:T(8,128)(2,1)}, bf16[4,512,128]{2,1,0:T(8,128)(2,1)}, u32[]{:S(2)}, u32[]{:S(2)}) collective-permute-start(bf16[4,512,128]{2,1,0:T(8,128)(2,1)} %copy-done.7), channel_id=1, source_target_pairs={{0,1},{1,0},{2,3},{3,2},{4,5},{5,4},{6,7},{7,6},{8,9},{9,8},{10,11... | collective-permute-start | bytes 1572872 | tf_op jit(solution)/shard_map/ppermute | solution.py:373
  156.6 31.7 %collective-permute-start.17 = (bf16[304,512]{1,0:T(8,128)(2,1)}, bf16[304,512]{1,0:T(8,128)(2,1)S(1)}, u32[]{:S(2)}, u32[]{:S(2)}) collective-permute-start(bf16[304,512]{1,0:T(8,128)(2,1)} %slice.8), channel_id=1, source_target_pairs={{0,32},{32,64},{64,96},{96,0},{1,33},{33,65},{65,97},{97,1},{2,34}... | collective-permute-start | bytes 933896 | tf_op jit(solution)/shard_map/ppermute | solution.py:365
  156.7 31.7 %collective-permute-start.18 = (bf16[304,512]{1,0:T(8,128)(2,1)S(1)}, bf16[304,512]{1,0:T(8,128)(2,1)S(1)}, u32[]{:S(2)}, u32[]{:S(2)}) collective-permute-start(bf16[304,512]{1,0:T(8,128)(2,1)S(1)} %slice.9), channel_id=1, source_target_pairs={{0,96},{32,0},{64,32},{96,64},{1,97},{33,1},{65,33},{97,65},{2,98}... | collective-permute-start | bytes 933896 | tf_op jit(solution)/shard_map/ppermute | solution.py:365
  160.3 0.8 copy-start.10
  188.4 0.7 copy-start.11
  189.1 0.7 copy-start.12
Sparse Core Ops, SparseCore 0:
  108.5 69.3 all-gather.4
  179.6 30.8 all-gather.6

commit v7 on v6

--- a/solution.py
+++ b/solution.py
@@ -17,7 +17,7 @@
 NS = 5
 GB = 608
 VP = 2432
-CUTS = ((0, 2), (2, 1), (3, 1))
+CUTS = ((0, 1), (1, 1), (2, 1), (3, 1))
 T = 512
 D = 4096
 DX = 1024
@@ -404,8 +404,8 @@
     others = [shift(to_right, 1), shift(to_left, 3), hop(after(hop(to_far), share))]
 
     w = row_weight.reshape(1, T)
-    gu, kl = grad(gathered, after(w, *others), s, t, CUTS[:1])
-    gm, gl, _ = grad(gathered, after(w, gu), s, t, CUTS[1:])
+    g0, kl = grad(gathered, after(w, *others), s, t, CUTS[:1])
+    g1, g2, g3, _ = grad(gathered, after(w, g0), s, t, CUTS[1:])
 
     def near(g):
         return [g, shift(g, 1), shift(g, 3)]
@@ -415,18 +415,21 @@
         left, right = after(parts[1], *first), after(parts[2], *first)
         return [shift(left[:half], 1), shift(right[half:], 3)]
 
-    all_u, all_m = lax.all_gather(gu, "x"), lax.all_gather(gm, "x")
-    near_l = near(gl)
-    far_l = far(near_l)
-    mine, other = hidden_part(pos, (gu, gm, gl), wt)
-    k = tokens(after(pos, mine), h, [x for other in others for x in (other, swap(other))])
-    both = (mine.astype(F32) + swap(after(other, *near_l[1:])).astype(F32)).astype(BF16)
+    all0, all1 = lax.all_gather(g0, "x"), lax.all_gather(g1, "x")
+    near2 = near(g2)
+    near3 = near(after(g3, *near2[1:]))
+    mine, other = hidden_part(pos, (g0, g1, g2, g3), wt)
+    others = [x for other in others for x in (other, swap(after(other, gathered)))]
+    k = tokens(after(pos, mine), h, others)
+    both = (mine.astype(F32) + swap(after(other, k, *near2[1:])).astype(F32)).astype(BF16)
     got = lax.all_to_all(both.reshape(16, T, 128), ("y", "z"), 0, 0, tiled=True)
 
-    head = head_all(pos, all_u, k, *CUTS[0])
-    head = head_piece(near_l, far_l, k, *CUTS[2], other=head)
+    head = head_all(pos, all0, k, *CUTS[0])
+    far2, far3 = far(near2, head), far(near3, head)
+    head = head_piece(near2, far2, k, *CUTS[2], other=head)
+    head = head_piece(near3, far3, k, *CUTS[3], other=head)
     grad_hidden = jnp.sum(after(got, head).astype(F32), axis=0).astype(BF16)
-    head = head_all(pos, all_m, k, *CUTS[1], other=head)
+    head = head_all(pos, all1, k, *CUTS[1], other=head)
     return kl.reshape(T), grad_hidden, head.T
 
 

time: 226 us -> 238 us (1.053)
  Pallas kernels: 89.2 us -> 93.8 us
  starting transfers between devices: 43.3 us -> 47.3 us
    ppermute x6 -> x10, waiting for transfers between devices: 8.46 us -> 35 us  [shift(): return lax.ppermute(x, 'x', [(i, (i + n) % 4) for i in range(4)])]
    all_gather x2, waiting for transfers between devices: 25.1 us -> 0.01 us  [per_device(): all0, all1 = (lax.all_gather(g0, 'x'), lax.all_gather(g1, 'x'))]
    pallas_call x1 -> x2, Pallas kernels: 6.69 us -> 13.4 us  [head_piece(): call(functools.partial(head_body, bool(near), bool(far), prior is not Non...]
    ppermute x6 -> x10, starting transfers between devices: 9.07 us -> 13.1 us  [shift(): return lax.ppermute(x, 'x', [(i, (i + n) % 4) for i in range(4)])]
    pallas_call x2, Pallas kernels: 17.7 us -> 14.9 us  [head_all(): call(head_all_body, out_shape=jax.ShapeDtypeStruct((VL, DX), BF16), grid_...]
    unnamed x28 -> x30, local copies, waits for them, and re-layouts: 5.42 us -> 4.51 us
  transfers between devices with their start and end apart: 27 -> 31, of which waited for: 16 -> 16; matrix products, arithmetic and copies ran while one was open for 2% -> 3% of each run, Pallas kernels for 34% -> 35%
where the time goes in v7:
time: 238 us; the launch traced here: 237 us
  Pallas kernels  93.8 us (39%)
  waiting for transfers between devices  69.1 us (29%)
  starting transfers between devices  47.3 us (20%)
  between operations  14.2 us (6%)
  local copies, waits for them, and re-layouts  7.5 us (3%)
  other arithmetic  5.19 us (2%)
    ppermute x10, waiting for transfers between devices, shift(): return lax.ppermute(x, 'x', [(i, (i + n) % 4) for i in range(4)])  35 us
    pallas_call x1, Pallas kernels, student(): call(student_body, out_shape=[jax.ShapeDtypeStruct((NS * SB, T), F32), pa...  20.5 us
    pallas_call x1, Pallas kernels, hidden_part(): call(hidden_body, out_shape=[jax.ShapeDtypeStruct((4, 4, T, 128), BF16)]...  17.1 us
    pallas_call x2, Pallas kernels, head_all(): call(head_all_body, out_shape=jax.ShapeDtypeStruct((VL, DX), BF16), grid_...  14.9 us
    ppermute x6, waiting for transfers between devices, spread(): got.append(lax.ppermute(x, V, pairs))  13.6 us
    pallas_call x2, Pallas kernels, head_piece(): call(functools.partial(head_body, bool(near), bool(far), prior is not Non...  13.4 us
    ppermute x10, starting transfers between devices, shift(): return lax.ppermute(x, 'x', [(i, (i + n) % 4) for i in range(4)])  13.1 us
    pallas_call x2, Pallas kernels, grad(): call(functools.partial(grad_body, cuts), out_shape=[jax.ShapeDtypeStruct(...  10.2 us
  transfers between devices with their start and end apart: 31, of which 16 were waited for; matrix products, arithmetic and copies ran while one was open for 3% of the time, Pallas kernels for 35%

profile of v7, /device:TPU:1, one launch (start us, length us, event | category | flops | bytes accessed | tf_op | source)
XLA Modules:
  0.0 237.2 jit_solution(5918872853871689111)
XLA Ops:
  7.2 3.6 %collective-permute-start.2 = (bf16[512,128]{1,0:T(8,128)(2,1)}, bf16[512,128]{1,0:T(8,128)(2,1)S(1)}, u32[]{:S(2)}, u32[]{:S(2)}) collective-permute-start(bf16[512,128]{1,0:T(8,128)(2,1)} %param.4), channel_id=1, source_target_pairs={{0,6},{1,25},{2,0},{3,27},{4,2},{5,29},{6,4},{7,31},{8,14},{9,1},{... | collective-permute-start | bytes 393224 | tf_op jit(solution)/shard_map/ppermute | solution.py:385
  11.8 4.4 %shard_map.67 = bf16[32,19,16,128]{3,2,1,0:T(8,128)(2,1)} custom-call(bf16[16,75968]{1,0:T(8,128)(2,1)} %t_ref.1), custom_call_target="tpu_custom_call" | custom-call | flops 1048576 | bytes 65536 | tf_op jit(solution)/shard_map/pallas_call | solution.py:55
  16.4 1.6 collective-permute-done
  18.1 1.4 collective-permute-start.3
  19.5 3.3 %collective-permute-start.4 = (bf16[4,512,128]{2,1,0:T(8,128)(2,1)S(1)}, bf16[4,512,128]{2,1,0:T(8,128)(2,1)}, u32[]{:S(2)}, u32[]{:S(2)}) collective-permute-start(bf16[4,512,128]{2,1,0:T(8,128)(2,1)S(1)} %pad_maximum_fusion.refs_0_), channel_id=1, source_target_pairs={{0,16},{1,5},{2,18},{3,7},{4,20},{5,1},{6,22},{7,3},{8,24},{9,13},... | collective-permute-start | bytes 1572872 | tf_op jit(solution)/shard_map/ppermute | solution.py:385
  23.6 5.0 %collective-permute-done.3.refs_1_ = bf16[4,512,128]{2,1,0:T(8,128)(2,1)S(1)} collective-permute-done((bf16[4,512,128]{2,1,0:T(8,128)(2,1)S(1)}, bf16[4,512,128]{2,1,0:T(8,128)(2,1)S(1)}, u32[]{:S(2)}, u32[]{:S(2)}) %collective-permute-start.3) | collective-permute-done | bytes 524320 | tf_op jit(solution)/shard_map/ppermute | solution.py:385
  28.5 6.9 %collective-permute-done.4.refs_2_ = bf16[4,512,128]{2,1,0:T(8,128)(2,1)} collective-permute-done((bf16[4,512,128]{2,1,0:T(8,128)(2,1)S(1)}, bf16[4,512,128]{2,1,0:T(8,128)(2,1)}, u32[]{:S(2)}, u32[]{:S(2)}) %collective-permute-start.4) | collective-permute-done | bytes 524320 | tf_op jit(solution)/shard_map/ppermute | solution.py:385
  35.4 7.3 %all-to-all-start = ((bf16[32,19,16,128]{3,2,1,0:T(8,128)(2,1)}), bf16[32,19,16,128]{3,2,1,0:T(8,128)(2,1)S(1)}, u32[]{:S(2)}, u32[]{:S(2)}) async-start(bf16[32,19,16,128]{3,2,1,0:T(8,128)(2,1)} %shard_map.67), calls=%async_computation | async-start | bytes 4980736 | tf_op jit(solution)/shard_map/all_to_all | solution.py:399
  44.9 1.5 collective-permute-done.7.refs_5_
  46.6 0.8 collective-permute-done.9.refs_7_
  47.3 20.5 %shard_map.68 = (f32[2560,512]{1,0:T(8,128)}, f32[8,512]{1,0:T(8,128)}, f32[8,512]{1,0:T(8,128)}, bf16[512,1024]{1,0:T(8,128)(2,1)}, bf16[4,512,128]{2,1,0:T(8,1...) custom-call(s32[4]{0:T(128)} %pad_add_fusion.pos, bf16[2374,4096]{1,0:T(8,128)(2,1)} %bitcast.16, ...), custom_call_target="tpu_custom_call" | custom-call | flops 1048576 | bytes 65536 | tf_op jit(solution)/shard_map/pallas_call | solution.py:103
  67.8 2.5 %collective-permute-start.12 = (bf16[4,512,128]{2,1,0:T(8,128)(2,1)}, bf16[4,512,128]{2,1,0:T(8,128)(2,1)}, u32[]{:S(2)}, u32[]{:S(2)}) collective-permute-start(bf16[4,512,128]{2,1,0:T(8,128)(2,1)} %get-tuple-element.43), channel_id=1, source_target_pairs={{0,32},{1,97},{32,64},{33,1},{64,96},{65,33},{96,0},{97,65},{2,34}... | collective-permute-start | bytes 1572872 | tf_op jit(solution)/shard_map/ppermute | solution.py:369
  70.4 2.7 %collective-permute-start.11 = (bf16[4,512,128]{2,1,0:T(8,128)(2,1)}, bf16[4,512,128]{2,1,0:T(8,128)(2,1)S(1)}, u32[]{:S(2)}, u32[]{:S(2)}) collective-permute-start(bf16[4,512,128]{2,1,0:T(8,128)(2,1)} %get-tuple-element.42), channel_id=1, source_target_pairs={{0,96},{32,0},{64,32},{96,64},{1,97},{33,1},{65,33},{97,65},{2,98}... | collective-permute-start | bytes 1572872 | tf_op jit(solution)/shard_map/ppermute | solution.py:365
  73.1 2.2 all-to-all-done.t_ref
  75.3 1.5 copy-done
  76.7 7.3 %shard_map.69 = (bf16[2560,512]{1,0:T(8,128)(2,1)}, f32[32,8,512]{2,1,0:T(8,128)}) custom-call(f32[8,512]{1,0:T(8,128)} %get-tuple-element.36.m_ref, f32[8,512]{1,0:T(8,128)} %get-tuple-element.37.l_ref, f32[2560,512]{1,0:T(8,128)} %get-tuple-element.38.s_ref, bf16[32,19,16,128]{3,2,1,0:T(8,128)(2,1)} %copy-done), custom_call_target="tpu_custom_call" | custom-call | flops 1048576 | bytes 65536 | tf_op jit(solution)/shard_map/pallas_call | solution.py:172
  84.0 2.5 %collective-permute-start.13 = (bf16[4,512,128]{2,1,0:T(8,128)(2,1)}, bf16[4,512,128]{2,1,0:T(8,128)(2,1)S(1)}, u32[]{:S(2)}, u32[]{:S(2)}) collective-permute-start(bf16[4,512,128]{2,1,0:T(8,128)(2,1)} %collective-permute-done.12), channel_id=1, source_target_pairs={{0,32},{1,97},{32,64},{33,1},{64,96},{65,33},{96,0},{97,65},{2,34}... | collective-permute-start | bytes 1572872 | tf_op jit(solution)/shard_map/ppermute | solution.py:369
  86.6 4.9 %all-to-all-start.1 = ((f32[32,8,512]{2,1,0:T(8,128)}), f32[32,8,512]{2,1,0:T(8,128)S(1)}, u32[]{:S(2)}, u32[]{:S(2)}) async-start(f32[32,8,512]{2,1,0:T(8,128)} %get-tuple-element.40), calls=%async_computation.1 | async-start | bytes 1048576 | tf_op jit(solution)/shard_map/all_to_all | solution.py:402
  91.8 1.9 collective-permute-done.13.refs_4_
  93.7 9.5 %all-to-all-done.1.all_ref = f32[32,8,512]{2,1,0:T(8,128)S(1)} async-done(((f32[32,8,512]{2,1,0:T(8,128)}), f32[32,8,512]{2,1,0:T(8,128)S(1)}, u32[]{:S(2)}, u32[]{:S(2)}) %all-to-all-start.1) | async-done | bytes 524320 | tf_op jit(solution)/shard_map/all_to_all | solution.py:402
  103.1 0.8 copy-done.1
  103.9 3.7 %shard_map.70 = (bf16[608,512]{1,0:T(8,128)(2,1)}, f32[1,512]{1,0:T(1,128)}) custom-call(f32[32,8,512]{2,1,0:T(8,128)} %copy-done.1, f32[1,512]{1,0:T(1,128)} %bitcast.30, f32[2560,512]{1,0:T(8,128)} %get-tuple-element.38.s_ref, bf16[2560,512]{1,0:T(8,128)(2,1)} %get-tuple-element.46.t_ref), custom_call_target="tpu_custom_call" | custom-call | flops 1048576 | bytes 65536 | tf_op jit(solution)/shard_map/pallas_call | solution.py:222
  107.7 6.5 %shard_map.71 = (bf16[608,512]{1,0:T(8,128)(2,1)}, bf16[608,512]{1,0:T(8,128)(2,1)}, bf16[608,512]{1,0:T(8,128)(2,1)}, f32[1,512]{1,0:T(1,128)}) custom-call(f32[32,8,512]{2,1,0:T(8,128)} %copy-done.1, f32[1,512]{1,0:T(1,128)} %bitcast.31, f32[2560,512]{1,0:T(8,128)} %get-tuple-element.38.s_ref, bf16[2560,512]{1,0:T(8,128)(2,1)} %get-tuple-element.46.t_ref), custom_call_target="tpu_custom_call" | custom-call | flops 1048576 | bytes 65536 | tf_op jit(solution)/shard_map/pallas_call | solution.py:222
  114.2 1.1 collective-permute-start.17
  115.3 1.6 collective-permute-start.18
  117.8 17.1 %shard_map.72 = (bf16[4,4,512,128]{3,2,1,0:T(8,128)(2,1)}, bf16[4,4,512,128]{3,2,1,0:T(8,128)(2,1)}) custom-call(s32[4]{0:T(128)} %pad_add_fusion.pos, bf16[608,512]{1,0:T(8,128)(2,1)} %get-tuple-element.48.refs_0_, bf16[608,512]{1,0:T(8,128)(2,1)} %get-tuple-element.50.refs_1_, bf16[608,512]{1,0:T(8,128)(2,1)} %get-tuple-element.51.refs_2_.refs_0_, ...), custom_call_target="tpu_custom_call" | custom-call | flops 1048576 | bytes 65536 | tf_op jit(solution)/shard_map/pallas_call | solution.py:256
  134.9 0.8 copy-done.11
  135.7 5.9 %shard_map.73.refs_4_.refs_5_ = bf16[2048,1024]{1,0:T(8,128)(2,1)} custom-call(s32[4]{0:T(128)} %pad_add_fusion.pos, bf16[512,1024]{1,0:T(8,128)(2,1)} %get-tuple-element.56.h_ref, bf16[4,512,128]{2,1,0:T(8,128)(2,1)} %copy-done.7, bf16[4,512,128]{2,1,0:T(8,128)(2,1)} %copy-done.11, bf16[4,512,128]{2,1,0:T(8,128)(2,1)} %copy-done.8, ...), custom_call_target="tpu_custom_call" | custom-call | flops 1048576 | bytes 65536 | tf_op jit(solution)/shard_map/pallas_call | solution.py:280
  141.6 2.7 %collective-permute-done.17.refs_1_ = bf16[608,512]{1,0:T(8,128)(2,1)S(1)} collective-permute-done((bf16[608,512]{1,0:T(8,128)(2,1)}, bf16[608,512]{1,0:T(8,128)(2,1)S(1)}, u32[]{:S(2)}, u32[]{:S(2)}) %collective-permute-start.17) | collective-permute-done | bytes 622624 | tf_op jit(solution)/shard_map/ppermute | solution.py:365
  144.7 0.7 collective-permute-start.19
  145.5 4.1 %collective-permute-done.19 = bf16[4,4,512,128]{3,2,1,0:T(8,128)(2,1)} collective-permute-done((bf16[4,4,512,128]{3,2,1,0:T(8,128)(2,1)}, bf16[4,4,512,128]{3,2,1,0:T(8,128)(2,1)}, u32[]{:S(2)}, u32[]{:S(2)}) %collective-permute-start.19) | collective-permute-done | bytes 2097184 | tf_op jit(solution)/shard_map/ppermute | solution.py:373
  149.6 3.5 %add_convert_fusion = bf16[4,4,512,128]{3,2,1,0:T(8,128)(2,1)} fusion(bf16[4,4,512,128]{3,2,1,0:T(8,128)(2,1)} %collective-permute-done.19, bf16[4,4,512,128]{3,2,1,0:T(8,128)(2,1)S(1)} %copy-done.3), kind=kLoop, calls=%fused_computation | loop fusion | flops 4194304 | bytes 6291456 | tf_op jit(solution)/shard_map/convert_element_type | solution.py:424
  153.1 3.8 %all-to-all-start.2 = ((bf16[16,512,128]{2,1,0:T(8,128)(2,1)}), bf16[16,512,128]{2,1,0:T(8,128)(2,1)S(1)}, u32[]{:S(2)}, u32[]{:S(2)}) async-start(bf16[16,512,128]{2,1,0:T(8,128)(2,1)} %bitcast.11), calls=%async_computation.2 | async-start | bytes 4194304 | tf_op jit(solution)/shard_map/all_to_all | solution.py:425
  157.0 1.0 collective-permute-start.20
  158.0 2.1 collective-permute-start.21
  160.1 7.6 %shard_map.74.refs_6_ = bf16[2374,1024]{1,0:T(8,128)(2,1)} custom-call(s32[4]{0:T(128)} %pad_add_fusion.pos, bf16[4,608,512]{2,1,0:T(8,128)(2,1)} %bitcast.18, bf16[4,608,512]{2,1,0:T(8,128)(2,1)} %bitcast.19, bf16[4,608,512]{2,1,0:T(8,128)(2,1)} %bitcast.20, bf16[4,608,512]{2,1,0:T(8,128)(2,1)} %bitcast.21, bf16[2048,1024]{1,0:T(8,128)(2,1)} %shard_map.73.refs_4_.refs_5_), custom_call_target="tpu_custom_call" | custom-call | flops 1048576 | bytes 65536 | tf_op jit(solution)/shard_map/pallas_call | solution.py:351
  167.7 15.5 %collective-permute-done.20.refs_1_ = bf16[608,512]{1,0:T(8,128)(2,1)} collective-permute-done((bf16[608,512]{1,0:T(8,128)(2,1)S(1)}, bf16[608,512]{1,0:T(8,128)(2,1)}, u32[]{:S(2)}, u32[]{:S(2)}) %collective-permute-start.20) | collective-permute-done | bytes 622624 | tf_op jit(solution)/shard_map/ppermute | solution.py:365
  183.1 1.0 slice.12
  184.6 1.0 slice.15
  185.5 2.5 %collective-permute-start.25 = (bf16[304,512]{1,0:T(8,128)(2,1)S(1)}, bf16[304,512]{1,0:T(8,128)(2,1)}, u32[]{:S(2)}, u32[]{:S(2)}) collective-permute-start(bf16[304,512]{1,0:T(8,128)(2,1)S(1)} %slice.15), channel_id=1, source_target_pairs={{0,96},{32,0},{64,32},{96,64},{1,97},{33,1},{65,33},{97,65},{2,98}... | collective-permute-start | bytes 933896 | tf_op jit(solution)/shard_map/ppermute | solution.py:365
  188.1 1.0 slice.13
  189.1 1.7 collective-permute-start.23
  190.8 16.4 %collective-permute-done.24.refs_3_ = bf16[304,512]{1,0:T(8,128)(2,1)S(1)} collective-permute-done((bf16[304,512]{1,0:T(8,128)(2,1)S(1)}, bf16[304,512]{1,0:T(8,128)(2,1)S(1)}, u32[]{:S(2)}, u32[]{:S(2)}) %collective-permute-start.24) | collective-permute-done | bytes 311328 | tf_op jit(solution)/shard_map/ppermute | solution.py:365
  207.9 6.7 %shard_map.75.refs_6_ = bf16[2374,1024]{1,0:T(8,128)(2,1)} custom-call(bf16[608,512]{1,0:T(8,128)(2,1)} %get-tuple-element.51.refs_2_.refs_0_, bf16[608,512]{1,0:T(8,128)(2,1)} %copy-done.5, bf16[608,512]{1,0:T(8,128)(2,1)} %copy-done.6, bf16[304,512]{1,0:T(8,128)(2,1)} %copy-done.13, ...), custom_call_target="tpu_custom_call", output_to_operand_aliasing={{}: (6, {})} | custom-call | flops 1048576 | bytes 65536 | tf_op jit(solution)/shard_map/pallas_call | solution.py:324
  214.6 0.7 copy-done.12
  215.4 6.7 %shard_map.76.refs_5_ = bf16[2374,1024]{1,0:T(8,128)(2,1)} custom-call(bf16[608,512]{1,0:T(8,128)(2,1)} %get-tuple-element.61.refs_3_.refs_0_, bf16[608,512]{1,0:T(8,128)(2,1)} %collective-permute-done.20.refs_1_, bf16[608,512]{1,0:T(8,128)(2,1)} %collective-permute-done.21.refs_2_, ...), custom_call_target="tpu_custom_call", output_to_operand_aliasing={{}: (6, {})} | custom-call | flops 1048576 | bytes 65536 | tf_op jit(solution)/shard_map/pallas_call | solution.py:324
  222.1 7.3 %shard_map.77 = bf16[2374,1024]{1,0:T(8,128)(2,1)} custom-call(s32[4]{0:T(128)} %pad_add_fusion.pos, bf16[4,608,512]{2,1,0:T(8,128)(2,1)} %bitcast.22, bf16[4,608,512]{2,1,0:T(8,128)(2,1)} %bitcast.23, bf16[4,608,512]{2,1,0:T(8,128)(2,1)} %bitcast.24, bf16[4,608,512]{2,1,0:T(8,128)(2,1)} %bitcast.25, ...), custom_call_target="tpu_custom_call", output_to_operand_aliasing={{}: (6, {})} | custom-call | flops 1048576 | bytes 65536 | tf_op jit(solution)/shard_map/pallas_call | solution.py:351
  229.4 1.0 reduce_sum.12
  (65 shorter events, 7.1 us)
Async XLA Ops:
  7.2 10.9 %copy-start.14 = (bf16[512,128]{1,0:T(8,128)(2,1)S(1)}, bf16[512,128]{1,0:T(8,128)(2,1)}, u32[]{:S(2)}) copy-start(bf16[512,128]{1,0:T(8,128)(2,1)} %param.4) | copy-start | bytes 393220
  7.2 9.1 %collective-permute-start.2 = (bf16[512,128]{1,0:T(8,128)(2,1)}, bf16[512,128]{1,0:T(8,128)(2,1)S(1)}, u32[]{:S(2)}, u32[]{:S(2)}) collective-permute-start(bf16[512,128]{1,0:T(8,128)(2,1)} %param.4), channel_id=1, source_target_pairs={{0,6},{1,25},{2,0},{3,27},{4,2},{5,29},{6,4},{7,31},{8,14},{9,1},{... | collective-permute-start | bytes 393224 | tf_op jit(solution)/shard_map/ppermute | solution.py:385
  10.8 5.6 %collective-permute-start.1 = (bf16[512,128]{1,0:T(8,128)(2,1)}, bf16[512,128]{1,0:T(8,128)(2,1)S(1)}, u32[]{:S(2)}, u32[]{:S(2)}) collective-permute-start(bf16[512,128]{1,0:T(8,128)(2,1)} %param.4), channel_id=1, source_target_pairs={{0,4},{1,17},{2,6},{3,19},{4,0},{5,21},{6,2},{7,23},{8,12},{9,25},... | collective-permute-start | bytes 393224 | tf_op jit(solution)/shard_map/ppermute | solution.py:385
  11.2 6.9 %collective-permute-start = (bf16[512,128]{1,0:T(8,128)(2,1)}, bf16[512,128]{1,0:T(8,128)(2,1)S(1)}, u32[]{:S(2)}, u32[]{:S(2)}) collective-permute-start(bf16[512,128]{1,0:T(8,128)(2,1)} %param.4), channel_id=1, source_target_pairs={{0,2},{1,9},{2,4},{3,11},{4,6},{5,13},{6,0},{7,15},{8,10},{9,17},{... | collective-permute-start | bytes 393224 | tf_op jit(solution)/shard_map/ppermute | solution.py:385
  18.1 24.6 %copy-start.4 = (bf16[4,512,128]{2,1,0:T(8,128)(2,1)}, bf16[4,512,128]{2,1,0:T(8,128)(2,1)S(1)}, u32[]{:S(2)}) copy-start(bf16[4,512,128]{2,1,0:T(8,128)(2,1)S(1)} %pad_maximum_fusion.refs_0_) | copy-start | bytes 1572868
  18.1 10.4 %collective-permute-start.3 = (bf16[4,512,128]{2,1,0:T(8,128)(2,1)S(1)}, bf16[4,512,128]{2,1,0:T(8,128)(2,1)S(1)}, u32[]{:S(2)}, u32[]{:S(2)}) collective-permute-start(bf16[4,512,128]{2,1,0:T(8,128)(2,1)S(1)} %pad_maximum_fusion.refs_0_), channel_id=1, source_target_pairs={{0,8},{1,3},{2,10},{3,5},{4,12},{5,7},{6,14},{7,1},{8,16},{9,11},{... | collective-permute-start | bytes 1572872 | tf_op jit(solution)/shard_map/ppermute | solution.py:385
  19.5 15.9 %collective-permute-start.4 = (bf16[4,512,128]{2,1,0:T(8,128)(2,1)S(1)}, bf16[4,512,128]{2,1,0:T(8,128)(2,1)}, u32[]{:S(2)}, u32[]{:S(2)}) collective-permute-start(bf16[4,512,128]{2,1,0:T(8,128)(2,1)S(1)} %pad_maximum_fusion.refs_0_), channel_id=1, source_target_pairs={{0,16},{1,5},{2,18},{3,7},{4,20},{5,1},{6,22},{7,3},{8,24},{9,13},... | collective-permute-start | bytes 1572872 | tf_op jit(solution)/shard_map/ppermute | solution.py:385
  22.8 12.6 %collective-permute-start.5 = (bf16[4,512,128]{2,1,0:T(8,128)(2,1)S(1)}, bf16[4,512,128]{2,1,0:T(8,128)(2,1)}, u32[]{:S(2)}, u32[]{:S(2)}) collective-permute-start(bf16[4,512,128]{2,1,0:T(8,128)(2,1)S(1)} %pad_maximum_fusion.refs_0_), channel_id=1, source_target_pairs={{0,24},{1,7},{2,26},{3,1},{4,28},{5,3},{6,30},{7,5},{8,0},{9,15},{... | collective-permute-start | bytes 1572872 | tf_op jit(solution)/shard_map/ppermute | solution.py:385
  28.5 14.5 %copy-start.9 = (bf16[4,512,128]{2,1,0:T(8,128)(2,1)}, bf16[4,512,128]{2,1,0:T(8,128)(2,1)S(1)}, u32[]{:S(2)}) copy-start(bf16[4,512,128]{2,1,0:T(8,128)(2,1)S(1)} %collective-permute-done.3.refs_1_) | copy-start | bytes 1572868
  35.4 39.8 %all-to-all-start = ((bf16[32,19,16,128]{3,2,1,0:T(8,128)(2,1)}), bf16[32,19,16,128]{3,2,1,0:T(8,128)(2,1)S(1)}, u32[]{:S(2)}, u32[]{:S(2)}) async-start(bf16[32,19,16,128]{3,2,1,0:T(8,128)(2,1)} %shard_map.67), calls=%async_computation | async-start | bytes 4980736 | tf_op jit(solution)/shard_map/all_to_all | solution.py:399
  42.7 2.1 collective-permute-start.6
  43.1 3.3 %collective-permute-start.7 = (bf16[4,512,128]{2,1,0:T(8,128)(2,1)S(1)}, bf16[4,512,128]{2,1,0:T(8,128)(2,1)}, u32[]{:S(2)}, u32[]{:S(2)}) collective-permute-start(bf16[4,512,128]{2,1,0:T(8,128)(2,1)S(1)} %collective-permute-done.3.refs_1_), channel_id=1, source_target_pairs={{0,1},{1,0},{2,3},{3,2},{4,5},{5,4},{6,7},{7,6},{8,9},{9,8},{10,11... | collective-permute-start | bytes 1572872 | tf_op jit(solution)/shard_map/ppermute | solution.py:373
  43.3 3.2 %collective-permute-start.8 = (bf16[4,512,128]{2,1,0:T(8,128)(2,1)}, bf16[4,512,128]{2,1,0:T(8,128)(2,1)}, u32[]{:S(2)}, u32[]{:S(2)}) collective-permute-start(bf16[4,512,128]{2,1,0:T(8,128)(2,1)} %collective-permute-done.4.refs_2_), channel_id=1, source_target_pairs={{0,1},{1,0},{2,3},{3,2},{4,5},{5,4},{6,7},{7,6},{8,9},{9,8},{10,11... | collective-permute-start | bytes 1572872 | tf_op jit(solution)/shard_map/ppermute | solution.py:373
  43.6 3.8 %collective-permute-start.9 = (bf16[4,512,128]{2,1,0:T(8,128)(2,1)}, bf16[4,512,128]{2,1,0:T(8,128)(2,1)}, u32[]{:S(2)}, u32[]{:S(2)}) collective-permute-start(bf16[4,512,128]{2,1,0:T(8,128)(2,1)} %collective-permute-done.5.refs_3_), channel_id=1, source_target_pairs={{0,1},{1,0},{2,3},{3,2},{4,5},{5,4},{6,7},{7,6},{8,9},{9,8},{10,11... | collective-permute-start | bytes 1572872 | tf_op jit(solution)/shard_map/ppermute | solution.py:373
  67.8 16.2 %collective-permute-start.12 = (bf16[4,512,128]{2,1,0:T(8,128)(2,1)}, bf16[4,512,128]{2,1,0:T(8,128)(2,1)}, u32[]{:S(2)}, u32[]{:S(2)}) collective-permute-start(bf16[4,512,128]{2,1,0:T(8,128)(2,1)} %get-tuple-element.43), channel_id=1, source_target_pairs={{0,32},{1,97},{32,64},{33,1},{64,96},{65,33},{96,0},{97,65},{2,34}... | collective-permute-start | bytes 1572872 | tf_op jit(solution)/shard_map/ppermute | solution.py:369
  70.4 21.4 %collective-permute-start.10 = (bf16[4,512,128]{2,1,0:T(8,128)(2,1)}, bf16[4,512,128]{2,1,0:T(8,128)(2,1)S(1)}, u32[]{:S(2)}, u32[]{:S(2)}) collective-permute-start(bf16[4,512,128]{2,1,0:T(8,128)(2,1)} %get-tuple-element.41), channel_id=1, source_target_pairs={{0,32},{32,64},{64,96},{96,0},{1,33},{33,65},{65,97},{97,1},{2,34}... | collective-permute-start | bytes 1572872 | tf_op jit(solution)/shard_map/ppermute | solution.py:365
  70.4 21.4 %collective-permute-start.11 = (bf16[4,512,128]{2,1,0:T(8,128)(2,1)}, bf16[4,512,128]{2,1,0:T(8,128)(2,1)S(1)}, u32[]{:S(2)}, u32[]{:S(2)}) collective-permute-start(bf16[4,512,128]{2,1,0:T(8,128)(2,1)} %get-tuple-element.42), channel_id=1, source_target_pairs={{0,96},{32,0},{64,32},{96,64},{1,97},{33,1},{65,33},{97,65},{2,98}... | collective-permute-start | bytes 1572872 | tf_op jit(solution)/shard_map/ppermute | solution.py:365
  75.3 1.5 copy-start
  84.0 9.7 %collective-permute-start.13 = (bf16[4,512,128]{2,1,0:T(8,128)(2,1)}, bf16[4,512,128]{2,1,0:T(8,128)(2,1)S(1)}, u32[]{:S(2)}, u32[]{:S(2)}) collective-permute-start(bf16[4,512,128]{2,1,0:T(8,128)(2,1)} %collective-permute-done.12), channel_id=1, source_target_pairs={{0,32},{1,97},{32,64},{33,1},{64,96},{65,33},{96,0},{97,65},{2,34}... | collective-permute-start | bytes 1572872 | tf_op jit(solution)/shard_map/ppermute | solution.py:369
  86.6 16.6 %all-to-all-start.1 = ((f32[32,8,512]{2,1,0:T(8,128)}), f32[32,8,512]{2,1,0:T(8,128)S(1)}, u32[]{:S(2)}, u32[]{:S(2)}) async-start(f32[32,8,512]{2,1,0:T(8,128)} %get-tuple-element.40), calls=%async_computation.1 | async-start | bytes 1048576 | tf_op jit(solution)/shard_map/all_to_all | solution.py:402
  91.5 68.6 %all-gather.5.cloned.1.call-start = ((), (), s32[]{:S(2)}) async-start(), calls=%async_computation.3 | async-start | bytes 3112960 | tf_op jit(solution)/shard_map/all_gather | solution.py:418
  91.8 25.2 %copy-start.7 = (bf16[4,512,128]{2,1,0:T(8,128)(2,1)}, bf16[4,512,128]{2,1,0:T(8,128)(2,1)S(1)}, u32[]{:S(2)}) copy-start(bf16[4,512,128]{2,1,0:T(8,128)(2,1)S(1)} %collective-permute-done.10.refs_0_) | copy-start | bytes 1572868
  91.8 25.5 %copy-start.8 = (bf16[4,512,128]{2,1,0:T(8,128)(2,1)}, bf16[4,512,128]{2,1,0:T(8,128)(2,1)S(1)}, u32[]{:S(2)}) copy-start(bf16[4,512,128]{2,1,0:T(8,128)(2,1)S(1)} %collective-permute-done.11.refs_2_) | copy-start | bytes 1572868
  93.7 23.8 %copy-start.10 = (bf16[4,512,128]{2,1,0:T(8,128)(2,1)}, bf16[4,512,128]{2,1,0:T(8,128)(2,1)S(1)}, u32[]{:S(2)}) copy-start(bf16[4,512,128]{2,1,0:T(8,128)(2,1)S(1)} %collective-permute-done.13.refs_4_) | copy-start | bytes 1572868
  103.1 0.8 copy-start.1
  107.7 114.4 %all-gather.7.cloned.1.call-start = ((), (), s32[]{:S(2)}) async-start(), calls=%async_computation.4 | async-start | bytes 3112960 | tf_op jit(solution)/shard_map/all_gather | solution.py:418
  114.2 30.1 %collective-permute-start.17 = (bf16[608,512]{1,0:T(8,128)(2,1)}, bf16[608,512]{1,0:T(8,128)(2,1)S(1)}, u32[]{:S(2)}, u32[]{:S(2)}) collective-permute-start(bf16[608,512]{1,0:T(8,128)(2,1)} %get-tuple-element.51.refs_2_.refs_0_), channel_id=1, source_target_pairs={{0,32},{32,64},{64,96},{96,0},{1,33},{33,65},{65,97},{97,1},{2,34}... | collective-permute-start | bytes 1867784 | tf_op jit(solution)/shard_map/ppermute | solution.py:365
  115.3 29.4 %collective-permute-start.18 = (bf16[608,512]{1,0:T(8,128)(2,1)}, bf16[608,512]{1,0:T(8,128)(2,1)S(1)}, u32[]{:S(2)}, u32[]{:S(2)}) collective-permute-start(bf16[608,512]{1,0:T(8,128)(2,1)} %get-tuple-element.51.refs_2_.refs_0_), channel_id=1, source_target_pairs={{0,96},{32,0},{64,32},{96,64},{1,97},{33,1},{65,33},{97,65},{2,98}... | collective-permute-start | bytes 1867784 | tf_op jit(solution)/shard_map/ppermute | solution.py:365
  116.9 18.0 %collective-permute-start.14 = (bf16[4,512,128]{2,1,0:T(8,128)(2,1)S(1)}, bf16[4,512,128]{2,1,0:T(8,128)(2,1)S(1)}, u32[]{:S(2)}, u32[]{:S(2)}) collective-permute-start(bf16[4,512,128]{2,1,0:T(8,128)(2,1)S(1)} %collective-permute-done.10.refs_0_), channel_id=1, source_target_pairs={{0,1},{1,0},{2,3},{3,2},{4,5},{5,4},{6,7},{7,6},{8,9},{9,8},{10,11... | collective-permute-start | bytes 1572872 | tf_op jit(solution)/shard_map/ppermute | solution.py:373
  117.3 17.6 %collective-permute-start.15 = (bf16[4,512,128]{2,1,0:T(8,128)(2,1)S(1)}, bf16[4,512,128]{2,1,0:T(8,128)(2,1)}, u32[]{:S(2)}, u32[]{:S(2)}) collective-permute-start(bf16[4,512,128]{2,1,0:T(8,128)(2,1)S(1)} %collective-permute-done.11.refs_2_), channel_id=1, source_target_pairs={{0,1},{1,0},{2,3},{3,2},{4,5},{5,4},{6,7},{7,6},{8,9},{9,8},{10,11... | collective-permute-start | bytes 1572872 | tf_op jit(solution)/shard_map/ppermute | solution.py:373
  117.4 17.5 %collective-permute-start.16 = (bf16[4,512,128]{2,1,0:T(8,128)(2,1)S(1)}, bf16[4,512,128]{2,1,0:T(8,128)(2,1)}, u32[]{:S(2)}, u32[]{:S(2)}) collective-permute-start(bf16[4,512,128]{2,1,0:T(8,128)(2,1)S(1)} %collective-permute-done.13.refs_4_), channel_id=1, source_target_pairs={{0,1},{1,0},{2,3},{3,2},{4,5},{5,4},{6,7},{7,6},{8,9},{9,8},{10,11... | collective-permute-start | bytes 1572872 | tf_op jit(solution)/shard_map/ppermute | solution.py:373
  134.9 0.8 copy-start.11
  135.7 13.9 %copy-start.3 = (bf16[4,4,512,128]{3,2,1,0:T(8,128)(2,1)S(1)}, bf16[4,4,512,128]{3,2,1,0:T(8,128)(2,1)}, u32[]{:S(2)}) copy-start(bf16[4,4,512,128]{3,2,1,0:T(8,128)(2,1)} %get-tuple-element.53) | copy-start | bytes 6291460
  144.3 39.9 %copy-start.5 = (bf16[608,512]{1,0:T(8,128)(2,1)}, bf16[608,512]{1,0:T(8,128)(2,1)S(1)}, u32[]{:S(2)}) copy-start(bf16[608,512]{1,0:T(8,128)(2,1)S(1)} %collective-permute-done.17.refs_1_) | copy-start | bytes 1867780
  144.7 4.9 %copy-start.6 = (bf16[608,512]{1,0:T(8,128)(2,1)}, bf16[608,512]{1,0:T(8,128)(2,1)S(1)}, u32[]{:S(2)}) copy-start(bf16[608,512]{1,0:T(8,128)(2,1)S(1)} %collective-permute-done.18.refs_2_) | copy-start | bytes 1867780
  144.7 4.9 %collective-permute-start.19 = (bf16[4,4,512,128]{3,2,1,0:T(8,128)(2,1)}, bf16[4,4,512,128]{3,2,1,0:T(8,128)(2,1)}, u32[]{:S(2)}, u32[]{:S(2)}) collective-permute-start(bf16[4,4,512,128]{3,2,1,0:T(8,128)(2,1)} %get-tuple-element.60), channel_id=1, source_target_pairs={{0,1},{1,0},{2,3},{3,2},{4,5},{5,4},{6,7},{7,6},{8,9},{9,8},{10,11... | collective-permute-start | bytes 6291464 | tf_op jit(solution)/shard_map/ppermute | solution.py:373
  153.1 3.9 %copy-start.2 = (bf16[608,512]{1,0:T(8,128)(2,1)S(1)}, bf16[608,512]{1,0:T(8,128)(2,1)}, u32[]{:S(2)}) copy-start(bf16[608,512]{1,0:T(8,128)(2,1)} %get-tuple-element.61.refs_3_.refs_0_) | copy-start | bytes 1867780
  153.1 69.0 %all-to-all-start.2 = ((bf16[16,512,128]{2,1,0:T(8,128)(2,1)}), bf16[16,512,128]{2,1,0:T(8,128)(2,1)S(1)}, u32[]{:S(2)}, u32[]{:S(2)}) async-start(bf16[16,512,128]{2,1,0:T(8,128)(2,1)} %bitcast.11), calls=%async_computation.2 | async-start | bytes 4194304 | tf_op jit(solution)/shard_map/all_to_all | solution.py:425
  157.0 26.2 %collective-permute-start.20 = (bf16[608,512]{1,0:T(8,128)(2,1)S(1)}, bf16[608,512]{1,0:T(8,128)(2,1)}, u32[]{:S(2)}, u32[]{:S(2)}) collective-permute-start(bf16[608,512]{1,0:T(8,128)(2,1)S(1)} %copy-done.2), channel_id=1, source_target_pairs={{0,32},{32,64},{64,96},{96,0},{1,33},{33,65},{65,97},{97,1},{2,34}... | collective-permute-start | bytes 1867784 | tf_op jit(solution)/shard_map/ppermute | solution.py:365
  158.0 30.1 %collective-permute-start.21 = (bf16[608,512]{1,0:T(8,128)(2,1)S(1)}, bf16[608,512]{1,0:T(8,128)(2,1)}, u32[]{:S(2)}, u32[]{:S(2)}) collective-permute-start(bf16[608,512]{1,0:T(8,128)(2,1)S(1)} %copy-done.2), channel_id=1, source_target_pairs={{0,96},{32,0},{64,32},{96,64},{1,97},{33,1},{65,33},{97,65},{2,98}... | collective-permute-start | bytes 1867784 | tf_op jit(solution)/shard_map/ppermute | solution.py:365
  184.1 30.5 %collective-permute-start.22 = (bf16[304,512]{1,0:T(8,128)(2,1)S(1)}, bf16[304,512]{1,0:T(8,128)(2,1)}, u32[]{:S(2)}, u32[]{:S(2)}) collective-permute-start(bf16[304,512]{1,0:T(8,128)(2,1)S(1)} %slice.12), channel_id=1, source_target_pairs={{0,32},{32,64},{64,96},{96,0},{1,33},{33,65},{65,97},{97,1},{2,34}... | collective-permute-start | bytes 933896 | tf_op jit(solution)/shard_map/ppermute | solution.py:365
  184.3 22.9 %collective-permute-start.24 = (bf16[304,512]{1,0:T(8,128)(2,1)S(1)}, bf16[304,512]{1,0:T(8,128)(2,1)S(1)}, u32[]{:S(2)}, u32[]{:S(2)}) collective-permute-start(bf16[304,512]{1,0:T(8,128)(2,1)S(1)} %slice.14), channel_id=1, source_target_pairs={{0,32},{32,64},{64,96},{96,0},{1,33},{33,65},{65,97},{97,1},{2,34}... | collective-permute-start | bytes 933896 | tf_op jit(solution)/shard_map/ppermute | solution.py:365
  185.5 22.3 %collective-permute-start.25 = (bf16[304,512]{1,0:T(8,128)(2,1)S(1)}, bf16[304,512]{1,0:T(8,128)(2,1)}, u32[]{:S(2)}, u32[]{:S(2)}) collective-permute-start(bf16[304,512]{1,0:T(8,128)(2,1)S(1)} %slice.15), channel_id=1, source_target_pairs={{0,96},{32,0},{64,32},{96,64},{1,97},{33,1},{65,33},{97,65},{2,98}... | collective-permute-start | bytes 933896 | tf_op jit(solution)/shard_map/ppermute | solution.py:365
  189.1 25.6 %collective-permute-start.23 = (bf16[304,512]{1,0:T(8,128)(2,1)S(1)}, bf16[304,512]{1,0:T(8,128)(2,1)S(1)}, u32[]{:S(2)}, u32[]{:S(2)}) collective-permute-start(bf16[304,512]{1,0:T(8,128)(2,1)S(1)} %slice.13), channel_id=1, source_target_pairs={{0,96},{32,0},{64,32},{96,64},{1,97},{33,1},{65,33},{97,65},{2,98}... | collective-permute-start | bytes 933896 | tf_op jit(solution)/shard_map/ppermute | solution.py:365
  207.2 0.7 copy-start.13
  214.6 0.7 copy-start.12
Sparse Core Ops, SparseCore 0:
  107.8 44.1 all-gather.4
  153.7 46.9 all-gather.6

commit v8 on v6

--- a/solution.py
+++ b/solution.py
@@ -15,9 +15,9 @@
 KT = 19
 SB = 512
 NS = 5
-GB = 608
+GB = 304
 VP = 2432
-CUTS = ((0, 2), (2, 1), (3, 1))
+CUTS = ((0, 4), (4, 1), (5, 3))
 T = 512
 D = 4096
 DX = 1024
@@ -289,73 +289,37 @@
     )(pos, h, *parts)
 
 
-def head_body(near, far, prior, *refs):
-    refs = list(refs)
-    parts = [refs.pop(0)[...] for _ in range(3)] if near else []
-    if far:
-        far0, far1 = refs.pop(0), refs.pop(0)
-        if far0.shape[0] < GB:
-            parts.append(jnp.concatenate([far0[...], far1[...]], axis=0))
-        else:
-            parts.append(jnp.where(pl.program_id(0) == 0, far0[...], far1[...]))
-    total = jnp.dot(jnp.concatenate(parts, axis=1), refs.pop(0)[...], preferred_element_type=F32)
-    if prior:
-        total = total + refs.pop(0)[...]
-    refs[-1][...] = total.astype(refs[-1].dtype)
-
-
-def head_piece(near, far, k, first, steps, prior=None, other=None):
-    specs = [pl.BlockSpec((GB, T), lambda i: (i, 0))] * len(near) + [whole(g.shape) for g in far]
-    rows = T * (len(near) + len(far) // 2)
-    specs.append(pl.BlockSpec((rows, DX), lambda i: (0 if near else 3, 0)))
-    args = [*near, *far, k]
-    kw = {}
-    if prior is not None:
-        specs.append(pl.BlockSpec((GB, DX), lambda i: (i, 0)))
-        args.append(prior)
-    if other is not None:
-        specs.append(pl.BlockSpec(memory_space=pl.ANY))
-        args.append(other)
-        kw["input_output_aliases"] = {len(args) - 1: 0}
-    if far:
-        out = jax.ShapeDtypeStruct((VL, DX), BF16)
+def head_body(pos, *refs):
+    g = jnp.concatenate([r[...].reshape(-1, T) for r in refs[:4]], axis=1)
+    refs[-1][...] = jnp.dot(g, refs[4][...], preferred_element_type=F32).astype(BF16)
+
+
+def head_rows(pos, gs, k, first, steps, other=None):
+    if len(gs) == 1:
+        rows = GB * 2 if steps % 2 == 0 else GB
+        specs = [
+            pl.BlockSpec((1, rows, T), functools.partial(lambda away, i, p: ((p[0] + away) % 4, i, 0), away))
+            for away in (0, 3, 1, 2)
+        ]
     else:
-        out, first = jax.ShapeDtypeStruct((steps * GB, DX), F32), 0
-    return call(
-        functools.partial(head_body, bool(near), bool(far), prior is not None),
-        out_shape=out,
-        grid=(steps,),
-        in_specs=specs,
-        out_specs=pl.BlockSpec((GB, DX), lambda i: (i + first, 0)),
-        **kw,
-    )(*args)
-
-
-def head_all_body(pos, *refs):
-    g = jnp.concatenate([r[0] for r in refs[:4]], axis=1)
-    refs[-1][...] = jnp.dot(g, refs[4][...], preferred_element_type=F32).astype(BF16)
-
-
-def head_all(pos, g, k, first, steps, other=None):
-    specs = [
-        pl.BlockSpec((1, GB, T), functools.partial(lambda away, i, p: ((p[0] + away) % 4, i, 0), away))
-        for away in (0, 3, 1, 2)
-    ]
+        rows = GB
+        specs = [pl.BlockSpec((rows, T), lambda i, p: (i, 0))] * 4
+    start = first * GB // rows
     specs.append(whole((4 * T, DX)))
-    args = [g] * 4 + [k]
+    args = [*(gs * 4 if len(gs) == 1 else gs), k]
     kw = {}
     if other is not None:
         specs.append(pl.BlockSpec(memory_space=pl.ANY))
         args.append(other)
         kw["input_output_aliases"] = {len(args): 0}
     return call(
-        head_all_body,
+        head_body,
         out_shape=jax.ShapeDtypeStruct((VL, DX), BF16),
         grid_spec=pltpu.PrefetchScalarGridSpec(
             num_scalar_prefetch=1,
-            grid=(steps,),
+            grid=(steps * GB // rows,),
             in_specs=specs,
-            out_specs=pl.BlockSpec((GB, DX), lambda i, p: (i + first, 0)),
+            out_specs=pl.BlockSpec((rows, DX), lambda i, p: (i + start, 0)),
         ),
         **kw,
     )(pos, *args)
@@ -410,10 +374,9 @@
     def near(g):
         return [g, shift(g, 1), shift(g, 3)]
 
-    def far(parts, *first):
-        half = parts[0].shape[0] // 2
-        left, right = after(parts[1], *first), after(parts[2], *first)
-        return [shift(left[:half], 1), shift(right[half:], 3)]
+    def far(parts):
+        half = (parts[0].shape[0] // 2 + 15) // 16 * 16
+        return jnp.concatenate([shift(parts[1][:half], 1), shift(parts[2][half:], 3)], axis=0)
 
     all_u, all_m = lax.all_gather(gu, "x"), lax.all_gather(gm, "x")
     near_l = near(gl)
@@ -423,10 +386,10 @@
     both = (mine.astype(F32) + swap(after(other, *near_l[1:])).astype(F32)).astype(BF16)
     got = lax.all_to_all(both.reshape(16, T, 128), ("y", "z"), 0, 0, tiled=True)
 
-    head = head_all(pos, all_u, k, *CUTS[0])
-    head = head_piece(near_l, far_l, k, *CUTS[2], other=head)
+    head = head_rows(pos, [all_u], k, *CUTS[0])
+    head = head_rows(pos, near_l + [far_l], k, *CUTS[2], other=head)
     grad_hidden = jnp.sum(after(got, head).astype(F32), axis=0).astype(BF16)
-    head = head_all(pos, all_m, k, *CUTS[1], other=head)
+    head = head_rows(after(pos, grad_hidden), [all_m], k, *CUTS[1], other=head)
     return kl.reshape(T), grad_hidden, head.T
 
 

time: 226 us -> 223 us (0.987)
  waiting for transfers between devices: 67.5 us -> 61.6 us
    all_gather x2, waiting for transfers between devices: 25.1 us -> 0.01 us  [per_device(): all_u, all_m = (lax.all_gather(gu, 'x'), lax.all_gather(gm, 'x'))]
    ppermute x6, waiting for transfers between devices: 8.46 us -> 26.9 us  [shift(): return lax.ppermute(x, 'x', [(i, (i + n) % 4) for i in range(4)])]
    unnamed x28 -> x26, local copies, waits for them, and re-layouts: 5.42 us -> 4.18 us
  transfers between devices with their start and end apart: 27 -> 27, of which waited for: 16 -> 16; matrix products, arithmetic and copies ran while one was open for 2% -> 4% of each run, Pallas kernels for 34% -> 36%
where the time goes in v8:
time: 223 us
  Pallas kernels  90.2 us (40%)
  waiting for transfers between devices  61.6 us (28%)
  starting transfers between devices  43.7 us (20%)
  between operations  14.2 us (6%)
  local copies, waits for them, and re-layouts  6.8 us (3%)
  other arithmetic  6.2 us (3%)
    ppermute x6, waiting for transfers between devices, shift(): return lax.ppermute(x, 'x', [(i, (i + n) % 4) for i in range(4)])  26.9 us
    pallas_call x3, Pallas kernels, head_rows(): call(head_body, out_shape=jax.ShapeDtypeStruct((VL, DX), BF16), grid_spec...  24.5 us
    pallas_call x1, Pallas kernels, student(): call(student_body, out_shape=[jax.ShapeDtypeStruct((NS * SB, T), F32), pa...  20.4 us
    pallas_call x1, Pallas kernels, hidden_part(): call(hidden_body, out_shape=[jax.ShapeDtypeStruct((4, 4, T, 128), BF16)]...  17.5 us
    ppermute x6, waiting for transfers between devices, spread(): got.append(lax.ppermute(x, V, pairs))  13.5 us
    pallas_call x2, Pallas kernels, grad(): call(functools.partial(grad_body, cuts), out_shape=[jax.ShapeDtypeStruct(...  10.3 us
    ppermute x6, starting transfers between devices, spread(): got.append(lax.ppermute(x, V, pairs))  10.1 us
    all_to_all x1, waiting for transfers between devices, per_device(): gathered = lax.all_to_all(share, V, 0, 0, tiled=True)  9.48 us
  transfers between devices with their start and end apart: 27, of which 16 were waited for; matrix products, arithmetic and copies ran while one was open for 4% of the time, Pallas kernels for 36%

profile of v8, /device:TPU:1, one launch (start us, length us, event | category | flops | bytes accessed | tf_op | source)
XLA Modules:
  0.0 222.6 jit_solution(4221662160918724002)
XLA Ops:
  7.2 3.6 %collective-permute-start.2 = (bf16[512,128]{1,0:T(8,128)(2,1)}, bf16[512,128]{1,0:T(8,128)(2,1)S(1)}, u32[]{:S(2)}, u32[]{:S(2)}) collective-permute-start(bf16[512,128]{1,0:T(8,128)(2,1)} %param.4), channel_id=1, source_target_pairs={{0,6},{1,25},{2,0},{3,27},{4,2},{5,29},{6,4},{7,31},{8,14},{9,1},{... | collective-permute-start | bytes 393224 | tf_op jit(solution)/shard_map/ppermute | solution.py:349
  11.2 0.7 collective-permute-start
  11.8 4.4 %shard_map.67 = bf16[32,19,16,128]{3,2,1,0:T(8,128)(2,1)} custom-call(bf16[16,75968]{1,0:T(8,128)(2,1)} %t_ref.1), custom_call_target="tpu_custom_call" | custom-call | flops 1048576 | bytes 65536 | tf_op jit(solution)/shard_map/pallas_call | solution.py:55
  16.4 1.6 collective-permute-done
  18.1 1.4 collective-permute-start.3
  19.5 3.3 %collective-permute-start.4 = (bf16[4,512,128]{2,1,0:T(8,128)(2,1)S(1)}, bf16[4,512,128]{2,1,0:T(8,128)(2,1)S(1)}, u32[]{:S(2)}, u32[]{:S(2)}) collective-permute-start(bf16[4,512,128]{2,1,0:T(8,128)(2,1)S(1)} %pad_maximum_fusion.1.refs_0_), channel_id=1, source_target_pairs={{0,16},{1,5},{2,18},{3,7},{4,20},{5,1},{6,22},{7,3},{8,24},{9,13},... | collective-permute-start | bytes 1572872 | tf_op jit(solution)/shard_map/ppermute | solution.py:349
  22.8 0.7 collective-permute-start.5
  23.6 5.0 %collective-permute-done.3.refs_1_ = bf16[4,512,128]{2,1,0:T(8,128)(2,1)S(1)} collective-permute-done((bf16[4,512,128]{2,1,0:T(8,128)(2,1)S(1)}, bf16[4,512,128]{2,1,0:T(8,128)(2,1)S(1)}, u32[]{:S(2)}, u32[]{:S(2)}) %collective-permute-start.3) | collective-permute-done | bytes 524320 | tf_op jit(solution)/shard_map/ppermute | solution.py:349
  28.5 6.8 %collective-permute-done.4.refs_2_ = bf16[4,512,128]{2,1,0:T(8,128)(2,1)S(1)} collective-permute-done((bf16[4,512,128]{2,1,0:T(8,128)(2,1)S(1)}, bf16[4,512,128]{2,1,0:T(8,128)(2,1)S(1)}, u32[]{:S(2)}, u32[]{:S(2)}) %collective-permute-start.4) | collective-permute-done | bytes 524320 | tf_op jit(solution)/shard_map/ppermute | solution.py:349
  35.3 0.8 copy-done.9
  36.4 7.1 %all-to-all-start = ((bf16[32,19,16,128]{3,2,1,0:T(8,128)(2,1)}), bf16[32,19,16,128]{3,2,1,0:T(8,128)(2,1)S(1)}, u32[]{:S(2)}, u32[]{:S(2)}) async-start(bf16[32,19,16,128]{3,2,1,0:T(8,128)(2,1)} %shard_map.67), calls=%async_computation | async-start | bytes 4980736 | tf_op jit(solution)/shard_map/all_to_all | solution.py:363
  45.6 1.5 collective-permute-done.7.refs_5_
  47.3 0.8 collective-permute-done.9.refs_7_
  48.1 20.4 %shard_map.68 = (f32[2560,512]{1,0:T(8,128)}, f32[8,512]{1,0:T(8,128)}, f32[8,512]{1,0:T(8,128)}, bf16[512,1024]{1,0:T(8,128)(2,1)}, bf16[4,512,128]{2,1,0:T(8,1...) custom-call(s32[4]{0:T(128)} %pad_add_fusion.pos, bf16[2374,4096]{1,0:T(8,128)(2,1)} %bitcast.19, ...), custom_call_target="tpu_custom_call" | custom-call | flops 1048576 | bytes 65536 | tf_op jit(solution)/shard_map/pallas_call | solution.py:103
  68.5 2.5 %collective-permute-start.12 = (bf16[4,512,128]{2,1,0:T(8,128)(2,1)}, bf16[4,512,128]{2,1,0:T(8,128)(2,1)}, u32[]{:S(2)}, u32[]{:S(2)}) collective-permute-start(bf16[4,512,128]{2,1,0:T(8,128)(2,1)} %get-tuple-element.35), channel_id=1, source_target_pairs={{0,32},{1,97},{32,64},{33,1},{64,96},{65,33},{96,0},{97,65},{2,34}... | collective-permute-start | bytes 1572872 | tf_op jit(solution)/shard_map/ppermute | solution.py:333
  71.0 2.7 %collective-permute-start.11 = (bf16[4,512,128]{2,1,0:T(8,128)(2,1)}, bf16[4,512,128]{2,1,0:T(8,128)(2,1)S(1)}, u32[]{:S(2)}, u32[]{:S(2)}) collective-permute-start(bf16[4,512,128]{2,1,0:T(8,128)(2,1)} %get-tuple-element.34), channel_id=1, source_target_pairs={{0,96},{32,0},{64,32},{96,64},{1,97},{33,1},{65,33},{97,65},{2,98}... | collective-permute-start | bytes 1572872 | tf_op jit(solution)/shard_map/ppermute | solution.py:329
  73.7 2.3 %all-to-all-done.t_ref = bf16[32,19,16,128]{3,2,1,0:T(8,128)(2,1)S(1)} async-done(((bf16[32,19,16,128]{3,2,1,0:T(8,128)(2,1)}), bf16[32,19,16,128]{3,2,1,0:T(8,128)(2,1)S(1)}, u32[]{:S(2)}, u32[]{:S(2)}) %all-to-all-start) | async-done | bytes 2490400 | tf_op jit(solution)/shard_map/all_to_all | solution.py:363
  76.0 1.5 copy-done
  77.5 7.3 %shard_map.69 = (bf16[2560,512]{1,0:T(8,128)(2,1)}, f32[32,8,512]{2,1,0:T(8,128)}) custom-call(f32[8,512]{1,0:T(8,128)} %get-tuple-element.28.m_ref, f32[8,512]{1,0:T(8,128)} %get-tuple-element.29.l_ref, f32[2560,512]{1,0:T(8,128)} %get-tuple-element.30.s_ref, bf16[32,19,16,128]{3,2,1,0:T(8,128)(2,1)} %copy-done), custom_call_target="tpu_custom_call" | custom-call | flops 1048576 | bytes 65536 | tf_op jit(solution)/shard_map/pallas_call | solution.py:172
  84.8 2.5 %collective-permute-start.13 = (bf16[4,512,128]{2,1,0:T(8,128)(2,1)}, bf16[4,512,128]{2,1,0:T(8,128)(2,1)S(1)}, u32[]{:S(2)}, u32[]{:S(2)}) collective-permute-start(bf16[4,512,128]{2,1,0:T(8,128)(2,1)} %collective-permute-done.12), channel_id=1, source_target_pairs={{0,32},{1,97},{32,64},{33,1},{64,96},{65,33},{96,0},{97,65},{2,34}... | collective-permute-start | bytes 1572872 | tf_op jit(solution)/shard_map/ppermute | solution.py:333
  87.4 4.8 %all-to-all-start.1 = ((f32[32,8,512]{2,1,0:T(8,128)}), f32[32,8,512]{2,1,0:T(8,128)S(1)}, u32[]{:S(2)}, u32[]{:S(2)}) async-start(f32[32,8,512]{2,1,0:T(8,128)} %get-tuple-element.32), calls=%async_computation.1 | async-start | bytes 1048576 | tf_op jit(solution)/shard_map/all_to_all | solution.py:366
  92.5 1.9 collective-permute-done.13.refs_4_
  94.3 9.5 %all-to-all-done.1.all_ref = f32[32,8,512]{2,1,0:T(8,128)S(1)} async-done(((f32[32,8,512]{2,1,0:T(8,128)}), f32[32,8,512]{2,1,0:T(8,128)S(1)}, u32[]{:S(2)}, u32[]{:S(2)}) %all-to-all-start.1) | async-done | bytes 524320 | tf_op jit(solution)/shard_map/all_to_all | solution.py:366
  103.8 0.8 copy-done.1
  104.6 5.2 %shard_map.70 = (bf16[1216,512]{1,0:T(8,128)(2,1)}, f32[1,512]{1,0:T(1,128)}) custom-call(f32[32,8,512]{2,1,0:T(8,128)} %copy-done.1, f32[1,512]{1,0:T(1,128)} %bitcast.30, f32[2560,512]{1,0:T(8,128)} %get-tuple-element.30.s_ref, bf16[2560,512]{1,0:T(8,128)(2,1)} %get-tuple-element.38.t_ref), custom_call_target="tpu_custom_call" | custom-call | flops 1048576 | bytes 65536 | tf_op jit(solution)/shard_map/pallas_call | solution.py:222
  109.8 5.2 %shard_map.71 = (bf16[304,512]{1,0:T(8,128)(2,1)}, bf16[912,512]{1,0:T(8,128)(2,1)}, f32[1,512]{1,0:T(1,128)}) custom-call(f32[32,8,512]{2,1,0:T(8,128)} %copy-done.1, f32[1,512]{1,0:T(1,128)} %bitcast.31, f32[2560,512]{1,0:T(8,128)} %get-tuple-element.30.s_ref, bf16[2560,512]{1,0:T(8,128)(2,1)} %get-tuple-element.38.t_ref), custom_call_target="tpu_custom_call" | custom-call | flops 1048576 | bytes 65536 | tf_op jit(solution)/shard_map/pallas_call | solution.py:222
  115.0 1.1 collective-permute-start.14
  116.1 1.7 collective-permute-start.15
  117.8 17.5 %shard_map.72 = (bf16[4,4,512,128]{3,2,1,0:T(8,128)(2,1)}, bf16[4,4,512,128]{3,2,1,0:T(8,128)(2,1)}) custom-call(s32[4]{0:T(128)} %pad_add_fusion.pos, bf16[1216,512]{1,0:T(8,128)(2,1)} %get-tuple-element.40.refs_0_, bf16[304,512]{1,0:T(8,128)(2,1)} %get-tuple-element.42.refs_1_, bf16[912,512]{1,0:T(8,128)(2,1)} %get-tuple-element.43.refs_2_.refs_0_, ...), custom_call_target="tpu_custom_call" | custom-call | flops 1048576 | bytes 65536 | tf_op jit(solution)/shard_map/pallas_call | solution.py:256
  135.2 21.0 %collective-permute-done.14.refs_1_ = bf16[912,512]{1,0:T(8,128)(2,1)S(1)} collective-permute-done((bf16[912,512]{1,0:T(8,128)(2,1)}, bf16[912,512]{1,0:T(8,128)(2,1)S(1)}, u32[]{:S(2)}, u32[]{:S(2)}) %collective-permute-start.14) | collective-permute-done | bytes 933920 | tf_op jit(solution)/shard_map/ppermute | solution.py:329
  156.2 1.0 collective-permute-done.15.refs_2_
  157.2 1.8 collective-permute-start.16
  159.0 4.0 %collective-permute-done.16 = bf16[4,4,512,128]{3,2,1,0:T(8,128)(2,1)S(1)} collective-permute-done((bf16[4,4,512,128]{3,2,1,0:T(8,128)(2,1)}, bf16[4,4,512,128]{3,2,1,0:T(8,128)(2,1)S(1)}, u32[]{:S(2)}, u32[]{:S(2)}) %collective-permute-start.16) | collective-permute-done | bytes 2097184 | tf_op jit(solution)/shard_map/ppermute | solution.py:337
  163.0 3.5 %add_convert_fusion = bf16[4,4,512,128]{3,2,1,0:T(8,128)(2,1)} fusion(bf16[4,4,512,128]{3,2,1,0:T(8,128)(2,1)S(1)} %collective-permute-done.16, bf16[4,4,512,128]{3,2,1,0:T(8,128)(2,1)} %get-tuple-element.44), kind=kLoop, calls=%fused_computation | loop fusion | flops 4194304 | bytes 6291456 | tf_op jit(solution)/shard_map/convert_element_type | solution.py:386
  166.5 3.7 %all-to-all-start.2 = ((bf16[16,512,128]{2,1,0:T(8,128)(2,1)}), bf16[16,512,128]{2,1,0:T(8,128)(2,1)S(1)}, u32[]{:S(2)}, u32[]{:S(2)}) async-start(bf16[16,512,128]{2,1,0:T(8,128)(2,1)} %bitcast.11), calls=%async_computation.2 | async-start | bytes 4194304 | tf_op jit(solution)/shard_map/all_to_all | solution.py:387
  170.3 0.7 all-gather.7.cloned.1.call-update
  172.0 0.8 slice.8
  172.8 1.8 slice.9
  174.6 3.3 %collective-permute-start.18 = (bf16[448,512]{1,0:T(8,128)(2,1)}, bf16[448,512]{1,0:T(8,128)(2,1)S(1)}, u32[]{:S(2)}, u32[]{:S(2)}) collective-permute-start(bf16[448,512]{1,0:T(8,128)(2,1)} %slice.9), channel_id=1, source_target_pairs={{0,96},{32,0},{64,32},{96,64},{1,97},{33,1},{65,33},{97,65},{2,98}... | collective-permute-start | bytes 1376264 | tf_op jit(solution)/shard_map/ppermute | solution.py:329
  177.9 0.8 copy-done.11
  178.7 5.7 %shard_map.73.refs_4_ = bf16[2048,1024]{1,0:T(8,128)(2,1)} custom-call(s32[4]{0:T(128)} %pad_add_fusion.pos, bf16[512,1024]{1,0:T(8,128)(2,1)} %get-tuple-element.48.h_ref, bf16[4,512,128]{2,1,0:T(8,128)(2,1)} %copy-done.5, bf16[4,512,128]{2,1,0:T(8,128)(2,1)} %copy-done.11, bf16[4,512,128]{2,1,0:T(8,128)(2,1)} %copy-done.6, ...), custom_call_target="tpu_custom_call" | custom-call | flops 1048576 | bytes 65536 | tf_op jit(solution)/shard_map/pallas_call | solution.py:280
  184.4 4.3 %collective-permute-done.18 = bf16[448,512]{1,0:T(8,128)(2,1)S(1)} collective-permute-done((bf16[448,512]{1,0:T(8,128)(2,1)}, bf16[448,512]{1,0:T(8,128)(2,1)S(1)}, u32[]{:S(2)}, u32[]{:S(2)}) %collective-permute-start.18) | collective-permute-done | bytes 458784 | tf_op jit(solution)/shard_map/ppermute | solution.py:329
  188.7 0.7 collective-permute-done.17
  189.3 1.0 pad_maximum_fusion.refs_3_
  190.3 10.4 %shard_map.74.refs_5_ = bf16[2374,1024]{1,0:T(8,128)(2,1)} custom-call(s32[4]{0:T(128)} %pad_add_fusion.pos, bf16[4,1216,512]{2,1,0:T(8,128)(2,1)} %bitcast.15, bf16[4,1216,512]{2,1,0:T(8,128)(2,1)} %bitcast.16, bf16[4,1216,512]{2,1,0:T(8,128)(2,1)} %bitcast.17, bf16[4,1216,512]{2,1,0:T(8,128)(2,1)} %bitcast.18, bf16[2048,1024]{1,0:T(8,128)(2,1)} %shard_map.73.refs_4_), custom_call_target="tpu_custom_call" | custom-call | flops 1048576 | bytes 65536 | tf_op jit(solution)/shard_map/pallas_call | solution.py:315
  200.8 8.6 %shard_map.75.refs_5_ = bf16[2374,1024]{1,0:T(8,128)(2,1)} custom-call(s32[4]{0:T(128)} %pad_add_fusion.pos, bf16[912,512]{1,0:T(8,128)(2,1)} %get-tuple-element.43.refs_2_.refs_0_, bf16[912,512]{1,0:T(8,128)(2,1)} %copy-done.2, bf16[912,512]{1,0:T(8,128)(2,1)} %copy-done.4, ...), custom_call_target="tpu_custom_call", output_to_operand_aliasing={{}: (6, {})} | custom-call | flops 1048576 | bytes 65536 | tf_op jit(solution)/shard_map/pallas_call | solution.py:315
  209.4 1.0 reduce_sum.12
  210.3 5.4 %shard_map.76 = bf16[2374,1024]{1,0:T(8,128)(2,1)} custom-call(s32[4]{0:T(128)} %pad_add_fusion.pos, bf16[4,304,512]{2,1,0:T(8,128)(2,1)} %bitcast.22, bf16[4,304,512]{2,1,0:T(8,128)(2,1)} %bitcast.23, bf16[4,304,512]{2,1,0:T(8,128)(2,1)} %bitcast.24, bf16[4,304,512]{2,1,0:T(8,128)(2,1)} %bitcast.25, ...), custom_call_target="tpu_custom_call", output_to_operand_aliasing={{}: (6, {})} | custom-call | flops 1048576 | bytes 65536 | tf_op jit(solution)/shard_map/pallas_call | solution.py:315
  (51 shorter events, 4.4 us)
Async XLA Ops:
  7.2 10.9 %copy-start.12 = (bf16[512,128]{1,0:T(8,128)(2,1)S(1)}, bf16[512,128]{1,0:T(8,128)(2,1)}, u32[]{:S(2)}) copy-start(bf16[512,128]{1,0:T(8,128)(2,1)} %param.4) | copy-start | bytes 393220
  7.2 9.1 %collective-permute-start.2 = (bf16[512,128]{1,0:T(8,128)(2,1)}, bf16[512,128]{1,0:T(8,128)(2,1)S(1)}, u32[]{:S(2)}, u32[]{:S(2)}) collective-permute-start(bf16[512,128]{1,0:T(8,128)(2,1)} %param.4), channel_id=1, source_target_pairs={{0,6},{1,25},{2,0},{3,27},{4,2},{5,29},{6,4},{7,31},{8,14},{9,1},{... | collective-permute-start | bytes 393224 | tf_op jit(solution)/shard_map/ppermute | solution.py:349
  10.8 5.6 %collective-permute-start.1 = (bf16[512,128]{1,0:T(8,128)(2,1)}, bf16[512,128]{1,0:T(8,128)(2,1)S(1)}, u32[]{:S(2)}, u32[]{:S(2)}) collective-permute-start(bf16[512,128]{1,0:T(8,128)(2,1)} %param.4), channel_id=1, source_target_pairs={{0,4},{1,17},{2,6},{3,19},{4,0},{5,21},{6,2},{7,23},{8,12},{9,25},... | collective-permute-start | bytes 393224 | tf_op jit(solution)/shard_map/ppermute | solution.py:349
  11.2 6.9 %collective-permute-start = (bf16[512,128]{1,0:T(8,128)(2,1)}, bf16[512,128]{1,0:T(8,128)(2,1)S(1)}, u32[]{:S(2)}, u32[]{:S(2)}) collective-permute-start(bf16[512,128]{1,0:T(8,128)(2,1)} %param.4), channel_id=1, source_target_pairs={{0,2},{1,9},{2,4},{3,11},{4,6},{5,13},{6,0},{7,15},{8,10},{9,17},{... | collective-permute-start | bytes 393224 | tf_op jit(solution)/shard_map/ppermute | solution.py:349
  18.1 25.3 %copy-start.3 = (bf16[4,512,128]{2,1,0:T(8,128)(2,1)}, bf16[4,512,128]{2,1,0:T(8,128)(2,1)S(1)}, u32[]{:S(2)}) copy-start(bf16[4,512,128]{2,1,0:T(8,128)(2,1)S(1)} %pad_maximum_fusion.1.refs_0_) | copy-start | bytes 1572868
  18.1 10.4 %collective-permute-start.3 = (bf16[4,512,128]{2,1,0:T(8,128)(2,1)S(1)}, bf16[4,512,128]{2,1,0:T(8,128)(2,1)S(1)}, u32[]{:S(2)}, u32[]{:S(2)}) collective-permute-start(bf16[4,512,128]{2,1,0:T(8,128)(2,1)S(1)} %pad_maximum_fusion.1.refs_0_), channel_id=1, source_target_pairs={{0,8},{1,3},{2,10},{3,5},{4,12},{5,7},{6,14},{7,1},{8,16},{9,11},{... | collective-permute-start | bytes 1572872 | tf_op jit(solution)/shard_map/ppermute | solution.py:349
  19.5 15.8 %collective-permute-start.4 = (bf16[4,512,128]{2,1,0:T(8,128)(2,1)S(1)}, bf16[4,512,128]{2,1,0:T(8,128)(2,1)S(1)}, u32[]{:S(2)}, u32[]{:S(2)}) collective-permute-start(bf16[4,512,128]{2,1,0:T(8,128)(2,1)S(1)} %pad_maximum_fusion.1.refs_0_), channel_id=1, source_target_pairs={{0,16},{1,5},{2,18},{3,7},{4,20},{5,1},{6,22},{7,3},{8,24},{9,13},... | collective-permute-start | bytes 1572872 | tf_op jit(solution)/shard_map/ppermute | solution.py:349
  22.8 12.5 %collective-permute-start.5 = (bf16[4,512,128]{2,1,0:T(8,128)(2,1)S(1)}, bf16[4,512,128]{2,1,0:T(8,128)(2,1)S(1)}, u32[]{:S(2)}, u32[]{:S(2)}) collective-permute-start(bf16[4,512,128]{2,1,0:T(8,128)(2,1)S(1)} %pad_maximum_fusion.1.refs_0_), channel_id=1, source_target_pairs={{0,24},{1,7},{2,26},{3,1},{4,28},{5,3},{6,30},{7,5},{8,0},{9,15},{... | collective-permute-start | bytes 1572872 | tf_op jit(solution)/shard_map/ppermute | solution.py:349
  28.5 15.3 %copy-start.8 = (bf16[4,512,128]{2,1,0:T(8,128)(2,1)}, bf16[4,512,128]{2,1,0:T(8,128)(2,1)S(1)}, u32[]{:S(2)}) copy-start(bf16[4,512,128]{2,1,0:T(8,128)(2,1)S(1)} %collective-permute-done.3.refs_1_) | copy-start | bytes 1572868
  35.3 0.8 copy-start.9
  35.3 1.0 copy-start.10
  36.4 39.6 %all-to-all-start = ((bf16[32,19,16,128]{3,2,1,0:T(8,128)(2,1)}), bf16[32,19,16,128]{3,2,1,0:T(8,128)(2,1)S(1)}, u32[]{:S(2)}, u32[]{:S(2)}) async-start(bf16[32,19,16,128]{3,2,1,0:T(8,128)(2,1)} %shard_map.67), calls=%async_computation | async-start | bytes 4980736 | tf_op jit(solution)/shard_map/all_to_all | solution.py:363
  43.5 2.1 collective-permute-start.6
  43.8 3.3 %collective-permute-start.7 = (bf16[4,512,128]{2,1,0:T(8,128)(2,1)S(1)}, bf16[4,512,128]{2,1,0:T(8,128)(2,1)}, u32[]{:S(2)}, u32[]{:S(2)}) collective-permute-start(bf16[4,512,128]{2,1,0:T(8,128)(2,1)S(1)} %collective-permute-done.3.refs_1_), channel_id=1, source_target_pairs={{0,1},{1,0},{2,3},{3,2},{4,5},{5,4},{6,7},{7,6},{8,9},{9,8},{10,11... | collective-permute-start | bytes 1572872 | tf_op jit(solution)/shard_map/ppermute | solution.py:337
  44.1 3.2 %collective-permute-start.8 = (bf16[4,512,128]{2,1,0:T(8,128)(2,1)}, bf16[4,512,128]{2,1,0:T(8,128)(2,1)}, u32[]{:S(2)}, u32[]{:S(2)}) collective-permute-start(bf16[4,512,128]{2,1,0:T(8,128)(2,1)} %copy-done.9), channel_id=1, source_target_pairs={{0,1},{1,0},{2,3},{3,2},{4,5},{5,4},{6,7},{7,6},{8,9},{9,8},{10,11... | collective-permute-start | bytes 1572872 | tf_op jit(solution)/shard_map/ppermute | solution.py:337
  44.3 3.8 %collective-permute-start.9 = (bf16[4,512,128]{2,1,0:T(8,128)(2,1)}, bf16[4,512,128]{2,1,0:T(8,128)(2,1)}, u32[]{:S(2)}, u32[]{:S(2)}) collective-permute-start(bf16[4,512,128]{2,1,0:T(8,128)(2,1)} %copy-done.10), channel_id=1, source_target_pairs={{0,1},{1,0},{2,3},{3,2},{4,5},{5,4},{6,7},{7,6},{8,9},{9,8},{10,11... | collective-permute-start | bytes 1572872 | tf_op jit(solution)/shard_map/ppermute | solution.py:337
  68.5 16.3 %collective-permute-start.12 = (bf16[4,512,128]{2,1,0:T(8,128)(2,1)}, bf16[4,512,128]{2,1,0:T(8,128)(2,1)}, u32[]{:S(2)}, u32[]{:S(2)}) collective-permute-start(bf16[4,512,128]{2,1,0:T(8,128)(2,1)} %get-tuple-element.35), channel_id=1, source_target_pairs={{0,32},{1,97},{32,64},{33,1},{64,96},{65,33},{96,0},{97,65},{2,34}... | collective-permute-start | bytes 1572872 | tf_op jit(solution)/shard_map/ppermute | solution.py:333
  71.0 21.4 %collective-permute-start.10 = (bf16[4,512,128]{2,1,0:T(8,128)(2,1)}, bf16[4,512,128]{2,1,0:T(8,128)(2,1)S(1)}, u32[]{:S(2)}, u32[]{:S(2)}) collective-permute-start(bf16[4,512,128]{2,1,0:T(8,128)(2,1)} %get-tuple-element.33), channel_id=1, source_target_pairs={{0,32},{32,64},{64,96},{96,0},{1,33},{33,65},{65,97},{97,1},{2,34}... | collective-permute-start | bytes 1572872 | tf_op jit(solution)/shard_map/ppermute | solution.py:329
  71.0 21.4 %collective-permute-start.11 = (bf16[4,512,128]{2,1,0:T(8,128)(2,1)}, bf16[4,512,128]{2,1,0:T(8,128)(2,1)S(1)}, u32[]{:S(2)}, u32[]{:S(2)}) collective-permute-start(bf16[4,512,128]{2,1,0:T(8,128)(2,1)} %get-tuple-element.34), channel_id=1, source_target_pairs={{0,96},{32,0},{64,32},{96,64},{1,97},{33,1},{65,33},{97,65},{2,98}... | collective-permute-start | bytes 1572872 | tf_op jit(solution)/shard_map/ppermute | solution.py:329
  76.0 1.5 copy-start
  84.8 9.5 %collective-permute-start.13 = (bf16[4,512,128]{2,1,0:T(8,128)(2,1)}, bf16[4,512,128]{2,1,0:T(8,128)(2,1)S(1)}, u32[]{:S(2)}, u32[]{:S(2)}) collective-permute-start(bf16[4,512,128]{2,1,0:T(8,128)(2,1)} %collective-permute-done.12), channel_id=1, source_target_pairs={{0,32},{1,97},{32,64},{33,1},{64,96},{65,33},{96,0},{97,65},{2,34}... | collective-permute-start | bytes 1572872 | tf_op jit(solution)/shard_map/ppermute | solution.py:333
  87.4 16.4 %all-to-all-start.1 = ((f32[32,8,512]{2,1,0:T(8,128)}), f32[32,8,512]{2,1,0:T(8,128)S(1)}, u32[]{:S(2)}, u32[]{:S(2)}) async-start(f32[32,8,512]{2,1,0:T(8,128)} %get-tuple-element.32), calls=%async_computation.1 | async-start | bytes 1048576 | tf_op jit(solution)/shard_map/all_to_all | solution.py:366
  92.2 98.2 %all-gather.5.cloned.1.call-start = ((), (), s32[]{:S(2)}) async-start(), calls=%async_computation.3 | async-start | bytes 6225920 | tf_op jit(solution)/shard_map/all_gather | solution.py:381
  92.4 78.6 %copy-start.5 = (bf16[4,512,128]{2,1,0:T(8,128)(2,1)}, bf16[4,512,128]{2,1,0:T(8,128)(2,1)S(1)}, u32[]{:S(2)}) copy-start(bf16[4,512,128]{2,1,0:T(8,128)(2,1)S(1)} %collective-permute-done.10.refs_0_) | copy-start | bytes 1572868
  92.5 22.6 %copy-start.6 = (bf16[4,512,128]{2,1,0:T(8,128)(2,1)}, bf16[4,512,128]{2,1,0:T(8,128)(2,1)S(1)}, u32[]{:S(2)}) copy-start(bf16[4,512,128]{2,1,0:T(8,128)(2,1)S(1)} %collective-permute-done.11.refs_2_) | copy-start | bytes 1572868
  94.3 20.7 %copy-start.7 = (bf16[4,512,128]{2,1,0:T(8,128)(2,1)}, bf16[4,512,128]{2,1,0:T(8,128)(2,1)S(1)}, u32[]{:S(2)}) copy-start(bf16[4,512,128]{2,1,0:T(8,128)(2,1)S(1)} %collective-permute-done.13.refs_4_) | copy-start | bytes 1572868
  103.8 0.8 copy-start.1
  115.0 41.2 %collective-permute-start.14 = (bf16[912,512]{1,0:T(8,128)(2,1)}, bf16[912,512]{1,0:T(8,128)(2,1)S(1)}, u32[]{:S(2)}, u32[]{:S(2)}) collective-permute-start(bf16[912,512]{1,0:T(8,128)(2,1)} %get-tuple-element.43.refs_2_.refs_0_), channel_id=1, source_target_pairs={{0,32},{32,64},{64,96},{96,0},{1,33},{33,65},{65,97},{97,1},{2,34}... | collective-permute-start | bytes 2801672 | tf_op jit(solution)/shard_map/ppermute | solution.py:329
  116.1 41.1 %collective-permute-start.15 = (bf16[912,512]{1,0:T(8,128)(2,1)}, bf16[912,512]{1,0:T(8,128)(2,1)S(1)}, u32[]{:S(2)}, u32[]{:S(2)}) collective-permute-start(bf16[912,512]{1,0:T(8,128)(2,1)} %get-tuple-element.43.refs_2_.refs_0_), channel_id=1, source_target_pairs={{0,96},{32,0},{64,32},{96,64},{1,97},{33,1},{65,33},{97,65},{2,98}... | collective-permute-start | bytes 2801672 | tf_op jit(solution)/shard_map/ppermute | solution.py:329
  156.2 15.7 %copy-start.2 = (bf16[912,512]{1,0:T(8,128)(2,1)}, bf16[912,512]{1,0:T(8,128)(2,1)S(1)}, u32[]{:S(2)}) copy-start(bf16[912,512]{1,0:T(8,128)(2,1)S(1)} %collective-permute-done.14.refs_1_) | copy-start | bytes 2801668
  157.2 9.3 %copy-start.4 = (bf16[912,512]{1,0:T(8,128)(2,1)}, bf16[912,512]{1,0:T(8,128)(2,1)S(1)}, u32[]{:S(2)}) copy-start(bf16[912,512]{1,0:T(8,128)(2,1)S(1)} %collective-permute-done.15.refs_2_) | copy-start | bytes 2801668
  157.2 5.8 %collective-permute-start.16 = (bf16[4,4,512,128]{3,2,1,0:T(8,128)(2,1)}, bf16[4,4,512,128]{3,2,1,0:T(8,128)(2,1)S(1)}, u32[]{:S(2)}, u32[]{:S(2)}) collective-permute-start(bf16[4,4,512,128]{3,2,1,0:T(8,128)(2,1)} %get-tuple-element.46), channel_id=1, source_target_pairs={{0,1},{1,0},{2,3},{3,2},{4,5},{5,4},{6,7},{7,6},{8,9},{9,8},{10,11... | collective-permute-start | bytes 6291464 | tf_op jit(solution)/shard_map/ppermute | solution.py:337
  166.5 42.9 %all-to-all-start.2 = ((bf16[16,512,128]{2,1,0:T(8,128)(2,1)}), bf16[16,512,128]{2,1,0:T(8,128)(2,1)S(1)}, u32[]{:S(2)}, u32[]{:S(2)}) async-start(bf16[16,512,128]{2,1,0:T(8,128)(2,1)} %bitcast.11), calls=%async_computation.2 | async-start | bytes 4194304 | tf_op jit(solution)/shard_map/all_to_all | solution.py:387
  170.2 40.1 %all-gather.7.cloned.1.call-start = ((), (), s32[]{:S(2)}) async-start(), calls=%async_computation.4 | async-start | bytes 1556480 | tf_op jit(solution)/shard_map/all_gather | solution.py:381
  171.0 6.9 %collective-permute-start.19 = (bf16[4,512,128]{2,1,0:T(8,128)(2,1)S(1)}, bf16[4,512,128]{2,1,0:T(8,128)(2,1)S(1)}, u32[]{:S(2)}, u32[]{:S(2)}) collective-permute-start(bf16[4,512,128]{2,1,0:T(8,128)(2,1)S(1)} %collective-permute-done.10.refs_0_), channel_id=1, source_target_pairs={{0,1},{1,0},{2,3},{3,2},{4,5},{5,4},{6,7},{7,6},{8,9},{9,8},{10,11... | collective-permute-start | bytes 1572872 | tf_op jit(solution)/shard_map/ppermute | solution.py:337
  171.4 6.4 %collective-permute-start.20 = (bf16[4,512,128]{2,1,0:T(8,128)(2,1)}, bf16[4,512,128]{2,1,0:T(8,128)(2,1)}, u32[]{:S(2)}, u32[]{:S(2)}) collective-permute-start(bf16[4,512,128]{2,1,0:T(8,128)(2,1)} %copy-done.6), channel_id=1, source_target_pairs={{0,1},{1,0},{2,3},{3,2},{4,5},{5,4},{6,7},{7,6},{8,9},{9,8},{10,11... | collective-permute-start | bytes 1572872 | tf_op jit(solution)/shard_map/ppermute | solution.py:337
  171.6 6.3 %collective-permute-start.21 = (bf16[4,512,128]{2,1,0:T(8,128)(2,1)}, bf16[4,512,128]{2,1,0:T(8,128)(2,1)}, u32[]{:S(2)}, u32[]{:S(2)}) collective-permute-start(bf16[4,512,128]{2,1,0:T(8,128)(2,1)} %copy-done.7), channel_id=1, source_target_pairs={{0,1},{1,0},{2,3},{3,2},{4,5},{5,4},{6,7},{7,6},{8,9},{9,8},{10,11... | collective-permute-start | bytes 1572872 | tf_op jit(solution)/shard_map/ppermute | solution.py:337
  172.8 16.6 %collective-permute-start.17 = (bf16[464,512]{1,0:T(8,128)(2,1)}, bf16[464,512]{1,0:T(8,128)(2,1)S(1)}, u32[]{:S(2)}, u32[]{:S(2)}) collective-permute-start(bf16[464,512]{1,0:T(8,128)(2,1)} %slice.8), channel_id=1, source_target_pairs={{0,32},{32,64},{64,96},{96,0},{1,33},{33,65},{65,97},{97,1},{2,34}... | collective-permute-start | bytes 1425416 | tf_op jit(solution)/shard_map/ppermute | solution.py:329
  174.6 14.1 %collective-permute-start.18 = (bf16[448,512]{1,0:T(8,128)(2,1)}, bf16[448,512]{1,0:T(8,128)(2,1)S(1)}, u32[]{:S(2)}, u32[]{:S(2)}) collective-permute-start(bf16[448,512]{1,0:T(8,128)(2,1)} %slice.9), channel_id=1, source_target_pairs={{0,96},{32,0},{64,32},{96,64},{1,97},{33,1},{65,33},{97,65},{2,98}... | collective-permute-start | bytes 1376264 | tf_op jit(solution)/shard_map/ppermute | solution.py:329
  177.9 0.8 copy-start.11
Sparse Core Ops, SparseCore 0:
  110.0 71.2 all-gather.4
  182.9 20.7 all-gather.6

commit v9 on v8

--- a/solution.py
+++ b/solution.py
@@ -376,17 +376,19 @@
 
     def far(parts):
         half = (parts[0].shape[0] // 2 + 15) // 16 * 16
-        return jnp.concatenate([shift(parts[1][:half], 1), shift(parts[2][half:], 3)], axis=0)
+        return [shift(parts[1][:half], 1), shift(parts[2][half:], 3)]
 
     all_u, all_m = lax.all_gather(gu, "x"), lax.all_gather(gm, "x")
     near_l = near(gl)
     far_l = far(near_l)
     mine, other = hidden_part(pos, (gu, gm, gl), wt)
-    k = tokens(after(pos, mine), h, [x for other in others for x in (other, swap(other))])
-    both = (mine.astype(F32) + swap(after(other, *near_l[1:])).astype(F32)).astype(BF16)
+    others = [x for other in others for x in (other, swap(after(other, gathered)))]
+    k = tokens(after(pos, mine), h, others)
+    both = (mine.astype(F32) + swap(after(other, k, *near_l[1:])).astype(F32)).astype(BF16)
     got = lax.all_to_all(both.reshape(16, T, 128), ("y", "z"), 0, 0, tiled=True)
 
     head = head_rows(pos, [all_u], k, *CUTS[0])
+    far_l = jnp.concatenate([after(x, head) for x in far_l], axis=0)
     head = head_rows(pos, near_l + [far_l], k, *CUTS[2], other=head)
     grad_hidden = jnp.sum(after(got, head).astype(F32), axis=0).astype(BF16)
     head = head_rows(after(pos, grad_hidden), [all_m], k, *CUTS[1], other=head)

time: 223 us -> 219 us (0.982)
    ppermute x6, waiting for transfers between devices: 26.9 us -> 14.5 us  [shift(): return lax.ppermute(x, 'x', [(i, (i + n) % 4) for i in range(4)])]
    all_gather x2, waiting for transfers between devices: 0.01 us -> 10.5 us  [per_device(): all_u, all_m = (lax.all_gather(gu, 'x'), lax.all_gather(gm, 'x'))]
  transfers between devices with their start and end apart: 27 -> 27, of which waited for: 16 -> 16; matrix products, arithmetic and copies ran while one was open for 4% -> 3% of each run, Pallas kernels for 36% -> 37%
where the time goes in v9:
time: 219 us; the launch traced here: 218 us
  Pallas kernels  90.3 us (41%)
  waiting for transfers between devices  59.8 us (27%)
  starting transfers between devices  44 us (20%)
  between operations  14.2 us (6%)
  local copies, waits for them, and re-layouts  5 us (2%)
  other arithmetic  4.57 us (2%)
    pallas_call x3, Pallas kernels, head_rows(): call(head_body, out_shape=jax.ShapeDtypeStruct((VL, DX), BF16), grid_spec...  24.5 us
    pallas_call x1, Pallas kernels, student(): call(student_body, out_shape=[jax.ShapeDtypeStruct((NS * SB, T), F32), pa...  20.4 us
    pallas_call x1, Pallas kernels, hidden_part(): call(hidden_body, out_shape=[jax.ShapeDtypeStruct((4, 4, T, 128), BF16)]...  17.3 us
    ppermute x6, waiting for transfers between devices, shift(): return lax.ppermute(x, 'x', [(i, (i + n) % 4) for i in range(4)])  14.5 us
    ppermute x6, waiting for transfers between devices, spread(): got.append(lax.ppermute(x, V, pairs))  13.6 us
    all_gather x2, waiting for transfers between devices, per_device(): all_u, all_m = (lax.all_gather(gu, 'x'), lax.all_gather(gm, 'x'))  10.5 us
    pallas_call x2, Pallas kernels, grad(): call(functools.partial(grad_body, cuts), out_shape=[jax.ShapeDtypeStruct(...  10.4 us
    ppermute x6, starting transfers between devices, spread(): got.append(lax.ppermute(x, V, pairs))  10.1 us
  transfers between devices with their start and end apart: 27, of which 16 were waited for; matrix products, arithmetic and copies ran while one was open for 3% of the time, Pallas kernels for 37%

profile of v9, /device:TPU:1, one launch (start us, length us, event | category | flops | bytes accessed | tf_op | source)
XLA Modules:
  0.0 217.9 jit_solution(10774346091620595629)
XLA Ops:
  7.2 3.6 %collective-permute-start.2 = (bf16[512,128]{1,0:T(8,128)(2,1)}, bf16[512,128]{1,0:T(8,128)(2,1)S(1)}, u32[]{:S(2)}, u32[]{:S(2)}) collective-permute-start(bf16[512,128]{1,0:T(8,128)(2,1)} %param.4), channel_id=1, source_target_pairs={{0,6},{1,25},{2,0},{3,27},{4,2},{5,29},{6,4},{7,31},{8,14},{9,1},{... | collective-permute-start | bytes 393224 | tf_op jit(solution)/shard_map/ppermute | solution.py:349
  11.2 0.7 collective-permute-start
  11.8 4.4 %shard_map.67 = bf16[32,19,16,128]{3,2,1,0:T(8,128)(2,1)} custom-call(bf16[16,75968]{1,0:T(8,128)(2,1)} %t_ref.1), custom_call_target="tpu_custom_call" | custom-call | flops 1048576 | bytes 65536 | tf_op jit(solution)/shard_map/pallas_call | solution.py:55
  16.4 1.6 collective-permute-done
  18.1 1.4 collective-permute-start.3
  19.5 3.3 %collective-permute-start.4 = (bf16[4,512,128]{2,1,0:T(8,128)(2,1)S(1)}, bf16[4,512,128]{2,1,0:T(8,128)(2,1)}, u32[]{:S(2)}, u32[]{:S(2)}) collective-permute-start(bf16[4,512,128]{2,1,0:T(8,128)(2,1)S(1)} %pad_maximum_fusion.1.refs_0_), channel_id=1, source_target_pairs={{0,16},{1,5},{2,18},{3,7},{4,20},{5,1},{6,22},{7,3},{8,24},{9,13},... | collective-permute-start | bytes 1572872 | tf_op jit(solution)/shard_map/ppermute | solution.py:349
  22.8 0.7 collective-permute-start.5
  23.6 5.0 %collective-permute-done.3.refs_1_ = bf16[4,512,128]{2,1,0:T(8,128)(2,1)S(1)} collective-permute-done((bf16[4,512,128]{2,1,0:T(8,128)(2,1)S(1)}, bf16[4,512,128]{2,1,0:T(8,128)(2,1)S(1)}, u32[]{:S(2)}, u32[]{:S(2)}) %collective-permute-start.3) | collective-permute-done | bytes 524320 | tf_op jit(solution)/shard_map/ppermute | solution.py:349
  28.5 6.9 %collective-permute-done.4.refs_2_ = bf16[4,512,128]{2,1,0:T(8,128)(2,1)} collective-permute-done((bf16[4,512,128]{2,1,0:T(8,128)(2,1)S(1)}, bf16[4,512,128]{2,1,0:T(8,128)(2,1)}, u32[]{:S(2)}, u32[]{:S(2)}) %collective-permute-start.4) | collective-permute-done | bytes 524320 | tf_op jit(solution)/shard_map/ppermute | solution.py:349
  35.4 7.3 %all-to-all-start = ((bf16[32,19,16,128]{3,2,1,0:T(8,128)(2,1)}), bf16[32,19,16,128]{3,2,1,0:T(8,128)(2,1)S(1)}, u32[]{:S(2)}, u32[]{:S(2)}) async-start(bf16[32,19,16,128]{3,2,1,0:T(8,128)(2,1)} %shard_map.67), calls=%async_computation | async-start | bytes 4980736 | tf_op jit(solution)/shard_map/all_to_all | solution.py:363
  43.9 0.7 pad_add_fusion.pos
  44.9 1.5 collective-permute-done.7.refs_5_
  46.6 0.8 collective-permute-done.9.refs_7_
  47.3 20.4 %shard_map.68 = (f32[2560,512]{1,0:T(8,128)}, f32[8,512]{1,0:T(8,128)}, f32[8,512]{1,0:T(8,128)}, bf16[512,1024]{1,0:T(8,128)(2,1)}, bf16[4,512,128]{2,1,0:T(8,1...) custom-call(s32[4]{0:T(128)} %pad_add_fusion.pos, bf16[2374,4096]{1,0:T(8,128)(2,1)} %bitcast.19, ...), custom_call_target="tpu_custom_call" | custom-call | flops 1048576 | bytes 65536 | tf_op jit(solution)/shard_map/pallas_call | solution.py:103
  67.8 2.5 %collective-permute-start.12 = (bf16[4,512,128]{2,1,0:T(8,128)(2,1)}, bf16[4,512,128]{2,1,0:T(8,128)(2,1)}, u32[]{:S(2)}, u32[]{:S(2)}) collective-permute-start(bf16[4,512,128]{2,1,0:T(8,128)(2,1)} %get-tuple-element.40), channel_id=1, source_target_pairs={{0,32},{1,97},{32,64},{33,1},{64,96},{65,33},{96,0},{97,65},{2,34}... | collective-permute-start | bytes 1572872 | tf_op jit(solution)/shard_map/ppermute | solution.py:333
  70.3 2.7 %collective-permute-start.11 = (bf16[4,512,128]{2,1,0:T(8,128)(2,1)}, bf16[4,512,128]{2,1,0:T(8,128)(2,1)S(1)}, u32[]{:S(2)}, u32[]{:S(2)}) collective-permute-start(bf16[4,512,128]{2,1,0:T(8,128)(2,1)} %get-tuple-element.39), channel_id=1, source_target_pairs={{0,96},{32,0},{64,32},{96,64},{1,97},{33,1},{65,33},{97,65},{2,98}... | collective-permute-start | bytes 1572872 | tf_op jit(solution)/shard_map/ppermute | solution.py:329
  73.0 2.3 %all-to-all-done.t_ref = bf16[32,19,16,128]{3,2,1,0:T(8,128)(2,1)S(1)} async-done(((bf16[32,19,16,128]{3,2,1,0:T(8,128)(2,1)}), bf16[32,19,16,128]{3,2,1,0:T(8,128)(2,1)S(1)}, u32[]{:S(2)}, u32[]{:S(2)}) %all-to-all-start) | async-done | bytes 2490400 | tf_op jit(solution)/shard_map/all_to_all | solution.py:363
  75.3 1.5 copy-done
  76.8 7.3 %shard_map.69 = (bf16[2560,512]{1,0:T(8,128)(2,1)}, f32[32,8,512]{2,1,0:T(8,128)}) custom-call(f32[8,512]{1,0:T(8,128)} %get-tuple-element.33.m_ref, f32[8,512]{1,0:T(8,128)} %get-tuple-element.34.l_ref, f32[2560,512]{1,0:T(8,128)} %get-tuple-element.35.s_ref, bf16[32,19,16,128]{3,2,1,0:T(8,128)(2,1)} %copy-done), custom_call_target="tpu_custom_call" | custom-call | flops 1048576 | bytes 65536 | tf_op jit(solution)/shard_map/pallas_call | solution.py:172
  84.1 2.5 %collective-permute-start.13 = (bf16[4,512,128]{2,1,0:T(8,128)(2,1)}, bf16[4,512,128]{2,1,0:T(8,128)(2,1)S(1)}, u32[]{:S(2)}, u32[]{:S(2)}) collective-permute-start(bf16[4,512,128]{2,1,0:T(8,128)(2,1)} %collective-permute-done.12), channel_id=1, source_target_pairs={{0,32},{1,97},{32,64},{33,1},{64,96},{65,33},{96,0},{97,65},{2,34}... | collective-permute-start | bytes 1572872 | tf_op jit(solution)/shard_map/ppermute | solution.py:333
  86.7 4.8 %all-to-all-start.1 = ((f32[32,8,512]{2,1,0:T(8,128)}), f32[32,8,512]{2,1,0:T(8,128)S(1)}, u32[]{:S(2)}, u32[]{:S(2)}) async-start(f32[32,8,512]{2,1,0:T(8,128)} %get-tuple-element.37), calls=%async_computation.1 | async-start | bytes 1048576 | tf_op jit(solution)/shard_map/all_to_all | solution.py:366
  91.7 1.9 collective-permute-done.13.refs_4_
  93.6 9.5 %all-to-all-done.1.all_ref = f32[32,8,512]{2,1,0:T(8,128)S(1)} async-done(((f32[32,8,512]{2,1,0:T(8,128)}), f32[32,8,512]{2,1,0:T(8,128)S(1)}, u32[]{:S(2)}, u32[]{:S(2)}) %all-to-all-start.1) | async-done | bytes 524320 | tf_op jit(solution)/shard_map/all_to_all | solution.py:366
  103.1 0.8 copy-done.1
  103.9 5.2 %shard_map.70 = (bf16[1216,512]{1,0:T(8,128)(2,1)}, f32[1,512]{1,0:T(1,128)}) custom-call(f32[32,8,512]{2,1,0:T(8,128)} %copy-done.1, f32[1,512]{1,0:T(1,128)} %bitcast.30, f32[2560,512]{1,0:T(8,128)} %get-tuple-element.35.s_ref, bf16[2560,512]{1,0:T(8,128)(2,1)} %get-tuple-element.43.t_ref), custom_call_target="tpu_custom_call" | custom-call | flops 1048576 | bytes 65536 | tf_op jit(solution)/shard_map/pallas_call | solution.py:222
  109.1 5.2 %shard_map.71 = (bf16[304,512]{1,0:T(8,128)(2,1)}, bf16[912,512]{1,0:T(8,128)(2,1)}, f32[1,512]{1,0:T(1,128)}) custom-call(f32[32,8,512]{2,1,0:T(8,128)} %copy-done.1, f32[1,512]{1,0:T(1,128)} %bitcast.31, f32[2560,512]{1,0:T(8,128)} %get-tuple-element.35.s_ref, bf16[2560,512]{1,0:T(8,128)(2,1)} %get-tuple-element.43.t_ref), custom_call_target="tpu_custom_call" | custom-call | flops 1048576 | bytes 65536 | tf_op jit(solution)/shard_map/pallas_call | solution.py:222
  114.3 1.1 collective-permute-start.17
  115.3 1.6 collective-permute-start.18
  117.8 17.3 %shard_map.72 = (bf16[4,4,512,128]{3,2,1,0:T(8,128)(2,1)}, bf16[4,4,512,128]{3,2,1,0:T(8,128)(2,1)}) custom-call(s32[4]{0:T(128)} %pad_add_fusion.pos, bf16[1216,512]{1,0:T(8,128)(2,1)} %get-tuple-element.45.refs_0_, bf16[304,512]{1,0:T(8,128)(2,1)} %get-tuple-element.47.refs_1_, bf16[912,512]{1,0:T(8,128)(2,1)} %get-tuple-element.48.refs_2_.refs_0_, ...), custom_call_target="tpu_custom_call" | custom-call | flops 1048576 | bytes 65536 | tf_op jit(solution)/shard_map/pallas_call | solution.py:256
  135.1 0.8 copy-done.9
  135.9 5.9 %shard_map.73.refs_4_ = bf16[2048,1024]{1,0:T(8,128)(2,1)} custom-call(s32[4]{0:T(128)} %pad_add_fusion.pos, bf16[512,1024]{1,0:T(8,128)(2,1)} %get-tuple-element.52.h_ref, bf16[4,512,128]{2,1,0:T(8,128)(2,1)} %copy-done.5, bf16[4,512,128]{2,1,0:T(8,128)(2,1)} %copy-done.9, bf16[4,512,128]{2,1,0:T(8,128)(2,1)} %copy-done.6, ...), custom_call_target="tpu_custom_call" | custom-call | flops 1048576 | bytes 65536 | tf_op jit(solution)/shard_map/pallas_call | solution.py:280
  141.8 13.5 %collective-permute-done.17.refs_1_ = bf16[912,512]{1,0:T(8,128)(2,1)S(1)} collective-permute-done((bf16[912,512]{1,0:T(8,128)(2,1)}, bf16[912,512]{1,0:T(8,128)(2,1)S(1)}, u32[]{:S(2)}, u32[]{:S(2)}) %collective-permute-start.17) | collective-permute-done | bytes 933920 | tf_op jit(solution)/shard_map/ppermute | solution.py:329
  155.3 1.0 collective-permute-done.18.refs_2_
  156.3 1.8 collective-permute-start.19
  158.1 4.0 %collective-permute-done.19 = bf16[4,4,512,128]{3,2,1,0:T(8,128)(2,1)S(1)} collective-permute-done((bf16[4,4,512,128]{3,2,1,0:T(8,128)(2,1)}, bf16[4,4,512,128]{3,2,1,0:T(8,128)(2,1)S(1)}, u32[]{:S(2)}, u32[]{:S(2)}) %collective-permute-start.19) | collective-permute-done | bytes 2097184 | tf_op jit(solution)/shard_map/ppermute | solution.py:337
  162.1 1.8 add_convert_fusion
  163.9 3.7 %all-to-all-start.2 = ((bf16[16,512,128]{2,1,0:T(8,128)(2,1)}), bf16[16,512,128]{2,1,0:T(8,128)(2,1)S(1)}, u32[]{:S(2)}, u32[]{:S(2)}) async-start(bf16[16,512,128]{2,1,0:T(8,128)(2,1)} %bitcast.11), calls=%async_computation.2 | async-start | bytes 4194304 | tf_op jit(solution)/shard_map/all_to_all | solution.py:388
  167.7 0.7 all-gather.7.cloned.1.call-update
  168.4 0.8 slice.8
  169.2 1.0 slice.9
  170.3 3.7 %collective-permute-start.21 = (bf16[448,512]{1,0:T(8,128)(2,1)S(1)}, bf16[448,512]{1,0:T(8,128)(2,1)S(1)}, u32[]{:S(2)}, u32[]{:S(2)}) collective-permute-start(bf16[448,512]{1,0:T(8,128)(2,1)S(1)} %slice.9), channel_id=1, source_target_pairs={{0,96},{32,0},{64,32},{96,64},{1,97},{33,1},{65,33},{97,65},{2,98}... | collective-permute-start | bytes 1376264 | tf_op jit(solution)/shard_map/ppermute | solution.py:329
  174.0 9.3 %all-gather.5.cloned.1.call-done = bf16[4864,512]{1,0:T(8,128)(2,1)} async-done(((bf16[1216,512]{1,0:T(8,128)(2,1)}), bf16[4864,512]{1,0:T(8,128)(2,1)}) %all-gather.5.cloned.1.call-update) | async-done | bytes 4980752 | tf_op jit(solution)/shard_map/all_gather | solution.py:381
  183.3 10.4 %shard_map.74.refs_5_ = bf16[2374,1024]{1,0:T(8,128)(2,1)} custom-call(s32[4]{0:T(128)} %pad_add_fusion.pos, bf16[4,1216,512]{2,1,0:T(8,128)(2,1)} %bitcast.15, bf16[4,1216,512]{2,1,0:T(8,128)(2,1)} %bitcast.16, bf16[4,1216,512]{2,1,0:T(8,128)(2,1)} %bitcast.17, bf16[4,1216,512]{2,1,0:T(8,128)(2,1)} %bitcast.18, bf16[2048,1024]{1,0:T(8,128)(2,1)} %shard_map.73.refs_4_), custom_call_target="tpu_custom_call" | custom-call | flops 1048576 | bytes 65536 | tf_op jit(solution)/shard_map/pallas_call | solution.py:315
  193.7 1.1 pad_maximum_fusion.refs_3_
  194.8 8.6 %shard_map.75.refs_5_ = bf16[2374,1024]{1,0:T(8,128)(2,1)} custom-call(s32[4]{0:T(128)} %pad_add_fusion.pos, bf16[912,512]{1,0:T(8,128)(2,1)} %get-tuple-element.48.refs_2_.refs_0_, bf16[912,512]{1,0:T(8,128)(2,1)} %copy-done.2, bf16[912,512]{1,0:T(8,128)(2,1)} %collective-permute-done.18.refs_2_, ...), custom_call_target="tpu_custom_call", output_to_operand_aliasing={{}: (6, {})} | custom-call | flops 1048576 | bytes 65536 | tf_op jit(solution)/shard_map/pallas_call | solution.py:315
  203.4 1.0 reduce_sum.12
  204.3 1.3 all-gather.7.cloned.1.call-done
  205.6 5.4 %shard_map.76 = bf16[2374,1024]{1,0:T(8,128)(2,1)} custom-call(s32[4]{0:T(128)} %pad_add_fusion.pos, bf16[4,304,512]{2,1,0:T(8,128)(2,1)} %bitcast.22, bf16[4,304,512]{2,1,0:T(8,128)(2,1)} %bitcast.23, bf16[4,304,512]{2,1,0:T(8,128)(2,1)} %bitcast.24, bf16[4,304,512]{2,1,0:T(8,128)(2,1)} %bitcast.25, ...), custom_call_target="tpu_custom_call", output_to_operand_aliasing={{}: (6, {})} | custom-call | flops 1048576 | bytes 65536 | tf_op jit(solution)/shard_map/pallas_call | solution.py:315
  (47 shorter events, 3.4 us)
Async XLA Ops:
  7.2 10.9 %copy-start.10 = (bf16[512,128]{1,0:T(8,128)(2,1)S(1)}, bf16[512,128]{1,0:T(8,128)(2,1)}, u32[]{:S(2)}) copy-start(bf16[512,128]{1,0:T(8,128)(2,1)} %param.4) | copy-start | bytes 393220
  7.2 9.1 %collective-permute-start.2 = (bf16[512,128]{1,0:T(8,128)(2,1)}, bf16[512,128]{1,0:T(8,128)(2,1)S(1)}, u32[]{:S(2)}, u32[]{:S(2)}) collective-permute-start(bf16[512,128]{1,0:T(8,128)(2,1)} %param.4), channel_id=1, source_target_pairs={{0,6},{1,25},{2,0},{3,27},{4,2},{5,29},{6,4},{7,31},{8,14},{9,1},{... | collective-permute-start | bytes 393224 | tf_op jit(solution)/shard_map/ppermute | solution.py:349
  10.8 5.6 %collective-permute-start.1 = (bf16[512,128]{1,0:T(8,128)(2,1)}, bf16[512,128]{1,0:T(8,128)(2,1)S(1)}, u32[]{:S(2)}, u32[]{:S(2)}) collective-permute-start(bf16[512,128]{1,0:T(8,128)(2,1)} %param.4), channel_id=1, source_target_pairs={{0,4},{1,17},{2,6},{3,19},{4,0},{5,21},{6,2},{7,23},{8,12},{9,25},... | collective-permute-start | bytes 393224 | tf_op jit(solution)/shard_map/ppermute | solution.py:349
  11.2 6.9 %collective-permute-start = (bf16[512,128]{1,0:T(8,128)(2,1)}, bf16[512,128]{1,0:T(8,128)(2,1)S(1)}, u32[]{:S(2)}, u32[]{:S(2)}) collective-permute-start(bf16[512,128]{1,0:T(8,128)(2,1)} %param.4), channel_id=1, source_target_pairs={{0,2},{1,9},{2,4},{3,11},{4,6},{5,13},{6,0},{7,15},{8,10},{9,17},{... | collective-permute-start | bytes 393224 | tf_op jit(solution)/shard_map/ppermute | solution.py:349
  18.1 24.6 %copy-start.4 = (bf16[4,512,128]{2,1,0:T(8,128)(2,1)}, bf16[4,512,128]{2,1,0:T(8,128)(2,1)S(1)}, u32[]{:S(2)}) copy-start(bf16[4,512,128]{2,1,0:T(8,128)(2,1)S(1)} %pad_maximum_fusion.1.refs_0_) | copy-start | bytes 1572868
  18.1 10.4 %collective-permute-start.3 = (bf16[4,512,128]{2,1,0:T(8,128)(2,1)S(1)}, bf16[4,512,128]{2,1,0:T(8,128)(2,1)S(1)}, u32[]{:S(2)}, u32[]{:S(2)}) collective-permute-start(bf16[4,512,128]{2,1,0:T(8,128)(2,1)S(1)} %pad_maximum_fusion.1.refs_0_), channel_id=1, source_target_pairs={{0,8},{1,3},{2,10},{3,5},{4,12},{5,7},{6,14},{7,1},{8,16},{9,11},{... | collective-permute-start | bytes 1572872 | tf_op jit(solution)/shard_map/ppermute | solution.py:349
  19.5 15.9 %collective-permute-start.4 = (bf16[4,512,128]{2,1,0:T(8,128)(2,1)S(1)}, bf16[4,512,128]{2,1,0:T(8,128)(2,1)}, u32[]{:S(2)}, u32[]{:S(2)}) collective-permute-start(bf16[4,512,128]{2,1,0:T(8,128)(2,1)S(1)} %pad_maximum_fusion.1.refs_0_), channel_id=1, source_target_pairs={{0,16},{1,5},{2,18},{3,7},{4,20},{5,1},{6,22},{7,3},{8,24},{9,13},... | collective-permute-start | bytes 1572872 | tf_op jit(solution)/shard_map/ppermute | solution.py:349
  22.8 12.6 %collective-permute-start.5 = (bf16[4,512,128]{2,1,0:T(8,128)(2,1)S(1)}, bf16[4,512,128]{2,1,0:T(8,128)(2,1)}, u32[]{:S(2)}, u32[]{:S(2)}) collective-permute-start(bf16[4,512,128]{2,1,0:T(8,128)(2,1)S(1)} %pad_maximum_fusion.1.refs_0_), channel_id=1, source_target_pairs={{0,24},{1,7},{2,26},{3,1},{4,28},{5,3},{6,30},{7,5},{8,0},{9,15},{... | collective-permute-start | bytes 1572872 | tf_op jit(solution)/shard_map/ppermute | solution.py:349
  28.5 14.5 %copy-start.7 = (bf16[4,512,128]{2,1,0:T(8,128)(2,1)}, bf16[4,512,128]{2,1,0:T(8,128)(2,1)S(1)}, u32[]{:S(2)}) copy-start(bf16[4,512,128]{2,1,0:T(8,128)(2,1)S(1)} %collective-permute-done.3.refs_1_) | copy-start | bytes 1572868
  35.4 39.8 %all-to-all-start = ((bf16[32,19,16,128]{3,2,1,0:T(8,128)(2,1)}), bf16[32,19,16,128]{3,2,1,0:T(8,128)(2,1)S(1)}, u32[]{:S(2)}, u32[]{:S(2)}) async-start(bf16[32,19,16,128]{3,2,1,0:T(8,128)(2,1)} %shard_map.67), calls=%async_computation | async-start | bytes 4980736 | tf_op jit(solution)/shard_map/all_to_all | solution.py:363
  42.7 2.1 collective-permute-start.6
  43.1 3.3 %collective-permute-start.7 = (bf16[4,512,128]{2,1,0:T(8,128)(2,1)S(1)}, bf16[4,512,128]{2,1,0:T(8,128)(2,1)}, u32[]{:S(2)}, u32[]{:S(2)}) collective-permute-start(bf16[4,512,128]{2,1,0:T(8,128)(2,1)S(1)} %collective-permute-done.3.refs_1_), channel_id=1, source_target_pairs={{0,1},{1,0},{2,3},{3,2},{4,5},{5,4},{6,7},{7,6},{8,9},{9,8},{10,11... | collective-permute-start | bytes 1572872 | tf_op jit(solution)/shard_map/ppermute | solution.py:337
  43.3 3.2 %collective-permute-start.8 = (bf16[4,512,128]{2,1,0:T(8,128)(2,1)}, bf16[4,512,128]{2,1,0:T(8,128)(2,1)}, u32[]{:S(2)}, u32[]{:S(2)}) collective-permute-start(bf16[4,512,128]{2,1,0:T(8,128)(2,1)} %collective-permute-done.4.refs_2_), channel_id=1, source_target_pairs={{0,1},{1,0},{2,3},{3,2},{4,5},{5,4},{6,7},{7,6},{8,9},{9,8},{10,11... | collective-permute-start | bytes 1572872 | tf_op jit(solution)/shard_map/ppermute | solution.py:337
  43.6 3.8 %collective-permute-start.9 = (bf16[4,512,128]{2,1,0:T(8,128)(2,1)}, bf16[4,512,128]{2,1,0:T(8,128)(2,1)}, u32[]{:S(2)}, u32[]{:S(2)}) collective-permute-start(bf16[4,512,128]{2,1,0:T(8,128)(2,1)} %collective-permute-done.5.refs_3_), channel_id=1, source_target_pairs={{0,1},{1,0},{2,3},{3,2},{4,5},{5,4},{6,7},{7,6},{8,9},{9,8},{10,11... | collective-permute-start | bytes 1572872 | tf_op jit(solution)/shard_map/ppermute | solution.py:337
  67.8 16.3 %collective-permute-start.12 = (bf16[4,512,128]{2,1,0:T(8,128)(2,1)}, bf16[4,512,128]{2,1,0:T(8,128)(2,1)}, u32[]{:S(2)}, u32[]{:S(2)}) collective-permute-start(bf16[4,512,128]{2,1,0:T(8,128)(2,1)} %get-tuple-element.40), channel_id=1, source_target_pairs={{0,32},{1,97},{32,64},{33,1},{64,96},{65,33},{96,0},{97,65},{2,34}... | collective-permute-start | bytes 1572872 | tf_op jit(solution)/shard_map/ppermute | solution.py:333
  70.3 21.4 %collective-permute-start.10 = (bf16[4,512,128]{2,1,0:T(8,128)(2,1)}, bf16[4,512,128]{2,1,0:T(8,128)(2,1)S(1)}, u32[]{:S(2)}, u32[]{:S(2)}) collective-permute-start(bf16[4,512,128]{2,1,0:T(8,128)(2,1)} %get-tuple-element.38), channel_id=1, source_target_pairs={{0,32},{32,64},{64,96},{96,0},{1,33},{33,65},{65,97},{97,1},{2,34}... | collective-permute-start | bytes 1572872 | tf_op jit(solution)/shard_map/ppermute | solution.py:329
  70.3 21.4 %collective-permute-start.11 = (bf16[4,512,128]{2,1,0:T(8,128)(2,1)}, bf16[4,512,128]{2,1,0:T(8,128)(2,1)S(1)}, u32[]{:S(2)}, u32[]{:S(2)}) collective-permute-start(bf16[4,512,128]{2,1,0:T(8,128)(2,1)} %get-tuple-element.39), channel_id=1, source_target_pairs={{0,96},{32,0},{64,32},{96,64},{1,97},{33,1},{65,33},{97,65},{2,98}... | collective-permute-start | bytes 1572872 | tf_op jit(solution)/shard_map/ppermute | solution.py:329
  75.3 1.5 copy-start
  84.1 9.5 %collective-permute-start.13 = (bf16[4,512,128]{2,1,0:T(8,128)(2,1)}, bf16[4,512,128]{2,1,0:T(8,128)(2,1)S(1)}, u32[]{:S(2)}, u32[]{:S(2)}) collective-permute-start(bf16[4,512,128]{2,1,0:T(8,128)(2,1)} %collective-permute-done.12), channel_id=1, source_target_pairs={{0,32},{1,97},{32,64},{33,1},{64,96},{65,33},{96,0},{97,65},{2,34}... | collective-permute-start | bytes 1572872 | tf_op jit(solution)/shard_map/ppermute | solution.py:333
  86.7 16.4 %all-to-all-start.1 = ((f32[32,8,512]{2,1,0:T(8,128)}), f32[32,8,512]{2,1,0:T(8,128)S(1)}, u32[]{:S(2)}, u32[]{:S(2)}) async-start(f32[32,8,512]{2,1,0:T(8,128)} %get-tuple-element.37), calls=%async_computation.1 | async-start | bytes 1048576 | tf_op jit(solution)/shard_map/all_to_all | solution.py:366
  91.5 91.8 %all-gather.5.cloned.1.call-start = ((), (), s32[]{:S(2)}) async-start(), calls=%async_computation.3 | async-start | bytes 6225920 | tf_op jit(solution)/shard_map/all_gather | solution.py:381
  91.7 25.3 %copy-start.5 = (bf16[4,512,128]{2,1,0:T(8,128)(2,1)}, bf16[4,512,128]{2,1,0:T(8,128)(2,1)S(1)}, u32[]{:S(2)}) copy-start(bf16[4,512,128]{2,1,0:T(8,128)(2,1)S(1)} %collective-permute-done.10.refs_0_) | copy-start | bytes 1572868
  91.7 25.6 %copy-start.6 = (bf16[4,512,128]{2,1,0:T(8,128)(2,1)}, bf16[4,512,128]{2,1,0:T(8,128)(2,1)S(1)}, u32[]{:S(2)}) copy-start(bf16[4,512,128]{2,1,0:T(8,128)(2,1)S(1)} %collective-permute-done.11.refs_2_) | copy-start | bytes 1572868
  93.6 23.9 %copy-start.8 = (bf16[4,512,128]{2,1,0:T(8,128)(2,1)}, bf16[4,512,128]{2,1,0:T(8,128)(2,1)S(1)}, u32[]{:S(2)}) copy-start(bf16[4,512,128]{2,1,0:T(8,128)(2,1)S(1)} %collective-permute-done.13.refs_4_) | copy-start | bytes 1572868
  103.1 0.8 copy-start.1
  114.3 41.1 %collective-permute-start.17 = (bf16[912,512]{1,0:T(8,128)(2,1)}, bf16[912,512]{1,0:T(8,128)(2,1)S(1)}, u32[]{:S(2)}, u32[]{:S(2)}) collective-permute-start(bf16[912,512]{1,0:T(8,128)(2,1)} %get-tuple-element.48.refs_2_.refs_0_), channel_id=1, source_target_pairs={{0,32},{32,64},{64,96},{96,0},{1,33},{33,65},{65,97},{97,1},{2,34}... | collective-permute-start | bytes 2801672 | tf_op jit(solution)/shard_map/ppermute | solution.py:329
  115.3 41.0 %collective-permute-start.18 = (bf16[912,512]{1,0:T(8,128)(2,1)}, bf16[912,512]{1,0:T(8,128)(2,1)}, u32[]{:S(2)}, u32[]{:S(2)}) collective-permute-start(bf16[912,512]{1,0:T(8,128)(2,1)} %get-tuple-element.48.refs_2_.refs_0_), channel_id=1, source_target_pairs={{0,96},{32,0},{64,32},{96,64},{1,97},{33,1},{65,33},{97,65},{2,98}... | collective-permute-start | bytes 2801672 | tf_op jit(solution)/shard_map/ppermute | solution.py:329
  117.0 18.2 %collective-permute-start.14 = (bf16[4,512,128]{2,1,0:T(8,128)(2,1)S(1)}, bf16[4,512,128]{2,1,0:T(8,128)(2,1)S(1)}, u32[]{:S(2)}, u32[]{:S(2)}) collective-permute-start(bf16[4,512,128]{2,1,0:T(8,128)(2,1)S(1)} %collective-permute-done.10.refs_0_), channel_id=1, source_target_pairs={{0,1},{1,0},{2,3},{3,2},{4,5},{5,4},{6,7},{7,6},{8,9},{9,8},{10,11... | collective-permute-start | bytes 1572872 | tf_op jit(solution)/shard_map/ppermute | solution.py:337
  117.3 17.8 %collective-permute-start.15 = (bf16[4,512,128]{2,1,0:T(8,128)(2,1)S(1)}, bf16[4,512,128]{2,1,0:T(8,128)(2,1)}, u32[]{:S(2)}, u32[]{:S(2)}) collective-permute-start(bf16[4,512,128]{2,1,0:T(8,128)(2,1)S(1)} %collective-permute-done.11.refs_2_), channel_id=1, source_target_pairs={{0,1},{1,0},{2,3},{3,2},{4,5},{5,4},{6,7},{7,6},{8,9},{9,8},{10,11... | collective-permute-start | bytes 1572872 | tf_op jit(solution)/shard_map/ppermute | solution.py:337
  117.5 17.7 %collective-permute-start.16 = (bf16[4,512,128]{2,1,0:T(8,128)(2,1)S(1)}, bf16[4,512,128]{2,1,0:T(8,128)(2,1)}, u32[]{:S(2)}, u32[]{:S(2)}) collective-permute-start(bf16[4,512,128]{2,1,0:T(8,128)(2,1)S(1)} %collective-permute-done.13.refs_4_), channel_id=1, source_target_pairs={{0,1},{1,0},{2,3},{3,2},{4,5},{5,4},{6,7},{7,6},{8,9},{9,8},{10,11... | collective-permute-start | bytes 1572872 | tf_op jit(solution)/shard_map/ppermute | solution.py:337
  135.1 0.8 copy-start.9
  135.9 26.2 %copy-start.3 = (bf16[4,4,512,128]{3,2,1,0:T(8,128)(2,1)S(1)}, bf16[4,4,512,128]{3,2,1,0:T(8,128)(2,1)}, u32[]{:S(2)}) copy-start(bf16[4,4,512,128]{3,2,1,0:T(8,128)(2,1)} %get-tuple-element.49) | copy-start | bytes 6291460
  155.3 13.1 %copy-start.2 = (bf16[912,512]{1,0:T(8,128)(2,1)}, bf16[912,512]{1,0:T(8,128)(2,1)S(1)}, u32[]{:S(2)}) copy-start(bf16[912,512]{1,0:T(8,128)(2,1)S(1)} %collective-permute-done.17.refs_1_) | copy-start | bytes 2801668
  156.3 5.8 %collective-permute-start.19 = (bf16[4,4,512,128]{3,2,1,0:T(8,128)(2,1)}, bf16[4,4,512,128]{3,2,1,0:T(8,128)(2,1)S(1)}, u32[]{:S(2)}, u32[]{:S(2)}) collective-permute-start(bf16[4,4,512,128]{3,2,1,0:T(8,128)(2,1)} %get-tuple-element.56), channel_id=1, source_target_pairs={{0,1},{1,0},{2,3},{3,2},{4,5},{5,4},{6,7},{7,6},{8,9},{9,8},{10,11... | collective-permute-start | bytes 6291464 | tf_op jit(solution)/shard_map/ppermute | solution.py:337
  163.9 39.5 %all-to-all-start.2 = ((bf16[16,512,128]{2,1,0:T(8,128)(2,1)}), bf16[16,512,128]{2,1,0:T(8,128)(2,1)S(1)}, u32[]{:S(2)}, u32[]{:S(2)}) async-start(bf16[16,512,128]{2,1,0:T(8,128)(2,1)} %bitcast.11), calls=%async_computation.2 | async-start | bytes 4194304 | tf_op jit(solution)/shard_map/all_to_all | solution.py:388
  167.6 37.9 %all-gather.7.cloned.1.call-start = ((), (), s32[]{:S(2)}) async-start(), calls=%async_computation.4 | async-start | bytes 1556480 | tf_op jit(solution)/shard_map/all_gather | solution.py:381
  169.2 24.5 %collective-permute-start.20 = (bf16[464,512]{1,0:T(8,128)(2,1)}, bf16[464,512]{1,0:T(8,128)(2,1)S(1)}, u32[]{:S(2)}, u32[]{:S(2)}) collective-permute-start(bf16[464,512]{1,0:T(8,128)(2,1)} %slice.8), channel_id=1, source_target_pairs={{0,32},{32,64},{64,96},{96,0},{1,33},{33,65},{65,97},{97,1},{2,34}... | collective-permute-start | bytes 1425416 | tf_op jit(solution)/shard_map/ppermute | solution.py:329
  170.3 23.4 %collective-permute-start.21 = (bf16[448,512]{1,0:T(8,128)(2,1)S(1)}, bf16[448,512]{1,0:T(8,128)(2,1)S(1)}, u32[]{:S(2)}, u32[]{:S(2)}) collective-permute-start(bf16[448,512]{1,0:T(8,128)(2,1)S(1)} %slice.9), channel_id=1, source_target_pairs={{0,96},{32,0},{64,32},{96,64},{1,97},{33,1},{65,33},{97,65},{2,98}... | collective-permute-start | bytes 1376264 | tf_op jit(solution)/shard_map/ppermute | solution.py:329
Sparse Core Ops, SparseCore 0:
  109.2 74.0 all-gather.4
  184.9 20.6 all-gather.6

commit v10 on v9

--- a/solution.py
+++ b/solution.py
@@ -384,7 +384,7 @@
     mine, other = hidden_part(pos, (gu, gm, gl), wt)
     others = [x for other in others for x in (other, swap(after(other, gathered)))]
     k = tokens(after(pos, mine), h, others)
-    both = (mine.astype(F32) + swap(after(other, k, *near_l[1:])).astype(F32)).astype(BF16)
+    both = (mine.astype(F32) + swap(after(other, k)).astype(F32)).astype(BF16)
     got = lax.all_to_all(both.reshape(16, T, 128), ("y", "z"), 0, 0, tiled=True)
 
     head = head_rows(pos, [all_u], k, *CUTS[0])

time: 219 us -> 227 us (1.037)
  waiting for transfers between devices: 59.8 us -> 69.5 us
  starting transfers between devices: 44 us -> 40.7 us
    ppermute x6, waiting for transfers between devices: 14.5 us -> 34.8 us  [shift(): return lax.ppermute(x, 'x', [(i, (i + n) % 4) for i in range(4)])]
    all_gather x2, waiting for transfers between devices: 10.5 us -> 0.01 us  [per_device(): all_u, all_m = (lax.all_gather(gu, 'x'), lax.all_gather(gm, 'x'))]
    unnamed x22 -> x32, local copies, waits for them, and re-layouts: 3.13 us -> 5.52 us
  transfers between devices with their start and end apart: 27 -> 27, of which waited for: 16 -> 15; matrix products, arithmetic and copies ran while one was open for 3% -> 2% of each run, Pallas kernels for 37% -> 35%
where the time goes in v10:
time: 227 us; the launch traced here: 226 us
  Pallas kernels  90.9 us (40%)
  waiting for transfers between devices  69.5 us (31%)
  starting transfers between devices  40.7 us (18%)
  between operations  14.2 us (6%)
  local copies, waits for them, and re-layouts  6.43 us (3%)
  other arithmetic  4.56 us (2%)
    ppermute x6, waiting for transfers between devices, shift(): return lax.ppermute(x, 'x', [(i, (i + n) % 4) for i in range(4)])  34.8 us
    pallas_call x3, Pallas kernels, head_rows(): call(head_body, out_shape=jax.ShapeDtypeStruct((VL, DX), BF16), grid_spec...  24.5 us
    pallas_call x1, Pallas kernels, student(): call(student_body, out_shape=[jax.ShapeDtypeStruct((NS * SB, T), F32), pa...  20.4 us
    pallas_call x1, Pallas kernels, hidden_part(): call(hidden_body, out_shape=[jax.ShapeDtypeStruct((4, 4, T, 128), BF16)]...  17.8 us
    ppermute x6, waiting for transfers between devices, spread(): got.append(lax.ppermute(x, V, pairs))  13.5 us
    pallas_call x2, Pallas kernels, grad(): call(functools.partial(grad_body, cuts), out_shape=[jax.ShapeDtypeStruct(...  10.4 us
    ppermute x6, starting transfers between devices, spread(): got.append(lax.ppermute(x, V, pairs))  10.1 us
    all_to_all x1, waiting for transfers between devices, per_device(): gathered = lax.all_to_all(share, V, 0, 0, tiled=True)  9.46 us
  transfers between devices with their start and end apart: 27, of which 15 were waited for; matrix products, arithmetic and copies ran while one was open for 2% of the time, Pallas kernels for 35%

profile of v10, /device:TPU:1, one launch (start us, length us, event | category | flops | bytes accessed | tf_op | source)
XLA Modules:
  0.0 226.3 jit_solution(11953626142265273509)
XLA Ops:
  7.2 3.6 %collective-permute-start.2 = (bf16[512,128]{1,0:T(8,128)(2,1)}, bf16[512,128]{1,0:T(8,128)(2,1)S(1)}, u32[]{:S(2)}, u32[]{:S(2)}) collective-permute-start(bf16[512,128]{1,0:T(8,128)(2,1)} %param.4), channel_id=1, source_target_pairs={{0,6},{1,25},{2,0},{3,27},{4,2},{5,29},{6,4},{7,31},{8,14},{9,1},{... | collective-permute-start | bytes 393224 | tf_op jit(solution)/shard_map/ppermute | solution.py:349
  11.2 0.7 collective-permute-start
  11.8 4.4 %shard_map.67 = bf16[32,19,16,128]{3,2,1,0:T(8,128)(2,1)} custom-call(bf16[16,75968]{1,0:T(8,128)(2,1)} %t_ref.1), custom_call_target="tpu_custom_call" | custom-call | flops 1048576 | bytes 65536 | tf_op jit(solution)/shard_map/pallas_call | solution.py:55
  16.4 1.6 collective-permute-done
  18.1 1.4 collective-permute-start.3
  19.5 3.3 %collective-permute-start.4 = (bf16[4,512,128]{2,1,0:T(8,128)(2,1)S(1)}, bf16[4,512,128]{2,1,0:T(8,128)(2,1)S(1)}, u32[]{:S(2)}, u32[]{:S(2)}) collective-permute-start(bf16[4,512,128]{2,1,0:T(8,128)(2,1)S(1)} %pad_maximum_fusion.1.refs_0_), channel_id=1, source_target_pairs={{0,16},{1,5},{2,18},{3,7},{4,20},{5,1},{6,22},{7,3},{8,24},{9,13},... | collective-permute-start | bytes 1572872 | tf_op jit(solution)/shard_map/ppermute | solution.py:349
  22.8 0.7 collective-permute-start.5
  23.6 5.0 %collective-permute-done.3.refs_1_ = bf16[4,512,128]{2,1,0:T(8,128)(2,1)S(1)} collective-permute-done((bf16[4,512,128]{2,1,0:T(8,128)(2,1)S(1)}, bf16[4,512,128]{2,1,0:T(8,128)(2,1)S(1)}, u32[]{:S(2)}, u32[]{:S(2)}) %collective-permute-start.3) | collective-permute-done | bytes 524320 | tf_op jit(solution)/shard_map/ppermute | solution.py:349
  28.5 6.8 %collective-permute-done.4.refs_2_ = bf16[4,512,128]{2,1,0:T(8,128)(2,1)S(1)} collective-permute-done((bf16[4,512,128]{2,1,0:T(8,128)(2,1)S(1)}, bf16[4,512,128]{2,1,0:T(8,128)(2,1)S(1)}, u32[]{:S(2)}, u32[]{:S(2)}) %collective-permute-start.4) | collective-permute-done | bytes 524320 | tf_op jit(solution)/shard_map/ppermute | solution.py:349
  35.3 0.8 copy-done.10
  36.2 6.6 %all-to-all-start = ((bf16[32,19,16,128]{3,2,1,0:T(8,128)(2,1)}), bf16[32,19,16,128]{3,2,1,0:T(8,128)(2,1)S(1)}, u32[]{:S(2)}, u32[]{:S(2)}) async-start(bf16[32,19,16,128]{3,2,1,0:T(8,128)(2,1)} %shard_map.67), calls=%async_computation | async-start | bytes 4980736 | tf_op jit(solution)/shard_map/all_to_all | solution.py:363
  43.8 0.6 pad_add_fusion.pos
  44.9 1.5 collective-permute-done.7.refs_5_
  46.6 0.8 collective-permute-done.9.refs_7_
  47.3 20.4 %shard_map.68 = (f32[2560,512]{1,0:T(8,128)}, f32[8,512]{1,0:T(8,128)}, f32[8,512]{1,0:T(8,128)}, bf16[512,1024]{1,0:T(8,128)(2,1)}, bf16[4,512,128]{2,1,0:T(8,1...) custom-call(s32[4]{0:T(128)} %pad_add_fusion.pos, bf16[2374,4096]{1,0:T(8,128)(2,1)} %bitcast.19, ...), custom_call_target="tpu_custom_call" | custom-call | flops 1048576 | bytes 65536 | tf_op jit(solution)/shard_map/pallas_call | solution.py:103
  67.8 2.5 %collective-permute-start.12 = (bf16[4,512,128]{2,1,0:T(8,128)(2,1)}, bf16[4,512,128]{2,1,0:T(8,128)(2,1)}, u32[]{:S(2)}, u32[]{:S(2)}) collective-permute-start(bf16[4,512,128]{2,1,0:T(8,128)(2,1)} %get-tuple-element.40), channel_id=1, source_target_pairs={{0,32},{1,97},{32,64},{33,1},{64,96},{65,33},{96,0},{97,65},{2,34}... | collective-permute-start | bytes 1572872 | tf_op jit(solution)/shard_map/ppermute | solution.py:333
  70.3 2.7 %collective-permute-start.11 = (bf16[4,512,128]{2,1,0:T(8,128)(2,1)}, bf16[4,512,128]{2,1,0:T(8,128)(2,1)S(1)}, u32[]{:S(2)}, u32[]{:S(2)}) collective-permute-start(bf16[4,512,128]{2,1,0:T(8,128)(2,1)} %get-tuple-element.39), channel_id=1, source_target_pairs={{0,96},{32,0},{64,32},{96,64},{1,97},{33,1},{65,33},{97,65},{2,98}... | collective-permute-start | bytes 1572872 | tf_op jit(solution)/shard_map/ppermute | solution.py:329
  73.0 2.3 all-to-all-done.t_ref
  75.3 1.5 copy-done
  76.8 7.3 %shard_map.69 = (bf16[2560,512]{1,0:T(8,128)(2,1)}, f32[32,8,512]{2,1,0:T(8,128)}) custom-call(f32[8,512]{1,0:T(8,128)} %get-tuple-element.33.m_ref, f32[8,512]{1,0:T(8,128)} %get-tuple-element.34.l_ref, f32[2560,512]{1,0:T(8,128)} %get-tuple-element.35.s_ref, bf16[32,19,16,128]{3,2,1,0:T(8,128)(2,1)} %copy-done), custom_call_target="tpu_custom_call" | custom-call | flops 1048576 | bytes 65536 | tf_op jit(solution)/shard_map/pallas_call | solution.py:172
  84.1 2.5 %collective-permute-start.13 = (bf16[4,512,128]{2,1,0:T(8,128)(2,1)}, bf16[4,512,128]{2,1,0:T(8,128)(2,1)S(1)}, u32[]{:S(2)}, u32[]{:S(2)}) collective-permute-start(bf16[4,512,128]{2,1,0:T(8,128)(2,1)} %collective-permute-done.12), channel_id=1, source_target_pairs={{0,32},{1,97},{32,64},{33,1},{64,96},{65,33},{96,0},{97,65},{2,34}... | collective-permute-start | bytes 1572872 | tf_op jit(solution)/shard_map/ppermute | solution.py:333
  86.6 4.8 %all-to-all-start.1 = ((f32[32,8,512]{2,1,0:T(8,128)}), f32[32,8,512]{2,1,0:T(8,128)S(1)}, u32[]{:S(2)}, u32[]{:S(2)}) async-start(f32[32,8,512]{2,1,0:T(8,128)} %get-tuple-element.37), calls=%async_computation.1 | async-start | bytes 1048576 | tf_op jit(solution)/shard_map/all_to_all | solution.py:366
  91.7 1.9 collective-permute-done.13.refs_4_
  93.6 9.5 %all-to-all-done.1.all_ref = f32[32,8,512]{2,1,0:T(8,128)S(1)} async-done(((f32[32,8,512]{2,1,0:T(8,128)}), f32[32,8,512]{2,1,0:T(8,128)S(1)}, u32[]{:S(2)}, u32[]{:S(2)}) %all-to-all-start.1) | async-done | bytes 524320 | tf_op jit(solution)/shard_map/all_to_all | solution.py:366
  103.1 0.8 copy-done.1
  103.9 5.2 %shard_map.70 = (bf16[1216,512]{1,0:T(8,128)(2,1)}, f32[1,512]{1,0:T(1,128)}) custom-call(f32[32,8,512]{2,1,0:T(8,128)} %copy-done.1, f32[1,512]{1,0:T(1,128)} %bitcast.30, f32[2560,512]{1,0:T(8,128)} %get-tuple-element.35.s_ref, bf16[2560,512]{1,0:T(8,128)(2,1)} %get-tuple-element.43.t_ref), custom_call_target="tpu_custom_call" | custom-call | flops 1048576 | bytes 65536 | tf_op jit(solution)/shard_map/pallas_call | solution.py:222
  109.2 0.5 collective-permute-start.15
  109.8 5.1 %shard_map.71 = (bf16[304,512]{1,0:T(8,128)(2,1)}, bf16[912,512]{1,0:T(8,128)(2,1)}, f32[1,512]{1,0:T(1,128)}) custom-call(f32[32,8,512]{2,1,0:T(8,128)} %copy-done.1, f32[1,512]{1,0:T(1,128)} %bitcast.31, f32[2560,512]{1,0:T(8,128)} %get-tuple-element.35.s_ref, bf16[2560,512]{1,0:T(8,128)(2,1)} %get-tuple-element.43.t_ref), custom_call_target="tpu_custom_call" | custom-call | flops 1048576 | bytes 65536 | tf_op jit(solution)/shard_map/pallas_call | solution.py:222
  115.0 17.8 %shard_map.72 = (bf16[4,4,512,128]{3,2,1,0:T(8,128)(2,1)}, bf16[4,4,512,128]{3,2,1,0:T(8,128)(2,1)}) custom-call(s32[4]{0:T(128)} %pad_add_fusion.pos, bf16[1216,512]{1,0:T(8,128)(2,1)} %get-tuple-element.45.refs_0_, bf16[304,512]{1,0:T(8,128)(2,1)} %get-tuple-element.47.refs_1_, bf16[912,512]{1,0:T(8,128)(2,1)} %get-tuple-element.48.refs_2_.refs_0_, ...), custom_call_target="tpu_custom_call" | custom-call | flops 1048576 | bytes 65536 | tf_op jit(solution)/shard_map/pallas_call | solution.py:256
  132.8 0.8 copy-done.14
  133.9 6.0 %shard_map.73.refs_4_ = bf16[2048,1024]{1,0:T(8,128)(2,1)} custom-call(s32[4]{0:T(128)} %pad_add_fusion.pos, bf16[512,1024]{1,0:T(8,128)(2,1)} %get-tuple-element.52.h_ref, bf16[4,512,128]{2,1,0:T(8,128)(2,1)} %copy-done.7, bf16[4,512,128]{2,1,0:T(8,128)(2,1)} %copy-done.12, bf16[4,512,128]{2,1,0:T(8,128)(2,1)} %copy-done.8, ...), custom_call_target="tpu_custom_call" | custom-call | flops 1048576 | bytes 65536 | tf_op jit(solution)/shard_map/pallas_call | solution.py:280
  140.3 4.0 %collective-permute-done.17 = bf16[4,4,512,128]{3,2,1,0:T(8,128)(2,1)S(1)} collective-permute-done((bf16[4,4,512,128]{3,2,1,0:T(8,128)(2,1)}, bf16[4,4,512,128]{3,2,1,0:T(8,128)(2,1)S(1)}, u32[]{:S(2)}, u32[]{:S(2)}) %collective-permute-start.17) | collective-permute-done | bytes 2097184 | tf_op jit(solution)/shard_map/ppermute | solution.py:337
  144.3 1.8 add_convert_fusion
  146.2 3.9 %all-to-all-start.2 = ((bf16[16,512,128]{2,1,0:T(8,128)(2,1)}), bf16[16,512,128]{2,1,0:T(8,128)(2,1)S(1)}, u32[]{:S(2)}, u32[]{:S(2)}) async-start(bf16[16,512,128]{2,1,0:T(8,128)(2,1)} %bitcast.11), calls=%async_computation.2 | async-start | bytes 4194304 | tf_op jit(solution)/shard_map/all_to_all | solution.py:388
  150.1 0.7 all-gather.7.cloned.1.call-update
  150.8 1.1 collective-permute-start.18
  151.9 1.7 collective-permute-start.19
  153.5 27.2 %collective-permute-done.18.refs_1_ = bf16[912,512]{1,0:T(8,128)(2,1)S(1)} collective-permute-done((bf16[912,512]{1,0:T(8,128)(2,1)S(1)}, bf16[912,512]{1,0:T(8,128)(2,1)S(1)}, u32[]{:S(2)}, u32[]{:S(2)}) %collective-permute-start.18) | collective-permute-done | bytes 933920 | tf_op jit(solution)/shard_map/ppermute | solution.py:329
  180.7 0.9 slice.8
  182.0 0.9 copy-done.6
  182.9 2.4 %collective-permute-start.21 = (bf16[448,512]{1,0:T(8,128)(2,1)S(1)}, bf16[448,512]{1,0:T(8,128)(2,1)S(1)}, u32[]{:S(2)}, u32[]{:S(2)}) collective-permute-start(bf16[448,512]{1,0:T(8,128)(2,1)S(1)} %slice.9), channel_id=1, source_target_pairs={{0,96},{32,0},{64,32},{96,64},{1,97},{33,1},{65,33},{97,65},{2,98}... | collective-permute-start | bytes 1376264 | tf_op jit(solution)/shard_map/ppermute | solution.py:329
  185.3 10.5 %shard_map.74.refs_5_ = bf16[2374,1024]{1,0:T(8,128)(2,1)} custom-call(s32[4]{0:T(128)} %pad_add_fusion.pos, bf16[4,1216,512]{2,1,0:T(8,128)(2,1)} %bitcast.15, bf16[4,1216,512]{2,1,0:T(8,128)(2,1)} %bitcast.16, bf16[4,1216,512]{2,1,0:T(8,128)(2,1)} %bitcast.17, bf16[4,1216,512]{2,1,0:T(8,128)(2,1)} %bitcast.18, bf16[2048,1024]{1,0:T(8,128)(2,1)} %shard_map.73.refs_4_), custom_call_target="tpu_custom_call" | custom-call | flops 1048576 | bytes 65536 | tf_op jit(solution)/shard_map/pallas_call | solution.py:315
  195.7 6.2 %collective-permute-done.21 = bf16[448,512]{1,0:T(8,128)(2,1)S(1)} collective-permute-done((bf16[448,512]{1,0:T(8,128)(2,1)S(1)}, bf16[448,512]{1,0:T(8,128)(2,1)S(1)}, u32[]{:S(2)}, u32[]{:S(2)}) %collective-permute-start.21) | collective-permute-done | bytes 458784 | tf_op jit(solution)/shard_map/ppermute | solution.py:329
  202.0 1.4 collective-permute-done.20
  203.4 1.1 pad_maximum_fusion.refs_3_
  204.4 8.6 %shard_map.75.refs_5_ = bf16[2374,1024]{1,0:T(8,128)(2,1)} custom-call(s32[4]{0:T(128)} %pad_add_fusion.pos, bf16[912,512]{1,0:T(8,128)(2,1)} %get-tuple-element.48.refs_2_.refs_0_, bf16[912,512]{1,0:T(8,128)(2,1)} %copy-done.3, bf16[912,512]{1,0:T(8,128)(2,1)} %copy-done.6, ...), custom_call_target="tpu_custom_call", output_to_operand_aliasing={{}: (6, {})} | custom-call | flops 1048576 | bytes 65536 | tf_op jit(solution)/shard_map/pallas_call | solution.py:315
  213.0 1.0 reduce_sum.12
  214.0 5.4 %shard_map.76 = bf16[2374,1024]{1,0:T(8,128)(2,1)} custom-call(s32[4]{0:T(128)} %pad_add_fusion.pos, bf16[4,304,512]{2,1,0:T(8,128)(2,1)} %bitcast.22, bf16[4,304,512]{2,1,0:T(8,128)(2,1)} %bitcast.23, bf16[4,304,512]{2,1,0:T(8,128)(2,1)} %bitcast.24, bf16[4,304,512]{2,1,0:T(8,128)(2,1)} %bitcast.25, ...), custom_call_target="tpu_custom_call", output_to_operand_aliasing={{}: (6, {})} | custom-call | flops 1048576 | bytes 65536 | tf_op jit(solution)/shard_map/pallas_call | solution.py:315
  (57 shorter events, 3.8 us)
Async XLA Ops:
  7.2 10.9 %copy-start.15 = (bf16[512,128]{1,0:T(8,128)(2,1)S(1)}, bf16[512,128]{1,0:T(8,128)(2,1)}, u32[]{:S(2)}) copy-start(bf16[512,128]{1,0:T(8,128)(2,1)} %param.4) | copy-start | bytes 393220
  7.2 9.1 %collective-permute-start.2 = (bf16[512,128]{1,0:T(8,128)(2,1)}, bf16[512,128]{1,0:T(8,128)(2,1)S(1)}, u32[]{:S(2)}, u32[]{:S(2)}) collective-permute-start(bf16[512,128]{1,0:T(8,128)(2,1)} %param.4), channel_id=1, source_target_pairs={{0,6},{1,25},{2,0},{3,27},{4,2},{5,29},{6,4},{7,31},{8,14},{9,1},{... | collective-permute-start | bytes 393224 | tf_op jit(solution)/shard_map/ppermute | solution.py:349
  10.8 5.6 %collective-permute-start.1 = (bf16[512,128]{1,0:T(8,128)(2,1)}, bf16[512,128]{1,0:T(8,128)(2,1)S(1)}, u32[]{:S(2)}, u32[]{:S(2)}) collective-permute-start(bf16[512,128]{1,0:T(8,128)(2,1)} %param.4), channel_id=1, source_target_pairs={{0,4},{1,17},{2,6},{3,19},{4,0},{5,21},{6,2},{7,23},{8,12},{9,25},... | collective-permute-start | bytes 393224 | tf_op jit(solution)/shard_map/ppermute | solution.py:349
  11.2 6.9 %collective-permute-start = (bf16[512,128]{1,0:T(8,128)(2,1)}, bf16[512,128]{1,0:T(8,128)(2,1)S(1)}, u32[]{:S(2)}, u32[]{:S(2)}) collective-permute-start(bf16[512,128]{1,0:T(8,128)(2,1)} %param.4), channel_id=1, source_target_pairs={{0,2},{1,9},{2,4},{3,11},{4,6},{5,13},{6,0},{7,15},{8,10},{9,17},{... | collective-permute-start | bytes 393224 | tf_op jit(solution)/shard_map/ppermute | solution.py:349
  18.1 24.6 %copy-start.5 = (bf16[4,512,128]{2,1,0:T(8,128)(2,1)}, bf16[4,512,128]{2,1,0:T(8,128)(2,1)S(1)}, u32[]{:S(2)}) copy-start(bf16[4,512,128]{2,1,0:T(8,128)(2,1)S(1)} %pad_maximum_fusion.1.refs_0_) | copy-start | bytes 1572868
  18.1 10.4 %collective-permute-start.3 = (bf16[4,512,128]{2,1,0:T(8,128)(2,1)S(1)}, bf16[4,512,128]{2,1,0:T(8,128)(2,1)S(1)}, u32[]{:S(2)}, u32[]{:S(2)}) collective-permute-start(bf16[4,512,128]{2,1,0:T(8,128)(2,1)S(1)} %pad_maximum_fusion.1.refs_0_), channel_id=1, source_target_pairs={{0,8},{1,3},{2,10},{3,5},{4,12},{5,7},{6,14},{7,1},{8,16},{9,11},{... | collective-permute-start | bytes 1572872 | tf_op jit(solution)/shard_map/ppermute | solution.py:349
  19.5 15.8 %collective-permute-start.4 = (bf16[4,512,128]{2,1,0:T(8,128)(2,1)S(1)}, bf16[4,512,128]{2,1,0:T(8,128)(2,1)S(1)}, u32[]{:S(2)}, u32[]{:S(2)}) collective-permute-start(bf16[4,512,128]{2,1,0:T(8,128)(2,1)S(1)} %pad_maximum_fusion.1.refs_0_), channel_id=1, source_target_pairs={{0,16},{1,5},{2,18},{3,7},{4,20},{5,1},{6,22},{7,3},{8,24},{9,13},... | collective-permute-start | bytes 1572872 | tf_op jit(solution)/shard_map/ppermute | solution.py:349
  22.8 13.3 %collective-permute-start.5 = (bf16[4,512,128]{2,1,0:T(8,128)(2,1)S(1)}, bf16[4,512,128]{2,1,0:T(8,128)(2,1)}, u32[]{:S(2)}, u32[]{:S(2)}) collective-permute-start(bf16[4,512,128]{2,1,0:T(8,128)(2,1)S(1)} %pad_maximum_fusion.1.refs_0_), channel_id=1, source_target_pairs={{0,24},{1,7},{2,26},{3,1},{4,28},{5,3},{6,30},{7,5},{8,0},{9,15},{... | collective-permute-start | bytes 1572872 | tf_op jit(solution)/shard_map/ppermute | solution.py:349
  28.5 14.5 %copy-start.9 = (bf16[4,512,128]{2,1,0:T(8,128)(2,1)}, bf16[4,512,128]{2,1,0:T(8,128)(2,1)S(1)}, u32[]{:S(2)}) copy-start(bf16[4,512,128]{2,1,0:T(8,128)(2,1)S(1)} %collective-permute-done.3.refs_1_) | copy-start | bytes 1572868
  35.3 0.8 copy-start.10
  36.2 39.1 %all-to-all-start = ((bf16[32,19,16,128]{3,2,1,0:T(8,128)(2,1)}), bf16[32,19,16,128]{3,2,1,0:T(8,128)(2,1)S(1)}, u32[]{:S(2)}, u32[]{:S(2)}) async-start(bf16[32,19,16,128]{3,2,1,0:T(8,128)(2,1)} %shard_map.67), calls=%async_computation | async-start | bytes 4980736 | tf_op jit(solution)/shard_map/all_to_all | solution.py:363
  42.7 2.1 collective-permute-start.6
  43.1 3.3 %collective-permute-start.7 = (bf16[4,512,128]{2,1,0:T(8,128)(2,1)S(1)}, bf16[4,512,128]{2,1,0:T(8,128)(2,1)}, u32[]{:S(2)}, u32[]{:S(2)}) collective-permute-start(bf16[4,512,128]{2,1,0:T(8,128)(2,1)S(1)} %collective-permute-done.3.refs_1_), channel_id=1, source_target_pairs={{0,1},{1,0},{2,3},{3,2},{4,5},{5,4},{6,7},{7,6},{8,9},{9,8},{10,11... | collective-permute-start | bytes 1572872 | tf_op jit(solution)/shard_map/ppermute | solution.py:337
  43.3 3.2 %collective-permute-start.8 = (bf16[4,512,128]{2,1,0:T(8,128)(2,1)}, bf16[4,512,128]{2,1,0:T(8,128)(2,1)}, u32[]{:S(2)}, u32[]{:S(2)}) collective-permute-start(bf16[4,512,128]{2,1,0:T(8,128)(2,1)} %copy-done.10), channel_id=1, source_target_pairs={{0,1},{1,0},{2,3},{3,2},{4,5},{5,4},{6,7},{7,6},{8,9},{9,8},{10,11... | collective-permute-start | bytes 1572872 | tf_op jit(solution)/shard_map/ppermute | solution.py:337
  43.6 3.8 %collective-permute-start.9 = (bf16[4,512,128]{2,1,0:T(8,128)(2,1)}, bf16[4,512,128]{2,1,0:T(8,128)(2,1)}, u32[]{:S(2)}, u32[]{:S(2)}) collective-permute-start(bf16[4,512,128]{2,1,0:T(8,128)(2,1)} %collective-permute-done.5.refs_3_), channel_id=1, source_target_pairs={{0,1},{1,0},{2,3},{3,2},{4,5},{5,4},{6,7},{7,6},{8,9},{9,8},{10,11... | collective-permute-start | bytes 1572872 | tf_op jit(solution)/shard_map/ppermute | solution.py:337
  67.8 16.3 %collective-permute-start.12 = (bf16[4,512,128]{2,1,0:T(8,128)(2,1)}, bf16[4,512,128]{2,1,0:T(8,128)(2,1)}, u32[]{:S(2)}, u32[]{:S(2)}) collective-permute-start(bf16[4,512,128]{2,1,0:T(8,128)(2,1)} %get-tuple-element.40), channel_id=1, source_target_pairs={{0,32},{1,97},{32,64},{33,1},{64,96},{65,33},{96,0},{97,65},{2,34}... | collective-permute-start | bytes 1572872 | tf_op jit(solution)/shard_map/ppermute | solution.py:333
  70.3 21.4 %collective-permute-start.10 = (bf16[4,512,128]{2,1,0:T(8,128)(2,1)}, bf16[4,512,128]{2,1,0:T(8,128)(2,1)S(1)}, u32[]{:S(2)}, u32[]{:S(2)}) collective-permute-start(bf16[4,512,128]{2,1,0:T(8,128)(2,1)} %get-tuple-element.38), channel_id=1, source_target_pairs={{0,32},{32,64},{64,96},{96,0},{1,33},{33,65},{65,97},{97,1},{2,34}... | collective-permute-start | bytes 1572872 | tf_op jit(solution)/shard_map/ppermute | solution.py:329
  70.3 21.4 %collective-permute-start.11 = (bf16[4,512,128]{2,1,0:T(8,128)(2,1)}, bf16[4,512,128]{2,1,0:T(8,128)(2,1)S(1)}, u32[]{:S(2)}, u32[]{:S(2)}) collective-permute-start(bf16[4,512,128]{2,1,0:T(8,128)(2,1)} %get-tuple-element.39), channel_id=1, source_target_pairs={{0,96},{32,0},{64,32},{96,64},{1,97},{33,1},{65,33},{97,65},{2,98}... | collective-permute-start | bytes 1572872 | tf_op jit(solution)/shard_map/ppermute | solution.py:329
  75.3 1.5 copy-start
  84.1 9.5 %collective-permute-start.13 = (bf16[4,512,128]{2,1,0:T(8,128)(2,1)}, bf16[4,512,128]{2,1,0:T(8,128)(2,1)S(1)}, u32[]{:S(2)}, u32[]{:S(2)}) collective-permute-start(bf16[4,512,128]{2,1,0:T(8,128)(2,1)} %collective-permute-done.12), channel_id=1, source_target_pairs={{0,32},{1,97},{32,64},{33,1},{64,96},{65,33},{96,0},{97,65},{2,34}... | collective-permute-start | bytes 1572872 | tf_op jit(solution)/shard_map/ppermute | solution.py:333
  86.6 16.4 %all-to-all-start.1 = ((f32[32,8,512]{2,1,0:T(8,128)}), f32[32,8,512]{2,1,0:T(8,128)S(1)}, u32[]{:S(2)}, u32[]{:S(2)}) async-start(f32[32,8,512]{2,1,0:T(8,128)} %get-tuple-element.37), calls=%async_computation.1 | async-start | bytes 1048576 | tf_op jit(solution)/shard_map/all_to_all | solution.py:366
  91.5 93.8 %all-gather.5.cloned.1.call-start = ((), (), s32[]{:S(2)}) async-start(), calls=%async_computation.3 | async-start | bytes 6225920 | tf_op jit(solution)/shard_map/all_gather | solution.py:381
  91.7 23.3 %copy-start.7 = (bf16[4,512,128]{2,1,0:T(8,128)(2,1)}, bf16[4,512,128]{2,1,0:T(8,128)(2,1)S(1)}, u32[]{:S(2)}) copy-start(bf16[4,512,128]{2,1,0:T(8,128)(2,1)S(1)} %collective-permute-done.10.refs_0_) | copy-start | bytes 1572868
  91.7 23.2 %copy-start.8 = (bf16[4,512,128]{2,1,0:T(8,128)(2,1)}, bf16[4,512,128]{2,1,0:T(8,128)(2,1)S(1)}, u32[]{:S(2)}) copy-start(bf16[4,512,128]{2,1,0:T(8,128)(2,1)S(1)} %collective-permute-done.11.refs_2_) | copy-start | bytes 1572868
  93.6 21.3 %copy-start.11 = (bf16[4,512,128]{2,1,0:T(8,128)(2,1)}, bf16[4,512,128]{2,1,0:T(8,128)(2,1)S(1)}, u32[]{:S(2)}) copy-start(bf16[4,512,128]{2,1,0:T(8,128)(2,1)S(1)} %collective-permute-done.13.refs_4_) | copy-start | bytes 1572868
  103.1 0.8 copy-start.1
  109.1 23.6 %collective-permute-start.14 = (bf16[4,512,128]{2,1,0:T(8,128)(2,1)S(1)}, bf16[4,512,128]{2,1,0:T(8,128)(2,1)S(1)}, u32[]{:S(2)}, u32[]{:S(2)}) collective-permute-start(bf16[4,512,128]{2,1,0:T(8,128)(2,1)S(1)} %collective-permute-done.10.refs_0_), channel_id=1, source_target_pairs={{0,1},{1,0},{2,3},{3,2},{4,5},{5,4},{6,7},{7,6},{8,9},{9,8},{10,11... | collective-permute-start | bytes 1572872 | tf_op jit(solution)/shard_map/ppermute | solution.py:337
  109.2 23.5 %collective-permute-start.15 = (bf16[4,512,128]{2,1,0:T(8,128)(2,1)S(1)}, bf16[4,512,128]{2,1,0:T(8,128)(2,1)S(1)}, u32[]{:S(2)}, u32[]{:S(2)}) collective-permute-start(bf16[4,512,128]{2,1,0:T(8,128)(2,1)S(1)} %collective-permute-done.11.refs_2_), channel_id=1, source_target_pairs={{0,1},{1,0},{2,3},{3,2},{4,5},{5,4},{6,7},{7,6},{8,9},{9,8},{10,11... | collective-permute-start | bytes 1572872 | tf_op jit(solution)/shard_map/ppermute | solution.py:337
  109.7 23.0 %collective-permute-start.16 = (bf16[4,512,128]{2,1,0:T(8,128)(2,1)S(1)}, bf16[4,512,128]{2,1,0:T(8,128)(2,1)S(1)}, u32[]{:S(2)}, u32[]{:S(2)}) collective-permute-start(bf16[4,512,128]{2,1,0:T(8,128)(2,1)S(1)} %collective-permute-done.13.refs_4_), channel_id=1, source_target_pairs={{0,1},{1,0},{2,3},{3,2},{4,5},{5,4},{6,7},{7,6},{8,9},{9,8},{10,11... | collective-permute-start | bytes 1572872 | tf_op jit(solution)/shard_map/ppermute | solution.py:337
  132.7 1.0 copy-start.12
  132.7 1.1 copy-start.13
  132.8 0.9 copy-start.14
  133.9 10.4 %copy-start.4 = (bf16[4,4,512,128]{3,2,1,0:T(8,128)(2,1)S(1)}, bf16[4,4,512,128]{3,2,1,0:T(8,128)(2,1)}, u32[]{:S(2)}) copy-start(bf16[4,4,512,128]{3,2,1,0:T(8,128)(2,1)} %get-tuple-element.49) | copy-start | bytes 6291460
  139.9 4.4 %collective-permute-start.17 = (bf16[4,4,512,128]{3,2,1,0:T(8,128)(2,1)}, bf16[4,4,512,128]{3,2,1,0:T(8,128)(2,1)S(1)}, u32[]{:S(2)}, u32[]{:S(2)}) collective-permute-start(bf16[4,4,512,128]{3,2,1,0:T(8,128)(2,1)} %get-tuple-element.56), channel_id=1, source_target_pairs={{0,1},{1,0},{2,3},{3,2},{4,5},{5,4},{6,7},{7,6},{8,9},{9,8},{10,11... | collective-permute-start | bytes 6291464 | tf_op jit(solution)/shard_map/ppermute | solution.py:337
  146.2 4.6 %copy-start.2 = (bf16[912,512]{1,0:T(8,128)(2,1)S(1)}, bf16[912,512]{1,0:T(8,128)(2,1)}, u32[]{:S(2)}) copy-start(bf16[912,512]{1,0:T(8,128)(2,1)} %get-tuple-element.48.refs_2_.refs_0_) | copy-start | bytes 2801668
  146.2 66.8 %all-to-all-start.2 = ((bf16[16,512,128]{2,1,0:T(8,128)(2,1)}), bf16[16,512,128]{2,1,0:T(8,128)(2,1)S(1)}, u32[]{:S(2)}, u32[]{:S(2)}) async-start(bf16[16,512,128]{2,1,0:T(8,128)(2,1)} %bitcast.11), calls=%async_computation.2 | async-start | bytes 4194304 | tf_op jit(solution)/shard_map/all_to_all | solution.py:388
  150.0 64.0 %all-gather.7.cloned.1.call-start = ((), (), s32[]{:S(2)}) async-start(), calls=%async_computation.4 | async-start | bytes 1556480 | tf_op jit(solution)/shard_map/all_gather | solution.py:381
  150.8 29.9 %collective-permute-start.18 = (bf16[912,512]{1,0:T(8,128)(2,1)S(1)}, bf16[912,512]{1,0:T(8,128)(2,1)S(1)}, u32[]{:S(2)}, u32[]{:S(2)}) collective-permute-start(bf16[912,512]{1,0:T(8,128)(2,1)S(1)} %copy-done.2), channel_id=1, source_target_pairs={{0,32},{32,64},{64,96},{96,0},{1,33},{33,65},{65,97},{97,1},{2,34}... | collective-permute-start | bytes 2801672 | tf_op jit(solution)/shard_map/ppermute | solution.py:329
  151.9 29.7 %collective-permute-start.19 = (bf16[912,512]{1,0:T(8,128)(2,1)S(1)}, bf16[912,512]{1,0:T(8,128)(2,1)S(1)}, u32[]{:S(2)}, u32[]{:S(2)}) collective-permute-start(bf16[912,512]{1,0:T(8,128)(2,1)S(1)} %copy-done.2), channel_id=1, source_target_pairs={{0,96},{32,0},{64,32},{96,64},{1,97},{33,1},{65,33},{97,65},{2,98}... | collective-permute-start | bytes 2801672 | tf_op jit(solution)/shard_map/ppermute | solution.py:329
  180.7 1.2 copy-start.3
  181.6 21.8 %collective-permute-start.20 = (bf16[464,512]{1,0:T(8,128)(2,1)}, bf16[464,512]{1,0:T(8,128)(2,1)S(1)}, u32[]{:S(2)}, u32[]{:S(2)}) collective-permute-start(bf16[464,512]{1,0:T(8,128)(2,1)} %slice.8), channel_id=1, source_target_pairs={{0,32},{32,64},{64,96},{96,0},{1,33},{33,65},{65,97},{97,1},{2,34}... | collective-permute-start | bytes 1425416 | tf_op jit(solution)/shard_map/ppermute | solution.py:329
  181.9 1.0 copy-start.6
  182.9 19.1 %collective-permute-start.21 = (bf16[448,512]{1,0:T(8,128)(2,1)S(1)}, bf16[448,512]{1,0:T(8,128)(2,1)S(1)}, u32[]{:S(2)}, u32[]{:S(2)}) collective-permute-start(bf16[448,512]{1,0:T(8,128)(2,1)S(1)} %slice.9), channel_id=1, source_target_pairs={{0,96},{32,0},{64,32},{96,64},{1,97},{33,1},{65,33},{97,65},{2,98}... | collective-permute-start | bytes 1376264 | tf_op jit(solution)/shard_map/ppermute | solution.py:329
Sparse Core Ops, SparseCore 0:
  109.2 57.5 all-gather.4
  168.5 32.3 all-gather.6
